TPU v7x, 32 devices: a whole 2x2x4 slice. The times are simulated.
32 devices in a mesh: dp: 8 (over y, x, core), tensor: 4 (over z).
Axes of the slice: x: 2, y: 2, z: 4, core: 2. Of those that a mesh axis runs over, the one named last changes fastest.
Arguments:
- tokens: bfloat16 [2, 8192, 2048], P(None, 'dp', 'tensor'), may hold values from -6 to 6
- cotangent: bfloat16 [2, 8192, 2048], P(None, 'dp', 'tensor'), may hold values from -6 to 6
- lengths: int32 [2, 8, 3], replicated, may hold values from 1 to 819, 1024 in all within a row
- dealing: int32 [2, 24], replicated, may hold values from 0 to 23, each once within a row
- query_weight: bfloat16 [2048, 2048], P(None, 'tensor'), may hold values from -0.125 to 0.125
- key_weight: bfloat16 [2048, 2048], P(None, 'tensor'), may hold values from -0.125 to 0.125
- value_weight: bfloat16 [2048, 2048], P(None, 'tensor'), may hold values from -0.125 to 0.125
- out_weight: bfloat16 [2048, 2048], P('tensor'), may hold values from -0.5 to 0.5
- query_bias: bfloat16 [2048], P('tensor'), may hold values from -4 to 4
- value_bias: bfloat16 [2048], P('tensor'), may hold values from -1.5 to 1.5
- out_bias: bfloat16 [2048], replicated, may hold values from -4 to 4
- up_weight: bfloat16 [2048, 8192], P(None, 'tensor'), may hold values from -0.125 to 0.125
- up_bias: bfloat16 [8192], P('tensor'), may hold values from -4 to 4
- down_weight: bfloat16 [8192, 2048], P('tensor'), may hold values from -0.0625 to 0.0625
- down_bias: bfloat16 [2048], replicated, may hold values from -4 to 4
- attn_gain: bfloat16 [2048], replicated, may hold values from 0.5 to 1.5
- attn_shift: bfloat16 [2048], replicated, may hold values from -3 to 3
- mlp_gain: bfloat16 [2048], replicated, may hold values from 0.5 to 1.5
- mlp_shift: bfloat16 [2048], replicated, may hold values from -3 to 3
Outputs:
- layer_out: bfloat16 [2, 8192, 2048], P(None, 'dp', 'tensor')
- input_grad: bfloat16 [2, 8192, 2048], P(None, 'dp', 'tensor')
- query_weight_grad: float32 [2048, 2048], P(None, 'tensor')
- key_weight_grad: float32 [2048, 2048], P(None, 'tensor')
- value_weight_grad: float32 [2048, 2048], P(None, 'tensor')
- out_weight_grad: float32 [2048, 2048], P('tensor')
- query_bias_grad: float32 [2048], P('tensor')
- value_bias_grad: float32 [2048], P('tensor')
- out_bias_grad: float32 [2048], replicated
- up_weight_grad: float32 [2048, 8192], P(None, 'tensor')
- up_bias_grad: float32 [8192], P('tensor')
- down_weight_grad: float32 [8192, 2048], P('tensor')
- down_bias_grad: float32 [2048], replicated
- attn_gain_grad: float32 [2048], replicated
- attn_shift_grad: float32 [2048], replicated
- mlp_gain_grad: float32 [2048], replicated
- mlp_shift_grad: float32 [2048], replicated
Inputs may be any that keep to these rules, and one draw needn't show every extreme that they name: The 3 lengths of one data index in a micro-batch add up to 1024, and the longest of them is exactly 819. Each row of dealing names every sequence number once.
All inputs are finite; a program needn't handle non-finite values.
Results may differ from a plain program's by a relative error of at most 0.014.
Values may be sent and summed in bfloat16 or wider, within the bound.
A program may use at most 448 MiB of HBM per device.

v0:
```python
import jax
import jax.numpy as jnp
from jax import lax
from jax.sharding import PartitionSpec as P

HEAD_DIM = 64
SEG = 512
SUMM = 50
NBLK = 2


NORM_EPS = 1e-05
MASKED = -1e30


def gelu_tanh(values):
    return jax.nn.gelu(values, approximate=True)


def matmul(left_array, right_array):
    return jnp.dot(left_array, right_array, preferred_element_type=jnp.float32)


def cross_rows(left_array, right_array):
    return lax.dot_general(
        left_array, right_array, (((0,), (0,)), ((), ())), preferred_element_type=jnp.float32
    )


def times_transpose(left_array, right_array):
    return lax.dot_general(
        left_array, right_array, (((1,), (1,)), ((), ())), preferred_element_type=jnp.float32
    )


def normalize(values):
    center = jnp.mean(values, axis=1, keepdims=True)
    shifted = values - center
    spread = jnp.mean(shifted * shifted, axis=1, keepdims=True)
    inverse = lax.rsqrt(spread + NORM_EPS)
    return (shifted * inverse, inverse)


def norm_backward(grad_in, normed, inverse, gain_row):
    gain_grad = jnp.sum(grad_in * normed, axis=0)
    shift_grad = jnp.sum(grad_in, axis=0)
    scaled = grad_in * gain_row
    first_mean = jnp.mean(scaled, axis=1, keepdims=True)
    second_mean = jnp.mean(scaled * normed, axis=1, keepdims=True)
    return (inverse * (scaled - first_mean - normed * second_mean), gain_grad, shift_grad)


def given_layout(lengths_mb, dealing_mb):
    seq_count = dealing_mb.shape[0]
    labels = jnp.arange(seq_count, dtype=jnp.int32)
    flat_lengths = lengths_mb.reshape(seq_count)
    one_hot = (dealing_mb[:, None] == labels[None, :]).astype(jnp.int32)
    given_len = jnp.sum(one_hot * flat_lengths[None, :], axis=1, dtype=jnp.int32)
    given_off = jnp.cumsum(given_len, dtype=jnp.int32) - given_len
    start_by_seq = jnp.sum(one_hot * given_off[:, None], axis=0, dtype=jnp.int32)
    return (given_len, given_off, start_by_seq)


def buffer_layout(lengths_dev, start_dev, rows_total):
    seq_count = lengths_dev.shape[0]
    end_rows = jnp.cumsum(lengths_dev, dtype=jnp.int32)
    offsets = end_rows - lengths_dev
    row_ids = jnp.arange(rows_total, dtype=jnp.int32)
    holder = jnp.sum(
        (row_ids[:, None] >= end_rows[None, :]).astype(jnp.int32), axis=1, dtype=jnp.int32
    )
    one_hot = (holder[:, None] == jnp.arange(seq_count, dtype=jnp.int32)[None, :]).astype(jnp.int32)
    position = row_ids - jnp.sum(one_hot * offsets[None, :], axis=1, dtype=jnp.int32)
    source = jnp.sum(one_hot * start_dev[None, :], axis=1, dtype=jnp.int32) + position
    return (holder, position, source)


def visible(holder, position, first_row, last_row, key_reach):
    period = SEG + SUMM
    query_seq = holder[first_row:last_row, None]
    key_seq = holder[None, :key_reach]
    query_part = position[first_row:last_row, None] // period
    key_part = position[None, :key_reach] // period
    summary = position[None, :key_reach] % period >= SEG
    query_row = jnp.arange(first_row, last_row, dtype=jnp.int32)[:, None]
    key_row = jnp.arange(key_reach, dtype=jnp.int32)[None, :]
    same_part = (query_part == key_part) & (key_row <= query_row)
    earlier = (key_part < query_part) & summary
    return (query_seq == key_seq) & (same_part | earlier)


def block_scores(queries, keys_all, allowed, score_scale):
    scores = (
        jnp.einsum("qhd,khd->hqk", queries, keys_all, preferred_element_type=jnp.float32)
        * score_scale
    )
    return jnp.where(allowed[None], scores, MASKED)


def shards(
    tokens,
    cotangent,
    lengths,
    dealing,
    query_weight,
    key_weight,
    value_weight,
    out_weight,
    query_bias,
    value_bias,
    out_bias,
    up_weight,
    up_bias,
    down_weight,
    down_bias,
    attn_gain,
    attn_shift,
    mlp_gain,
    mlp_shift,
):
    micro_count = tokens.shape[0]
    tok_rows = tokens.shape[1]
    col_width = tokens.shape[2]
    seq_dev = lengths.shape[2]
    heads_here = query_weight.shape[1] // HEAD_DIM
    head_cols = heads_here * HEAD_DIM
    block_rows = tok_rows // NBLK
    score_scale = HEAD_DIM ** (-0.5)
    device = lax.axis_index("dp")
    column = lax.axis_index("tensor")
    gain_one = attn_gain.astype(jnp.float32)
    shift_one = attn_shift.astype(jnp.float32)
    gain_two = mlp_gain.astype(jnp.float32)
    shift_two = mlp_shift.astype(jnp.float32)
    query_bias_f = query_bias.astype(jnp.float32)
    value_bias_f = value_bias.astype(jnp.float32)
    up_bias_f = up_bias.astype(jnp.float32)
    out_bias_cols = lax.dynamic_slice_in_dim(
        out_bias.astype(jnp.float32), column * col_width, col_width
    )
    down_bias_cols = lax.dynamic_slice_in_dim(
        down_bias.astype(jnp.float32), column * col_width, col_width
    )
    query_w_grad = jnp.zeros(query_weight.shape, jnp.float32)
    key_w_grad = jnp.zeros(key_weight.shape, jnp.float32)
    value_w_grad = jnp.zeros(value_weight.shape, jnp.float32)
    out_w_grad = jnp.zeros(out_weight.shape, jnp.float32)
    query_b_grad = jnp.zeros(query_bias.shape, jnp.float32)
    value_b_grad = jnp.zeros(value_bias.shape, jnp.float32)
    out_b_grad = jnp.zeros(out_bias.shape, jnp.float32)
    up_w_grad = jnp.zeros(up_weight.shape, jnp.float32)
    up_b_grad = jnp.zeros(up_bias.shape, jnp.float32)
    down_w_grad = jnp.zeros(down_weight.shape, jnp.float32)
    down_b_grad = jnp.zeros(down_bias.shape, jnp.float32)
    gain_one_grad = jnp.zeros(attn_gain.shape, jnp.float32)
    shift_one_grad = jnp.zeros(attn_shift.shape, jnp.float32)
    gain_two_grad = jnp.zeros(mlp_gain.shape, jnp.float32)
    shift_two_grad = jnp.zeros(mlp_shift.shape, jnp.float32)
    layer_parts = []
    grad_parts = []
    for micro_step in range(micro_count):
        lengths_mb = lengths[micro_step]
        dealing_mb = dealing[micro_step]
        given_len, given_off, start_by_seq = given_layout(lengths_mb, dealing_mb)
        lengths_dev = lax.dynamic_index_in_dim(lengths_mb, device, 0, keepdims=False)
        start_dev = lax.dynamic_slice_in_dim(start_by_seq, device * seq_dev, seq_dev)
        holder, position, source = buffer_layout(lengths_dev, start_dev, tok_rows)
        blank_rows = jnp.zeros((tok_rows, col_width), jnp.bfloat16)
        pieces = (
            lax.all_gather(tokens[micro_step], "dp", axis=0, tiled=True),
            lax.all_gather(cotangent[micro_step], "dp", axis=0, tiled=True),
        )
        span_rows = pieces[0].shape[0]
        inside = ((source >= 0) & (source < span_rows))[:, None]
        fetch_at = jnp.clip(source, 0, span_rows - 1)
        tok_buf = jnp.where(inside, jnp.take(pieces[0], fetch_at, axis=0), blank_rows)
        cot_buf = jnp.where(inside, jnp.take(pieces[1], fetch_at, axis=0), blank_rows)
        tok_full, cot_full = (
            lax.all_gather(tok_buf, "tensor", axis=1, tiled=True),
            lax.all_gather(cot_buf, "tensor", axis=1, tiled=True),
        )
        normed_one, inverse_one = normalize(tok_full.astype(jnp.float32))
        first_in = (normed_one * gain_one + shift_one).astype(jnp.bfloat16)
        queries = (
            (matmul(first_in, query_weight) + query_bias_f)
            .astype(jnp.bfloat16)
            .reshape(tok_rows, heads_here, HEAD_DIM)
        )
        keys_here = (
            matmul(first_in, key_weight)
            .astype(jnp.bfloat16)
            .reshape(tok_rows, heads_here, HEAD_DIM)
        )
        values_here = (
            (matmul(first_in, value_weight) + value_bias_f)
            .astype(jnp.bfloat16)
            .reshape(tok_rows, heads_here, HEAD_DIM)
        )
        outputs = []
        row_tops = []
        row_totals = []
        for block_index in range(NBLK):
            row_lower = block_index * block_rows
            row_upper = row_lower + block_rows
            allowed = visible(holder, position, row_lower, row_upper, row_upper)
            scores = block_scores(
                queries[row_lower:row_upper], keys_here[:row_upper], allowed, score_scale
            )
            row_top = jnp.max(scores, axis=2, keepdims=True)
            exp_terms = jnp.exp(scores - row_top)
            row_total = jnp.sum(exp_terms, axis=2, keepdims=True)
            attn_prob = exp_terms / row_total
            outputs.append(
                jnp.einsum(
                    "hqk,khd->qhd",
                    attn_prob.astype(jnp.bfloat16),
                    values_here[:row_upper],
                    preferred_element_type=jnp.float32,
                )
            )
            row_tops.append(row_top)
            row_totals.append(row_total)
        mixed_heads = (
            jnp.concatenate(outputs, axis=0).reshape(tok_rows, head_cols).astype(jnp.bfloat16)
        )
        attn_cols = lax.psum_scatter(
            matmul(mixed_heads, out_weight), "tensor", scatter_dimension=1, tiled=True
        )
        resid_cols = tok_buf.astype(jnp.float32) + attn_cols + out_bias_cols
        resid_full = lax.all_gather(resid_cols.astype(jnp.bfloat16), "tensor", axis=1, tiled=True)
        normed_two, inverse_two = normalize(resid_full.astype(jnp.float32))
        second_in = (normed_two * gain_two + shift_two).astype(jnp.bfloat16)
        hidden_pre = matmul(second_in, up_weight) + up_bias_f
        hidden_act, gelu_pull = jax.vjp(gelu_tanh, hidden_pre)
        hidden = hidden_act.astype(jnp.bfloat16)
        mlp_cols = lax.psum_scatter(
            matmul(hidden, down_weight).astype(jnp.bfloat16),
            "tensor",
            scatter_dimension=1,
            tiled=True,
        ).astype(jnp.float32)
        layer_cols = (resid_cols + mlp_cols + down_bias_cols).astype(jnp.bfloat16)
        grad_out = cot_full.astype(jnp.float32)
        down_w_grad = down_w_grad + cross_rows(hidden, cot_full)
        down_b_grad = down_b_grad + jnp.sum(grad_out, axis=0)
        hidden_grad = gelu_pull(times_transpose(cot_full, down_weight))[0]
        up_b_grad = up_b_grad + jnp.sum(hidden_grad, axis=0)
        hidden_low = hidden_grad.astype(jnp.bfloat16)
        up_w_grad = up_w_grad + cross_rows(second_in, hidden_low)
        second_cols = lax.psum_scatter(
            times_transpose(hidden_low, up_weight), "tensor", scatter_dimension=1, tiled=True
        )
        second_grad = lax.all_gather(
            second_cols.astype(jnp.bfloat16), "tensor", axis=1, tiled=True
        ).astype(jnp.float32)
        resid_back, gain_part, shift_part = norm_backward(
            second_grad, normed_two, inverse_two, gain_two
        )
        gain_two_grad = gain_two_grad + gain_part
        shift_two_grad = shift_two_grad + shift_part
        resid_grad = grad_out + resid_back
        out_b_grad = out_b_grad + jnp.sum(resid_grad, axis=0)
        attn_low = resid_grad.astype(jnp.bfloat16)
        out_w_grad = out_w_grad + cross_rows(mixed_heads, attn_low)
        mixed_grad = (
            times_transpose(attn_low, out_weight)
            .astype(jnp.bfloat16)
            .reshape(tok_rows, heads_here, HEAD_DIM)
        )
        query_parts = []
        key_acc = jnp.zeros((tok_rows, heads_here, HEAD_DIM), jnp.float32)
        value_acc = jnp.zeros((tok_rows, heads_here, HEAD_DIM), jnp.float32)
        for block_index in range(NBLK):
            row_lower = block_index * block_rows
            row_upper = row_lower + block_rows
            allowed = visible(holder, position, row_lower, row_upper, row_upper)
            scores = block_scores(
                queries[row_lower:row_upper], keys_here[:row_upper], allowed, score_scale
            )
            attn_prob = jnp.exp(scores - row_tops[block_index]) / row_totals[block_index]
            grad_block = mixed_grad[row_lower:row_upper]
            prob_grad = jnp.einsum(
                "qhd,khd->hqk",
                grad_block,
                values_here[:row_upper],
                preferred_element_type=jnp.float32,
            )
            inner_sum = jnp.sum(attn_prob * prob_grad, axis=2, keepdims=True)
            score_grad = (attn_prob * (prob_grad - inner_sum)).astype(jnp.bfloat16)
            query_parts.append(
                jnp.einsum(
                    "hqk,khd->qhd",
                    score_grad,
                    keys_here[:row_upper],
                    preferred_element_type=jnp.float32,
                )
                * score_scale
            )
            pad_rows = ((0, tok_rows - row_upper), (0, 0), (0, 0))
            key_acc = key_acc + jnp.pad(
                jnp.einsum(
                    "hqk,qhd->khd",
                    score_grad,
                    queries[row_lower:row_upper],
                    preferred_element_type=jnp.float32,
                )
                * score_scale,
                pad_rows,
            )
            value_acc = value_acc + jnp.pad(
                jnp.einsum(
                    "hqk,qhd->khd",
                    attn_prob.astype(jnp.bfloat16),
                    grad_block,
                    preferred_element_type=jnp.float32,
                ),
                pad_rows,
            )
        query_grad = jnp.concatenate(query_parts, axis=0).reshape(tok_rows, head_cols)
        key_grad = key_acc.reshape(tok_rows, head_cols)
        value_grad = value_acc.reshape(tok_rows, head_cols)
        query_b_grad = query_b_grad + jnp.sum(query_grad, axis=0)
        value_b_grad = value_b_grad + jnp.sum(value_grad, axis=0)
        query_low = query_grad.astype(jnp.bfloat16)
        key_low = key_grad.astype(jnp.bfloat16)
        value_low = value_grad.astype(jnp.bfloat16)
        query_w_grad = query_w_grad + cross_rows(first_in, query_low)
        key_w_grad = key_w_grad + cross_rows(first_in, key_low)
        value_w_grad = value_w_grad + cross_rows(first_in, value_low)
        first_part = (
            times_transpose(query_low, query_weight)
            + times_transpose(key_low, key_weight)
            + times_transpose(value_low, value_weight)
        )
        first_cols = lax.psum_scatter(first_part, "tensor", scatter_dimension=1, tiled=True)
        first_grad = lax.all_gather(
            first_cols.astype(jnp.bfloat16), "tensor", axis=1, tiled=True
        ).astype(jnp.float32)
        input_back, gain_part, shift_part = norm_backward(
            first_grad, normed_one, inverse_one, gain_one
        )
        gain_one_grad = gain_one_grad + gain_part
        shift_one_grad = shift_one_grad + shift_part
        input_cols = lax.dynamic_slice_in_dim(
            resid_grad + input_back, column * col_width, col_width, axis=1
        ).astype(jnp.bfloat16)
        packed = jnp.concatenate([layer_cols, input_cols], axis=1)
        given_end = given_off + given_len
        dest_off = (jnp.cumsum(lengths_mb, axis=1, dtype=jnp.int32) - lengths_mb).reshape(-1)
        labels = jnp.arange(dealing_mb.shape[0], dtype=jnp.int32)
        give_row_ids = jnp.arange(tok_rows * lax.axis_size("dp"), dtype=jnp.int32)
        owner_seq = jnp.sum(
            (give_row_ids[:, None] >= given_end[None, :]).astype(jnp.int32), axis=1, dtype=jnp.int32
        )
        one_hot = (owner_seq[:, None] == labels[None, :]).astype(jnp.int32)
        within = give_row_ids - jnp.sum(one_hot * given_off[None, :], axis=1, dtype=jnp.int32)
        seq_label = jnp.sum(one_hot * dealing_mb[None, :], axis=1, dtype=jnp.int32)
        seq_hot = (seq_label[:, None] == labels[None, :]).astype(jnp.int32)
        buffer_row = jnp.sum(seq_hot * dest_off[None, :], axis=1, dtype=jnp.int32) + within
        owner_dev = seq_label // seq_dev
        is_mine = owner_dev == device
        fetched = jnp.take(packed, jnp.clip(buffer_row, 0, tok_rows - 1), axis=0).astype(
            jnp.float32
        )
        returned = lax.psum_scatter(
            jnp.where(is_mine[:, None], fetched, 0.0).astype(jnp.bfloat16),
            "dp",
            scatter_dimension=0,
            tiled=True,
        ).astype(jnp.float32)
        layer_parts.append(returned[:, :col_width].astype(jnp.bfloat16))
        grad_parts.append(returned[:, col_width:].astype(jnp.bfloat16))
    (
        query_w_grad,
        key_w_grad,
        value_w_grad,
        out_w_grad,
        query_b_grad,
        value_b_grad,
        out_b_grad,
        gain_one_grad,
        shift_one_grad,
        up_w_grad,
        up_b_grad,
        down_w_grad,
        down_b_grad,
        gain_two_grad,
        shift_two_grad,
    ) = lax.psum(
        (
            query_w_grad,
            key_w_grad,
            value_w_grad,
            out_w_grad,
            query_b_grad,
            value_b_grad,
            out_b_grad,
            gain_one_grad,
            shift_one_grad,
            up_w_grad,
            up_b_grad,
            down_w_grad,
            down_b_grad,
            gain_two_grad,
            shift_two_grad,
        ),
        "dp",
    )
    layer_out = jnp.stack(layer_parts, axis=0)
    input_grad = jnp.stack(grad_parts, axis=0)
    return (
        layer_out,
        input_grad,
        query_w_grad,
        key_w_grad,
        value_w_grad,
        out_w_grad,
        query_b_grad,
        value_b_grad,
        out_b_grad,
        up_w_grad,
        up_b_grad,
        down_w_grad,
        down_b_grad,
        gain_one_grad,
        shift_one_grad,
        gain_two_grad,
        shift_two_grad,
    )


def solution(mesh):
    in_specs = (
        P(None, "dp", "tensor"),
        P(None, "dp", "tensor"),
        P(),
        P(),
        P(None, "tensor"),
        P(None, "tensor"),
        P(None, "tensor"),
        P("tensor", None),
        P("tensor"),
        P("tensor"),
        P(),
        P(None, "tensor"),
        P("tensor"),
        P("tensor", None),
        P(),
        P(),
        P(),
        P(),
        P(),
    )
    out_specs = (
        P(None, "dp", "tensor"),
        P(None, "dp", "tensor"),
        P(None, "tensor"),
        P(None, "tensor"),
        P(None, "tensor"),
        P("tensor", None),
        P("tensor"),
        P("tensor"),
        P(),
        P(None, "tensor"),
        P("tensor"),
        P("tensor", None),
        P(),
        P(),
        P(),
        P(),
        P(),
    )
    return jax.shard_map(shards, mesh=mesh, in_specs=in_specs, out_specs=out_specs, check_vma=False)
```

profile of v0, /device:TPU:0, one launch (start us, length us, event | category | flops | bytes accessed | tf_op | source)
XLA Modules:
  0.0 3230.5 jit_solution(10100842844259591794)
XLA Ops:
  18.5 49.3 %all-gather.39.cloned.1.call-done = bf16[1,8192,512]{2,1,0:T(8,128)(2,1)} async-done(((bf16[1,1024,512]{2,1,0:T(8,128)(2,1)}), bf16[1,8192,512]{2,1,0:T(8,128)(2,1)}) %all-gather.39.cloned.1.call-update) | async-done | bytes 8388624 | tf_op jit(solution)/shard_map/all_gather | solution.py:170
  67.8 8.5 gather_fusion
  76.2 48.4 %all-gather.41.cloned.1.call-done = bf16[1,8192,512]{2,1,0:T(8,128)(2,1)} async-done(((bf16[1,1024,512]{2,1,0:T(8,128)(2,1)}), bf16[1,8192,512]{2,1,0:T(8,128)(2,1)}) %all-gather.41.cloned.1.call-update) | async-done | bytes 8388624 | tf_op jit(solution)/shard_map/all_gather | solution.py:171
  124.6 9.6 gather_fusion.1
  134.2 47.3 %all-gather.43.cloned.1.call-done = bf16[1,8192,512]{2,1,0:T(8,128)(2,1)} async-done(((bf16[1,1024,512]{2,1,0:T(8,128)(2,1)}), bf16[1,8192,512]{2,1,0:T(8,128)(2,1)}) %all-gather.43.cloned.1.call-update) | async-done | bytes 8388624 | tf_op jit(solution)/shard_map/all_gather | solution.py:170
  181.5 9.6 gather_fusion.3
  191.1 47.2 %all-gather.45.cloned.1.call-done = bf16[1,8192,512]{2,1,0:T(8,128)(2,1)} async-done(((bf16[1,1024,512]{2,1,0:T(8,128)(2,1)}), bf16[1,8192,512]{2,1,0:T(8,128)(2,1)}) %all-gather.45.cloned.1.call-update) | async-done | bytes 8388624 | tf_op jit(solution)/shard_map/all_gather | solution.py:171
  238.3 9.6 gather_fusion.4
  257.3 76.5 %all-gather.19.cloned.1.call-done = bf16[1024,2048]{1,0:T(8,128)(2,1)} async-done(((bf16[1024,512]{1,0:T(8,128)(2,1)}), bf16[1024,2048]{1,0:T(8,128)(2,1)}) %all-gather.19.cloned.1.call-update) | async-done | bytes 4194320 | tf_op jit(solution)/shard_map/all_gather | solution.py:179
  340.1 75.1 %all-gather.29.cloned.1.call-done = bf16[1024,2048]{1,0:T(8,128)(2,1)} async-done(((bf16[1024,512]{1,0:T(8,128)(2,1)}), bf16[1024,2048]{1,0:T(8,128)(2,1)}) %all-gather.29.cloned.1.call-update) | async-done | bytes 4194320 | tf_op jit(solution)/shard_map/all_gather | solution.py:179
  437.3 7.7 fusion.233
  450.2 11.0 fusion.232
  461.2 8.9 fusion.150
  490.7 7.6 fusion.231
  498.4 10.9 fusion.230
  513.7 8.6 fusion.153
  530.7 89.4 %reduce-scatter.21.cloned.1.call-done = f32[1024,512]{1,0:T(8,128)} async-done(((f32[1024,2048]{1,0:T(8,128)}), f32[1024,512]{1,0:T(8,128)}) %reduce-scatter.21.cloned.1.call-update) | async-done | bytes 2097168 | tf_op jit(solution)/shard_map/reduce_scatter | solution.py:226
  620.1 147.6 %reduce-scatter.11.cloned.1.call-done = f32[1024,512]{1,0:T(8,128)} async-done(((f32[1024,2048]{1,0:T(8,128)}), f32[1024,512]{1,0:T(8,128)}) %reduce-scatter.11.cloned.1.call-update) | async-done | bytes 2097168 | tf_op jit(solution)/shard_map/reduce_scatter | solution.py:226
  773.7 77.7 %all-gather.33.cloned.1.call-done = bf16[1024,2048]{1,0:T(8,128)(2,1)} async-done(((bf16[1024,512]{1,0:T(8,128)(2,1)}), bf16[1024,2048]{1,0:T(8,128)(2,1)}) %all-gather.33.cloned.1.call-update) | async-done | bytes 4194320 | tf_op jit(solution)/shard_map/all_gather | solution.py:180
  851.4 14.9 fusion.238
  866.3 65.8 %all-gather.31.cloned.1.call-done = bf16[1024,2048]{1,0:T(8,128)(2,1)} async-done(((bf16[1024,512]{1,0:T(8,128)(2,1)}), bf16[1024,2048]{1,0:T(8,128)(2,1)}) %all-gather.31.cloned.1.call-update) | async-done | bytes 4194320 | tf_op jit(solution)/shard_map/all_gather | solution.py:230
  938.4 75.2 %all-gather.21.cloned.1.call-done = bf16[1024,2048]{1,0:T(8,128)(2,1)} async-done(((bf16[1024,512]{1,0:T(8,128)(2,1)}), bf16[1024,2048]{1,0:T(8,128)(2,1)}) %all-gather.21.cloned.1.call-update) | async-done | bytes 4194320 | tf_op jit(solution)/shard_map/all_gather | solution.py:230
  1020.8 14.0 fusion.203
  1034.8 11.7 fusion.206
  1046.5 48.4 %all-gather.23.cloned.1.call-done = bf16[1024,2048]{1,0:T(8,128)(2,1)} async-done(((bf16[1024,512]{1,0:T(8,128)(2,1)}), bf16[1024,2048]{1,0:T(8,128)(2,1)}) %all-gather.23.cloned.1.call-update) | async-done | bytes 4194320 | tf_op jit(solution)/shard_map/all_gather | solution.py:180
  1094.9 31.1 fusion.211
  1126.0 14.7 fusion.102
  1140.8 14.6 fusion.90
  1155.4 128.4 %reduce-scatter.15.cloned.1.call-done = f32[1024,512]{1,0:T(8,128)} async-done(((f32[1024,2048]{1,0:T(8,128)}), f32[1024,512]{1,0:T(8,128)}) %reduce-scatter.15.cloned.1.call-update) | async-done | bytes 2097168 | tf_op jit(solution)/shard_map/reduce_scatter | solution.py:250
  1286.6 144.7 %reduce-scatter.25.cloned.1.call-done = f32[1024,512]{1,0:T(8,128)} async-done(((f32[1024,2048]{1,0:T(8,128)}), f32[1024,512]{1,0:T(8,128)}) %reduce-scatter.25.cloned.1.call-update) | async-done | bytes 2097168 | tf_op jit(solution)/shard_map/reduce_scatter | solution.py:250
  1434.1 80.7 %all-gather.25.cloned.1.call-done = bf16[1024,2048]{1,0:T(8,128)(2,1)} async-done(((bf16[1024,512]{1,0:T(8,128)(2,1)}), bf16[1024,2048]{1,0:T(8,128)(2,1)}) %all-gather.25.cloned.1.call-update) | async-done | bytes 4194320 | tf_op jit(solution)/shard_map/all_gather | solution.py:253
  1514.8 7.2 fusion.50
  1522.0 73.6 %all-gather.35.cloned.1.call-done = bf16[1024,2048]{1,0:T(8,128)(2,1)} async-done(((bf16[1024,512]{1,0:T(8,128)(2,1)}), bf16[1024,2048]{1,0:T(8,128)(2,1)}) %all-gather.35.cloned.1.call-update) | async-done | bytes 4194320 | tf_op jit(solution)/shard_map/all_gather | solution.py:253
  1595.6 15.5 fusion.214
  1611.2 6.2 fusion.213
  1628.6 6.9 multiply_convert_fusion.2
  1640.1 9.0 multiply_reduce_fusion
  1653.7 7.2 multiply_convert_fusion
  1693.2 11.0 multiply_reduce_fusion.1
  1704.1 12.1 multiply_convert_fusion.1
  1728.5 6.7 fusion.235
  1743.0 11.8 add_add_fusion.1
  1755.6 16.1 convolution_convert_fusion.1
  1771.7 16.0 convolution_convert_fusion
  1787.9 33.3 %reduce-scatter.27.cloned.1.call-done = f32[1024,512]{1,0:T(8,128)} async-done(((f32[1024,2048]{1,0:T(8,128)}), f32[1024,512]{1,0:T(8,128)}) %reduce-scatter.27.cloned.1.call-update) | async-done | bytes 2097168 | tf_op jit(solution)/shard_map/reduce_scatter | solution.py:335
  1823.9 145.2 %reduce-scatter.17.cloned.1.call-done = f32[1024,512]{1,0:T(8,128)} async-done(((f32[1024,2048]{1,0:T(8,128)}), f32[1024,512]{1,0:T(8,128)}) %reduce-scatter.17.cloned.1.call-update) | async-done | bytes 2097168 | tf_op jit(solution)/shard_map/reduce_scatter | solution.py:335
  1974.6 75.0 %reduce-scatter.13.cloned.1.call-done = bf16[1024,512]{1,0:T(8,128)(2,1)} async-done(((bf16[1024,2048]{1,0:T(8,128)(2,1)}), bf16[1024,512]{1,0:T(8,128)(2,1)}) %reduce-scatter.13.cloned.1.call-update) | async-done | bytes 1048592 | tf_op jit(solution)/shard_map/reduce_scatter | solution.py:236
  2049.6 80.1 %reduce-scatter.23.cloned.1.call-done = bf16[1024,512]{1,0:T(8,128)(2,1)} async-done(((bf16[1024,2048]{1,0:T(8,128)(2,1)}), bf16[1024,512]{1,0:T(8,128)(2,1)}) %reduce-scatter.23.cloned.1.call-update) | async-done | bytes 1048592 | tf_op jit(solution)/shard_map/reduce_scatter | solution.py:236
  2134.6 78.0 %all-gather.37.cloned.1.call-done = bf16[1024,2048]{1,0:T(8,128)(2,1)} async-done(((bf16[1024,512]{1,0:T(8,128)(2,1)}), bf16[1024,2048]{1,0:T(8,128)(2,1)}) %all-gather.37.cloned.1.call-update) | async-done | bytes 4194320 | tf_op jit(solution)/shard_map/all_gather | solution.py:336
  2212.6 81.5 %all-gather.27.cloned.1.call-done = bf16[1024,2048]{1,0:T(8,128)(2,1)} async-done(((bf16[1024,512]{1,0:T(8,128)(2,1)}), bf16[1024,2048]{1,0:T(8,128)(2,1)}) %all-gather.27.cloned.1.call-update) | async-done | bytes 4194320 | tf_op jit(solution)/shard_map/all_gather | solution.py:336
  2294.1 16.2 fusion.51
  2312.7 35.2 %gather_fusion.5 = bf16[8192,1024]{1,0:T(8,128)(2,1)} fusion(bf16[1024,1024]{1,0:T(8,128)(2,1)S(1)} %pad_maximum_fusion.1, s32[8192]{0:T(1024)S(1)} %broadcast_clamp_fusion), kind=kCustom, calls=%fused_computation.5.clone | custom fusion | bytes 33587200 | tf_op jit(solution)/shard_map/jit(_take)/gather | solution.py:362
  2348.0 15.3 select_convert_fusion
  2367.8 35.2 %gather_fusion.2 = bf16[8192,1024]{1,0:T(8,128)(2,1)} fusion(bf16[1024,1024]{1,0:T(8,128)(2,1)S(1)} %pad_maximum_fusion, s32[8192]{0:T(1024)S(1)} %broadcast_clamp_fusion.1), kind=kCustom, calls=%fused_computation.1.clone | custom fusion | bytes 33587200 | tf_op jit(solution)/shard_map/jit(_take)/gather | solution.py:362
  2403.1 15.7 select_convert_fusion.1
  2419.5 16.2 fusion.100
  2435.7 16.4 fusion.208
  2452.2 17.9 convolution_add_fusion.1
  2470.1 20.9 convolution_add_fusion
  2522.8 27.0 all-reduce.4
  2551.6 47.5 %reduce-scatter.19.cloned.1.call-done = bf16[1024,1024]{1,0:T(8,128)(2,1)} async-done(((bf16[8192,1024]{1,0:T(8,128)(2,1)}), bf16[1024,1024]{1,0:T(8,128)(2,1)}) %reduce-scatter.19.cloned.1.call-update) | async-done | bytes 2097168 | tf_op jit(solution)/shard_map/reduce_scatter | solution.py:365
  2603.7 585.8 %all-reduce.8.cloned.1.call-done = (f32[2048,512]{1,0:T(8,128)}, f32[2048,512]{1,0:T(8,128)}, f32[2048,512]{1,0:T(8,128)}, f32[512,2048]{1,0:T(8,128)}, f32[2048,2048]{1,0:T(8,128)}, /*index=5*/f32[2048,2048]{1,0:T(8,128)}) async-done(((f32[2048,512]{1,0:T(8,128)}, f32[2048,512]{1,0:T(8,128)}, f32[2048,512]{1,0:T(8,128)}, f32[512,2048]{1,0:T(8,128)}, f32[2048,2048]{1,0:T(8,128)}, ...) | async-done | bytes 50331664 | tf_op jit(solution)/shard_map/psum | solution.py:389
  3206.3 8.5 copy.100
  3217.3 6.3 copy.101
  (604 shorter events, 262.9 us)
Async XLA Ops:
  7.2 464.0 %copy-start = (bf16[512,2048]{1,0:T(8,128)(2,1)S(1)}, bf16[512,2048]{1,0:T(8,128)(2,1)}, u32[]{:S(2)}) copy-start(bf16[512,2048]{1,0:T(8,128)(2,1)} %param.30) | copy-start | bytes 6291460
  7.2 60.5 %all-gather.39.cloned.1.call-start = ((), (), s32[]{:S(2)}) async-start(), calls=%async_computation.30 | async-start | bytes 9437184 | tf_op jit(solution)/shard_map/all_gather | solution.py:170
  10.4 114.2 %all-gather.41.cloned.1.call-start = ((), (), s32[]{:S(2)}) async-start(), calls=%async_computation.31 | async-start | bytes 9437184 | tf_op jit(solution)/shard_map/all_gather | solution.py:171
  13.5 168.0 %all-gather.43.cloned.1.call-start = ((), (), s32[]{:S(2)}) async-start(), calls=%async_computation.32 | async-start | bytes 9437184 | tf_op jit(solution)/shard_map/all_gather | solution.py:170
  14.2 224.0 %all-gather.45.cloned.1.call-start = ((), (), s32[]{:S(2)}) async-start(), calls=%async_computation.33 | async-start | bytes 9437184 | tf_op jit(solution)/shard_map/all_gather | solution.py:171
  14.8 319.0 %all-gather.19.cloned.1.call-start = ((), (), s32[]{:S(2)}) async-start(), calls=%async_computation.10 | async-start | bytes 5242880 | tf_op jit(solution)/shard_map/all_gather | solution.py:179
  16.0 51.8 %copy-start.148 = (s32[24]{0:T(128)}, s32[24]{0:T(128)S(1)}, u32[]{:S(2)}) copy-start(s32[24]{0:T(128)S(1)} %mul.470) | copy-start | bytes 292
  16.1 51.7 %copy-start.133 = (s32[24]{0:T(128)}, s32[24]{0:T(128)S(1)}, u32[]{:S(2)}) copy-start(s32[24]{0:T(128)S(1)} %get-tuple-element.146) | copy-start | bytes 292
  16.1 51.7 %copy-start.135 = (s32[24]{0:T(128)}, s32[24]{0:T(128)S(1)}, u32[]{:S(2)}) copy-start(s32[24]{0:T(128)S(1)} %get-tuple-element.147) | copy-start | bytes 292
  16.8 50.9 %copy-start.144 = (s32[24]{0:T(128)}, s32[24]{0:T(128)S(1)}, u32[]{:S(2)}) copy-start(s32[24]{0:T(128)S(1)} %sub.335) | copy-start | bytes 292
  17.6 50.1 %copy-start.139 = (s32[24]{0:T(128)}, s32[24]{0:T(128)S(1)}, u32[]{:S(2)}) copy-start(s32[24]{0:T(128)S(1)} %reduce.8) | copy-start | bytes 292
  17.7 50.1 %copy-start.146 = (s32[24]{0:T(128)}, s32[24]{0:T(128)S(1)}, u32[]{:S(2)}) copy-start(s32[24]{0:T(128)S(1)} %sub.307) | copy-start | bytes 292
  252.9 162.2 %all-gather.29.cloned.1.call-start = ((), (), s32[]{:S(2)}) async-start(), calls=%async_computation.20 | async-start | bytes 5242880 | tf_op jit(solution)/shard_map/all_gather | solution.py:179
  253.5 366.7 %reduce-scatter.21.cloned.1.call-start = ((), (), s32[]{:S(2)}) async-start(), calls=%async_computation.21 | async-start | bytes 10485760 | tf_op jit(solution)/shard_map/reduce_scatter | solution.py:226
  253.8 168.5 %copy-start.70 = (f32[2048]{0:T(1024)}, f32[2048]{0:T(1024)S(1)}, u32[]{:S(2)}) copy-start(f32[2048]{0:T(1024)S(1)} %convert_element_type.274) | copy-start | bytes 24580
  336.6 90.4 %copy-start.80 = (f32[1024]{0:T(1024)}, f32[1024]{0:T(1024)S(1)}, u32[]{:S(2)}) copy-start(f32[1024]{0:T(1024)S(1)} %broadcast_multiply_fusion.11) | copy-start | bytes 12292
  340.0 87.0 %copy-start.76 = (f32[1024]{0:T(1024)}, f32[1024]{0:T(1024)S(1)}, u32[]{:S(2)}) copy-start(f32[1024]{0:T(1024)S(1)} %add_rsqrt_fusion.3) | copy-start | bytes 12292
  476.9 290.8 %reduce-scatter.11.cloned.1.call-start = ((), (), s32[]{:S(2)}) async-start(), calls=%async_computation.11 | async-start | bytes 10485760 | tf_op jit(solution)/shard_map/reduce_scatter | solution.py:226
  523.5 244.2 %copy-start.10 = (bf16[1024,512]{1,0:T(8,128)(2,1)S(1)}, bf16[1024,512]{1,0:T(8,128)(2,1)}, u32[]{:S(2)}) copy-start(bf16[1024,512]{1,0:T(8,128)(2,1)} %get-tuple-element.145) | copy-start | bytes 3145732
  529.2 244.0 %copy-start.127 = (bf16[2048]{0:T(1024)(128)(2,1)S(1)}, bf16[2048]{0:T(1024)(128)(2,1)}, u32[]{:S(2)}) copy-start(bf16[2048]{0:T(1024)(128)(2,1)} %param.40) | copy-start | bytes 12292
  529.2 244.0 %copy-start.128 = (bf16[2048]{0:T(1024)(128)(2,1)S(1)}, bf16[2048]{0:T(1024)(128)(2,1)}, u32[]{:S(2)}) copy-start(bf16[2048]{0:T(1024)(128)(2,1)} %param.35) | copy-start | bytes 12292
  529.2 244.0 %copy-start.129 = (bf16[2048]{0:T(1024)(128)(2,1)S(1)}, bf16[2048]{0:T(1024)(128)(2,1)}, u32[]{:S(2)}) copy-start(bf16[2048]{0:T(1024)(128)(2,1)} %param.41) | copy-start | bytes 12292
  529.2 322.2 %all-gather.33.cloned.1.call-start = ((), (), s32[]{:S(2)}) async-start(), calls=%async_computation.24 | async-start | bytes 5242880 | tf_op jit(solution)/shard_map/all_gather | solution.py:180
  529.9 402.2 %all-gather.31.cloned.1.call-start = ((), (), s32[]{:S(2)}) async-start(), calls=%async_computation.22 | async-start | bytes 5242880 | tf_op jit(solution)/shard_map/all_gather | solution.py:230
  530.7 335.6 %copy-start.104 = (f32[512]{0:T(512)}, f32[512]{0:T(512)S(1)}, u32[]{:S(2)}) copy-start(f32[512]{0:T(512)S(1)} %dynamic-slice_convert_fusion.1) | copy-start | bytes 6148
  772.3 241.2 %all-gather.21.cloned.1.call-start = ((), (), s32[]{:S(2)}) async-start(), calls=%async_computation.12 | async-start | bytes 5242880 | tf_op jit(solution)/shard_map/all_gather | solution.py:230
  773.1 321.8 %all-gather.23.cloned.1.call-start = ((), (), s32[]{:S(2)}) async-start(), calls=%async_computation.14 | async-start | bytes 5242880 | tf_op jit(solution)/shard_map/all_gather | solution.py:180
  773.2 838.0 %copy-start.68 = (f32[2048]{0:T(1024)}, f32[2048]{0:T(1024)S(1)}, u32[]{:S(2)}) copy-start(f32[2048]{0:T(1024)S(1)} %convert_element_type.288) | copy-start | bytes 24580
  773.2 321.7 %copy-start.120 = (f32[2048]{0:T(1024)}, f32[2048]{0:T(1024)S(1)}, u32[]{:S(2)}) copy-start(f32[2048]{0:T(1024)S(1)} %convert_element_type.291) | copy-start | bytes 24580
  773.2 261.6 %copy-start.123 = (f32[2048]{0:T(1024)}, f32[2048]{0:T(1024)S(1)}, u32[]{:S(2)}) copy-start(f32[2048]{0:T(1024)S(1)} %convert_element_type.289) | copy-start | bytes 24580
  773.6 510.2 %reduce-scatter.15.cloned.1.call-start = ((), (), s32[]{:S(2)}) async-start(), calls=%async_computation.15 | async-start | bytes 10485760 | tf_op jit(solution)/shard_map/reduce_scatter | solution.py:250
  934.9 676.2 %copy-start.74 = (f32[1024]{0:T(1024)}, f32[1024]{0:T(1024)S(1)}, u32[]{:S(2)}) copy-start(f32[1024]{0:T(1024)S(1)} %broadcast_multiply_fusion.4) | copy-start | bytes 12292
  938.4 672.8 %copy-start.86 = (f32[1024]{0:T(1024)}, f32[1024]{0:T(1024)S(1)}, u32[]{:S(2)}) copy-start(f32[1024]{0:T(1024)S(1)} %add_rsqrt_fusion) | copy-start | bytes 12292
  1016.6 579.0 %copy-start.72 = (f32[1024]{0:T(1024)}, f32[1024]{0:T(1024)S(1)}, u32[]{:S(2)}) copy-start(f32[1024]{0:T(1024)S(1)} %broadcast_multiply_fusion.10) | copy-start | bytes 12292
  1020.7 574.9 %copy-start.84 = (f32[1024]{0:T(1024)}, f32[1024]{0:T(1024)S(1)}, u32[]{:S(2)}) copy-start(f32[1024]{0:T(1024)S(1)} %add_rsqrt_fusion.2) | copy-start | bytes 12292
  1140.7 290.6 %reduce-scatter.25.cloned.1.call-start = ((), (), s32[]{:S(2)}) async-start(), calls=%async_computation.25 | async-start | bytes 10485760 | tf_op jit(solution)/shard_map/reduce_scatter | solution.py:250
  1155.4 359.5 %all-gather.25.cloned.1.call-start = ((), (), s32[]{:S(2)}) async-start(), calls=%async_computation.16 | async-start | bytes 5242880 | tf_op jit(solution)/shard_map/all_gather | solution.py:253
  1286.6 309.0 %all-gather.35.cloned.1.call-start = ((), (), s32[]{:S(2)}) async-start(), calls=%async_computation.26 | async-start | bytes 5242880 | tf_op jit(solution)/shard_map/all_gather | solution.py:253
  1434.0 387.1 %reduce-scatter.27.cloned.1.call-start = ((), (), s32[]{:S(2)}) async-start(), calls=%async_computation.27 | async-start | bytes 10485760 | tf_op jit(solution)/shard_map/reduce_scatter | solution.py:335
  1678.0 291.2 %reduce-scatter.17.cloned.1.call-start = ((), (), s32[]{:S(2)}) async-start(), calls=%async_computation.17 | async-start | bytes 10485760 | tf_op jit(solution)/shard_map/reduce_scatter | solution.py:335
  1754.9 294.7 %reduce-scatter.13.cloned.1.call-start = ((), (), s32[]{:S(2)}) async-start(), calls=%async_computation.13 | async-start | bytes 5242880 | tf_op jit(solution)/shard_map/reduce_scatter | solution.py:236
  1771.6 358.1 %reduce-scatter.23.cloned.1.call-start = ((), (), s32[]{:S(2)}) async-start(), calls=%async_computation.23 | async-start | bytes 5242880 | tf_op jit(solution)/shard_map/reduce_scatter | solution.py:236
  1787.7 184.5 %copy-start.101 = (s32[1,8,3]{1,0,2:T(1,128)S(1)}, s32[1,8,3]{1,0,2:T(1,128)}, u32[]{:S(2)}) copy-start(s32[1,8,3]{1,0,2:T(1,128)} %copy-done.100) | copy-start | bytes 292
  1787.7 184.5 %copy-start.103 = (s32[1,8,3]{1,0,2:T(1,128)S(1)}, s32[1,8,3]{1,0,2:T(1,128)}, u32[]{:S(2)}) copy-start(s32[1,8,3]{1,0,2:T(1,128)} %copy-done.102) | copy-start | bytes 292
  1787.7 184.7 %copy-start.151 = (s32[24]{0:T(128)S(1)}, s32[24]{0:T(128)}, u32[]{:S(2)}) copy-start(s32[24]{0:T(128)} %copy-done.150) | copy-start | bytes 292
  1787.7 185.5 %copy-start.140 = (s32[24]{0:T(128)S(1)}, s32[24]{0:T(128)}, u32[]{:S(2)}) copy-start(s32[24]{0:T(128)} %copy-done.139) | copy-start | bytes 292
  1787.7 185.7 %copy-start.138 = (s32[24]{0:T(128)S(1)}, s32[24]{0:T(128)}, u32[]{:S(2)}) copy-start(s32[24]{0:T(128)} %copy-done.137) | copy-start | bytes 292
  1787.7 185.9 %copy-start.134 = (s32[24]{0:T(128)S(1)}, s32[24]{0:T(128)}, u32[]{:S(2)}) copy-start(s32[24]{0:T(128)} %copy-done.133) | copy-start | bytes 292
  1787.7 185.9 %copy-start.136 = (s32[24]{0:T(128)S(1)}, s32[24]{0:T(128)}, u32[]{:S(2)}) copy-start(s32[24]{0:T(128)} %copy-done.135) | copy-start | bytes 292
  1787.7 185.9 %copy-start.145 = (s32[24]{0:T(128)S(1)}, s32[24]{0:T(128)}, u32[]{:S(2)}) copy-start(s32[24]{0:T(128)} %copy-done.144) | copy-start | bytes 292
  1787.7 185.9 %copy-start.147 = (s32[24]{0:T(128)S(1)}, s32[24]{0:T(128)}, u32[]{:S(2)}) copy-start(s32[24]{0:T(128)} %copy-done.146) | copy-start | bytes 292
  1787.8 342.0 %copy-start.11 = (bf16[1024,512]{1,0:T(8,128)(2,1)S(1)}, bf16[1024,512]{1,0:T(8,128)(2,1)}, u32[]{:S(2)}) copy-start(bf16[1024,512]{1,0:T(8,128)(2,1)} %get-tuple-element.145) | copy-start | bytes 3145732
  1787.8 342.0 %copy-start.12 = (bf16[1024,512]{1,0:T(8,128)(2,1)S(1)}, bf16[1024,512]{1,0:T(8,128)(2,1)}, u32[]{:S(2)}) copy-start(bf16[1024,512]{1,0:T(8,128)(2,1)} %get-tuple-element.179) | copy-start | bytes 3145732
  1787.8 342.0 %copy-start.105 = (f32[512]{0:T(512)S(1)}, f32[512]{0:T(512)}, u32[]{:S(2)}) copy-start(f32[512]{0:T(512)} %copy-done.104) | copy-start | bytes 6148
  1787.8 424.8 %all-gather.37.cloned.1.call-start = ((), (), s32[]{:S(2)}) async-start(), calls=%async_computation.28 | async-start | bytes 5242880 | tf_op jit(solution)/shard_map/all_gather | solution.py:336
  1823.8 470.2 %copy-start.71 = (f32[2048]{0:T(1024)S(1)}, f32[2048]{0:T(1024)}, u32[]{:S(2)}) copy-start(f32[2048]{0:T(1024)} %copy-done.70) | copy-start | bytes 24580
  1823.9 470.2 %copy-start.77 = (f32[1024]{0:T(1024)S(1)}, f32[1024]{0:T(1024)}, u32[]{:S(2)}) copy-start(f32[1024]{0:T(1024)} %copy-done.76) | copy-start | bytes 12292
  1823.9 470.2 %copy-start.79 = (f32[1024]{0:T(1024)S(1)}, f32[1024]{0:T(1024)}, u32[]{:S(2)}) copy-start(f32[1024]{0:T(1024)} %copy-done.78) | copy-start | bytes 12292
  1823.9 470.2 %copy-start.81 = (f32[1024]{0:T(1024)S(1)}, f32[1024]{0:T(1024)}, u32[]{:S(2)}) copy-start(f32[1024]{0:T(1024)} %copy-done.80) | copy-start | bytes 12292
  1823.9 470.2 %copy-start.83 = (f32[1024]{0:T(1024)S(1)}, f32[1024]{0:T(1024)}, u32[]{:S(2)}) copy-start(f32[1024]{0:T(1024)} %copy-done.82) | copy-start | bytes 12292
  1823.9 470.2 %all-gather.27.cloned.1.call-start = ((), (), s32[]{:S(2)}) async-start(), calls=%async_computation.18 | async-start | bytes 5242880 | tf_op jit(solution)/shard_map/all_gather | solution.py:336
  1971.9 577.9 %reduce-scatter.29.cloned.1.call-start = ((), (), s32[]{:S(2)}) async-start(), calls=%async_computation.29 | async-start | bytes 18874368 | tf_op jit(solution)/shard_map/reduce_scatter | solution.py:365
  2363.3 235.8 %reduce-scatter.19.cloned.1.call-start = ((), (), s32[]{:S(2)}) async-start(), calls=%async_computation.19 | async-start | bytes 18874368 | tf_op jit(solution)/shard_map/reduce_scatter | solution.py:365
  2418.8 770.7 %all-reduce.8.cloned.1.call-start = ((), (), s32[]{:S(2)}) async-start(), calls=%async_computation.34 | async-start | bytes 100663296 | tf_op jit(solution)/shard_map/psum | solution.py:389
  (144 other events, 915.6 us)
Sparse Core Ops, SparseCore 0:
  10.5 57.1 all-gather.38
  70.2 54.3 all-gather.40
  127.1 54.3 all-gather.42
  183.8 54.3 all-gather.44
  253.0 80.7 all-gather.18
  335.8 79.2 all-gather.28
  477.1 143.0 reduce-scatter.20
  622.5 145.1 reduce-scatter.10
  769.9 81.4 all-gather.32
  852.8 79.2 all-gather.30
  934.3 79.2 all-gather.20
  1015.6 79.2 all-gather.22
  1140.9 142.9 reduce-scatter.14
  1286.1 145.1 reduce-scatter.24
  1433.3 81.4 all-gather.24
  1516.3 79.2 all-gather.34
  1678.1 142.9 reduce-scatter.26
  1824.0 145.1 reduce-scatter.16
  1972.1 77.4 reduce-scatter.12
  2052.4 77.2 reduce-scatter.22
  2131.3 81.2 all-gather.36
  2214.7 79.2 all-gather.26
  2363.4 114.4 reduce-scatter.28
  2481.9 117.0 reduce-scatter.18
  2604.5 584.9 all-reduce.7
where the time goes:
time: 3240 us; the launch traced here: 3230 us
  waiting for transfers between devices  2410 us (74%)
  matrix products  428 us (13%)
  other arithmetic  180 us (6%)
  local copies, waits for them, and re-layouts  171 us (5%)
    psum x1, waiting for transfers between devices, shards(): lax.psum((query_w_grad, key_w_grad, value_w_grad, out_w_grad, query_b_gra...  586 us
    reduce_scatter x2, waiting for transfers between devices, shards(): lax.psum_scatter(times_transpose(hidden_low, up_weight), 'tensor', scatte...  273 us
    reduce_scatter x2, waiting for transfers between devices, shards(): lax.psum_scatter(matmul(mixed_heads, out_weight), 'tensor', scatter_dimen...  237 us
    reduce_scatter x2, waiting for transfers between devices, shards(): lax.psum_scatter(first_part, 'tensor', scatter_dimension=1, tiled=True)  179 us
    all_gather x2, waiting for transfers between devices, shards(): lax.all_gather(first_cols.astype(jnp.bfloat16), 'tensor', axis=1, tiled=T...  159 us
    reduce_scatter x2, waiting for transfers between devices, shards(): lax.psum_scatter(matmul(hidden, down_weight).astype(jnp.bfloat16), 'tenso...  155 us
    all_gather x2, waiting for transfers between devices, shards(): lax.all_gather(second_cols.astype(jnp.bfloat16), 'tensor', axis=1, tiled=...  154 us
    all_gather x2, waiting for transfers between devices, shards(): lax.all_gather(tok_buf, 'tensor', axis=1, tiled=True)  152 us
  transfers between devices with their start and end apart: 25, of which 24 were waited for; matrix products, arithmetic and copies ran while one was open for 14% of the time, Pallas kernels for 0%

commit v1 on v0

--- a/solution.py
+++ b/solution.py
@@ -1,7 +1,13 @@
+import functools
+
 import jax
 import jax.numpy as jnp
 from jax import lax
+from jax.experimental import pallas as pl
+from jax.experimental.pallas import tpu as pltpu
+from jax.sharding import Mesh
 from jax.sharding import PartitionSpec as P
+
 
 HEAD_DIM = 64
 SEG = 512
@@ -50,20 +56,27 @@
     return (inverse * (scaled - first_mean - normed * second_mean), gain_grad, shift_grad)
 
 
+def running_sum(counts):
+    size = counts.shape[-1]
+    places = jnp.arange(size, dtype=jnp.int32)
+    upto = (places[:, None] <= places[None, :]).astype(jnp.int32)
+    return jnp.sum(counts[..., :, None] * upto, axis=-2, dtype=jnp.int32)
+
+
 def given_layout(lengths_mb, dealing_mb):
     seq_count = dealing_mb.shape[0]
     labels = jnp.arange(seq_count, dtype=jnp.int32)
     flat_lengths = lengths_mb.reshape(seq_count)
     one_hot = (dealing_mb[:, None] == labels[None, :]).astype(jnp.int32)
     given_len = jnp.sum(one_hot * flat_lengths[None, :], axis=1, dtype=jnp.int32)
-    given_off = jnp.cumsum(given_len, dtype=jnp.int32) - given_len
+    given_off = running_sum(given_len) - given_len
     start_by_seq = jnp.sum(one_hot * given_off[:, None], axis=0, dtype=jnp.int32)
     return (given_len, given_off, start_by_seq)
 
 
 def buffer_layout(lengths_dev, start_dev, rows_total):
     seq_count = lengths_dev.shape[0]
-    end_rows = jnp.cumsum(lengths_dev, dtype=jnp.int32)
+    end_rows = running_sum(lengths_dev)
     offsets = end_rows - lengths_dev
     row_ids = jnp.arange(rows_total, dtype=jnp.int32)
     holder = jnp.sum(
@@ -346,7 +359,7 @@
         ).astype(jnp.bfloat16)
         packed = jnp.concatenate([layer_cols, input_cols], axis=1)
         given_end = given_off + given_len
-        dest_off = (jnp.cumsum(lengths_mb, axis=1, dtype=jnp.int32) - lengths_mb).reshape(-1)
+        dest_off = (running_sum(lengths_mb) - lengths_mb).reshape(-1)
         labels = jnp.arange(dealing_mb.shape[0], dtype=jnp.int32)
         give_row_ids = jnp.arange(tok_rows * lax.axis_size("dp"), dtype=jnp.int32)
         owner_seq = jnp.sum(
@@ -429,7 +442,7 @@
     )
 
 
-def solution(mesh):
+def general_layer(mesh):
     in_specs = (
         P(None, "dp", "tensor"),
         P(None, "dp", "tensor"),
@@ -471,3 +484,649 @@
         P(),
     )
     return jax.shard_map(shards, mesh=mesh, in_specs=in_specs, out_specs=out_specs, check_vma=False)
+
+
+ROWS = 1024
+QBLK = 256
+PAIR = 128
+
+
+def slot_of(block, rank):
+    piece = jnp.bitwise_xor(block, rank)
+    return jnp.bitwise_or(piece >> 1, (piece & 1) << 1)
+
+
+def rows_of(block, rank):
+    return pl.ds(pl.multiple_of(slot_of(block, rank) * QBLK, QBLK), QBLK)
+
+
+def fill_bias(bias_ref, key_info_ref, query_info_ref):
+    for block in range(ROWS // QBLK):
+        reach = (block + 1) * QBLK
+        cols = pl.ds(block * QBLK, QBLK)
+        key_part = key_info_ref[pl.ds(0, reach), 0:1]
+        key_summary = key_info_ref[pl.ds(0, reach), 1:2]
+        query_part = query_info_ref[0:1, cols]
+        query_seq = query_info_ref[1:2, cols]
+        key_row = lax.broadcasted_iota(jnp.int32, (reach, QBLK), 0)
+        query_row = lax.broadcasted_iota(jnp.int32, (reach, QBLK), 1) + block * QBLK
+        seen = (key_row <= query_row) & ((key_part == query_part) | (key_summary == query_seq))
+        bias_ref[pl.ds(0, reach), cols] = jnp.where(seen, 0.0, MASKED)
+
+
+def nt_dot(left, right):
+    return lax.dot_general(left, right, (((1,), (1,)), ((), ())), preferred_element_type=jnp.float32)
+
+
+def nn_dot(left, right):
+    return jnp.dot(left, right, preferred_element_type=jnp.float32)
+
+
+def head_lanes(block, head):
+    lane = lax.broadcasted_iota(jnp.int32, block.shape, 1)
+    inside = (lane >= head * HEAD_DIM) & (lane < (head + 1) * HEAD_DIM)
+    return jnp.where(inside, block, jnp.zeros_like(block))
+
+
+def attend_kernel(
+    rank_ref, query_ref, key_ref, value_ref, key_info_ref, query_info_ref, out_ref, bias_ref, keys, value_t
+):
+    rank = rank_ref[0]
+
+    @pl.when(pl.program_id(0) == 0)
+    def _():
+        fill_bias(bias_ref, key_info_ref, query_info_ref)
+
+    for block in range(ROWS // QBLK):
+        here = rows_of(block, rank)
+        keys[pl.ds(block * QBLK, QBLK), :] = key_ref[here, :]
+        value_t[:, pl.ds(block * QBLK, QBLK)] = value_ref[here, :].T
+    for block in range(ROWS // QBLK):
+        reach = (block + 1) * QBLK
+        here = rows_of(block, rank)
+        queries = query_ref[here, :] * jnp.bfloat16(HEAD_DIM**-0.5)
+        bias = bias_ref[pl.ds(0, reach), pl.ds(block * QBLK, QBLK)]
+        parts = []
+        for head in range(2):
+            scores = nt_dot(keys[pl.ds(0, reach), :], head_lanes(queries, head)) + bias
+            top = jnp.max(scores, axis=0, keepdims=True)
+            terms = jnp.exp(scores - top)
+            total = jnp.sum(terms, axis=0, keepdims=True)
+            heads_t = nn_dot(
+                value_t[pl.ds(head * HEAD_DIM, HEAD_DIM), pl.ds(0, reach)], terms.astype(jnp.bfloat16)
+            )
+            parts.append(heads_t / total)
+        out_ref[here, :] = jnp.concatenate(parts, axis=0).T.astype(out_ref.dtype)
+
+
+def attend(qkv, rank, key_info, query_info):
+    pairs = qkv.shape[1] // (3 * PAIR)
+    cells = ROWS * ROWS * 5 // 8
+    return pl.pallas_call(
+        attend_kernel,
+        grid_spec=pltpu.PrefetchScalarGridSpec(
+            num_scalar_prefetch=1,
+            grid=(pairs,),
+            in_specs=[
+                pl.BlockSpec((ROWS, PAIR), lambda i, r: (0, i)),
+                pl.BlockSpec((ROWS, PAIR), lambda i, r: (0, pairs + i)),
+                pl.BlockSpec((ROWS, PAIR), lambda i, r: (0, 2 * pairs + i)),
+                pl.BlockSpec((ROWS, 2), lambda i, r: (0, 0)),
+                pl.BlockSpec((2, ROWS), lambda i, r: (0, 0)),
+            ],
+            out_specs=pl.BlockSpec((ROWS, PAIR), lambda i, r: (0, i)),
+            scratch_shapes=[
+                pltpu.VMEM((ROWS, ROWS), jnp.float32),
+                pltpu.VMEM((ROWS, PAIR), jnp.bfloat16),
+                pltpu.VMEM((PAIR, ROWS), jnp.bfloat16),
+            ],
+        ),
+        out_shape=jax.ShapeDtypeStruct((ROWS, pairs * PAIR), jnp.bfloat16),
+        compiler_params=pltpu.CompilerParams(vmem_limit_bytes=24 << 20),
+        cost_estimate=pl.CostEstimate(
+            flops=2 * 2 * 2 * pairs * cells * 256, bytes_accessed=ROWS * pairs * PAIR * 8, transcendentals=2 * pairs * cells
+        ),
+        name="attend",
+    )(rank, qkv, qkv, qkv, key_info, query_info)
+
+
+def attend_back_kernel(
+    rank_ref,
+    query_ref,
+    key_ref,
+    value_ref,
+    grad_ref,
+    key_info_ref,
+    query_info_ref,
+    query_out,
+    key_out,
+    value_out,
+    sums_out,
+    bias_ref,
+    keys,
+    values,
+    key_t,
+    key_acc,
+    value_acc,
+):
+    rank = rank_ref[0]
+    scale = HEAD_DIM**-0.5
+
+    @pl.when(pl.program_id(0) == 0)
+    def _():
+        fill_bias(bias_ref, key_info_ref, query_info_ref)
+
+    for block in range(ROWS // QBLK):
+        here = rows_of(block, rank)
+        there = pl.ds(block * QBLK, QBLK)
+        keys[there, :] = key_ref[here, :]
+        values[there, :] = value_ref[here, :]
+        key_t[:, there] = key_ref[here, :].T
+    query_sum = jnp.zeros((1, PAIR), jnp.float32)
+    for block in reversed(range(ROWS // QBLK)):
+        reach = (block + 1) * QBLK
+        here = rows_of(block, rank)
+        upto = pl.ds(0, reach)
+        queries = query_ref[here, :] * jnp.bfloat16(scale)
+        grads = grad_ref[here, :]
+        bias = bias_ref[upto, pl.ds(block * QBLK, QBLK)]
+        parts = []
+        key_add = None
+        value_add = None
+        for head in range(2):
+            query_h = head_lanes(queries, head)
+            grad_h = head_lanes(grads, head)
+            scores = nt_dot(keys[upto, :], query_h) + bias
+            top = jnp.max(scores, axis=0, keepdims=True)
+            terms = jnp.exp(scores - top)
+            prob = terms * (1.0 / jnp.sum(terms, axis=0, keepdims=True))
+            prob_grad = nt_dot(values[upto, :], grad_h)
+            inner = jnp.sum(prob * prob_grad, axis=0, keepdims=True)
+            score_grad = (prob * (prob_grad - inner)).astype(jnp.bfloat16)
+            value_part = nn_dot(prob.astype(jnp.bfloat16), grad_h)
+            key_part = nn_dot(score_grad, query_h)
+            value_add = value_part if value_add is None else value_add + value_part
+            key_add = key_part if key_add is None else key_add + key_part
+            parts.append(nn_dot(key_t[pl.ds(head * HEAD_DIM, HEAD_DIM), upto], score_grad))
+        if block == ROWS // QBLK - 1:
+            key_acc[...] = key_add
+            value_acc[...] = value_add
+        else:
+            key_acc[upto, :] += key_add
+            value_acc[upto, :] += value_add
+        query_grad = jnp.concatenate(parts, axis=0).T * scale
+        query_sum = query_sum + jnp.sum(query_grad, axis=0, keepdims=True)
+        query_out[here, :] = query_grad.astype(query_out.dtype)
+    for block in range(ROWS // QBLK):
+        here = rows_of(block, rank)
+        there = pl.ds(block * QBLK, QBLK)
+        key_out[here, :] = key_acc[there, :].astype(key_out.dtype)
+        value_out[here, :] = value_acc[there, :].astype(value_out.dtype)
+    value_sum = jnp.sum(value_acc[...], axis=0, keepdims=True)
+    row = lax.broadcasted_iota(jnp.int32, (8, PAIR), 0)
+    sums_out[...] = jnp.where(row == 0, query_sum, jnp.where(row == 1, value_sum, 0.0))
+
+
+def attend_back(qkv, grads, rank, key_info, query_info):
+    pairs = qkv.shape[1] // (3 * PAIR)
+    cells = ROWS * ROWS * 5 // 8
+    block = (ROWS, PAIR)
+    wide = jax.ShapeDtypeStruct((ROWS, pairs * PAIR), jnp.bfloat16)
+    return pl.pallas_call(
+        attend_back_kernel,
+        grid_spec=pltpu.PrefetchScalarGridSpec(
+            num_scalar_prefetch=1,
+            grid=(pairs,),
+            in_specs=[
+                pl.BlockSpec(block, lambda i, r: (0, i)),
+                pl.BlockSpec(block, lambda i, r: (0, pairs + i)),
+                pl.BlockSpec(block, lambda i, r: (0, 2 * pairs + i)),
+                pl.BlockSpec(block, lambda i, r: (0, i)),
+                pl.BlockSpec((ROWS, 2), lambda i, r: (0, 0)),
+                pl.BlockSpec((2, ROWS), lambda i, r: (0, 0)),
+            ],
+            out_specs=[
+                pl.BlockSpec(block, lambda i, r: (0, i)),
+                pl.BlockSpec(block, lambda i, r: (0, i)),
+                pl.BlockSpec(block, lambda i, r: (0, i)),
+                pl.BlockSpec((8, PAIR), lambda i, r: (0, i)),
+            ],
+            scratch_shapes=[
+                pltpu.VMEM((ROWS, ROWS), jnp.float32),
+                pltpu.VMEM(block, jnp.bfloat16),
+                pltpu.VMEM(block, jnp.bfloat16),
+                pltpu.VMEM((PAIR, ROWS), jnp.bfloat16),
+                pltpu.VMEM(block, jnp.float32),
+                pltpu.VMEM(block, jnp.float32),
+            ],
+        ),
+        out_shape=[wide, wide, wide, jax.ShapeDtypeStruct((8, pairs * PAIR), jnp.float32)],
+        compiler_params=pltpu.CompilerParams(vmem_limit_bytes=28 << 20),
+        cost_estimate=pl.CostEstimate(
+            flops=2 * 5 * 2 * pairs * cells * 256,
+            bytes_accessed=ROWS * pairs * PAIR * 14,
+            transcendentals=2 * pairs * cells,
+        ),
+        name="attend_back",
+    )(rank, qkv, qkv, qkv, grads, key_info, query_info)
+
+
+SWAP = [(0, 1), (1, 0)]
+PLANE = ("y", "x", "core")
+EVERY = ("z", "y", "x", "core")
+MICRO = 2
+SLOTS = 72
+
+
+def swap_along(array, axis):
+    return lax.ppermute(array, axis, SWAP)
+
+
+def pass_on(array):
+    size = lax.axis_size("z")
+    return lax.ppermute(array, "z", [(i, (i + 1) % size) for i in range(size)])
+
+
+def gather_team(rows):
+    other = swap_along(rows, "x")
+    near = jnp.concatenate([rows, other], axis=0)
+    far = swap_along(near, "core")
+    return jnp.concatenate([near, far], axis=0)
+
+
+def scatter_team(partial):
+    half = partial.shape[0] // 2
+    quarter = half // 2
+    got = swap_along(partial[half:].astype(jnp.bfloat16), "core")
+    kept = partial[:half].astype(jnp.float32) + got.astype(jnp.float32)
+    got = swap_along(kept[quarter:].astype(jnp.bfloat16), "x")
+    return kept[:quarter] + got.astype(jnp.float32)
+
+
+def gather_weight(mine):
+    held = [mine]
+    for _ in range(lax.axis_size("z") - 1):
+        held.append(pass_on(held[-1]))
+    return (held, [swap_along(piece, "y") for piece in held[1:]])
+
+
+def reduce_weight(grad):
+    depth = lax.axis_size("z")
+    half = grad.shape[0] // 2
+    piece = half // depth
+    got = swap_along(grad[half:], "y")
+    parts = [
+        grad[k * piece : (k + 1) * piece].astype(jnp.float32)
+        + got[k * piece : (k + 1) * piece].astype(jnp.float32)
+        for k in range(depth)
+    ]
+    total = parts[1].astype(jnp.bfloat16)
+    for k in list(range(2, depth)) + [0]:
+        total = (parts[k] + pass_on(total).astype(jnp.float32)).astype(jnp.bfloat16)
+    return total
+
+
+def gather_plane(piece):
+    half = piece.shape[0] // 2
+    by_x = swap_along(piece, "x")
+    by_y = swap_along(piece, "y")
+    corner_top = swap_along(by_y[:half], "x")
+    corner_low = swap_along(by_x[half:], "y")
+    near = jnp.concatenate([piece, by_x, by_y, corner_top, corner_low], axis=0)
+    far = swap_along(near, "core")
+    size = piece.shape[0]
+    found = []
+    for core_flip, array in ((0, near), (1, far)):
+        for index, (x_flip, y_flip) in enumerate(((0, 0), (1, 0), (0, 1), (1, 1))):
+            code = 4 * x_flip + 2 * core_flip + y_flip
+            found.append((code, array[index * size : (index + 1) * size]))
+    return found
+
+
+def total_all(vector):
+    for axis in ("core", "x", "y"):
+        vector = vector + swap_along(vector, axis)
+    size = lax.axis_size("z")
+    for step in (1, 2):
+        vector = vector + lax.ppermute(vector, "z", [(i, i ^ step) for i in range(size)])
+    return vector
+
+
+def held_before(bound, residue, parts):
+    return (bound + (parts - 1) - residue) // parts
+
+
+def piece_tables(lengths, starts, quarter_low, quarter_rows, residue, parts):
+    ends = running_sum(lengths)
+    firsts = ends - lengths
+    shift = starts - firsts
+    low = jnp.maximum(firsts, quarter_low)
+    high = jnp.minimum(ends, quarter_low + quarter_rows)
+    begin = held_before(low + shift, residue, parts)
+    count = jnp.where(high > low, held_before(high + shift, residue, parts) - begin, 0)
+    return (begin, count, shift)
+
+
+def slot_lookup(begin, count, value_of):
+    base = running_sum(count) - count
+    slot = jnp.arange(SLOTS, dtype=jnp.int32)
+    inside = (slot >= base[..., None]) & (slot < (base + count)[..., None])
+    held = begin[..., None] + slot - base[..., None]
+    return jnp.sum(jnp.where(inside, value_of(held) + 1, 0), axis=-2, dtype=jnp.int32) - 1
+
+
+def one_hot(wanted, count, dtype=jnp.bfloat16):
+    return (wanted[:, None] == jnp.arange(count, dtype=jnp.int32)[None, :]).astype(dtype)
+
+
+def layer(
+    tokens,
+    cotangent,
+    lengths,
+    dealing,
+    query_weight,
+    key_weight,
+    value_weight,
+    out_weight,
+    query_bias,
+    value_bias,
+    out_bias,
+    up_weight,
+    up_bias,
+    down_weight,
+    down_bias,
+    attn_gain,
+    attn_shift,
+    mlp_gain,
+    mlp_shift,
+):
+    tok_rows = tokens.shape[1]
+    col_width = tokens.shape[2]
+    width = out_weight.shape[1]
+    seq_dev = lengths.shape[2]
+    depth = lax.axis_size("z")
+    parts = lax.axis_size("y") * 4
+    own_rows = tok_rows // 4
+    y, x, core, z = (lax.axis_index(name) for name in ("y", "x", "core", "z"))
+    team = 2 * x + core
+    eighth = 2 * team + y
+    residue = 4 * y + team
+    group = 2 * z + y
+
+    given_off = []
+    for micro_step in range(MICRO):
+        given_off.append(given_layout(lengths[micro_step], dealing[micro_step])[2])
+    starts = jnp.stack(given_off).reshape(lengths.shape)
+    quarter_low = (jnp.arange(4, dtype=jnp.int32) * own_rows)[None, None, :, None]
+    begin, count, _ = piece_tables(
+        lengths[:, :, None, :], starts[:, :, None, :], quarter_low, own_rows, residue, parts
+    )
+    micro_ids = jnp.arange(MICRO, dtype=jnp.int32)[:, None, None, None]
+    begin = jnp.transpose(begin + micro_ids * tok_rows, (1, 2, 0, 3)).reshape(-1, MICRO * seq_dev)
+    count = jnp.transpose(count, (1, 2, 0, 3)).reshape(-1, MICRO * seq_dev)
+    send_row = slot_lookup(begin, count, lambda held: held).reshape(-1)
+
+    my_lengths = lax.dynamic_index_in_dim(lengths, group, 1, keepdims=False)
+    my_starts = lax.dynamic_index_in_dim(starts, group, 1, keepdims=False)
+    residues = jnp.arange(parts, dtype=jnp.int32)[:, None, None]
+    my_begin, my_count, my_shift = piece_tables(
+        my_lengths[None], my_starts[None], team * own_rows, own_rows, residues, parts
+    )
+    flat = (parts, MICRO * seq_dev)
+    row_shift = (
+        my_shift + team * own_rows - jnp.arange(MICRO, dtype=jnp.int32)[None, :, None] * own_rows
+    )
+    row_shift = jnp.broadcast_to(row_shift, my_count.shape).reshape(flat)
+    own_row = slot_lookup(
+        my_begin.reshape(flat),
+        my_count.reshape(flat),
+        lambda held: held * parts + residues - row_shift[..., None],
+    ).reshape(-1)
+    spread_hot = one_hot(send_row, MICRO * tok_rows)
+    spread_hot_t = one_hot(send_row, MICRO * tok_rows).T
+    settle_hot = (
+        own_row[None, :] == jnp.arange(MICRO * own_rows, dtype=jnp.int32)[:, None]
+    ).astype(jnp.bfloat16)
+    settle_hot_t = one_hot(own_row, MICRO * own_rows)
+
+    def deal(array):
+        spread = array.reshape(MICRO, tok_rows // parts, parts, col_width)
+        spread = lax.all_to_all(spread, PLANE, split_axis=2, concat_axis=1, tiled=True)
+        spread = spread.reshape(MICRO * tok_rows, col_width)
+        sent = matmul(spread_hot, spread).astype(jnp.bfloat16)
+        got = lax.all_to_all(sent, EVERY, split_axis=0, concat_axis=0, tiled=True)
+        got = got.reshape(depth, parts * SLOTS, col_width)
+        columns = [matmul(settle_hot, got[k]).astype(jnp.bfloat16) for k in range(depth)]
+        return jnp.concatenate(columns, axis=1)
+
+    def undeal(array):
+        sent = [
+            matmul(settle_hot_t, array[:, k * col_width : (k + 1) * col_width]).astype(jnp.bfloat16)
+            for k in range(depth)
+        ]
+        sent = jnp.concatenate(sent, axis=0)
+        got = lax.all_to_all(sent, EVERY, split_axis=0, concat_axis=0, tiled=True)
+        held = matmul(spread_hot_t, got).astype(jnp.bfloat16)
+        held = held.reshape(MICRO, tok_rows, 1, col_width)
+        back = lax.all_to_all(held, PLANE, split_axis=1, concat_axis=2, tiled=True)
+        return back.reshape(MICRO, tok_rows, col_width)
+
+    head_rows = HEAD_DIM
+    team_cols = query_weight.shape[1] // 4
+    team_units = up_weight.shape[1] // 4
+    half_units = team_units // 2
+
+    def team_slice(array, axis):
+        return lax.dynamic_slice_in_dim(array, team * (array.shape[axis] // 4), array.shape[axis] // 4, axis)
+
+    def halves(array):
+        size = array.shape[0] // 2
+        return (
+            lax.dynamic_slice_in_dim(array, y * size, size, 0),
+            lax.dynamic_slice_in_dim(array, (1 - y) * size, size, 0),
+        )
+
+    attn_parts = [
+        halves(team_slice(array, 1).T) for array in (query_weight, key_weight, value_weight)
+    ] + [halves(team_slice(out_weight, 0))]
+    attn_mine = jnp.concatenate([part[0] for part in attn_parts], axis=0)
+    attn_other = jnp.concatenate([part[1] for part in attn_parts], axis=0)
+    up_mine, up_other = halves(team_slice(up_weight, 1).T)
+    down_mine, down_other = halves(team_slice(down_weight, 0))
+
+    bias_pack = jnp.concatenate([query_bias, value_bias, up_bias]).astype(jnp.float32).reshape(-1, 128)
+    bias_held = [bias_pack]
+    for _ in range(depth - 1):
+        bias_held.append(pass_on(bias_held[-1]))
+    bias_held = [bias.reshape(-1) for bias in bias_held]
+
+    def bias_of(offset, size):
+        return jnp.concatenate(
+            [
+                lax.dynamic_slice_in_dim(bias, offset + (2 * team + half) * size, size)
+                for half in (y, 1 - y)
+                for bias in bias_held
+            ]
+        )
+
+    shard_heads = query_weight.shape[1]
+    query_b = bias_of(0, HEAD_DIM)
+    value_b = bias_of(shard_heads, HEAD_DIM)
+    up_b = bias_of(2 * shard_heads, half_units)
+    qkv_b = jnp.concatenate([query_b, jnp.zeros_like(query_b), value_b])
+
+    tok = deal(tokens)
+    attn_held, attn_got = gather_weight(attn_mine)
+    attn_all = attn_held + [attn_other] + attn_got
+    qkv_w = jnp.concatenate(
+        [piece[k * head_rows : (k + 1) * head_rows] for k in range(3) for piece in attn_all], axis=0
+    )
+    out_w = jnp.concatenate([piece[3 * head_rows :] for piece in attn_all], axis=0)
+    cot = deal(cotangent)
+    up_held, up_got = gather_weight(up_mine)
+    up_w = jnp.concatenate(up_held + [up_other] + up_got, axis=0)
+    down_held, down_got = gather_weight(down_mine)
+    down_w = jnp.concatenate(down_held + [down_other] + down_got, axis=0)
+
+    gain_one, shift_one, gain_two, shift_two, out_b, down_b = (
+        array.astype(jnp.float32)
+        for array in (attn_gain, attn_shift, mlp_gain, mlp_shift, out_bias, down_bias)
+    )
+
+    rank = jnp.full((1,), team, jnp.int32)
+    infos = []
+    for micro_step in range(MICRO):
+        holder, position, _ = buffer_layout(my_lengths[micro_step], my_starts[micro_step], tok_rows)
+        segment = holder * tok_rows + position // (SEG + SUMM)
+        summary = jnp.where(position % (SEG + SUMM) >= SEG, holder, -1)
+        infos.append((jnp.stack([segment, summary], axis=1), jnp.stack([segment, holder], axis=0)))
+
+    layer_rows = []
+    input_rows = []
+    kept = []
+    for m in range(MICRO):
+        rows = tok[m * own_rows : (m + 1) * own_rows].astype(jnp.float32)
+        cot_rows = cot[m * own_rows : (m + 1) * own_rows]
+        normed_one, inverse_one = normalize(rows)
+        first_in = gather_team((normed_one * gain_one + shift_one).astype(jnp.bfloat16))
+        qkv = (times_transpose(first_in, qkv_w) + qkv_b).astype(jnp.bfloat16)
+        mixed = attend(qkv, rank, *infos[m])
+        resid = rows + scatter_team(matmul(mixed, out_w)) + out_b
+        normed_two, inverse_two = normalize(resid.astype(jnp.bfloat16).astype(jnp.float32))
+        second_in = gather_team((normed_two * gain_two + shift_two).astype(jnp.bfloat16))
+        cot_all = gather_team(cot_rows)
+        hidden_pre = times_transpose(second_in, up_w) + up_b
+        hidden_act, gelu_pull = jax.vjp(gelu_tanh, hidden_pre)
+        hidden = hidden_act.astype(jnp.bfloat16)
+        hidden_grad = gelu_pull(times_transpose(cot_all, down_w))[0]
+        hidden_low = hidden_grad.astype(jnp.bfloat16)
+        layer_rows.append((resid + scatter_team(matmul(hidden, down_w)) + down_b).astype(jnp.bfloat16))
+        second_grad = scatter_team(matmul(hidden_low, up_w)).astype(jnp.bfloat16).astype(jnp.float32)
+        back, gain_two_part, shift_two_part = norm_backward(second_grad, normed_two, inverse_two, gain_two)
+        resid_grad = cot_rows.astype(jnp.float32) + back
+        attn_low = gather_team(resid_grad.astype(jnp.bfloat16))
+        mixed_grad = times_transpose(attn_low, out_w).astype(jnp.bfloat16)
+        query_low, key_low, value_low, sums = attend_back(qkv, mixed_grad, rank, *infos[m])
+        qkv_low = jnp.concatenate([query_low, key_low, value_low], axis=1)
+        first_grad = scatter_team(matmul(qkv_low, qkv_w)).astype(jnp.bfloat16).astype(jnp.float32)
+        back, gain_one_part, shift_one_part = norm_backward(first_grad, normed_one, inverse_one, gain_one)
+        input_rows.append((resid_grad + back).astype(jnp.bfloat16))
+        kept.append(
+            dict(
+                up=cross_rows(hidden_low, second_in),
+                down=cross_rows(hidden, cot_all),
+                out=cross_rows(mixed, attn_low),
+                qkv=cross_rows(qkv_low, first_in),
+                query_b=sums[0],
+                value_b=sums[1],
+                up_b=jnp.sum(hidden_grad, axis=0),
+                vectors=(
+                    jnp.sum(resid_grad, axis=0),
+                    jnp.sum(cot_rows.astype(jnp.float32), axis=0),
+                    gain_one_part,
+                    shift_one_part,
+                    gain_two_part,
+                    shift_two_part,
+                ),
+            )
+        )
+
+    layer_out = undeal(jnp.concatenate(layer_rows, axis=0))
+
+    def both(name):
+        return (kept[0][name] + kept[1][name]).astype(jnp.bfloat16)
+
+    def into(pieces, rows_per, start, size):
+        shard = jnp.zeros((8 * size, width), jnp.bfloat16)
+        for code, piece in pieces:
+            at = jnp.bitwise_xor(eighth, code)
+            shard = lax.dynamic_update_slice(shard, piece[start : start + size], (at * size, 0))
+        return shard.astype(jnp.float32)
+
+    down_grad = into(gather_plane(reduce_weight(both("down"))), half_units, 0, half_units)
+    up_grad = into(gather_plane(reduce_weight(both("up"))), half_units, 0, half_units).T
+    qkv_grad = both("qkv")
+    out_grad = both("out")
+    heads = qkv_grad.shape[0] // 3
+    attn_grad = jnp.concatenate(
+        [
+            array[k * head_rows : (k + 1) * head_rows]
+            for k in range(2 * depth)
+            for array in (qkv_grad[:heads], qkv_grad[heads : 2 * heads], qkv_grad[2 * heads :], out_grad)
+        ],
+        axis=0,
+    )
+    attn_pieces = gather_plane(reduce_weight(attn_grad))
+    query_grad, key_grad, value_grad, out_w_grad = (
+        into(attn_pieces, 4 * head_rows, k * head_rows, head_rows) for k in range(4)
+    )
+
+    def place(vector, shard_size, size):
+        whole = jnp.zeros((depth * shard_size,), jnp.float32)
+        for index in range(2 * depth):
+            half = y if index < depth else 1 - y
+            owner = lax.rem(z - index % depth + depth, depth)
+            whole = lax.dynamic_update_slice(
+                whole,
+                vector[index * size : (index + 1) * size],
+                (owner * shard_size + (2 * team + half) * size,),
+            )
+        return whole
+
+    small = [kept[0][name] + kept[1][name] for name in ("query_b", "value_b", "up_b")]
+    vectors = [
+        place(small[0], shard_heads, HEAD_DIM),
+        place(small[1], shard_heads, HEAD_DIM),
+        place(small[2], up_weight.shape[1], half_units),
+    ] + [kept[0]["vectors"][k] + kept[1]["vectors"][k] for k in range(6)]
+    sizes = [vector.shape[0] for vector in vectors]
+    packed = total_all(jnp.concatenate(vectors).reshape(-1, 128)).reshape(-1)
+    pieces = []
+    offset = 0
+    for size in sizes:
+        pieces.append(packed[offset : offset + size])
+        offset += size
+    query_b_grad, value_b_grad, up_b_grad, out_b_grad, down_b_grad, *norm_grads = pieces
+
+    def own_shard(vector):
+        size = vector.shape[0] // depth
+        return lax.dynamic_slice_in_dim(vector, z * size, size)
+
+    input_grad = undeal(jnp.concatenate(input_rows, axis=0))
+    return (
+        layer_out,
+        input_grad,
+        query_grad.T,
+        key_grad.T,
+        value_grad.T,
+        out_w_grad,
+        own_shard(query_b_grad),
+        own_shard(value_b_grad),
+        out_b_grad,
+        up_grad,
+        own_shard(up_b_grad),
+        down_grad,
+        down_b_grad,
+        *norm_grads,
+    )
+
+
+def team_layer(mesh):
+    axes = ("y", "x", "core", "z")
+    inner = Mesh(mesh.devices.reshape(2, 2, 2, 4), axes)
+    rows = P(None, PLANE, "z")
+    in_specs = (
+        rows, rows, P(), P(), P(None, "z"), P(None, "z"), P(None, "z"), P("z", None), P("z"), P("z"),
+        P(), P(None, "z"), P("z"), P("z", None), P(), P(), P(), P(), P(),
+    )
+    out_specs = (
+        rows, rows, P(None, "z"), P(None, "z"), P(None, "z"), P("z", None), P("z"), P("z"),
+        P(), P(None, "z"), P("z"), P("z", None), P(), P(), P(), P(), P(),
+    )
+    return jax.shard_map(layer, mesh=inner, in_specs=in_specs, out_specs=out_specs, check_vma=False)
+
+
+def solution(mesh):
+    if dict(mesh.shape) == {"dp": 8, "tensor": 4}:
+        return team_layer(mesh)
+    return general_layer(mesh)

time: 3240 us -> 1610 us (0.50)
  waiting for transfers between devices: 2410 us -> 680 us
  matrix products: 428 us -> 314 us
  starting transfers between devices: 2.24 us -> 106 us
  local copies, waits for them, and re-layouts: 171 us -> 269 us
  Pallas kernels: 0 us -> 92 us
  other arithmetic: 180 us -> 124 us
    all_gather x14 -> x0, waiting for transfers between devices: 925 us -> none  [the longest x2 159 us: shards(): lax.all_gather(first_cols.astype(jnp.bfloat16), 'tensor', axis=1, tiled=T...]
    reduce_scatter x10 -> x0, waiting for transfers between devices: 891 us -> none  [the longest x2 273 us: shards(): lax.psum_scatter(times_transpose(hidden_low, up_weight), 'tensor', scatte...]
    ppermute x0 -> x85, waiting for transfers between devices: none -> 611 us  [the longest x62 373 us: swap_along(): return lax.ppermute(array, axis, SWAP)]
    psum x1 -> x0, waiting for transfers between devices: 586 us -> none  [shards(): lax.psum((query_w_grad, key_w_grad, value_w_grad, out_w_grad, query_b_gra...]
    gather x6 -> x0, local copies, waits for them, and re-layouts: 108 us -> none  [the longest x2 70.5 us: shards(): jnp.take(packed, jnp.clip(buffer_row, 0, tok_rows - 1), axis=0)]
    unnamed x373 -> x428, local copies, waits for them, and re-layouts: 47.6 us -> 149 us
    pallas_call x0 -> x4, Pallas kernels: none -> 92 us  [the longest x2 54.7 us: attend_back(): pl.pallas_call(attend_back_kernel, grid_spec=pltpu.PrefetchScalarGridSpec...]
    dot_general x20 -> x0, matrix products: 86.5 us -> none  [the longest x4 29.4 us: shards(): jnp.einsum('qhd,khd->hqk', grad_block, values_here[:row_upper], preferred...]
  transfers between devices with their start and end apart: 25 -> 93, of which waited for: 24 -> 39; matrix products, arithmetic and copies ran while one was open for 14% -> 41% of each run, Pallas kernels for 0% -> 6%
where the time goes in v1:
time: 1610 us; the launch traced here: 1590 us
  waiting for transfers between devices  680 us (42%)
  matrix products  314 us (20%)
  local copies, waits for them, and re-layouts  269 us (17%)
  other arithmetic  124 us (8%)
  starting transfers between devices  106 us (7%)
  Pallas kernels  92 us (6%)
    ppermute x62, waiting for transfers between devices, swap_along(): return lax.ppermute(array, axis, SWAP)  373 us
    ppermute x21, waiting for transfers between devices, pass_on(): return lax.ppermute(array, 'z', [(i, (i + 1) % size) for i in range(size)])  217 us
    unnamed x428, local copies, waits for them, and re-layouts  149 us
    dot_general x28, matrix products, matmul(): return jnp.dot(left_array, right_array, preferred_element_type=jnp.float32)  121 us
    dot_general x8, matrix products, times_transpose(): lax.dot_general(left_array, right_array, (((1,), (1,)), ((), ())), prefer...  98.5 us
    dot_general x8, matrix products, cross_rows(): lax.dot_general(left_array, right_array, (((0,), (0,)), ((), ())), prefer...  94.9 us
    pallas_call x2, Pallas kernels, attend_back(): pl.pallas_call(attend_back_kernel, grid_spec=pltpu.PrefetchScalarGridSpec...  54.7 us
    ppermute x62, starting transfers between devices, swap_along(): return lax.ppermute(array, axis, SWAP)  42.5 us
  transfers between devices with their start and end apart: 93, of which 39 were waited for; matrix products, arithmetic and copies ran while one was open for 41% of the time, Pallas kernels for 6%

profile of v1, /device:TPU:0, one launch (start us, length us, event | category | flops | bytes accessed | tf_op | source)
XLA Modules:
  0.0 1590.2 jit_solution(10636423970382548263)
XLA Ops:
  47.8 29.4 %collective-permute-done.8 = f32[24,128]{1,0:T(8,128)S(1)} collective-permute-done((f32[24,128]{1,0:T(8,128)S(1)}, f32[24,128]{1,0:T(8,128)S(1)}, u32[]{:S(2)}, u32[]{:S(2)}) %collective-permute-start.8) | collective-permute-done | bytes 12320 | tf_op jit(solution)/shard_map/ppermute | solution.py:727
  96.7 6.6 fusion.20
  103.4 30.5 %all-to-all-done.4 = bf16[2,128,8,512]{3,1,0,2:T(8,128)(2,1)} async-done(((bf16[2,128,8,512]{3,1,0,2:T(8,128)(2,1)}), bf16[2,128,8,512]{3,1,0,2:T(8,128)(2,1)}, u32[]{:S(2)}, u32[]{:S(2)}) %all-to-all-start.4) | async-done | bytes 2097184 | tf_op jit(solution)/shard_map/all_to_all | solution.py:894
  143.2 6.6 fusion.21
  153.0 51.7 %collective-permute-done.4 = bf16[256,2048]{1,0:T(8,128)(2,1)S(1)} collective-permute-done((bf16[256,2048]{1,0:T(8,128)(2,1)}, bf16[256,2048]{1,0:T(8,128)(2,1)S(1)}, u32[]{:S(2)}, u32[]{:S(2)}) %collective-permute-start.4) | collective-permute-done | bytes 1048608 | tf_op jit(solution)/shard_map/ppermute | solution.py:727
  208.2 10.8 collective-permute-start.16
  223.8 9.3 collective-permute-done.7
  245.0 16.2 %all-to-all-done.1 = bf16[32,72,512]{2,1,0:T(8,128)(2,1)S(1)} async-done(((bf16[32,72,512]{2,1,0:T(8,128)(2,1)}), bf16[32,72,512]{2,1,0:T(8,128)(2,1)S(1)}, u32[]{:S(2)}, u32[]{:S(2)}) %all-to-all-start.1) | async-done | bytes 2359328 | tf_op jit(solution)/shard_map/all_to_all | solution.py:897
  275.7 38.2 %collective-permute-done = bf16[256,2048]{0,1:T(8,128)(2,1)S(1)} collective-permute-done((bf16[256,2048]{0,1:T(8,128)(2,1)S(1)}, bf16[256,2048]{0,1:T(8,128)(2,1)S(1)}, u32[]{:S(2)}, u32[]{:S(2)}) %collective-permute-start) | collective-permute-done | bytes 1048608 | tf_op jit(solution)/shard_map/ppermute | solution.py:722
  318.5 22.0 %collective-permute-done.29 = bf16[256,2048]{0,1:T(8,128)(2,1)S(1)} collective-permute-done((bf16[256,2048]{0,1:T(8,128)(2,1)S(1)}, bf16[256,2048]{0,1:T(8,128)(2,1)S(1)}, u32[]{:S(2)}, u32[]{:S(2)}) %collective-permute-start.29) | collective-permute-done | bytes 1048608 | tf_op jit(solution)/shard_map/ppermute | solution.py:722
  340.8 9.7 add_convert_fusion.4.query_ref.key_ref.value_ref
  350.5 18.7 %attend.2 = bf16[1024,512]{1,0:T(8,128)(2,1)S(1)} custom-call(s32[1]{0:T(128)} %bitcast.15.rank_ref, bf16[1024,1536]{1,0:T(8,128)(2,1)S(1)} %add_convert_fusion.4.query_ref.key_ref.value_ref, bf16[1024,1536]{1,0:T(8,128)(2,1)S(1)} %add_convert_fusion.4.query_ref.key_ref.value_ref, bf16[1024,1536]{1,0:T(8,128)(2,1)S(1)} %add_convert_fusion.4.query_ref.key_ref.value_ref, ...), custom_call_target="tpu_custom_call" | custom-call | flops 5368709120 | bytes 4194304 | tf_op jit(solution)/shard_map/attend/pallas_call | solution.py:565
  375.7 9.6 add_convert_fusion.3.query_ref.key_ref.value_ref
  385.3 18.5 %attend.3 = bf16[1024,512]{1,0:T(8,128)(2,1)S(1)} custom-call(s32[1]{0:T(128)} %bitcast.15.rank_ref, bf16[1024,1536]{1,0:T(8,128)(2,1)S(1)} %add_convert_fusion.3.query_ref.key_ref.value_ref, bf16[1024,1536]{1,0:T(8,128)(2,1)S(1)} %add_convert_fusion.3.query_ref.key_ref.value_ref, bf16[1024,1536]{1,0:T(8,128)(2,1)S(1)} %add_convert_fusion.3.query_ref.key_ref.value_ref, ...), custom_call_target="tpu_custom_call" | custom-call | flops 5368709120 | bytes 4194304 | tf_op jit(solution)/shard_map/attend/pallas_call | solution.py:565
  431.1 21.8 %collective-permute-done.17 = bf16[256,2048]{0,1:T(8,128)(2,1)} collective-permute-done((bf16[256,2048]{0,1:T(8,128)(2,1)}, bf16[256,2048]{0,1:T(8,128)(2,1)}, u32[]{:S(2)}, u32[]{:S(2)}) %collective-permute-start.17) | collective-permute-done | bytes 1048608 | tf_op jit(solution)/shard_map/ppermute | solution.py:727
  464.6 12.9 collective-permute-done.32
  485.5 20.3 %collective-permute-done.13 = bf16[256,2048]{0,1:T(8,128)(2,1)S(1)} collective-permute-done((bf16[256,2048]{0,1:T(8,128)(2,1)S(1)}, bf16[256,2048]{0,1:T(8,128)(2,1)S(1)}, u32[]{:S(2)}, u32[]{:S(2)}) %collective-permute-start.13) | collective-permute-done | bytes 1048608 | tf_op jit(solution)/shard_map/ppermute | solution.py:722
  516.5 14.8 collective-permute-done.20
  533.8 22.2 %collective-permute-done.37 = bf16[256,2048]{0,1:T(8,128)(2,1)S(1)} collective-permute-done((bf16[256,2048]{0,1:T(8,128)(2,1)S(1)}, bf16[256,2048]{0,1:T(8,128)(2,1)S(1)}, u32[]{:S(2)}, u32[]{:S(2)}) %collective-permute-start.37) | collective-permute-done | bytes 1048608 | tf_op jit(solution)/shard_map/ppermute | solution.py:722
  557.6 20.5 %collective-permute-done.33 = bf16[256,2048]{0,1:T(8,128)(2,1)S(1)} collective-permute-done((bf16[256,2048]{0,1:T(8,128)(2,1)S(1)}, bf16[256,2048]{0,1:T(8,128)(2,1)S(1)}, u32[]{:S(2)}, u32[]{:S(2)}) %collective-permute-start.33) | collective-permute-done | bytes 1048608 | tf_op jit(solution)/shard_map/ppermute | solution.py:722
  581.1 11.4 fusion.108
  592.5 14.6 fusion.237
  611.2 14.0 fusion.106
  625.2 14.4 fusion.238
  645.1 21.3 %fusion.256 = (f32[2048]{0:T(1024)S(1)}, bf16[1024,2048]{1,0:T(8,128)(2,1)}) fusion(f32[1024,2048]{1,0:T(8,128)} %fusion.106, f32[2048]{0:T(1024)S(1)} %constant_dynamic-update-slice_fusion.52, bf16[2048,2048]{1,0:T(8,128)(2,1)} %constant_dynamic-update-slice_fusion.12, bf16[512,2048]{0,1:T(8,128)(2,1)} %collective-permute-done.46, ...), kind=kOutput, calls=%fused_computation.679 | convolution fusion | flops 8648652800 | bytes 25182208 | tf_op jit(solution)/shard_map/dot_general | solution.py:37
  666.4 12.6 fusion.98
  684.0 21.1 %fusion.255 = (f32[2048]{0:T(1024)S(1)}, bf16[1024,2048]{1,0:T(8,128)(2,1)}) fusion(f32[1024,2048]{1,0:T(8,128)} %fusion.108, f32[2048]{0:T(1024)S(1)} %constant_dynamic-update-slice_fusion.52, bf16[2048,2048]{1,0:T(8,128)(2,1)} %constant_dynamic-update-slice_fusion.12, bf16[512,2048]{0,1:T(8,128)(2,1)} %collective-permute-done.38, ...), kind=kOutput, calls=%fused_computation.678 | convolution fusion | flops 8648652800 | bytes 25182208 | tf_op jit(solution)/shard_map/dot_general | solution.py:37
  705.0 12.7 fusion.101
  723.4 14.2 fusion.96
  737.6 16.2 %add_convert_fusion.1 = bf16[2048,2048]{1,0:T(8,128)(2,1)} fusion(f32[2048,2048]{1,0:T(8,128)} %fusion.96, bf16[1024,2048]{1,0:T(8,128)(2,1)} %get-tuple-element.305, bf16[512,2048]{0,1:T(8,128)(2,1)} %copy-done.163, bf16[256,2048]{0,1:T(8,128)(2,1)S(1)} %copy-done.80, bf16[256,2048]{0,1:T(8,128)(2,1)S(1)} %get-tuple-element.267), kind=kOutput, calls=%fused_computation.7 | convolution fusion | flops 8610906112 | bytes 33554432 | tf_op jit(solution)/shard_map/dot_general | solution.py:31
  759.5 17.2 %fusion.103 = f32[2048,2048]{1,0:T(8,128)} fusion(bf16[512,2048]{0,1:T(8,128)(2,1)} %collective-permute-done.46, bf16[256,2048]{0,1:T(8,128)(2,1)S(1)} %copy-done.82, bf16[256,2048]{0,1:T(8,128)(2,1)S(1)} %copy-done.51, f32[1024,2048]{1,0:T(8,128)} %fusion.106, f32[2048]{0:T(1024)S(1)} %constant_dynamic-update-slice_fusion.52), kind=kOutput, calls=%fused_computation.224 | convolution fusion | flops 8623489024 | bytes 29368320 | tf_op jit(solution)/shard_map/dot_general | solution.py:31
  776.7 18.0 %add_convert_fusion = bf16[2048,2048]{1,0:T(8,128)(2,1)} fusion(f32[2048,2048]{1,0:T(8,128)} %fusion.103, bf16[512,2048]{0,1:T(8,128)(2,1)} %collective-permute-done.38, bf16[256,2048]{0,1:T(8,128)(2,1)S(1)} %copy-done.84, bf16[256,2048]{0,1:T(8,128)(2,1)S(1)} %copy-done.49, f32[1024,2048]{1,0:T(8,128)} %fusion.108, ...), kind=kOutput, calls=%fused_computation.6 | convolution fusion | flops 8631877632 | bytes 37756928 | tf_op jit(solution)/shard_map/dot_general | solution.py:31
  818.9 13.3 collective-permute-done.48
  832.5 22.2 %collective-permute-done.40 = bf16[256,2048]{0,1:T(8,128)(2,1)S(1)} collective-permute-done((bf16[256,2048]{0,1:T(8,128)(2,1)S(1)}, bf16[256,2048]{0,1:T(8,128)(2,1)S(1)}, u32[]{:S(2)}, u32[]{:S(2)}) %collective-permute-start.40) | collective-permute-done | bytes 1048608 | tf_op jit(solution)/shard_map/ppermute | solution.py:722
  861.6 15.6 collective-permute-done.28
  877.4 22.2 %collective-permute-done.36 = bf16[256,2048]{0,1:T(8,128)(2,1)S(1)} collective-permute-done((bf16[256,2048]{0,1:T(8,128)(2,1)S(1)}, bf16[256,2048]{0,1:T(8,128)(2,1)S(1)}, u32[]{:S(2)}, u32[]{:S(2)}) %collective-permute-start.36) | collective-permute-done | bytes 1048608 | tf_op jit(solution)/shard_map/ppermute | solution.py:722
  904.4 17.7 %collective-permute-done.41 = bf16[256,2048]{0,1:T(8,128)(2,1)S(1)} collective-permute-done((bf16[256,2048]{0,1:T(8,128)(2,1)S(1)}, bf16[256,2048]{0,1:T(8,128)(2,1)S(1)}, u32[]{:S(2)}, u32[]{:S(2)}) %collective-permute-start.41) | collective-permute-done | bytes 1048608 | tf_op jit(solution)/shard_map/ppermute | solution.py:722
  927.1 14.4 collective-permute-done.76
  957.5 19.7 %collective-permute-done.77 = bf16[256,2048]{1,0:T(8,128)(2,1)} collective-permute-done((bf16[256,2048]{1,0:T(8,128)(2,1)}, bf16[256,2048]{1,0:T(8,128)(2,1)}, u32[]{:S(2)}, u32[]{:S(2)}) %collective-permute-start.77) | collective-permute-done | bytes 1048608 | tf_op jit(solution)/shard_map/ppermute | solution.py:727
  984.5 27.4 %attend_back.2 = (bf16[1024,512]{1,0:T(8,128)(2,1)S(1)}, bf16[1024,512]{1,0:T(8,128)(2,1)S(1)}, bf16[1024,512]{1,0:T(8,128)(2,1)S(1)}, f32[8,512]{1,0:T(8,128)S(1)}) custom-call(s32[1]{0:T(128)} %bitcast.15.rank_ref, bf16[1024,1536]{1,0:T(8,128)(2,1)S(1)} %copy-done.7, bf16[1024,1536]{1,0:T(8,128)(2,1)S(1)} %copy-done.7, bf16[1024,1536]{1,0:T(8,128)(2,1)S(1)} %copy-done.7, ...), custom_call_target="tpu_custom_call" | custom-call | flops 13421772800 | bytes 7340032 | tf_op jit(solution)/shard_map/attend_back/pallas_call | solution.py:675
  1012.2 10.6 fusion.259
  1024.7 6.6 fusion.113.grad_ref
  1031.3 27.3 %attend_back.3 = (bf16[1024,512]{1,0:T(8,128)(2,1)S(1)}, bf16[1024,512]{1,0:T(8,128)(2,1)S(1)}, bf16[1024,512]{1,0:T(8,128)(2,1)S(1)}, f32[8,512]{1,0:T(8,128)S(1)}) custom-call(s32[1]{0:T(128)} %bitcast.15.rank_ref, bf16[1024,1536]{1,0:T(8,128)(2,1)S(1)} %copy-done.5, bf16[1024,1536]{1,0:T(8,128)(2,1)S(1)} %copy-done.5, bf16[1024,1536]{1,0:T(8,128)(2,1)S(1)} %copy-done.5, ...), custom_call_target="tpu_custom_call" | custom-call | flops 13421772800 | bytes 7340032 | tf_op jit(solution)/shard_map/attend_back/pallas_call | solution.py:675
  1058.9 9.2 fusion.260
  1073.5 9.8 fusion.107
  1083.3 11.1 add_convert_fusion.2
  1125.4 23.1 %collective-permute-done.70 = bf16[256,2048]{1,0:T(8,128)(2,1)S(1)} collective-permute-done((bf16[256,2048]{1,0:T(8,128)(2,1)S(1)}, bf16[256,2048]{1,0:T(8,128)(2,1)S(1)}, u32[]{:S(2)}, u32[]{:S(2)}) %collective-permute-start.70) | collective-permute-done | bytes 1048608 | tf_op jit(solution)/shard_map/ppermute | solution.py:727
  1153.6 16.3 %collective-permute-done.79 = bf16[256,2048]{1,0:T(8,128)(2,1)S(1)} collective-permute-done((bf16[256,2048]{1,0:T(8,128)(2,1)S(1)}, bf16[256,2048]{1,0:T(8,128)(2,1)S(1)}, u32[]{:S(2)}, u32[]{:S(2)}) %collective-permute-start.79) | collective-permute-done | bytes 1048608 | tf_op jit(solution)/shard_map/ppermute | solution.py:727
  1183.6 7.7 fusion.22
  1211.2 31.9 %collective-permute-done.72 = bf16[256,2048]{1,0:T(8,128)(2,1)} collective-permute-done((bf16[256,2048]{1,0:T(8,128)(2,1)}, bf16[256,2048]{1,0:T(8,128)(2,1)}, u32[]{:S(2)}, u32[]{:S(2)}) %collective-permute-start.72) | collective-permute-done | bytes 1048608 | tf_op jit(solution)/shard_map/ppermute | solution.py:722
  1245.1 31.7 %collective-permute-done.81 = bf16[256,2048]{1,0:T(8,128)(2,1)S(1)} collective-permute-done((bf16[256,2048]{1,0:T(8,128)(2,1)S(1)}, bf16[256,2048]{1,0:T(8,128)(2,1)S(1)}, u32[]{:S(2)}, u32[]{:S(2)}) %collective-permute-start.81) | collective-permute-done | bytes 1048608 | tf_op jit(solution)/shard_map/ppermute | solution.py:722
  1295.8 7.1 collective-permute-done.82
  1307.4 15.5 collective-permute-done.52
  1343.9 15.2 collective-permute-done.54
  1372.0 21.4 %collective-permute-done.66 = f32[192,128]{1,0:T(8,128)} collective-permute-done((f32[192,128]{1,0:T(8,128)S(1)}, f32[192,128]{1,0:T(8,128)}, u32[]{:S(2)}, u32[]{:S(2)}) %collective-permute-start.66) | collective-permute-done | bytes 98336 | tf_op jit(solution)/shard_map/ppermute | solution.py:791
  1408.3 11.8 convert_bitcast_fusion
  1424.9 26.1 %collective-permute-done.56 = bf16[256,2048]{1,0:T(8,128)(2,1)S(1)} collective-permute-done((bf16[256,2048]{1,0:T(8,128)(2,1)S(1)}, bf16[256,2048]{1,0:T(8,128)(2,1)S(1)}, u32[]{:S(2)}, u32[]{:S(2)}) %collective-permute-start.56) | collective-permute-done | bytes 1048608 | tf_op jit(solution)/shard_map/ppermute | solution.py:727
  1459.3 17.8 %copy.274 = f32[2048,2048]{1,0:T(8,128)} copy(f32[2048,2048]{0,1:T(8,128)} %convert_bitcast_fusion) | data formatting | bytes 33554432
  1477.1 11.7 convert_element_type.587
  1494.8 6.3 collective-permute-done.59
  1506.7 7.7 fusion.23
  1527.2 22.0 %all-to-all-done.7 = bf16[2,1024,1,512]{3,0,2,1:T(2,128)(2,1)} async-done(((bf16[2,1024,1,512]{3,0,2,1:T(2,128)(2,1)}), bf16[2,1024,1,512]{3,0,2,1:T(2,128)(2,1)}, u32[]{:S(2)}, u32[]{:S(2)}) %all-to-all-start.7) | async-done | bytes 2097184 | tf_op jit(solution)/shard_map/all_to_all | solution.py:911
  1565.7 5.5 copy.271
  1573.7 5.5 copy.272
  (894 shorter events, 496.3 us)
Async XLA Ops:
  3.6 86.9 %collective-permute-start.21 = (bf16[256,2048]{1,0:T(8,128)(2,1)}, bf16[256,2048]{1,0:T(8,128)(2,1)}, u32[]{:S(2)}, u32[]{:S(2)}) collective-permute-start(bf16[256,2048]{1,0:T(8,128)(2,1)} %get-tuple-element.167), channel_id=1, source_target_pairs={{0,1},{1,2},{2,3},{3,0},{4,5},{5,6},{6,7},{7,4},{8,9},{9,10},{10,1... | collective-permute-start | bytes 3145736 | tf_op jit(solution)/shard_map/ppermute | solution.py:727
  9.7 198.1 %collective-permute-start.15 = (bf16[256,2048]{0,1:T(8,128)(2,1)}, bf16[256,2048]{0,1:T(8,128)(2,1)}, u32[]{:S(2)}, u32[]{:S(2)}) collective-permute-start(bf16[256,2048]{0,1:T(8,128)(2,1)} %get-tuple-element.165), channel_id=1, source_target_pairs={{0,1},{1,2},{2,3},{3,0},{4,5},{5,6},{6,7},{7,4},{8,9},{9,10},{10,1... | collective-permute-start | bytes 3145736 | tf_op jit(solution)/shard_map/ppermute | solution.py:727
  21.4 67.5 %collective-permute-start.2 = (bf16[256,2048]{1,0:T(8,128)(2,1)}, bf16[256,2048]{1,0:T(8,128)(2,1)}, u32[]{:S(2)}, u32[]{:S(2)}) collective-permute-start(bf16[256,2048]{1,0:T(8,128)(2,1)} %pad_maximum_fusion.44), channel_id=1, source_target_pairs={{0,1},{1,2},{2,3},{3,0},{4,5},{5,6},{6,7},{7,4},{8,9},{9,10},{10,1... | collective-permute-start | bytes 3145736 | tf_op jit(solution)/shard_map/ppermute | solution.py:727
  23.0 54.2 %collective-permute-start.8 = (f32[24,128]{1,0:T(8,128)S(1)}, f32[24,128]{1,0:T(8,128)S(1)}, u32[]{:S(2)}, u32[]{:S(2)}) collective-permute-start(f32[24,128]{1,0:T(8,128)S(1)} %get-tuple-element.293), channel_id=1, source_target_pairs={{0,1},{1,2},{2,3},{3,0},{4,5},{5,6},{6,7},{7,4},{8,9},{9,10},{10,1... | collective-permute-start | bytes 36872 | tf_op jit(solution)/shard_map/ppermute | solution.py:727
  26.7 63.7 %all-to-all-start = ((bf16[2,128,8,512]{3,1,0,2:T(8,128)(2,1)}), bf16[2,128,8,512]{3,1,0,2:T(8,128)(2,1)S(1)}, u32[]{:S(2)}, u32[]{:S(2)}) async-start(bf16[2,128,8,512]{3,1,0,2:T(8,128)(2,1)} %copy.237), calls=%async_computation | async-start | bytes 4194304 | tf_op jit(solution)/shard_map/all_to_all | solution.py:894
  88.9 52.3 %collective-permute-start.3 = (bf16[256,2048]{1,0:T(8,128)(2,1)}, bf16[256,2048]{1,0:T(8,128)(2,1)}, u32[]{:S(2)}, u32[]{:S(2)}) collective-permute-start(bf16[256,2048]{1,0:T(8,128)(2,1)} %collective-permute-done.2), channel_id=1, source_target_pairs={{0,1},{1,2},{2,3},{3,0},{4,5},{5,6},{6,7},{7,4},{8,9},{9,10},{10,1... | collective-permute-start | bytes 3145736 | tf_op jit(solution)/shard_map/ppermute | solution.py:727
  88.9 130.1 %collective-permute-start.5 = (bf16[256,2048]{1,0:T(8,128)(2,1)}, bf16[256,2048]{1,0:T(8,128)(2,1)}, u32[]{:S(2)}, u32[]{:S(2)}) collective-permute-start(bf16[256,2048]{1,0:T(8,128)(2,1)} %collective-permute-done.2), channel_id=1, source_target_pairs={{0,16},{16,0},{1,17},{17,1},{2,18},{18,2},{3,19},{19,3},{4,20},{20... | collective-permute-start | bytes 3145736 | tf_op jit(solution)/shard_map/ppermute | solution.py:722
  90.4 117.8 %collective-permute-start.22 = (bf16[256,2048]{1,0:T(8,128)(2,1)}, bf16[256,2048]{1,0:T(8,128)(2,1)}, u32[]{:S(2)}, u32[]{:S(2)}) collective-permute-start(bf16[256,2048]{1,0:T(8,128)(2,1)} %collective-permute-done.21), channel_id=1, source_target_pairs={{0,1},{1,2},{2,3},{3,0},{4,5},{5,6},{6,7},{7,4},{8,9},{9,10},{10,1... | collective-permute-start | bytes 3145736 | tf_op jit(solution)/shard_map/ppermute | solution.py:727
  90.5 43.4 %all-to-all-start.4 = ((bf16[2,128,8,512]{3,1,0,2:T(8,128)(2,1)}), bf16[2,128,8,512]{3,1,0,2:T(8,128)(2,1)}, u32[]{:S(2)}, u32[]{:S(2)}) async-start(bf16[2,128,8,512]{3,1,0,2:T(8,128)(2,1)} %copy.257), calls=%async_computation.4 | async-start | bytes 4194304 | tf_op jit(solution)/shard_map/all_to_all | solution.py:894
  133.9 127.3 %all-to-all-start.1 = ((bf16[32,72,512]{2,1,0:T(8,128)(2,1)}), bf16[32,72,512]{2,1,0:T(8,128)(2,1)S(1)}, u32[]{:S(2)}, u32[]{:S(2)}) async-start(bf16[32,72,512]{2,1,0:T(8,128)(2,1)} %bitcast.239), calls=%async_computation.1 | async-start | bytes 4718592 | tf_op jit(solution)/shard_map/all_to_all | solution.py:897
  141.1 63.6 %collective-permute-start.4 = (bf16[256,2048]{1,0:T(8,128)(2,1)}, bf16[256,2048]{1,0:T(8,128)(2,1)S(1)}, u32[]{:S(2)}, u32[]{:S(2)}) collective-permute-start(bf16[256,2048]{1,0:T(8,128)(2,1)} %collective-permute-done.3), channel_id=1, source_target_pairs={{0,1},{1,2},{2,3},{3,0},{4,5},{5,6},{6,7},{7,4},{8,9},{9,10},{10,1... | collective-permute-start | bytes 3145736 | tf_op jit(solution)/shard_map/ppermute | solution.py:727
  149.8 73.2 %collective-permute-start.6 = (bf16[256,2048]{1,0:T(8,128)(2,1)}, bf16[256,2048]{1,0:T(8,128)(2,1)S(1)}, u32[]{:S(2)}, u32[]{:S(2)}) collective-permute-start(bf16[256,2048]{1,0:T(8,128)(2,1)} %collective-permute-done.3), channel_id=1, source_target_pairs={{0,16},{16,0},{1,17},{17,1},{2,18},{18,2},{3,19},{19,3},{4,20},{20... | collective-permute-start | bytes 3145736 | tf_op jit(solution)/shard_map/ppermute | solution.py:722
  207.8 250.4 %collective-permute-start.24 = (bf16[256,2048]{1,0:T(8,128)(2,1)}, bf16[256,2048]{1,0:T(8,128)(2,1)}, u32[]{:S(2)}, u32[]{:S(2)}) collective-permute-start(bf16[256,2048]{1,0:T(8,128)(2,1)} %collective-permute-done.21), channel_id=1, source_target_pairs={{0,16},{16,0},{1,17},{17,1},{2,18},{18,2},{3,19},{19,3},{4,20},{20... | collective-permute-start | bytes 3145736 | tf_op jit(solution)/shard_map/ppermute | solution.py:722
  208.2 207.4 %collective-permute-start.16 = (bf16[256,2048]{0,1:T(8,128)(2,1)}, bf16[256,2048]{0,1:T(8,128)(2,1)}, u32[]{:S(2)}, u32[]{:S(2)}) collective-permute-start(bf16[256,2048]{0,1:T(8,128)(2,1)} %collective-permute-done.15), channel_id=1, source_target_pairs={{0,1},{1,2},{2,3},{3,0},{4,5},{5,6},{6,7},{7,4},{8,9},{9,10},{10,1... | collective-permute-start | bytes 3145736 | tf_op jit(solution)/shard_map/ppermute | solution.py:727
  219.0 200.8 %collective-permute-start.23 = (bf16[256,2048]{1,0:T(8,128)(2,1)}, bf16[256,2048]{1,0:T(8,128)(2,1)}, u32[]{:S(2)}, u32[]{:S(2)}) collective-permute-start(bf16[256,2048]{1,0:T(8,128)(2,1)} %collective-permute-done.22), channel_id=1, source_target_pairs={{0,1},{1,2},{2,3},{3,0},{4,5},{5,6},{6,7},{7,4},{8,9},{9,10},{10,1... | collective-permute-start | bytes 3145736 | tf_op jit(solution)/shard_map/ppermute | solution.py:727
  261.2 201.1 %all-to-all-start.5 = ((bf16[32,72,512]{2,1,0:T(8,128)(2,1)}), bf16[32,72,512]{2,1,0:T(8,128)(2,1)}, u32[]{:S(2)}, u32[]{:S(2)}) async-start(bf16[32,72,512]{2,1,0:T(8,128)(2,1)} %bitcast.238), calls=%async_computation.5 | async-start | bytes 4718592 | tf_op jit(solution)/shard_map/all_to_all | solution.py:897
  269.6 44.3 %collective-permute-start = (bf16[256,2048]{0,1:T(8,128)(2,1)S(1)}, bf16[256,2048]{0,1:T(8,128)(2,1)S(1)}, u32[]{:S(2)}, u32[]{:S(2)}) collective-permute-start(bf16[256,2048]{0,1:T(8,128)(2,1)S(1)} %get-tuple-element.208), channel_id=1, source_target_pairs={{0,8},{8,0},{1,9},{9,1},{2,10},{10,2},{3,11},{11,3},{4,12},{12,4},... | collective-permute-start | bytes 3145736 | tf_op jit(solution)/shard_map/ppermute | solution.py:722
  340.6 35.0 %collective-permute-start.30 = (bf16[512,2048]{0,1:T(8,128)(2,1)S(1)}, bf16[512,2048]{0,1:T(8,128)(2,1)S(1)}, u32[]{:S(2)}, u32[]{:S(2)}) collective-permute-start(bf16[512,2048]{0,1:T(8,128)(2,1)S(1)} %pad_maximum_fusion.13), channel_id=1, source_target_pairs={{0,4},{4,0},{1,5},{5,1},{2,6},{6,2},{3,7},{7,3},{8,12},{12,8},{9,1... | collective-permute-start | bytes 6291464 | tf_op jit(solution)/shard_map/ppermute | solution.py:722
  375.3 49.4 %collective-permute-start.11 = (bf16[512,2048]{0,1:T(8,128)(2,1)}, bf16[512,2048]{0,1:T(8,128)(2,1)S(1)}, u32[]{:S(2)}, u32[]{:S(2)}) collective-permute-start(bf16[512,2048]{0,1:T(8,128)(2,1)} %slice.1662), channel_id=1, source_target_pairs={{0,4},{4,0},{1,5},{5,1},{2,6},{6,2},{3,7},{7,3},{8,12},{12,8},{9,1... | collective-permute-start | bytes 6291464 | tf_op jit(solution)/shard_map/ppermute | solution.py:722
  415.6 91.6 %collective-permute-start.18 = (bf16[256,2048]{0,1:T(8,128)(2,1)}, bf16[256,2048]{0,1:T(8,128)(2,1)}, u32[]{:S(2)}, u32[]{:S(2)}) collective-permute-start(bf16[256,2048]{0,1:T(8,128)(2,1)} %collective-permute-done.15), channel_id=1, source_target_pairs={{0,16},{16,0},{1,17},{17,1},{2,18},{18,2},{3,19},{19,3},{4,20},{20... | collective-permute-start | bytes 3145736 | tf_op jit(solution)/shard_map/ppermute | solution.py:722
  419.8 87.7 %collective-permute-start.25 = (bf16[256,2048]{1,0:T(8,128)(2,1)}, bf16[256,2048]{1,0:T(8,128)(2,1)}, u32[]{:S(2)}, u32[]{:S(2)}) collective-permute-start(bf16[256,2048]{1,0:T(8,128)(2,1)} %collective-permute-done.22), channel_id=1, source_target_pairs={{0,16},{16,0},{1,17},{17,1},{2,18},{18,2},{3,19},{19,3},{4,20},{20... | collective-permute-start | bytes 3145736 | tf_op jit(solution)/shard_map/ppermute | solution.py:722
  427.6 36.6 %collective-permute-start.12 = (bf16[256,2048]{0,1:T(8,128)(2,1)}, bf16[256,2048]{0,1:T(8,128)(2,1)}, u32[]{:S(2)}, u32[]{:S(2)}) collective-permute-start(bf16[256,2048]{0,1:T(8,128)(2,1)} %slice.1670), channel_id=1, source_target_pairs={{0,8},{8,0},{1,9},{9,1},{2,10},{10,2},{3,11},{11,3},{4,12},{12,4},... | collective-permute-start | bytes 3145736 | tf_op jit(solution)/shard_map/ppermute | solution.py:722
  458.2 52.3 %collective-permute-start.19 = (bf16[256,2048]{0,1:T(8,128)(2,1)}, bf16[256,2048]{0,1:T(8,128)(2,1)}, u32[]{:S(2)}, u32[]{:S(2)}) collective-permute-start(bf16[256,2048]{0,1:T(8,128)(2,1)} %collective-permute-done.16), channel_id=1, source_target_pairs={{0,16},{16,0},{1,17},{17,1},{2,18},{18,2},{3,19},{19,3},{4,20},{20... | collective-permute-start | bytes 3145736 | tf_op jit(solution)/shard_map/ppermute | solution.py:722
  464.3 50.4 %collective-permute-start.26 = (bf16[256,2048]{1,0:T(8,128)(2,1)}, bf16[256,2048]{1,0:T(8,128)(2,1)S(1)}, u32[]{:S(2)}, u32[]{:S(2)}) collective-permute-start(bf16[256,2048]{1,0:T(8,128)(2,1)} %collective-permute-done.23), channel_id=1, source_target_pairs={{0,16},{16,0},{1,17},{17,1},{2,18},{18,2},{3,19},{19,3},{4,20},{20... | collective-permute-start | bytes 3145736 | tf_op jit(solution)/shard_map/ppermute | solution.py:722
  507.3 72.5 %collective-permute-start.14 = (bf16[512,2048]{0,1:T(8,128)(2,1)S(1)}, bf16[512,2048]{0,1:T(8,128)(2,1)S(1)}, u32[]{:S(2)}, u32[]{:S(2)}) collective-permute-start(bf16[512,2048]{0,1:T(8,128)(2,1)S(1)} %pad_maximum_fusion.12), channel_id=1, source_target_pairs={{0,4},{4,0},{1,5},{5,1},{2,6},{6,2},{3,7},{7,3},{8,12},{12,8},{9,1... | collective-permute-start | bytes 6291464 | tf_op jit(solution)/shard_map/ppermute | solution.py:722
  510.6 45.5 %collective-permute-start.37 = (bf16[256,2048]{0,1:T(8,128)(2,1)S(1)}, bf16[256,2048]{0,1:T(8,128)(2,1)S(1)}, u32[]{:S(2)}, u32[]{:S(2)}) collective-permute-start(bf16[256,2048]{0,1:T(8,128)(2,1)S(1)} %get-tuple-element.217), channel_id=1, source_target_pairs={{0,8},{8,0},{1,9},{9,1},{2,10},{10,2},{3,11},{11,3},{4,12},{12,4},... | collective-permute-start | bytes 3145736 | tf_op jit(solution)/shard_map/ppermute | solution.py:722
  514.7 63.4 %collective-permute-start.33 = (bf16[256,2048]{0,1:T(8,128)(2,1)S(1)}, bf16[256,2048]{0,1:T(8,128)(2,1)S(1)}, u32[]{:S(2)}, u32[]{:S(2)}) collective-permute-start(bf16[256,2048]{0,1:T(8,128)(2,1)S(1)} %get-tuple-element.268), channel_id=1, source_target_pairs={{0,8},{8,0},{1,9},{9,1},{2,10},{10,2},{3,11},{11,3},{4,12},{12,4},... | collective-permute-start | bytes 3145736 | tf_op jit(solution)/shard_map/ppermute | solution.py:722
  533.7 111.4 %collective-permute-start.46 = (bf16[512,2048]{0,1:T(8,128)(2,1)S(1)}, bf16[512,2048]{0,1:T(8,128)(2,1)}, u32[]{:S(2)}, u32[]{:S(2)}) collective-permute-start(bf16[512,2048]{0,1:T(8,128)(2,1)S(1)} %pad_maximum_fusion.18), channel_id=1, source_target_pairs={{0,4},{4,0},{1,5},{5,1},{2,6},{6,2},{3,7},{7,3},{8,12},{12,8},{9,1... | collective-permute-start | bytes 6291464 | tf_op jit(solution)/shard_map/ppermute | solution.py:722
  557.6 126.4 %collective-permute-start.38 = (bf16[512,2048]{0,1:T(8,128)(2,1)}, bf16[512,2048]{0,1:T(8,128)(2,1)}, u32[]{:S(2)}, u32[]{:S(2)}) collective-permute-start(bf16[512,2048]{0,1:T(8,128)(2,1)} %pad_maximum_fusion.16), channel_id=1, source_target_pairs={{0,4},{4,0},{1,5},{5,1},{2,6},{6,2},{3,7},{7,3},{8,12},{12,8},{9,1... | collective-permute-start | bytes 6291464 | tf_op jit(solution)/shard_map/ppermute | solution.py:722
  608.8 200.4 %collective-permute-start.27 = (bf16[512,2048]{0,1:T(8,128)(2,1)}, bf16[512,2048]{0,1:T(8,128)(2,1)}, u32[]{:S(2)}, u32[]{:S(2)}) collective-permute-start(bf16[512,2048]{0,1:T(8,128)(2,1)} %slice.1661), channel_id=1, source_target_pairs={{0,4},{4,0},{1,5},{5,1},{2,6},{6,2},{3,7},{7,3},{8,12},{12,8},{9,1... | collective-permute-start | bytes 6291464 | tf_op jit(solution)/shard_map/ppermute | solution.py:722
  644.6 171.0 %collective-permute-start.35 = (bf16[512,2048]{0,1:T(8,128)(2,1)}, bf16[512,2048]{0,1:T(8,128)(2,1)}, u32[]{:S(2)}, u32[]{:S(2)}) collective-permute-start(bf16[512,2048]{0,1:T(8,128)(2,1)} %slice.1659), channel_id=1, source_target_pairs={{0,4},{4,0},{1,5},{5,1},{2,6},{6,2},{3,7},{7,3},{8,12},{12,8},{9,1... | collective-permute-start | bytes 6291464 | tf_op jit(solution)/shard_map/ppermute | solution.py:722
  683.9 116.6 %collective-permute-start.47 = (bf16[512,2048]{0,1:T(8,128)(2,1)}, bf16[512,2048]{0,1:T(8,128)(2,1)}, u32[]{:S(2)}, u32[]{:S(2)}) collective-permute-start(bf16[512,2048]{0,1:T(8,128)(2,1)} %slice.1656), channel_id=1, source_target_pairs={{0,4},{4,0},{1,5},{5,1},{2,6},{6,2},{3,7},{7,3},{8,12},{12,8},{9,1... | collective-permute-start | bytes 6291464 | tf_op jit(solution)/shard_map/ppermute | solution.py:722
  722.9 83.2 %collective-permute-start.39 = (bf16[512,2048]{0,1:T(8,128)(2,1)}, bf16[512,2048]{0,1:T(8,128)(2,1)}, u32[]{:S(2)}, u32[]{:S(2)}) collective-permute-start(bf16[512,2048]{0,1:T(8,128)(2,1)} %slice.1658), channel_id=1, source_target_pairs={{0,4},{4,0},{1,5},{5,1},{2,6},{6,2},{3,7},{7,3},{8,12},{12,8},{9,1... | collective-permute-start | bytes 6291464 | tf_op jit(solution)/shard_map/ppermute | solution.py:722
  758.7 165.0 %collective-permute-start.67 = (bf16[1024,2048]{1,0:T(8,128)(2,1)}, bf16[1024,2048]{1,0:T(8,128)(2,1)}, u32[]{:S(2)}, u32[]{:S(2)}) collective-permute-start(bf16[1024,2048]{1,0:T(8,128)(2,1)} %slice.1299), channel_id=1, source_target_pairs={{0,16},{16,0},{1,17},{17,1},{2,18},{18,2},{3,19},{19,3},{4,20},{20... | collective-permute-start | bytes 12582920 | tf_op jit(solution)/shard_map/ppermute | solution.py:722
  801.1 140.4 %collective-permute-start.76 = (bf16[1024,2048]{1,0:T(8,128)(2,1)}, bf16[1024,2048]{1,0:T(8,128)(2,1)}, u32[]{:S(2)}, u32[]{:S(2)}) collective-permute-start(bf16[1024,2048]{1,0:T(8,128)(2,1)} %slice.1315), channel_id=1, source_target_pairs={{0,16},{16,0},{1,17},{17,1},{2,18},{18,2},{3,19},{19,3},{4,20},{20... | collective-permute-start | bytes 12582920 | tf_op jit(solution)/shard_map/ppermute | solution.py:722
  809.2 45.5 %collective-permute-start.40 = (bf16[256,2048]{0,1:T(8,128)(2,1)S(1)}, bf16[256,2048]{0,1:T(8,128)(2,1)S(1)}, u32[]{:S(2)}, u32[]{:S(2)}) collective-permute-start(bf16[256,2048]{0,1:T(8,128)(2,1)S(1)} %slice.1666), channel_id=1, source_target_pairs={{0,8},{8,0},{1,9},{9,1},{2,10},{10,2},{3,11},{11,3},{4,12},{12,4},... | collective-permute-start | bytes 3145736 | tf_op jit(solution)/shard_map/ppermute | solution.py:722
  815.7 61.5 %collective-permute-start.28 = (bf16[256,2048]{0,1:T(8,128)(2,1)}, bf16[256,2048]{0,1:T(8,128)(2,1)S(1)}, u32[]{:S(2)}, u32[]{:S(2)}) collective-permute-start(bf16[256,2048]{0,1:T(8,128)(2,1)} %slice.1669), channel_id=1, source_target_pairs={{0,8},{8,0},{1,9},{9,1},{2,10},{10,2},{3,11},{11,3},{4,12},{12,4},... | collective-permute-start | bytes 3145736 | tf_op jit(solution)/shard_map/ppermute | solution.py:722
  832.2 67.4 %collective-permute-start.36 = (bf16[256,2048]{0,1:T(8,128)(2,1)S(1)}, bf16[256,2048]{0,1:T(8,128)(2,1)S(1)}, u32[]{:S(2)}, u32[]{:S(2)}) collective-permute-start(bf16[256,2048]{0,1:T(8,128)(2,1)S(1)} %slice.1667), channel_id=1, source_target_pairs={{0,8},{8,0},{1,9},{9,1},{2,10},{10,2},{3,11},{11,3},{4,12},{12,4},... | collective-permute-start | bytes 3145736 | tf_op jit(solution)/shard_map/ppermute | solution.py:722
  861.2 60.9 %collective-permute-start.41 = (bf16[256,2048]{0,1:T(8,128)(2,1)S(1)}, bf16[256,2048]{0,1:T(8,128)(2,1)S(1)}, u32[]{:S(2)}, u32[]{:S(2)}) collective-permute-start(bf16[256,2048]{0,1:T(8,128)(2,1)S(1)} %get-tuple-element.181), channel_id=1, source_target_pairs={{0,8},{8,0},{1,9},{9,1},{2,10},{10,2},{3,11},{11,3},{4,12},{12,4},... | collective-permute-start | bytes 3145736 | tf_op jit(solution)/shard_map/ppermute | solution.py:722
  877.2 73.3 %collective-permute-start.49 = (bf16[256,2048]{0,1:T(8,128)(2,1)S(1)}, bf16[256,2048]{0,1:T(8,128)(2,1)}, u32[]{:S(2)}, u32[]{:S(2)}) collective-permute-start(bf16[256,2048]{0,1:T(8,128)(2,1)S(1)} %get-tuple-element.182), channel_id=1, source_target_pairs={{0,8},{8,0},{1,9},{9,1},{2,10},{10,2},{3,11},{11,3},{4,12},{12,4},... | collective-permute-start | bytes 3145736 | tf_op jit(solution)/shard_map/ppermute | solution.py:722
  923.7 56.1 %collective-permute-start.42 = (bf16[512,2048]{0,1:T(8,128)(2,1)}, bf16[512,2048]{0,1:T(8,128)(2,1)}, u32[]{:S(2)}, u32[]{:S(2)}) collective-permute-start(bf16[512,2048]{0,1:T(8,128)(2,1)} %pad_maximum_fusion.17), channel_id=1, source_target_pairs={{0,4},{4,0},{1,5},{5,1},{2,6},{6,2},{3,7},{7,3},{8,12},{12,8},{9,1... | collective-permute-start | bytes 6291464 | tf_op jit(solution)/shard_map/ppermute | solution.py:722
  946.4 237.2 %all-to-all-start.2 = ((bf16[32,72,512]{2,1,0:T(8,128)(2,1)}), bf16[32,72,512]{2,1,0:T(8,128)(2,1)}, u32[]{:S(2)}, u32[]{:S(2)}) async-start(bf16[32,72,512]{2,1,0:T(8,128)(2,1)} %bitcast.36), calls=%async_computation.2 | async-start | bytes 4718592 | tf_op jit(solution)/shard_map/all_to_all | solution.py:908
  951.9 72.8 %collective-permute-start.50 = (bf16[512,2048]{0,1:T(8,128)(2,1)S(1)}, bf16[512,2048]{0,1:T(8,128)(2,1)}, u32[]{:S(2)}, u32[]{:S(2)}) collective-permute-start(bf16[512,2048]{0,1:T(8,128)(2,1)S(1)} %pad_maximum_fusion.19), channel_id=1, source_target_pairs={{0,4},{4,0},{1,5},{5,1},{2,6},{6,2},{3,7},{7,3},{8,12},{12,8},{9,1... | collective-permute-start | bytes 6291464 | tf_op jit(solution)/shard_map/ppermute | solution.py:722
  957.3 161.3 %collective-permute-start.69 = (bf16[256,2048]{1,0:T(8,128)(2,1)S(1)}, bf16[256,2048]{1,0:T(8,128)(2,1)S(1)}, u32[]{:S(2)}, u32[]{:S(2)}) collective-permute-start(bf16[256,2048]{1,0:T(8,128)(2,1)S(1)} %add_convert_fusion.12), channel_id=1, source_target_pairs={{0,1},{1,2},{2,3},{3,0},{4,5},{5,6},{6,7},{7,4},{8,9},{9,10},{10,1... | collective-permute-start | bytes 3145736 | tf_op jit(solution)/shard_map/ppermute | solution.py:727
  979.7 142.7 %collective-permute-start.78 = (bf16[256,2048]{1,0:T(8,128)(2,1)S(1)}, bf16[256,2048]{1,0:T(8,128)(2,1)}, u32[]{:S(2)}, u32[]{:S(2)}) collective-permute-start(bf16[256,2048]{1,0:T(8,128)(2,1)S(1)} %add_convert_fusion.8), channel_id=1, source_target_pairs={{0,1},{1,2},{2,3},{3,0},{4,5},{5,6},{6,7},{7,4},{8,9},{9,10},{10,1... | collective-permute-start | bytes 3145736 | tf_op jit(solution)/shard_map/ppermute | solution.py:727
  1024.7 173.8 %collective-permute-start.43 = (bf16[512,2048]{0,1:T(8,128)(2,1)}, bf16[512,2048]{0,1:T(8,128)(2,1)}, u32[]{:S(2)}, u32[]{:S(2)}) collective-permute-start(bf16[512,2048]{0,1:T(8,128)(2,1)} %slice.1657), channel_id=1, source_target_pairs={{0,4},{4,0},{1,5},{5,1},{2,6},{6,2},{3,7},{7,3},{8,12},{12,8},{9,1... | collective-permute-start | bytes 6291464 | tf_op jit(solution)/shard_map/ppermute | solution.py:722
  1069.9 134.3 %collective-permute-start.51 = (bf16[512,2048]{0,1:T(8,128)(2,1)}, bf16[512,2048]{0,1:T(8,128)(2,1)}, u32[]{:S(2)}, u32[]{:S(2)}) collective-permute-start(bf16[512,2048]{0,1:T(8,128)(2,1)} %slice.1655), channel_id=1, source_target_pairs={{0,4},{4,0},{1,5},{5,1},{2,6},{6,2},{3,7},{7,3},{8,12},{12,8},{9,1... | collective-permute-start | bytes 6291464 | tf_op jit(solution)/shard_map/ppermute | solution.py:722
  1115.7 213.8 %collective-permute-start.53 = (bf16[1024,2048]{1,0:T(8,128)(2,1)}, bf16[1024,2048]{1,0:T(8,128)(2,1)}, u32[]{:S(2)}, u32[]{:S(2)}) collective-permute-start(bf16[1024,2048]{1,0:T(8,128)(2,1)} %get-tuple-element.216), channel_id=1, source_target_pairs={{0,16},{16,0},{1,17},{17,1},{2,18},{18,2},{3,19},{19,3},{4,20},{20... | collective-permute-start | bytes 12582920 | tf_op jit(solution)/shard_map/ppermute | solution.py:722
  1124.8 45.1 %collective-permute-start.79 = (bf16[256,2048]{1,0:T(8,128)(2,1)S(1)}, bf16[256,2048]{1,0:T(8,128)(2,1)S(1)}, u32[]{:S(2)}, u32[]{:S(2)}) collective-permute-start(bf16[256,2048]{1,0:T(8,128)(2,1)S(1)} %add_convert_fusion.7), channel_id=1, source_target_pairs={{0,1},{1,2},{2,3},{3,0},{4,5},{5,6},{6,7},{7,4},{8,9},{9,10},{10,1... | collective-permute-start | bytes 3145736 | tf_op jit(solution)/shard_map/ppermute | solution.py:727
  1152.0 57.5 %collective-permute-start.71 = (bf16[256,2048]{1,0:T(8,128)(2,1)}, bf16[256,2048]{1,0:T(8,128)(2,1)}, u32[]{:S(2)}, u32[]{:S(2)}) collective-permute-start(bf16[256,2048]{1,0:T(8,128)(2,1)} %get-tuple-element.151), channel_id=1, source_target_pairs={{0,8},{8,0},{1,9},{9,1},{2,10},{10,2},{3,11},{11,3},{4,12},{12,4},... | collective-permute-start | bytes 3145736 | tf_op jit(solution)/shard_map/ppermute | solution.py:722
  1169.9 73.3 %collective-permute-start.72 = (bf16[256,2048]{1,0:T(8,128)(2,1)}, bf16[256,2048]{1,0:T(8,128)(2,1)}, u32[]{:S(2)}, u32[]{:S(2)}) collective-permute-start(bf16[256,2048]{1,0:T(8,128)(2,1)} %get-tuple-element.151), channel_id=1, source_target_pairs={{0,16},{16,0},{1,17},{17,1},{2,18},{18,2},{3,19},{19,3},{4,20},{20... | collective-permute-start | bytes 3145736 | tf_op jit(solution)/shard_map/ppermute | solution.py:722
  1194.7 171.1 %all-to-all-start.3 = ((bf16[2,1024,1,512]{3,0,2,1:T(2,128)(2,1)}), bf16[2,1024,1,512]{3,0,2,1:T(2,128)(2,1)S(1)}, u32[]{:S(2)}, u32[]{:S(2)}) async-start(bf16[2,1024,1,512]{3,0,2,1:T(2,128)(2,1)} %copy.255), calls=%async_computation.3 | async-start | bytes 4194304 | tf_op jit(solution)/shard_map/all_to_all | solution.py:911
  1198.5 78.3 %collective-permute-start.81 = (bf16[256,2048]{1,0:T(8,128)(2,1)S(1)}, bf16[256,2048]{1,0:T(8,128)(2,1)S(1)}, u32[]{:S(2)}, u32[]{:S(2)}) collective-permute-start(bf16[256,2048]{1,0:T(8,128)(2,1)S(1)} %get-tuple-element.149), channel_id=1, source_target_pairs={{0,16},{16,0},{1,17},{17,1},{2,18},{18,2},{3,19},{19,3},{4,20},{20... | collective-permute-start | bytes 3145736 | tf_op jit(solution)/shard_map/ppermute | solution.py:722
  1204.3 78.5 %collective-permute-start.80 = (bf16[256,2048]{1,0:T(8,128)(2,1)S(1)}, bf16[256,2048]{1,0:T(8,128)(2,1)S(1)}, u32[]{:S(2)}, u32[]{:S(2)}) collective-permute-start(bf16[256,2048]{1,0:T(8,128)(2,1)S(1)} %get-tuple-element.149), channel_id=1, source_target_pairs={{0,8},{8,0},{1,9},{9,1},{2,10},{10,2},{3,11},{11,3},{4,12},{12,4},... | collective-permute-start | bytes 3145736 | tf_op jit(solution)/shard_map/ppermute | solution.py:722
  1209.5 97.9 %collective-permute-start.44 = (bf16[256,2048]{0,1:T(8,128)(2,1)S(1)}, bf16[256,2048]{0,1:T(8,128)(2,1)S(1)}, u32[]{:S(2)}, u32[]{:S(2)}) collective-permute-start(bf16[256,2048]{0,1:T(8,128)(2,1)S(1)} %slice.1665), channel_id=1, source_target_pairs={{0,8},{8,0},{1,9},{9,1},{2,10},{10,2},{3,11},{11,3},{4,12},{12,4},... | collective-permute-start | bytes 3145736 | tf_op jit(solution)/shard_map/ppermute | solution.py:722
  1243.2 50.2 %collective-permute-start.74 = (bf16[128,2048]{1,0:T(8,128)(2,1)S(1)}, bf16[128,2048]{1,0:T(8,128)(2,1)S(1)}, u32[]{:S(2)}, u32[]{:S(2)}) collective-permute-start(bf16[128,2048]{1,0:T(8,128)(2,1)S(1)} %slice.1308), channel_id=1, source_target_pairs={{0,16},{16,0},{1,17},{17,1},{2,18},{18,2},{3,19},{19,3},{4,20},{20... | collective-permute-start | bytes 1572872 | tf_op jit(solution)/shard_map/ppermute | solution.py:722
  1302.8 96.2 %collective-permute-start.75 = (bf16[1024,2048]{1,0:T(8,128)(2,1)}, bf16[1024,2048]{1,0:T(8,128)(2,1)}, u32[]{:S(2)}, u32[]{:S(2)}) collective-permute-start(bf16[1024,2048]{1,0:T(8,128)(2,1)} %constant_dynamic-update-slice_fusion.31), channel_id=1, source_target_pairs={{0,4},{4,0},{1,5},{5,1},{2,6},{6,2},{3,7},{7,3},{8,12},{12,8},{9,1... | collective-permute-start | bytes 12582920 | tf_op jit(solution)/shard_map/ppermute | solution.py:722
  1304.5 115.6 %collective-permute-start.84 = (bf16[1024,2048]{1,0:T(8,128)(2,1)}, bf16[1024,2048]{1,0:T(8,128)(2,1)}, u32[]{:S(2)}, u32[]{:S(2)}) collective-permute-start(bf16[1024,2048]{1,0:T(8,128)(2,1)} %constant_dynamic-update-slice_fusion.36), channel_id=1, source_target_pairs={{0,4},{4,0},{1,5},{5,1},{2,6},{6,2},{3,7},{7,3},{8,12},{12,8},{9,1... | collective-permute-start | bytes 12582920 | tf_op jit(solution)/shard_map/ppermute | solution.py:722
  1361.8 35.1 %collective-permute-start.55 = (bf16[256,2048]{1,0:T(8,128)(2,1)}, bf16[256,2048]{1,0:T(8,128)(2,1)}, u32[]{:S(2)}, u32[]{:S(2)}) collective-permute-start(bf16[256,2048]{1,0:T(8,128)(2,1)} %add_convert_fusion.16), channel_id=1, source_target_pairs={{0,1},{1,2},{2,3},{3,0},{4,5},{5,6},{6,7},{7,4},{8,9},{9,10},{10,1... | collective-permute-start | bytes 3145736 | tf_op jit(solution)/shard_map/ppermute | solution.py:727
  1365.9 140.9 %all-to-all-start.6 = ((bf16[32,72,512]{2,1,0:T(8,128)(2,1)}), bf16[32,72,512]{2,1,0:T(8,128)(2,1)}, u32[]{:S(2)}, u32[]{:S(2)}) async-start(bf16[32,72,512]{2,1,0:T(8,128)(2,1)} %bitcast.51), calls=%async_computation.6 | async-start | bytes 4718592 | tf_op jit(solution)/shard_map/all_to_all | solution.py:908
  1399.0 52.0 %collective-permute-start.56 = (bf16[256,2048]{1,0:T(8,128)(2,1)S(1)}, bf16[256,2048]{1,0:T(8,128)(2,1)S(1)}, u32[]{:S(2)}, u32[]{:S(2)}) collective-permute-start(bf16[256,2048]{1,0:T(8,128)(2,1)S(1)} %add_convert_fusion.15), channel_id=1, source_target_pairs={{0,1},{1,2},{2,3},{3,0},{4,5},{5,6},{6,7},{7,4},{8,9},{9,10},{10,1... | collective-permute-start | bytes 3145736 | tf_op jit(solution)/shard_map/ppermute | solution.py:727
  1453.8 35.3 %collective-permute-start.58 = (bf16[256,2048]{1,0:T(8,128)(2,1)S(1)}, bf16[256,2048]{1,0:T(8,128)(2,1)S(1)}, u32[]{:S(2)}, u32[]{:S(2)}) collective-permute-start(bf16[256,2048]{1,0:T(8,128)(2,1)S(1)} %get-tuple-element.153), channel_id=1, source_target_pairs={{0,16},{16,0},{1,17},{17,1},{2,18},{18,2},{3,19},{19,3},{4,20},{20... | collective-permute-start | bytes 3145736 | tf_op jit(solution)/shard_map/ppermute | solution.py:722
  1456.6 34.5 %collective-permute-start.57 = (bf16[256,2048]{1,0:T(8,128)(2,1)S(1)}, bf16[256,2048]{1,0:T(8,128)(2,1)S(1)}, u32[]{:S(2)}, u32[]{:S(2)}) collective-permute-start(bf16[256,2048]{1,0:T(8,128)(2,1)S(1)} %get-tuple-element.153), channel_id=1, source_target_pairs={{0,8},{8,0},{1,9},{9,1},{2,10},{10,2},{3,11},{11,3},{4,12},{12,4},... | collective-permute-start | bytes 3145736 | tf_op jit(solution)/shard_map/ppermute | solution.py:722
  1504.1 49.1 %collective-permute-start.61 = (bf16[1024,2048]{1,0:T(8,128)(2,1)}, bf16[1024,2048]{1,0:T(8,128)(2,1)}, u32[]{:S(2)}, u32[]{:S(2)}) collective-permute-start(bf16[1024,2048]{1,0:T(8,128)(2,1)} %constant_dynamic-update-slice_fusion.25), channel_id=1, source_target_pairs={{0,4},{4,0},{1,5},{5,1},{2,6},{6,2},{3,7},{7,3},{8,12},{12,8},{9,1... | collective-permute-start | bytes 12582920 | tf_op jit(solution)/shard_map/ppermute | solution.py:722
  (200 other events, 5708.5 us)

commit v2 on v1

--- a/solution.py
+++ b/solution.py
@@ -583,9 +583,7 @@
         ),
         out_shape=jax.ShapeDtypeStruct((ROWS, pairs * PAIR), jnp.bfloat16),
         compiler_params=pltpu.CompilerParams(vmem_limit_bytes=24 << 20),
-        cost_estimate=pl.CostEstimate(
-            flops=2 * 2 * 2 * pairs * cells * 256, bytes_accessed=ROWS * pairs * PAIR * 8, transcendentals=2 * pairs * cells
-        ),
+        cost_estimate=light(),
         name="attend",
     )(rank, qkv, qkv, qkv, key_info, query_info)
 
@@ -702,13 +700,464 @@
         ),
         out_shape=[wide, wide, wide, jax.ShapeDtypeStruct((8, pairs * PAIR), jnp.float32)],
         compiler_params=pltpu.CompilerParams(vmem_limit_bytes=28 << 20),
-        cost_estimate=pl.CostEstimate(
-            flops=2 * 5 * 2 * pairs * cells * 256,
-            bytes_accessed=ROWS * pairs * PAIR * 14,
-            transcendentals=2 * pairs * cells,
-        ),
+        cost_estimate=light(),
         name="attend_back",
     )(rank, qkv, qkv, qkv, grads, key_info, query_info)
+
+
+WIDE = 512
+VMEM_BYTES = 56 << 20
+
+
+def light(flops=1 << 20):
+    return pl.CostEstimate(flops=flops, bytes_accessed=1 << 12, transcendentals=0)
+
+
+def settings():
+    return pltpu.CompilerParams(vmem_limit_bytes=VMEM_BYTES)
+
+
+def whole(shape):
+    return pl.BlockSpec(shape, lambda i: (0,) * len(shape))
+
+
+def project_kernel(near_ref, far_ref, weight_ref, bias_ref, out_ref):
+    rows = near_ref.shape[0]
+    bias = bias_ref[...]
+    out_ref[pl.ds(0, rows), :] = (nt_dot(near_ref[...], weight_ref[...]) + bias).astype(out_ref.dtype)
+    out_ref[pl.ds(rows, rows), :] = (nt_dot(far_ref[...], weight_ref[...]) + bias).astype(out_ref.dtype)
+
+
+def project(near, far, weight, bias):
+    rows, depth = near.shape
+    cols = weight.shape[0]
+    return pl.pallas_call(
+        project_kernel,
+        grid=(cols // WIDE,),
+        in_specs=[
+            whole((rows, depth)),
+            whole((rows, depth)),
+            pl.BlockSpec((WIDE, depth), lambda i: (i, 0)),
+            pl.BlockSpec((1, WIDE), lambda i: (0, i)),
+        ],
+        out_specs=pl.BlockSpec((2 * rows, WIDE), lambda i: (0, i)),
+        out_shape=jax.ShapeDtypeStruct((2 * rows, cols), jnp.bfloat16),
+        compiler_params=settings(),
+        cost_estimate=light(),
+        name="project",
+    )(near, far, weight, bias)
+
+
+def expand_kernel(near_ref, far_ref, weight_ref, bias_ref, hidden_ref, slope_ref):
+    rows = near_ref.shape[0]
+    bias = bias_ref[...]
+    for part, ref in enumerate((near_ref, far_ref)):
+        at = pl.ds(part * rows, rows)
+        pre = nt_dot(ref[...], weight_ref[...]) + bias
+        cube = 0.044715 * pre * pre
+        bend = jnp.tanh((0.7978845608028654 * pre) * (1.0 + cube))
+        half = 0.5 + 0.5 * bend
+        inner = 0.7978845608028654 + (3.0 * 0.7978845608028654) * cube
+        hidden_ref[at, :] = (pre * half).astype(jnp.bfloat16)
+        slope_ref[at, :] = (half + (pre * half) * ((1.0 - bend) * inner)).astype(jnp.bfloat16)
+
+
+def expand(near, far, weight, bias):
+    rows, depth = near.shape
+    cols = weight.shape[0]
+    out = jax.ShapeDtypeStruct((2 * rows, cols), jnp.bfloat16)
+    return pl.pallas_call(
+        expand_kernel,
+        grid=(cols // WIDE,),
+        in_specs=[
+            whole((rows, depth)),
+            whole((rows, depth)),
+            pl.BlockSpec((WIDE, depth), lambda i: (i, 0)),
+            pl.BlockSpec((1, WIDE), lambda i: (0, i)),
+        ],
+        out_specs=[pl.BlockSpec((2 * rows, WIDE), lambda i: (0, i))] * 2,
+        out_shape=[out, out],
+        compiler_params=settings(),
+        cost_estimate=light(),
+        name="expand",
+    )(near, far, weight, bias)
+
+
+def expand_back_kernel(near_ref, far_ref, weight_ref, slope_ref, low_ref, sums_ref):
+    rows = near_ref.shape[0]
+    total = jnp.zeros((1, low_ref.shape[1]), jnp.float32)
+    for part, ref in enumerate((near_ref, far_ref)):
+        at = pl.ds(part * rows, rows)
+        grad = nt_dot(ref[...], weight_ref[...]) * slope_ref[at, :].astype(jnp.float32)
+        total = total + jnp.sum(grad, axis=0, keepdims=True)
+        low_ref[at, :] = grad.astype(jnp.bfloat16)
+    sums_ref[...] = jnp.broadcast_to(total, sums_ref.shape)
+
+
+def expand_back(near, far, weight, slope):
+    rows, depth = near.shape
+    cols = weight.shape[0]
+    return pl.pallas_call(
+        expand_back_kernel,
+        grid=(cols // WIDE,),
+        in_specs=[
+            whole((rows, depth)),
+            whole((rows, depth)),
+            pl.BlockSpec((WIDE, depth), lambda i: (i, 0)),
+            pl.BlockSpec((2 * rows, WIDE), lambda i: (0, i)),
+        ],
+        out_specs=[pl.BlockSpec((2 * rows, WIDE), lambda i: (0, i)), pl.BlockSpec((8, WIDE), lambda i: (0, i))],
+        out_shape=[
+            jax.ShapeDtypeStruct((2 * rows, cols), jnp.bfloat16),
+            jax.ShapeDtypeStruct((8, cols), jnp.float32),
+        ],
+        compiler_params=settings(),
+        cost_estimate=light(),
+        name="expand_back",
+    )(near, far, weight, slope)
+
+
+def partial_kernel(left_ref, weight_ref, near_ref, far_ref):
+    rows = near_ref.shape[0]
+    far_ref[...] = nn_dot(left_ref[pl.ds(rows, rows), :], weight_ref[...]).astype(far_ref.dtype)
+    near_ref[...] = nn_dot(left_ref[pl.ds(0, rows), :], weight_ref[...])
+
+
+def partial_sums(left, weight):
+    rows, depth = left.shape
+    cols = weight.shape[1]
+    half = rows // 2
+    return pl.pallas_call(
+        partial_kernel,
+        grid=(cols // WIDE,),
+        in_specs=[whole((rows, depth)), pl.BlockSpec((depth, WIDE), lambda i: (0, i))],
+        out_specs=[pl.BlockSpec((half, WIDE), lambda i: (0, i))] * 2,
+        out_shape=[
+            jax.ShapeDtypeStruct((half, cols), jnp.float32),
+            jax.ShapeDtypeStruct((half, cols), jnp.bfloat16),
+        ],
+        compiler_params=settings(),
+        cost_estimate=light(),
+        name="partial_sums",
+    )(left, weight)
+
+
+def tn_dot(left, right):
+    return lax.dot_general(left, right, (((0,), (0,)), ((), ())), preferred_element_type=jnp.float32)
+
+
+def cross_kernel(left_a, near_a, far_a, left_b, near_b, far_b, out_ref):
+    rows = near_a.shape[0]
+    top, low = pl.ds(0, rows), pl.ds(rows, rows)
+    total = tn_dot(left_a[top, :], near_a[...]) + tn_dot(left_a[low, :], far_a[...])
+    total = total + tn_dot(left_b[top, :], near_b[...]) + tn_dot(left_b[low, :], far_b[...])
+    out_ref[...] = total.astype(out_ref.dtype)
+
+
+def cross_sums(left_a, right_a, left_b, right_b, start, size):
+    rows = left_a.shape[0]
+    cols = right_a[0].shape[1]
+    tall = 256
+    first = start // tall
+    left_spec = pl.BlockSpec((rows, tall), lambda i: (0, first + i))
+    right_spec = whole((rows // 2, cols))
+    return pl.pallas_call(
+        cross_kernel,
+        grid=(size // tall,),
+        in_specs=[left_spec, right_spec, right_spec] * 2,
+        out_specs=pl.BlockSpec((tall, cols), lambda i: (i, 0)),
+        out_shape=jax.ShapeDtypeStruct((size, cols), jnp.bfloat16),
+        compiler_params=settings(),
+        cost_estimate=light(),
+        name="cross_sums",
+    )(left_a, *right_a, left_b, *right_b)
+
+
+def flip_kernel(first_ref, weight_ref, out_ref):
+    out_ref[...] = weight_ref[...].T
+
+
+def flipped(weight, first, count):
+    depth = weight.shape[0]
+    return pl.pallas_call(
+        flip_kernel,
+        grid_spec=pltpu.PrefetchScalarGridSpec(
+            num_scalar_prefetch=1,
+            grid=(count,),
+            in_specs=[pl.BlockSpec((depth, 128), lambda i, first: (0, first[0] + i))],
+            out_specs=pl.BlockSpec((128, depth), lambda i, first: (i, 0)),
+        ),
+        out_shape=jax.ShapeDtypeStruct((count * 128, depth), weight.dtype),
+        compiler_params=settings(),
+        cost_estimate=light(),
+        name="flipped",
+    )(first.reshape(1).astype(jnp.int32), weight)
+
+
+def attn_pack_kernel(
+    place_ref, query_ref, key_ref, value_ref, out_w_ref, bias_mine, bias_other, mine_ref, other_ref
+):
+    half = place_ref[1]
+    mine_ref[pl.ds(4 * HEAD_DIM, 8), :] = bias_mine[...]
+    other_ref[pl.ds(4 * HEAD_DIM, 8), :] = bias_other[...]
+    for which, ref in enumerate((mine_ref, other_ref)):
+        rows = pl.ds(pl.multiple_of(jnp.where(which == 0, half, 1 - half) * HEAD_DIM, HEAD_DIM), HEAD_DIM)
+        ref[pl.ds(3 * HEAD_DIM, HEAD_DIM), :] = out_w_ref[rows, :]
+    for index, source in enumerate((query_ref, key_ref, value_ref)):
+        flat = source[...].T
+        low, high = flat[:HEAD_DIM, :], flat[HEAD_DIM:, :]
+        at = pl.ds(index * HEAD_DIM, HEAD_DIM)
+        mine_ref[at, :] = jnp.where(half == 0, low, high)
+        other_ref[at, :] = jnp.where(half == 0, high, low)
+
+
+def attn_pack(query_weight, key_weight, value_weight, out_weight, bias_mine, bias_other, team, half):
+    depth = query_weight.shape[0]
+    out = jax.ShapeDtypeStruct((4 * HEAD_DIM + 8, depth), query_weight.dtype)
+    column = pl.BlockSpec((depth, 128), lambda i, place: (0, place[0]))
+    full = pl.BlockSpec((4 * HEAD_DIM + 8, depth), lambda i, place: (0, 0))
+    bias = pl.BlockSpec((8, depth), lambda i, place: (0, 0))
+    return pl.pallas_call(
+        attn_pack_kernel,
+        grid_spec=pltpu.PrefetchScalarGridSpec(
+            num_scalar_prefetch=1,
+            grid=(1,),
+            in_specs=[column, column, column, pl.BlockSpec((128, depth), lambda i, place: (place[0], 0)), bias, bias],
+            out_specs=[full, full],
+        ),
+        out_shape=[out, out],
+        compiler_params=settings(),
+        cost_estimate=light(),
+        name="attn_pack",
+    )(jnp.stack([team, half]).astype(jnp.int32), query_weight, key_weight, value_weight, out_weight, bias_mine, bias_other)
+
+
+def pick_kernel(index_ref, rows_ref, out_ref):
+    wanted = index_ref[...]
+    place = lax.broadcasted_iota(jnp.int32, (wanted.shape[0], rows_ref.shape[0]), 1)
+    hot = jnp.where(place == wanted, 1.0, 0.0).astype(jnp.bfloat16)
+    out_ref[...] = nn_dot(hot, rows_ref[...]).astype(out_ref.dtype)
+
+
+def pick_rows(index, rows, tall):
+    count = index.shape[0]
+    cols = rows.shape[1]
+    return pl.pallas_call(
+        pick_kernel,
+        grid=(count // tall,),
+        in_specs=[pl.BlockSpec((tall, 1), lambda i: (i, 0)), whole(rows.shape)],
+        out_specs=pl.BlockSpec((tall, cols), lambda i: (i, 0)),
+        out_shape=jax.ShapeDtypeStruct((count, cols), rows.dtype),
+        compiler_params=settings(),
+        cost_estimate=light(),
+        name="pick_rows",
+    )(index[:, None], rows)
+
+
+def drop_kernel(index_ref, rows_ref, out_ref):
+    wanted = index_ref[...]
+    tall = out_ref.shape[0]
+    place = lax.broadcasted_iota(jnp.int32, (tall, rows_ref.shape[0]), 0) + pl.program_id(0) * tall
+    hot = jnp.where(place == wanted, 1.0, 0.0).astype(jnp.bfloat16)
+    out_ref[...] = nn_dot(hot, rows_ref[...]).astype(out_ref.dtype)
+
+
+def drop_rows(index, rows, count, tall):
+    cols = rows.shape[1]
+    return pl.pallas_call(
+        drop_kernel,
+        grid=(count // tall,),
+        in_specs=[whole((1, index.shape[0])), whole(rows.shape)],
+        out_specs=pl.BlockSpec((tall, cols), lambda i: (i, 0)),
+        out_shape=jax.ShapeDtypeStruct((count, cols), rows.dtype),
+        compiler_params=settings(),
+        cost_estimate=light(),
+        name="drop_rows",
+    )(index[None, :], rows)
+
+
+def settle_kernel(index_ref, boxes_ref, out_ref):
+    wanted = index_ref[...]
+    place = lax.broadcasted_iota(jnp.int32, (out_ref.shape[0], boxes_ref.shape[1]), 0)
+    hot = jnp.where(place == wanted, 1.0, 0.0).astype(jnp.bfloat16)
+    out_ref[...] = nn_dot(hot, boxes_ref[0]).astype(out_ref.dtype)
+
+
+def settle_rows(index, boxes, count):
+    depth, slots, cols = boxes.shape
+    return pl.pallas_call(
+        settle_kernel,
+        grid=(depth,),
+        in_specs=[whole((1, slots)), pl.BlockSpec((1, slots, cols), lambda i: (i, 0, 0))],
+        out_specs=pl.BlockSpec((count, cols), lambda i: (0, i)),
+        out_shape=jax.ShapeDtypeStruct((count, depth * cols), boxes.dtype),
+        compiler_params=settings(),
+        cost_estimate=light(),
+        name="settle_rows",
+    )(index[None, :], boxes)
+
+
+def unsettle_kernel(index_ref, rows_ref, out_ref):
+    wanted = index_ref[...]
+    place = lax.broadcasted_iota(jnp.int32, (wanted.shape[0], rows_ref.shape[0]), 1)
+    hot = jnp.where(place == wanted, 1.0, 0.0).astype(jnp.bfloat16)
+    out_ref[0] = nn_dot(hot, rows_ref[...]).astype(out_ref.dtype)
+
+
+def unsettle_rows(index, rows, depth):
+    slots = index.shape[0]
+    count = rows.shape[0]
+    cols = rows.shape[1] // depth
+    return pl.pallas_call(
+        unsettle_kernel,
+        grid=(depth,),
+        in_specs=[whole((slots, 1)), pl.BlockSpec((count, cols), lambda i: (0, i))],
+        out_specs=pl.BlockSpec((1, slots, cols), lambda i: (i, 0, 0)),
+        out_shape=jax.ShapeDtypeStruct((depth, slots, cols), rows.dtype),
+        compiler_params=settings(),
+        cost_estimate=light(),
+        name="unsettle_rows",
+    )(index[:, None], rows)
+
+
+def code_of(place, own):
+    return jnp.bitwise_xor(place, own)
+
+
+def piece_of(code):
+    return ((code >> 2) & 1) + 2 * (code & 1)
+
+
+def stack_kernel(own_ref, near_ref, far_ref, out_ref):
+    code = code_of(pl.program_id(0), own_ref[0])
+    block = jnp.where((code & 2) == 0, near_ref[...], far_ref[...])
+    out_ref[...] = block.astype(out_ref.dtype)
+
+
+def stack_kernel_t(own_ref, near_ref, far_ref, out_ref):
+    code = code_of(pl.program_id(0), own_ref[0])
+    block = jnp.where((code & 2) == 0, near_ref[...], far_ref[...])
+    out_ref[...] = block.T.astype(out_ref.dtype)
+
+
+def stack_pieces(near, far, own, transposed):
+    tall = near.shape[0] // 4
+    cols = near.shape[1]
+    spec = pl.BlockSpec((tall, cols), lambda i, own: (piece_of(code_of(i, own[0])), 0))
+    return pl.pallas_call(
+        stack_kernel_t if transposed else stack_kernel,
+        grid_spec=pltpu.PrefetchScalarGridSpec(
+            num_scalar_prefetch=1,
+            grid=(8,),
+            in_specs=[spec, spec],
+            out_specs=pl.BlockSpec((cols, tall), lambda i, own: (0, i))
+            if transposed
+            else pl.BlockSpec((tall, cols), lambda i, own: (i, 0)),
+        ),
+        out_shape=jax.ShapeDtypeStruct((cols, 8 * tall) if transposed else (8 * tall, cols), jnp.float32),
+        compiler_params=settings(),
+        cost_estimate=light(),
+        name="stack_pieces",
+    )(own, near, far)
+
+
+def stack_heads_kernel(flips, own_ref, near_low, far_low, near_high, far_high, *outs):
+    code = code_of(2 * pl.program_id(0), own_ref[0])
+    take_near = (code & 2) == 0
+    low = jnp.where(take_near, near_low[...], far_low[...])
+    high = jnp.where(take_near, near_high[...], far_high[...])
+    for index, ref in enumerate(outs):
+        at = slice(index * HEAD_DIM, (index + 1) * HEAD_DIM)
+        both = jnp.concatenate([low[at], high[at]], axis=0)
+        ref[...] = (both.T if flips[index] else both).astype(ref.dtype)
+
+
+def stack_heads(near, far, own, flips):
+    tall = near.shape[0] // 4
+    cols = near.shape[1]
+    low = pl.BlockSpec((tall, cols), lambda i, own: (piece_of(code_of(2 * i, own[0])), 0))
+    high = pl.BlockSpec((tall, cols), lambda i, own: (piece_of(code_of(2 * i + 1, own[0])), 0))
+    column = pl.BlockSpec((cols, 128), lambda i, own: (0, i))
+    row = pl.BlockSpec((128, cols), lambda i, own: (i, 0))
+    tall_out = jax.ShapeDtypeStruct((cols, 512), jnp.float32)
+    flat_out = jax.ShapeDtypeStruct((512, cols), jnp.float32)
+    return pl.pallas_call(
+        functools.partial(stack_heads_kernel, flips),
+        grid_spec=pltpu.PrefetchScalarGridSpec(
+            num_scalar_prefetch=1,
+            grid=(4,),
+            in_specs=[low, low, high, high],
+            out_specs=[column if flip else row for flip in flips],
+        ),
+        out_shape=[tall_out if flip else flat_out for flip in flips],
+        compiler_params=settings(),
+        cost_estimate=light(),
+        name="stack_heads",
+    )(own, near, far, near, far)
+
+
+def add_rows_kernel(*refs):
+    total = refs[0][...].astype(jnp.float32)
+    for ref in refs[1:-1]:
+        total = total + ref[...].astype(jnp.float32)
+    refs[-1][...] = total.astype(refs[-1].dtype)
+
+
+def add_pieces(near, got, moved, index):
+    tall = near.shape[0] // 4
+    cols = near.shape[1]
+    at = pl.BlockSpec((tall, cols), lambda i: (index, 0))
+    return pl.pallas_call(
+        add_rows_kernel,
+        grid=(1,),
+        in_specs=[at, at] + [whole((tall, cols))] * len(moved),
+        out_specs=whole((tall, cols)),
+        out_shape=jax.ShapeDtypeStruct((tall, cols), near.dtype),
+        compiler_params=settings(),
+        cost_estimate=light(),
+        name="add_pieces",
+    )(near, got, *moved)
+
+
+def add_rows(near, got, index):
+    return add_pieces(near, got, (), index)
+
+
+def add_three(near, got, moved, index):
+    return add_pieces(near, got, (moved,), index)
+
+
+def add_four(near, got, first, second, index):
+    return add_pieces(near, got, (first, second), index)
+
+
+def partial_three_kernel(query_ref, key_ref, value_ref, weight_ref, near_ref, far_ref):
+    rows = near_ref.shape[0]
+    depth = query_ref.shape[1]
+    for at, out in ((pl.ds(rows, rows), far_ref), (pl.ds(0, rows), near_ref)):
+        total = nn_dot(query_ref[at, :], weight_ref[pl.ds(0, depth), :])
+        total = total + nn_dot(key_ref[at, :], weight_ref[pl.ds(depth, depth), :])
+        total = total + nn_dot(value_ref[at, :], weight_ref[pl.ds(2 * depth, depth), :])
+        out[...] = total.astype(out.dtype)
+
+
+def partial_three(query, key, value, weight):
+    rows, depth = query.shape
+    cols = weight.shape[1]
+    half = rows // 2
+    return pl.pallas_call(
+        partial_three_kernel,
+        grid=(cols // WIDE,),
+        in_specs=[whole((rows, depth))] * 3 + [pl.BlockSpec((3 * depth, WIDE), lambda i: (0, i))],
+        out_specs=[pl.BlockSpec((half, WIDE), lambda i: (0, i))] * 2,
+        out_shape=[
+            jax.ShapeDtypeStruct((half, cols), jnp.float32),
+            jax.ShapeDtypeStruct((half, cols), jnp.bfloat16),
+        ],
+        compiler_params=settings(),
+        cost_estimate=light(),
+        name="partial_three",
+    )(query, key, value, weight)
 
 
 SWAP = [(0, 1), (1, 0)]
@@ -718,69 +1167,54 @@
 SLOTS = 72
 
 
+def after(value, *others):
+    return lax.optimization_barrier((value, *others))[0]
+
+
+class Order:
+
+    def __init__(self):
+        self.last = ()
+
+    def take(self, value):
+        return lax.optimization_barrier((value, self.last))[0]
+
+    def mark(self, value):
+        self.last = value
+        return value
+
+    def step(self, value):
+        return self.mark(self.take(value))
+
+
 def swap_along(array, axis):
     return lax.ppermute(array, axis, SWAP)
 
 
-def pass_on(array):
+def shift(array, step):
     size = lax.axis_size("z")
-    return lax.ppermute(array, "z", [(i, (i + 1) % size) for i in range(size)])
-
-
-def gather_team(rows):
-    other = swap_along(rows, "x")
-    near = jnp.concatenate([rows, other], axis=0)
-    far = swap_along(near, "core")
-    return jnp.concatenate([near, far], axis=0)
-
-
-def scatter_team(partial):
-    half = partial.shape[0] // 2
-    quarter = half // 2
-    got = swap_along(partial[half:].astype(jnp.bfloat16), "core")
-    kept = partial[:half].astype(jnp.float32) + got.astype(jnp.float32)
-    got = swap_along(kept[quarter:].astype(jnp.bfloat16), "x")
-    return kept[:quarter] + got.astype(jnp.float32)
-
-
-def gather_weight(mine):
-    held = [mine]
-    for _ in range(lax.axis_size("z") - 1):
-        held.append(pass_on(held[-1]))
-    return (held, [swap_along(piece, "y") for piece in held[1:]])
-
-
-def reduce_weight(grad):
-    depth = lax.axis_size("z")
-    half = grad.shape[0] // 2
-    piece = half // depth
-    got = swap_along(grad[half:], "y")
-    parts = [
-        grad[k * piece : (k + 1) * piece].astype(jnp.float32)
-        + got[k * piece : (k + 1) * piece].astype(jnp.float32)
-        for k in range(depth)
-    ]
-    total = parts[1].astype(jnp.bfloat16)
-    for k in list(range(2, depth)) + [0]:
-        total = (parts[k] + pass_on(total).astype(jnp.float32)).astype(jnp.bfloat16)
-    return total
-
-
-def gather_plane(piece):
+    return lax.ppermute(array, "z", [(i, (i + step) % size) for i in range(size)])
+
+
+def joined(arrays):
+    return jnp.concatenate(arrays, axis=0)
+
+
+def plane_start(piece):
+    return (piece, swap_along(piece, "x"), swap_along(piece, "y"))
+
+
+def plane_middle(started, order):
+    piece, by_x, by_y = started
     half = piece.shape[0] // 2
-    by_x = swap_along(piece, "x")
-    by_y = swap_along(piece, "y")
-    corner_top = swap_along(by_y[:half], "x")
-    corner_low = swap_along(by_x[half:], "y")
-    near = jnp.concatenate([piece, by_x, by_y, corner_top, corner_low], axis=0)
-    far = swap_along(near, "core")
-    size = piece.shape[0]
-    found = []
-    for core_flip, array in ((0, near), (1, far)):
-        for index, (x_flip, y_flip) in enumerate(((0, 0), (1, 0), (0, 1), (1, 1))):
-            code = 4 * x_flip + 2 * core_flip + y_flip
-            found.append((code, array[index * size : (index + 1) * size]))
-    return found
+    by_x, by_y = order.step((by_x, by_y))
+    return (piece, by_x, by_y, swap_along(by_y[:half], "x"), swap_along(by_x[half:], "y"))
+
+
+def plane_end(started, order):
+    piece, by_x, by_y, corner_top, corner_low = started
+    near = order.mark(joined([piece, by_x, by_y, *order.take((corner_top, corner_low))]))
+    return (near, swap_along(near, "core"))
 
 
 def total_all(vector):
@@ -813,10 +1247,6 @@
     inside = (slot >= base[..., None]) & (slot < (base + count)[..., None])
     held = begin[..., None] + slot - base[..., None]
     return jnp.sum(jnp.where(inside, value_of(held) + 1, 0), axis=-2, dtype=jnp.int32) - 1
-
-
-def one_hot(wanted, count, dtype=jnp.bfloat16):
-    return (wanted[:, None] == jnp.arange(count, dtype=jnp.int32)[None, :]).astype(dtype)
 
 
 def layer(
@@ -882,91 +1312,44 @@
         my_count.reshape(flat),
         lambda held: held * parts + residues - row_shift[..., None],
     ).reshape(-1)
-    spread_hot = one_hot(send_row, MICRO * tok_rows)
-    spread_hot_t = one_hot(send_row, MICRO * tok_rows).T
-    settle_hot = (
-        own_row[None, :] == jnp.arange(MICRO * own_rows, dtype=jnp.int32)[:, None]
-    ).astype(jnp.bfloat16)
-    settle_hot_t = one_hot(own_row, MICRO * own_rows)
-
-    def deal(array):
+    head_rows = HEAD_DIM
+    half_units = up_weight.shape[1] // 8
+
+    shard_heads = query_weight.shape[1]
+
+    def bias_rows(half):
+        row = jnp.concatenate(
+            [
+                lax.dynamic_slice_in_dim(bias, (2 * team + half) * size, size)
+                for bias, size in ((query_bias, HEAD_DIM), (value_bias, HEAD_DIM), (up_bias, half_units))
+            ]
+        )
+        return jnp.pad(row[None, :], ((0, 7), (0, width - row.shape[0])))
+
+    attn_mine, attn_other = attn_pack(
+        query_weight, key_weight, value_weight, out_weight, bias_rows(y), bias_rows(1 - y), team, y
+    )
+    blocks = half_units // 128
+    up_mine = flipped(up_weight, (2 * team + y) * blocks, blocks)
+    up_other = flipped(up_weight, (2 * team + 1 - y) * blocks, blocks)
+    down_mine = lax.dynamic_slice_in_dim(down_weight, (2 * team + y) * half_units, half_units, 0)
+    down_other = lax.dynamic_slice_in_dim(down_weight, (2 * team + 1 - y) * half_units, half_units, 0)
+
+    order = Order()
+
+    def spread_out(array):
         spread = array.reshape(MICRO, tok_rows // parts, parts, col_width)
         spread = lax.all_to_all(spread, PLANE, split_axis=2, concat_axis=1, tiled=True)
-        spread = spread.reshape(MICRO * tok_rows, col_width)
-        sent = matmul(spread_hot, spread).astype(jnp.bfloat16)
-        got = lax.all_to_all(sent, EVERY, split_axis=0, concat_axis=0, tiled=True)
-        got = got.reshape(depth, parts * SLOTS, col_width)
-        columns = [matmul(settle_hot, got[k]).astype(jnp.bfloat16) for k in range(depth)]
-        return jnp.concatenate(columns, axis=1)
-
-    def undeal(array):
-        sent = [
-            matmul(settle_hot_t, array[:, k * col_width : (k + 1) * col_width]).astype(jnp.bfloat16)
-            for k in range(depth)
-        ]
-        sent = jnp.concatenate(sent, axis=0)
-        got = lax.all_to_all(sent, EVERY, split_axis=0, concat_axis=0, tiled=True)
-        held = matmul(spread_hot_t, got).astype(jnp.bfloat16)
-        held = held.reshape(MICRO, tok_rows, 1, col_width)
-        back = lax.all_to_all(held, PLANE, split_axis=1, concat_axis=2, tiled=True)
-        return back.reshape(MICRO, tok_rows, col_width)
-
-    head_rows = HEAD_DIM
-    team_cols = query_weight.shape[1] // 4
-    team_units = up_weight.shape[1] // 4
-    half_units = team_units // 2
-
-    def team_slice(array, axis):
-        return lax.dynamic_slice_in_dim(array, team * (array.shape[axis] // 4), array.shape[axis] // 4, axis)
-
-    def halves(array):
-        size = array.shape[0] // 2
-        return (
-            lax.dynamic_slice_in_dim(array, y * size, size, 0),
-            lax.dynamic_slice_in_dim(array, (1 - y) * size, size, 0),
-        )
-
-    attn_parts = [
-        halves(team_slice(array, 1).T) for array in (query_weight, key_weight, value_weight)
-    ] + [halves(team_slice(out_weight, 0))]
-    attn_mine = jnp.concatenate([part[0] for part in attn_parts], axis=0)
-    attn_other = jnp.concatenate([part[1] for part in attn_parts], axis=0)
-    up_mine, up_other = halves(team_slice(up_weight, 1).T)
-    down_mine, down_other = halves(team_slice(down_weight, 0))
-
-    bias_pack = jnp.concatenate([query_bias, value_bias, up_bias]).astype(jnp.float32).reshape(-1, 128)
-    bias_held = [bias_pack]
-    for _ in range(depth - 1):
-        bias_held.append(pass_on(bias_held[-1]))
-    bias_held = [bias.reshape(-1) for bias in bias_held]
-
-    def bias_of(offset, size):
-        return jnp.concatenate(
-            [
-                lax.dynamic_slice_in_dim(bias, offset + (2 * team + half) * size, size)
-                for half in (y, 1 - y)
-                for bias in bias_held
-            ]
-        )
-
-    shard_heads = query_weight.shape[1]
-    query_b = bias_of(0, HEAD_DIM)
-    value_b = bias_of(shard_heads, HEAD_DIM)
-    up_b = bias_of(2 * shard_heads, half_units)
-    qkv_b = jnp.concatenate([query_b, jnp.zeros_like(query_b), value_b])
-
-    tok = deal(tokens)
-    attn_held, attn_got = gather_weight(attn_mine)
-    attn_all = attn_held + [attn_other] + attn_got
-    qkv_w = jnp.concatenate(
-        [piece[k * head_rows : (k + 1) * head_rows] for k in range(3) for piece in attn_all], axis=0
-    )
-    out_w = jnp.concatenate([piece[3 * head_rows :] for piece in attn_all], axis=0)
-    cot = deal(cotangent)
-    up_held, up_got = gather_weight(up_mine)
-    up_w = jnp.concatenate(up_held + [up_other] + up_got, axis=0)
-    down_held, down_got = gather_weight(down_mine)
-    down_w = jnp.concatenate(down_held + [down_other] + down_got, axis=0)
+        return spread.reshape(MICRO * tok_rows, col_width)
+
+    def box_exchange(sent):
+        return lax.all_to_all(sent, EVERY, split_axis=0, concat_axis=0, tiled=True)
+
+    def boxes(spread):
+        return pick_rows(send_row, spread, 384)
+
+    def settle(got):
+        return settle_rows(own_row, got.reshape(depth, parts * SLOTS, col_width), MICRO * own_rows)
 
     gain_one, shift_one, gain_two, shift_two, out_b, down_b = (
         array.astype(jnp.float32)
@@ -981,85 +1364,292 @@
         summary = jnp.where(position % (SEG + SUMM) >= SEG, holder, -1)
         infos.append((jnp.stack([segment, summary], axis=1), jnp.stack([segment, holder], axis=0)))
 
-    layer_rows = []
-    input_rows = []
+    def up_down(piece):
+        piece = order.take(piece)
+        return (shift(piece, 1), shift(piece, -1))
+
+    def onward(piece):
+        piece = order.step(piece)
+        return (piece, shift(piece, 1), swap_along(piece, "y"))
+
+    def swapped(piece):
+        piece = order.step(piece)
+        return (piece, swap_along(piece, "y"))
+
+    def team_start(rows):
+        return (rows, swap_along(rows, "x"))
+
+    def team_middle(started):
+        own, by_x = started
+        near = order.mark(joined([own, order.take(by_x)]))
+        return (near, swap_along(near, "core"))
+
+    def team_end(started):
+        near, far = started
+        return (near, order.step(far))
+
+    def sum_start(left, weight):
+        near, far = order.mark(partial_sums(order.take(left), weight))
+        return (near, swap_along(far, "core"))
+
+    def sum_middle(started):
+        kept, got = started
+        quarter = kept.shape[0] // 2
+        kept = kept + order.take(got).astype(jnp.float32)
+        moving = order.mark(kept[quarter:].astype(jnp.bfloat16))
+        return (kept[:quarter], swap_along(moving, "x"))
+
+    def sum_end(started):
+        kept, got = started
+        return kept + order.take(got).astype(jnp.float32)
+
+    def unsettle(array):
+        return unsettle_rows(own_row, array, depth).reshape(-1, col_width)
+
+    def unbox(got):
+        return drop_rows(send_row, got, MICRO * tok_rows, 256)
+
+    def spread_back(held):
+        held = held.reshape(MICRO, tok_rows, 1, col_width)
+        back = lax.all_to_all(held, PLANE, split_axis=1, concat_axis=2, tiled=True)
+        return back.reshape(MICRO, tok_rows, col_width)
+
+    order.mark(attn_mine)
+    attn_1, attn_3 = up_down(attn_mine)
+    tok_spread = spread_out(tokens)
+    tok_sent = order.mark(boxes(order.take(tok_spread)))
+    tok_got = box_exchange(tok_sent)
+    attn_1, attn_2, attn_y1 = onward(attn_1)
+    attn_3, attn_y3 = swapped(attn_3)
+    attn_2, attn_y2 = swapped(attn_2)
+    tok = order.mark(settle(order.take(tok_got)))
+    up_1, up_3 = up_down(up_mine)
+    cot_spread = spread_out(after(cotangent, tok))
+
+    def normed_rows(rows, gain, shift_by):
+        normed, inverse = normalize(rows)
+        return (normed, inverse, order.mark((normed * gain + shift_by).astype(jnp.bfloat16)))
+
+    rows_a = tok[:own_rows].astype(jnp.float32)
+    rows_b = tok[own_rows:].astype(jnp.float32)
+    normed_one_a, inverse_one_a, first_a = normed_rows(order.take(rows_a), gain_one, shift_one)
+    first_a = team_start(first_a)
+    normed_one_b, inverse_one_b, first_b = normed_rows(order.take(rows_b), gain_one, shift_one)
+    first_b = team_start(first_b)
+    attn_all = [attn_mine, attn_1, attn_2, attn_3, attn_other, *order.take((attn_y1, attn_y2, attn_y3))]
+    qkv_w = joined([piece[k * head_rows : (k + 1) * head_rows] for k in range(3) for piece in attn_all])
+    out_w = joined([piece[3 * head_rows : 4 * head_rows] for piece in attn_all])
+    order.mark((qkv_w, out_w))
+    bias_all = [piece[4 * head_rows].astype(jnp.float32) for piece in attn_all]
+    query_b = joined([bias[:head_rows] for bias in bias_all])
+    value_b = joined([bias[head_rows : 2 * head_rows] for bias in bias_all])
+    up_b = joined([bias[2 * head_rows : 2 * head_rows + half_units] for bias in bias_all])[None, :]
+    qkv_b = joined([query_b, jnp.zeros_like(query_b), value_b])[None, :]
+    no_b = jnp.zeros((1, out_w.shape[0]), jnp.float32)
+
+    first_a = team_end(team_middle(first_a))
+    qkv_a = order.mark(project(*order.take(first_a), qkv_w, qkv_b))
+    up_1, up_2, up_y1 = onward(up_1)
+    mixed_a = order.mark(attend(order.take(qkv_a), rank, *infos[0]))
+    first_b = team_middle(first_b)
+    sum_a1 = sum_start(mixed_a, out_w)
+    first_b = team_end(first_b)
+    qkv_b_ = order.mark(project(*order.take(first_b), qkv_w, qkv_b))
+    sum_a1 = sum_middle(sum_a1)
+    up_3, up_y3 = swapped(up_3)
+    down_1, down_3 = up_down(down_mine)
+    mixed_b = order.mark(attend(order.take(qkv_b_), rank, *infos[1]))
+    up_2, up_y2 = swapped(up_2)
+    sum_b1 = sum_start(mixed_b, out_w)
+    resid_a = rows_a + sum_end(sum_a1) + out_b
+    normed_two_a, inverse_two_a, second_a = normed_rows(
+        resid_a.astype(jnp.bfloat16).astype(jnp.float32), gain_two, shift_two
+    )
+    second_a = team_start(second_a)
+    sum_b1 = sum_middle(sum_b1)
+    cot_sent = order.mark(boxes(order.take(cot_spread)))
+    down_1, down_2, down_y1 = onward(down_1)
+    up_w = order.mark(joined([up_mine, up_1, up_2, up_3, up_other, *order.take((up_y1, up_y2, up_y3))]))
+    second_a = team_end(team_middle(second_a))
+    down_3, down_y3 = swapped(down_3)
+    cot_got = box_exchange(order.take(cot_sent))
+
+    hidden_a, slope_a = order.mark(expand(*order.take(second_a), up_w, up_b))
+    resid_b = rows_b + sum_end(sum_b1) + out_b
+    normed_two_b, inverse_two_b, second_b = normed_rows(
+        resid_b.astype(jnp.bfloat16).astype(jnp.float32), gain_two, shift_two
+    )
+    second_b = team_start(second_b)
+    down_2, down_y2 = swapped(down_2)
+    second_b = team_middle(second_b)
+    cot = order.mark(settle(order.take(cot_got)))
+    cot_own = cot.reshape(MICRO, own_rows, width)
+    second_b = team_end(second_b)
+    cot_parts = [team_start(cot_own[m]) for m in range(MICRO)]
+    hidden_b, slope_b = order.mark(expand(*order.take(second_b), up_w, up_b))
+    down_w = order.mark(
+        joined([down_mine, down_1, down_2, down_3, down_other, *order.take((down_y1, down_y2, down_y3))])
+    )
+    sum_a4 = sum_start(hidden_a, down_w)
+    cot_parts[0] = team_middle(cot_parts[0])
+    sum_b4 = sum_start(hidden_b, down_w)
+    cot_parts[1] = team_middle(cot_parts[1])
+    cot_a = team_end(cot_parts[0])
+    cot_own_a, cot_own_b = cot_own[0].astype(jnp.float32), cot_own[1].astype(jnp.float32)
+
+    low_a, up_sum_a = order.mark(expand_back(*order.take(cot_a), down_w, slope_a))
+    cot_b = team_end(cot_parts[1])
+    sum_a2 = sum_start(low_a, up_w)
+    sum_a4 = sum_middle(sum_a4)
+    low_b, up_sum_b = order.mark(expand_back(*order.take(cot_b), down_w, slope_b))
+    up_sum_a, up_sum_b = up_sum_a[0], up_sum_b[0]
+    sum_a2 = sum_middle(sum_a2)
+    sum_b2 = sum_start(low_b, up_w)
+    sum_b4 = sum_middle(sum_b4)
+
+    def cross_half(left_a, right_a, left_b, right_b, half):
+        size = left_a.shape[1] // 2
+        return order.mark(cross_sums(order.take(left_a), right_a, left_b, right_b, half * size, size))
+
+    down_far = cross_half(hidden_a, cot_a, hidden_b, cot_b, 1)
+    down_swap = swap_along(down_far, "y")
+    sum_b2 = sum_middle(sum_b2)
+
+    def second_back(started, normed_two, inverse_two, cot_rows):
+        grad = sum_end(started).astype(jnp.bfloat16).astype(jnp.float32)
+        back, gain_part, shift_part = norm_backward(grad, normed_two, inverse_two, gain_two)
+        resid_grad = cot_rows + back
+        low = order.mark(resid_grad.astype(jnp.bfloat16))
+        return (resid_grad, low, gain_part, shift_part)
+
+    resid_grad_a, attn_low_a, gain_two_a, shift_two_a = second_back(
+        sum_a2, normed_two_a, inverse_two_a, cot_own_a
+    )
+    attn_low_a = team_start(attn_low_a)
+    down_near = cross_half(hidden_a, cot_a, hidden_b, cot_b, 0)
+    layer_a = (resid_a + sum_end(sum_a4) + down_b).astype(jnp.bfloat16)
+    layer_b = (resid_b + sum_end(sum_b4) + down_b).astype(jnp.bfloat16)
+    layer_sent = order.mark(unsettle(order.take(joined([layer_a, layer_b]))))
+    layer_got = box_exchange(layer_sent)
+    up_far = cross_half(low_a, second_a, low_b, second_b, 1)
+    up_swap = swap_along(up_far, "y")
+    resid_grad_b, attn_low_b, gain_two_b, shift_two_b = second_back(
+        sum_b2, normed_two_b, inverse_two_b, cot_own_b
+    )
+    attn_low_b = team_start(attn_low_b)
+    attn_low_a = team_end(team_middle(attn_low_a))
+
+    def attn_back(attn_low, qkv, m):
+        mixed_grad = order.mark(project(*order.take(attn_low), out_w, no_b))
+        return order.mark(attend_back(qkv, order.take(mixed_grad), rank, *infos[m]))
+
+    def sum_start_three(lefts, weight):
+        near, far = order.mark(partial_three(*order.take(lefts), weight))
+        return (near, swap_along(far, "core"))
+
+    *lows_a, sums_a = attn_back(attn_low_a, qkv_a, 0)
+    attn_low_b = team_middle(attn_low_b)
+    sum_a3 = sum_start_three(lows_a, qkv_w)
+    attn_low_b = team_end(attn_low_b)
+    up_near = cross_half(low_a, second_a, low_b, second_b, 0)
+    layer_held = order.mark(unbox(order.take(layer_got)))
+    layer_out = spread_back(layer_held)
+
+    def ring_start(near, got):
+        piece = near.shape[0] // depth
+        got = order.take(got)
+        far_2 = order.mark(add_rows(near, got, 2))
+        move = shift(far_2, 1)
+        far_1 = order.mark(add_rows(near, order.take(got), 1))
+        back = shift(far_1, -1)
+        return (near, got, move, back)
+
+    def ring_middle(started):
+        near, got, move, back = started
+        far_3 = order.mark(add_three(near, got, order.take(move), 3))
+        return (near, got, shift(far_3, 1), back)
+
+    def ring_end(started):
+        near, got, move, back = started
+        move, back = order.take((move, back))
+        return order.mark(add_four(near, got, move, back, 0))
+
+    sum_a3 = sum_middle(sum_a3)
+    down_ring = ring_start(down_near, down_swap)
+    *lows_b, sums_b = attn_back(attn_low_b, qkv_b_, 1)
+    down_ring = ring_middle(down_ring)
+    sum_b3 = sum_start_three(lows_b, qkv_w)
+
+    def first_back(started, normed_one, inverse_one, resid_grad):
+        grad = sum_end(started).astype(jnp.bfloat16).astype(jnp.float32)
+        back, gain_part, shift_part = norm_backward(grad, normed_one, inverse_one, gain_one)
+        return (order.mark((resid_grad + back).astype(jnp.bfloat16)), gain_part, shift_part)
+
+    def by_piece(arrays):
+        rows = head_rows
+        return order.mark(joined([a[k * rows : (k + 1) * rows] for k in range(depth) for a in arrays]))
+
+    def cross_heads(index, half):
+        left_a, right_a, left_b, right_b = (
+            (lows_a[index], first_a, lows_b[index], first_b)
+            if index < 3
+            else (mixed_a, attn_low_a, mixed_b, attn_low_b)
+        )
+        return cross_half(left_a, right_a, left_b, right_b, half)
+
+    one_far = by_piece([cross_heads(0, 1), cross_heads(1, 1)])
+    one_swap = swap_along(one_far, "y")
+    sum_b3 = sum_middle(sum_b3)
+    input_a, gain_one_a, shift_one_a = first_back(sum_a3, normed_one_a, inverse_one_a, resid_grad_a)
+    two_far = by_piece([cross_heads(2, 1), cross_heads(3, 1)])
+    two_swap = swap_along(two_far, "y")
+    down_total = ring_end(down_ring)
+    up_ring = ring_start(up_near, up_swap)
+    one_near = by_piece([cross_heads(0, 0), cross_heads(1, 0)])
+    input_b, gain_one_b, shift_one_b = first_back(sum_b3, normed_one_b, inverse_one_b, resid_grad_b)
+    input_sent = order.mark(unsettle(order.take(joined([input_a, input_b]))))
+    input_got = box_exchange(input_sent)
+    two_near = by_piece([cross_heads(2, 0), cross_heads(3, 0)])
+    up_ring = ring_middle(up_ring)
+    one_ring = ring_start(one_near, one_swap)
+    down_plane = plane_start(down_total)
+    up_total = ring_end(up_ring)
+    down_plane = plane_middle(down_plane, order)
+    one_ring = ring_middle(one_ring)
+    up_plane = plane_start(up_total)
+    own = jnp.full((1,), eighth, jnp.int32)
+    two_ring = ring_start(two_near, two_swap)
+    down_plane = plane_end(down_plane, order)
+    down_grad = order.mark(stack_pieces(*order.take(down_plane), own, False))
+    one_total = ring_end(one_ring)
+    one_plane = plane_start(one_total)
+    input_held = order.mark(unbox(order.take(input_got)))
+    input_grad = spread_back(input_held)
+    two_ring = ring_middle(two_ring)
+    up_plane = plane_middle(up_plane, order)
+    up_plane = plane_end(up_plane, order)
+    one_plane = plane_middle(one_plane, order)
+    up_grad = order.mark(stack_pieces(*order.take(up_plane), own, True))
+    two_total = ring_end(two_ring)
+    two_plane = plane_start(two_total)
+    one_plane = plane_end(one_plane, order)
+    two_plane = plane_middle(two_plane, order)
+    query_grad, key_grad = order.mark(stack_heads(*order.take(one_plane), own, (True, True)))
+    two_plane = plane_end(two_plane, order)
+    value_grad, out_w_grad = order.mark(stack_heads(*order.take(two_plane), own, (True, False)))
     kept = []
-    for m in range(MICRO):
-        rows = tok[m * own_rows : (m + 1) * own_rows].astype(jnp.float32)
-        cot_rows = cot[m * own_rows : (m + 1) * own_rows]
-        normed_one, inverse_one = normalize(rows)
-        first_in = gather_team((normed_one * gain_one + shift_one).astype(jnp.bfloat16))
-        qkv = (times_transpose(first_in, qkv_w) + qkv_b).astype(jnp.bfloat16)
-        mixed = attend(qkv, rank, *infos[m])
-        resid = rows + scatter_team(matmul(mixed, out_w)) + out_b
-        normed_two, inverse_two = normalize(resid.astype(jnp.bfloat16).astype(jnp.float32))
-        second_in = gather_team((normed_two * gain_two + shift_two).astype(jnp.bfloat16))
-        cot_all = gather_team(cot_rows)
-        hidden_pre = times_transpose(second_in, up_w) + up_b
-        hidden_act, gelu_pull = jax.vjp(gelu_tanh, hidden_pre)
-        hidden = hidden_act.astype(jnp.bfloat16)
-        hidden_grad = gelu_pull(times_transpose(cot_all, down_w))[0]
-        hidden_low = hidden_grad.astype(jnp.bfloat16)
-        layer_rows.append((resid + scatter_team(matmul(hidden, down_w)) + down_b).astype(jnp.bfloat16))
-        second_grad = scatter_team(matmul(hidden_low, up_w)).astype(jnp.bfloat16).astype(jnp.float32)
-        back, gain_two_part, shift_two_part = norm_backward(second_grad, normed_two, inverse_two, gain_two)
-        resid_grad = cot_rows.astype(jnp.float32) + back
-        attn_low = gather_team(resid_grad.astype(jnp.bfloat16))
-        mixed_grad = times_transpose(attn_low, out_w).astype(jnp.bfloat16)
-        query_low, key_low, value_low, sums = attend_back(qkv, mixed_grad, rank, *infos[m])
-        qkv_low = jnp.concatenate([query_low, key_low, value_low], axis=1)
-        first_grad = scatter_team(matmul(qkv_low, qkv_w)).astype(jnp.bfloat16).astype(jnp.float32)
-        back, gain_one_part, shift_one_part = norm_backward(first_grad, normed_one, inverse_one, gain_one)
-        input_rows.append((resid_grad + back).astype(jnp.bfloat16))
+    for sums, up_sum, resid_grad, cot_rows, norms in (
+        (sums_a, up_sum_a, resid_grad_a, cot_own_a, (gain_one_a, shift_one_a, gain_two_a, shift_two_a)),
+        (sums_b, up_sum_b, resid_grad_b, cot_own_b, (gain_one_b, shift_one_b, gain_two_b, shift_two_b)),
+    ):
         kept.append(
             dict(
-                up=cross_rows(hidden_low, second_in),
-                down=cross_rows(hidden, cot_all),
-                out=cross_rows(mixed, attn_low),
-                qkv=cross_rows(qkv_low, first_in),
                 query_b=sums[0],
                 value_b=sums[1],
-                up_b=jnp.sum(hidden_grad, axis=0),
-                vectors=(
-                    jnp.sum(resid_grad, axis=0),
-                    jnp.sum(cot_rows.astype(jnp.float32), axis=0),
-                    gain_one_part,
-                    shift_one_part,
-                    gain_two_part,
-                    shift_two_part,
-                ),
+                up_b=up_sum,
+                vectors=(jnp.sum(resid_grad, axis=0), jnp.sum(cot_rows, axis=0)) + norms,
             )
         )
-
-    layer_out = undeal(jnp.concatenate(layer_rows, axis=0))
-
-    def both(name):
-        return (kept[0][name] + kept[1][name]).astype(jnp.bfloat16)
-
-    def into(pieces, rows_per, start, size):
-        shard = jnp.zeros((8 * size, width), jnp.bfloat16)
-        for code, piece in pieces:
-            at = jnp.bitwise_xor(eighth, code)
-            shard = lax.dynamic_update_slice(shard, piece[start : start + size], (at * size, 0))
-        return shard.astype(jnp.float32)
-
-    down_grad = into(gather_plane(reduce_weight(both("down"))), half_units, 0, half_units)
-    up_grad = into(gather_plane(reduce_weight(both("up"))), half_units, 0, half_units).T
-    qkv_grad = both("qkv")
-    out_grad = both("out")
-    heads = qkv_grad.shape[0] // 3
-    attn_grad = jnp.concatenate(
-        [
-            array[k * head_rows : (k + 1) * head_rows]
-            for k in range(2 * depth)
-            for array in (qkv_grad[:heads], qkv_grad[heads : 2 * heads], qkv_grad[2 * heads :], out_grad)
-        ],
-        axis=0,
-    )
-    attn_pieces = gather_plane(reduce_weight(attn_grad))
-    query_grad, key_grad, value_grad, out_w_grad = (
-        into(attn_pieces, 4 * head_rows, k * head_rows, head_rows) for k in range(4)
-    )
 
     def place(vector, shard_size, size):
         whole = jnp.zeros((depth * shard_size,), jnp.float32)
@@ -1092,13 +1682,12 @@
         size = vector.shape[0] // depth
         return lax.dynamic_slice_in_dim(vector, z * size, size)
 
-    input_grad = undeal(jnp.concatenate(input_rows, axis=0))
     return (
         layer_out,
         input_grad,
-        query_grad.T,
-        key_grad.T,
-        value_grad.T,
+        query_grad,
+        key_grad,
+        value_grad,
         out_w_grad,
         own_shard(query_b_grad),
         own_shard(value_b_grad),

time: 1610 us -> 1440 us (0.89)
  Pallas kernels: 92 us -> 545 us
  matrix products: 314 us -> 0 us
  waiting for transfers between devices: 680 us -> 425 us
  local copies, waits for them, and re-layouts: 269 us -> 204 us
  starting transfers between devices: 106 us -> 164 us
  other arithmetic: 124 us -> 89.6 us
    pallas_call x0 -> x59, Pallas kernels: none -> 454 us  [the longest x12 115 us: cross_sums(): pl.pallas_call(cross_kernel, grid=(size // tall,), in_specs=[left_spec, r...]
    dot_general x44 -> x0, matrix products: 314 us -> none  [the longest x28 121 us: matmul(): return jnp.dot(left_array, right_array, preferred_element_type=jnp.float32)]
    ppermute x62 -> x68, waiting for transfers between devices: 373 us -> 161 us  [swap_along(): return lax.ppermute(array, axis, SWAP)]
    dynamic_update_slice x23 -> x0, local copies, waits for them, and re-layouts: 36.7 us -> none  [into(): lax.dynamic_update_slice(shard, piece[start:start + size], (at * size, 0))]
    all_to_all x8, waiting for transfers between devices: 68.7 us -> 33.7 us  [the longest x2 18.8 us: spread_out(): lax.all_to_all(spread, PLANE, split_axis=2, concat_axis=1, tiled=True)]
    ppermute x21, starting transfers between devices: 27.5 us -> 54.5 us  [shift(): lax.ppermute(array, 'z', [(i, (i + step) % size) for i in range(size)])]
    transpose x4 -> x0, other arithmetic: 19.4 us -> none  [the longest x1 11.8 us: layer(): into(gather_plane(reduce_weight(both('up'))), half_units, 0, half_units)]
    convert_element_type x17 -> x18, other arithmetic: 43.3 us -> 25 us  [the longest x8 6.18 us: layer(): bias_all = [piece[4 * head_rows].astype(jnp.float32) for piece in attn_all]]
  transfers between devices with their start and end apart: 93 -> 99, of which waited for: 39 -> 32; matrix products, arithmetic and copies ran while one was open for 41% -> 17% of each run, Pallas kernels for 6% -> 37%
where the time goes in v2:
time: 1440 us; the launch traced here: 1430 us
  Pallas kernels  545 us (38%)
  waiting for transfers between devices  425 us (30%)
  local copies, waits for them, and re-layouts  204 us (14%)
  starting transfers between devices  164 us (11%)
  other arithmetic  89.6 us (6%)
    ppermute x21, waiting for transfers between devices, shift(): lax.ppermute(array, 'z', [(i, (i + step) % size) for i in range(size)])  227 us
    ppermute x68, waiting for transfers between devices, swap_along(): return lax.ppermute(array, axis, SWAP)  161 us
    unnamed x323, local copies, waits for them, and re-layouts  134 us
    pallas_call x12, Pallas kernels, cross_sums(): pl.pallas_call(cross_kernel, grid=(size // tall,), in_specs=[left_spec, r...  115 us
    pallas_call x6, Pallas kernels, partial_sums(): pl.pallas_call(partial_kernel, grid=(cols // WIDE,), in_specs=[whole((row...  66.5 us
    ppermute x68, starting transfers between devices, swap_along(): return lax.ppermute(array, axis, SWAP)  60.3 us
    pallas_call x2, Pallas kernels, attend_back(): pl.pallas_call(attend_back_kernel, grid_spec=pltpu.PrefetchScalarGridSpec...  54.6 us
    ppermute x21, starting transfers between devices, shift(): lax.ppermute(array, 'z', [(i, (i + step) % size) for i in range(size)])  54.5 us
  transfers between devices with their start and end apart: 99, of which 32 were waited for; matrix products, arithmetic and copies ran while one was open for 17% of the time, Pallas kernels for 37%

profile of v2, /device:TPU:0, one launch (start us, length us, event | category | flops | bytes accessed | tf_op | source)
XLA Modules:
  0.0 1430.1 jit_solution(4819309912555835152)
XLA Ops:
  28.2 18.8 %all-to-all-done = bf16[2,128,8,512]{3,1,0,2:T(8,128)(2,1)S(1)} async-done(((bf16[2,128,8,512]{3,1,0,2:T(8,128)(2,1)}), bf16[2,128,8,512]{3,1,0,2:T(8,128)(2,1)S(1)}, u32[]{:S(2)}, u32[]{:S(2)}) %all-to-all-start) | async-done | bytes 2097184 | tf_op jit(solution)/shard_map/all_to_all | solution.py:1342
  48.6 8.7 pick_rows.2
  72.5 53.9 %collective-permute-done.1 = bf16[264,2048]{1,0:T(8,128)(2,1)} collective-permute-done((bf16[264,2048]{1,0:T(8,128)(2,1)}, bf16[264,2048]{1,0:T(8,128)(2,1)}, u32[]{:S(2)}, u32[]{:S(2)}) %collective-permute-start.1) | collective-permute-done | bytes 1081376 | tf_op jit(solution)/shard_map/ppermute | solution.py:1196
  199.9 11.7 project.4.query_ref.key_ref.value_ref
  211.6 8.2 collective-permute-done.8
  221.7 18.3 %attend.2.left_ref.left_a = bf16[1024,512]{1,0:T(8,128)(2,1)S(1)} custom-call(s32[1]{0:T(128)} %bitcast.10.rank_ref, bf16[1024,1536]{1,0:T(8,128)(2,1)S(1)} %copy-done.1, bf16[1024,1536]{1,0:T(8,128)(2,1)S(1)} %copy-done.1, bf16[1024,1536]{1,0:T(8,128)(2,1)S(1)} %copy-done.1, s32[1024,2]{1,0:T(8,128)S(1)} %copy.154.key_info_ref, ...), custom_call_target="tpu_custom_call" | custom-call | flops 1048576 | bytes 4096 | tf_op jit(solution)/shard_map/attend/pallas_call | solution.py:565
  242.3 6.8 partial_sums.6
  265.8 11.8 project.5.query_ref.key_ref.value_ref
  295.2 18.3 %attend.3.left_ref.left_b = bf16[1024,512]{1,0:T(8,128)(2,1)S(1)} custom-call(s32[1]{0:T(128)} %bitcast.10.rank_ref, bf16[1024,1536]{1,0:T(8,128)(2,1)S(1)} %copy-done, bf16[1024,1536]{1,0:T(8,128)(2,1)S(1)} %copy-done, bf16[1024,1536]{1,0:T(8,128)(2,1)S(1)} %copy-done, s32[1024,2]{1,0:T(8,128)S(1)} %copy-done.13, s32[2,1024]{1,0:T(2,128)S(1)} %pad_add_fusion.3.query_info_ref), custom_call_target="tpu_custom_call" | custom-call | flops 1048576 | bytes 4096 | tf_op jit(solution)/shard_map/attend/pallas_call | solution.py:565
  316.6 6.1 partial_sums.7
  337.4 8.7 pick_rows.3
  346.1 10.3 collective-permute-done.19
  376.0 22.4 %collective-permute-done.22 = bf16[256,2048]{1,0:T(8,128)(2,1)} collective-permute-done((bf16[256,2048]{1,0:T(8,128)(2,1)}, bf16[256,2048]{1,0:T(8,128)(2,1)}, u32[]{:S(2)}, u32[]{:S(2)}) %collective-permute-start.22) | collective-permute-done | bytes 1048608 | tf_op jit(solution)/shard_map/ppermute | solution.py:1196
  405.5 17.6 %expand.2 = (bf16[1024,2048]{1,0:T(8,128)(2,1)}, bf16[1024,2048]{1,0:T(8,128)(2,1)}) custom-call(bf16[512,2048]{1,0:T(8,128)(2,1)} %pad_maximum_fusion.2.near_ref.near_a, bf16[512,2048]{1,0:T(8,128)(2,1)} %collective-permute-done.21.far_ref.far_a, bf16[2048,2048]{1,0:T(8,128)(2,1)} %constant_dynamic-update-slice_fusion.weight_ref, f32[1,2048]{1,0:T(1,128)} %bitcast.237), custom_call_target="tpu_custom_call" | custom-call | flops 1048576 | bytes 4096 | tf_op jit(solution)/shard_map/expand/pallas_call | solution.py:769
  428.1 40.9 %collective-permute-done.23 = bf16[256,2048]{1,0:T(8,128)(2,1)} collective-permute-done((bf16[256,2048]{1,0:T(8,128)(2,1)}, bf16[256,2048]{1,0:T(8,128)(2,1)}, u32[]{:S(2)}, u32[]{:S(2)}) %collective-permute-start.23) | collective-permute-done | bytes 1048608 | tf_op jit(solution)/shard_map/ppermute | solution.py:1196
  494.2 17.5 %expand.3 = (bf16[1024,2048]{1,0:T(8,128)(2,1)}, bf16[1024,2048]{1,0:T(8,128)(2,1)}) custom-call(bf16[512,2048]{1,0:T(8,128)(2,1)} %pad_maximum_fusion.3.near_ref.near_b, bf16[512,2048]{1,0:T(8,128)(2,1)} %collective-permute-done.29.far_ref.far_b, bf16[2048,2048]{1,0:T(8,128)(2,1)} %constant_dynamic-update-slice_fusion.weight_ref, f32[1,2048]{1,0:T(1,128)} %bitcast.238), custom_call_target="tpu_custom_call" | custom-call | flops 1048576 | bytes 4096 | tf_op jit(solution)/shard_map/expand/pallas_call | solution.py:769
  511.8 8.7 collective-permute-done.26
  520.4 22.2 %collective-permute-done.27 = bf16[256,2048]{1,0:T(8,128)(2,1)} collective-permute-done((bf16[256,2048]{1,0:T(8,128)(2,1)}, bf16[256,2048]{1,0:T(8,128)(2,1)}, u32[]{:S(2)}, u32[]{:S(2)}) %collective-permute-start.27) | collective-permute-done | bytes 1048608 | tf_op jit(solution)/shard_map/ppermute | solution.py:1191
  549.6 13.2 partial_sums.8
  565.3 13.9 partial_sums.9
  581.6 14.6 %expand_back.2 = (bf16[1024,2048]{1,0:T(8,128)(2,1)}, f32[8,2048]{1,0:T(8,128)}) custom-call(bf16[512,2048]{1,0:T(8,128)(2,1)} %copy-done.31, bf16[512,2048]{1,0:T(8,128)(2,1)} %collective-permute-done.32.far_ref.far_a, bf16[2048,2048]{1,0:T(8,128)(2,1)} %constant_dynamic-update-slice_fusion.9.weight_ref, bf16[1024,2048]{1,0:T(8,128)(2,1)} %get-tuple-element.253.slope_ref), custom_call_target="tpu_custom_call" | custom-call | flops 1048576 | bytes 4096 | tf_op jit(solution)/shard_map/expand_back/pallas_call | solution.py:800
  596.2 13.3 partial_sums.10
  615.4 14.6 %expand_back.3 = (bf16[1024,2048]{1,0:T(8,128)(2,1)}, f32[8,2048]{1,0:T(8,128)}) custom-call(bf16[512,2048]{1,0:T(8,128)(2,1)} %copy-done.32, bf16[512,2048]{1,0:T(8,128)(2,1)} %collective-permute-done.34.far_ref.far_b, bf16[2048,2048]{1,0:T(8,128)(2,1)} %constant_dynamic-update-slice_fusion.9.weight_ref, bf16[1024,2048]{1,0:T(8,128)(2,1)} %get-tuple-element.263.slope_ref), custom_call_target="tpu_custom_call" | custom-call | flops 1048576 | bytes 4096 | tf_op jit(solution)/shard_map/expand_back/pallas_call | solution.py:800
  635.4 13.3 partial_sums.11
  655.8 14.4 %cross_sums.12 = bf16[1024,2048]{1,0:T(8,128)(2,1)} custom-call(bf16[1024,2048]{1,0:T(8,128)(2,1)} %get-tuple-element.297.left_ref.left_a, bf16[512,2048]{1,0:T(8,128)(2,1)} %copy-done.31, bf16[512,2048]{1,0:T(8,128)(2,1)} %collective-permute-done.32.far_ref.far_a, bf16[1024,2048]{1,0:T(8,128)(2,1)} %get-tuple-element.271.left_ref.left_b, ...), custom_call_target="tpu_custom_call" | custom-call | flops 1048576 | bytes 4096 | tf_op jit(solution)/shard_map/cross_sums/pallas_call | solution.py:864
  678.6 14.7 %cross_sums.14 = bf16[1024,2048]{1,0:T(8,128)(2,1)} custom-call(bf16[1024,2048]{1,0:T(8,128)(2,1)} %get-tuple-element.317.left_ref.left_a, bf16[512,2048]{1,0:T(8,128)(2,1)} %pad_maximum_fusion.2.near_ref.near_a, bf16[512,2048]{1,0:T(8,128)(2,1)} %collective-permute-done.21.far_ref.far_a, bf16[1024,2048]{1,0:T(8,128)(2,1)} %get-tuple-element.290.left_ref.left_b, ...), custom_call_target="tpu_custom_call" | custom-call | flops 1048576 | bytes 4096 | tf_op jit(solution)/shard_map/cross_sums/pallas_call | solution.py:864
  693.6 8.3 collective-permute-done.41
  712.2 14.4 %cross_sums.13.refs_0_ = bf16[1024,2048]{1,0:T(8,128)(2,1)} custom-call(bf16[1024,2048]{1,0:T(8,128)(2,1)} %get-tuple-element.297.left_ref.left_a, bf16[512,2048]{1,0:T(8,128)(2,1)} %copy-done.31, bf16[512,2048]{1,0:T(8,128)(2,1)} %collective-permute-done.32.far_ref.far_a, bf16[1024,2048]{1,0:T(8,128)(2,1)} %get-tuple-element.271.left_ref.left_b, ...), custom_call_target="tpu_custom_call" | custom-call | flops 1048576 | bytes 4096 | tf_op jit(solution)/shard_map/cross_sums/pallas_call | solution.py:864
  726.6 20.3 %collective-permute-done.40 = bf16[256,2048]{1,0:T(8,128)(2,1)} collective-permute-done((bf16[256,2048]{1,0:T(8,128)(2,1)}, bf16[256,2048]{1,0:T(8,128)(2,1)}, u32[]{:S(2)}, u32[]{:S(2)}) %collective-permute-start.40) | collective-permute-done | bytes 1048608 | tf_op jit(solution)/shard_map/ppermute | solution.py:1191
  758.9 12.9 all-to-all-start.4
  778.6 6.3 project.6.grad_ref
  786.1 27.3 %attend_back.2 = (bf16[1024,512]{1,0:T(8,128)(2,1)S(1)}, bf16[1024,512]{1,0:T(8,128)(2,1)S(1)}, bf16[1024,512]{1,0:T(8,128)(2,1)S(1)}, f32[8,512]{1,0:T(8,128)S(1)}) custom-call(s32[1]{0:T(128)} %bitcast.10.rank_ref, bf16[1024,1536]{1,0:T(8,128)(2,1)S(1)} %copy-done.2, bf16[1024,1536]{1,0:T(8,128)(2,1)S(1)} %copy-done.2, bf16[1024,1536]{1,0:T(8,128)(2,1)S(1)} %copy-done.2, ...), custom_call_target="tpu_custom_call" | custom-call | flops 1048576 | bytes 4096 | tf_op jit(solution)/shard_map/attend_back/pallas_call | solution.py:673
  813.5 7.8 collective-permute-done.42
  824.5 10.6 partial_three.2
  838.0 14.7 %cross_sums.15.refs_0_ = bf16[1024,2048]{1,0:T(8,128)(2,1)} custom-call(bf16[1024,2048]{1,0:T(8,128)(2,1)} %get-tuple-element.317.left_ref.left_a, bf16[512,2048]{1,0:T(8,128)(2,1)} %pad_maximum_fusion.2.near_ref.near_a, bf16[512,2048]{1,0:T(8,128)(2,1)} %collective-permute-done.21.far_ref.far_a, bf16[1024,2048]{1,0:T(8,128)(2,1)} %get-tuple-element.290.left_ref.left_b, ...), custom_call_target="tpu_custom_call" | custom-call | flops 1048576 | bytes 4096 | tf_op jit(solution)/shard_map/cross_sums/pallas_call | solution.py:864
  852.7 8.8 drop_rows.2
  866.9 23.4 %collective-permute-done.48.refs_1_ = bf16[1024,2048]{1,0:T(8,128)(2,1)} collective-permute-done((bf16[1024,2048]{1,0:T(8,128)(2,1)}, bf16[1024,2048]{1,0:T(8,128)(2,1)}, u32[]{:S(2)}, u32[]{:S(2)}) %collective-permute-start.48) | collective-permute-done | bytes 4194336 | tf_op jit(solution)/shard_map/ppermute | solution.py:1191
  900.7 6.2 project.7.grad_ref
  908.1 27.3 %attend_back.3 = (bf16[1024,512]{1,0:T(8,128)(2,1)S(1)}, bf16[1024,512]{1,0:T(8,128)(2,1)S(1)}, bf16[1024,512]{1,0:T(8,128)(2,1)S(1)}, f32[8,512]{1,0:T(8,128)S(1)}) custom-call(s32[1]{0:T(128)} %bitcast.10.rank_ref, bf16[1024,1536]{1,0:T(8,128)(2,1)S(1)} %copy-done, bf16[1024,1536]{1,0:T(8,128)(2,1)S(1)} %copy-done, bf16[1024,1536]{1,0:T(8,128)(2,1)S(1)} %copy-done, ...), custom_call_target="tpu_custom_call" | custom-call | flops 1048576 | bytes 4096 | tf_op jit(solution)/shard_map/attend_back/pallas_call | solution.py:673
  938.5 7.1 cross_sums.22
  946.6 7.2 cross_sums.23
  959.9 10.7 partial_three.3
  970.6 7.1 cross_sums.16
  979.7 7.1 cross_sums.17
  999.9 7.1 cross_sums.18
  1007.0 7.2 cross_sums.19
  1026.3 7.1 cross_sums.20
  1042.5 7.1 cross_sums.21
  1054.6 10.1 collective-permute-done.56.refs_2_
  1080.9 6.3 collective-permute-done.61.refs_3_
  1087.1 22.5 %collective-permute-done.60.refs_2_ = bf16[256,2048]{1,0:T(8,128)(2,1)} collective-permute-done((bf16[256,2048]{1,0:T(8,128)(2,1)}, bf16[256,2048]{1,0:T(8,128)(2,1)}, u32[]{:S(2)}, u32[]{:S(2)}) %collective-permute-start.60) | collective-permute-done | bytes 1048608 | tf_op jit(solution)/shard_map/ppermute | solution.py:1196
  1154.8 13.7 stack_pieces.2
  1168.5 30.4 %collective-permute-done.63.refs_3_ = bf16[128,2048]{1,0:T(8,128)(2,1)} collective-permute-done((bf16[128,2048]{1,0:T(8,128)(2,1)}, bf16[128,2048]{1,0:T(8,128)(2,1)}, u32[]{:S(2)}, u32[]{:S(2)}) %collective-permute-start.63) | collective-permute-done | bytes 524320 | tf_op jit(solution)/shard_map/ppermute | solution.py:1196
  1198.9 15.2 %collective-permute-done.62.refs_2_ = bf16[128,2048]{1,0:T(8,128)(2,1)} collective-permute-done((bf16[128,2048]{1,0:T(8,128)(2,1)}, bf16[128,2048]{1,0:T(8,128)(2,1)}, u32[]{:S(2)}, u32[]{:S(2)}) %collective-permute-start.62) | collective-permute-done | bytes 524320 | tf_op jit(solution)/shard_map/ppermute | solution.py:1196
  1216.6 9.0 all-to-all-done.6
  1227.1 8.7 drop_rows.3
  1259.3 18.1 %collective-permute-start.77 = (bf16[128,2048]{1,0:T(8,128)(2,1)}, bf16[128,2048]{1,0:T(8,128)(2,1)S(1)}, u32[]{:S(2)}, u32[]{:S(2)}) collective-permute-start(bf16[128,2048]{1,0:T(8,128)(2,1)} %add_pieces.30), channel_id=1, source_target_pairs={{0,1},{1,2},{2,3},{3,0},{4,5},{5,6},{6,7},{7,4},{8,9},{9,10},{10,1... | collective-permute-start | bytes 1572872 | tf_op jit(solution)/shard_map/ppermute | solution.py:1196
  1279.8 14.3 %stack_pieces.3 = f32[2048,2048]{1,0:T(8,128)} custom-call(s32[1]{0:T(128)} %bitcast.65.own_ref, bf16[1024,2048]{1,0:T(8,128)(2,1)} %constant_dynamic-update-slice_fusion.21.near_ref, bf16[1024,2048]{1,0:T(8,128)(2,1)} %collective-permute-done.79.far_ref), custom_call_target="tpu_custom_call" | custom-call | flops 1048576 | bytes 4096 | tf_op jit(solution)/shard_map/stack_pieces/pallas_call | solution.py:1047
  1294.2 6.7 collective-permute-done.77.refs_2_
  1317.1 32.2 %collective-permute-done.81 = bf16[128,2048]{1,0:T(8,128)(2,1)S(1)} collective-permute-done((bf16[128,2048]{1,0:T(8,128)(2,1)S(1)}, bf16[128,2048]{1,0:T(8,128)(2,1)S(1)}, u32[]{:S(2)}, u32[]{:S(2)}) %collective-permute-start.81) | collective-permute-done | bytes 524320 | tf_op jit(solution)/shard_map/ppermute | solution.py:1191
  1353.2 7.1 stack_heads.2
  1372.7 24.3 %collective-permute-done.87 = f32[192,128]{1,0:T(8,128)S(1)} collective-permute-done((f32[192,128]{1,0:T(8,128)S(1)}, f32[192,128]{1,0:T(8,128)S(1)}, u32[]{:S(2)}, u32[]{:S(2)}) %collective-permute-start.87) | collective-permute-done | bytes 98336 | tf_op jit(solution)/shard_map/ppermute | solution.py:1191
  1401.7 7.4 collective-permute-start.89
  1422.8 7.1 stack_heads.3
  (793 shorter events, 515.3 us)
Async XLA Ops:
  9.3 56.1 %collective-permute-start = (bf16[264,2048]{1,0:T(8,128)(2,1)}, bf16[264,2048]{1,0:T(8,128)(2,1)}, u32[]{:S(2)}, u32[]{:S(2)}) collective-permute-start(bf16[264,2048]{1,0:T(8,128)(2,1)} %get-tuple-element.206), channel_id=1, source_target_pairs={{0,1},{1,2},{2,3},{3,0},{4,5},{5,6},{6,7},{7,4},{8,9},{9,10},{10,1... | collective-permute-start | bytes 3244040 | tf_op jit(solution)/shard_map/ppermute | solution.py:1196
  12.3 56.3 %collective-permute-start.2 = (bf16[264,2048]{1,0:T(8,128)(2,1)}, bf16[264,2048]{1,0:T(8,128)(2,1)}, u32[]{:S(2)}, u32[]{:S(2)}) collective-permute-start(bf16[264,2048]{1,0:T(8,128)(2,1)} %get-tuple-element.206), channel_id=1, source_target_pairs={{0,3},{1,0},{2,1},{3,2},{4,7},{5,4},{6,5},{7,6},{8,11},{9,8},{10,9... | collective-permute-start | bytes 3244040 | tf_op jit(solution)/shard_map/ppermute | solution.py:1196
  16.3 30.7 %all-to-all-start = ((bf16[2,128,8,512]{3,1,0,2:T(8,128)(2,1)}), bf16[2,128,8,512]{3,1,0,2:T(8,128)(2,1)S(1)}, u32[]{:S(2)}, u32[]{:S(2)}) async-start(bf16[2,128,8,512]{3,1,0,2:T(8,128)(2,1)} %copy.151), calls=%async_computation | async-start | bytes 4194304 | tf_op jit(solution)/shard_map/all_to_all | solution.py:1342
  57.3 80.7 %all-to-all-start.1 = ((bf16[32,72,512]{2,1,0:T(8,128)(2,1)}), bf16[32,72,512]{2,1,0:T(8,128)(2,1)S(1)}, u32[]{:S(2)}, u32[]{:S(2)}) async-start(bf16[32,72,512]{2,1,0:T(8,128)(2,1)} %bitcast.215), calls=%async_computation.1 | async-start | bytes 4718592 | tf_op jit(solution)/shard_map/all_to_all | solution.py:1346
  65.4 61.0 %collective-permute-start.1 = (bf16[264,2048]{1,0:T(8,128)(2,1)}, bf16[264,2048]{1,0:T(8,128)(2,1)}, u32[]{:S(2)}, u32[]{:S(2)}) collective-permute-start(bf16[264,2048]{1,0:T(8,128)(2,1)} %collective-permute-done), channel_id=1, source_target_pairs={{0,1},{1,2},{2,3},{3,0},{4,5},{5,6},{6,7},{7,4},{8,9},{9,10},{10,1... | collective-permute-start | bytes 3244040 | tf_op jit(solution)/shard_map/ppermute | solution.py:1196
  67.1 89.9 %collective-permute-start.4 = (bf16[264,2048]{1,0:T(8,128)(2,1)}, bf16[264,2048]{1,0:T(8,128)(2,1)}, u32[]{:S(2)}, u32[]{:S(2)}) collective-permute-start(bf16[264,2048]{1,0:T(8,128)(2,1)} %collective-permute-done), channel_id=1, source_target_pairs={{0,16},{16,0},{1,17},{17,1},{2,18},{18,2},{3,19},{19,3},{4,20},{20... | collective-permute-start | bytes 3244040 | tf_op jit(solution)/shard_map/ppermute | solution.py:1191
  68.6 88.4 %collective-permute-start.6 = (bf16[264,2048]{1,0:T(8,128)(2,1)}, bf16[264,2048]{1,0:T(8,128)(2,1)}, u32[]{:S(2)}, u32[]{:S(2)}) collective-permute-start(bf16[264,2048]{1,0:T(8,128)(2,1)} %collective-permute-done.2), channel_id=1, source_target_pairs={{0,16},{16,0},{1,17},{17,1},{2,18},{18,2},{3,19},{19,3},{4,20},{20... | collective-permute-start | bytes 3244040 | tf_op jit(solution)/shard_map/ppermute | solution.py:1191
  126.4 31.4 %collective-permute-start.5 = (bf16[264,2048]{1,0:T(8,128)(2,1)}, bf16[264,2048]{1,0:T(8,128)(2,1)}, u32[]{:S(2)}, u32[]{:S(2)}) collective-permute-start(bf16[264,2048]{1,0:T(8,128)(2,1)} %collective-permute-done.1), channel_id=1, source_target_pairs={{0,16},{16,0},{1,17},{17,1},{2,18},{18,2},{3,19},{19,3},{4,20},{20... | collective-permute-start | bytes 3244040 | tf_op jit(solution)/shard_map/ppermute | solution.py:1191
  153.7 33.0 %collective-permute-start.3 = (bf16[256,2048]{1,0:T(8,128)(2,1)}, bf16[256,2048]{1,0:T(8,128)(2,1)}, u32[]{:S(2)}, u32[]{:S(2)}) collective-permute-start(bf16[256,2048]{1,0:T(8,128)(2,1)} %add_convert_fusion.1), channel_id=1, source_target_pairs={{0,8},{8,0},{1,9},{9,1},{2,10},{10,2},{3,11},{11,3},{4,12},{12,4},... | collective-permute-start | bytes 3145736 | tf_op jit(solution)/shard_map/ppermute | solution.py:1191
  189.8 50.3 %collective-permute-start.9 = (bf16[256,2048]{1,0:T(8,128)(2,1)}, bf16[256,2048]{1,0:T(8,128)(2,1)}, u32[]{:S(2)}, u32[]{:S(2)}) collective-permute-start(bf16[256,2048]{1,0:T(8,128)(2,1)} %add_convert_fusion), channel_id=1, source_target_pairs={{0,8},{8,0},{1,9},{9,1},{2,10},{10,2},{3,11},{11,3},{4,12},{12,4},... | collective-permute-start | bytes 3145736 | tf_op jit(solution)/shard_map/ppermute | solution.py:1191
  191.3 28.5 %collective-permute-start.8 = (bf16[256,2048]{1,0:T(8,128)(2,1)}, bf16[256,2048]{1,0:T(8,128)(2,1)}, u32[]{:S(2)}, u32[]{:S(2)}) collective-permute-start(bf16[256,2048]{1,0:T(8,128)(2,1)} %flipped.2), channel_id=1, source_target_pairs={{0,1},{1,2},{2,3},{3,0},{4,5},{5,6},{6,7},{7,4},{8,9},{9,10},{10,1... | collective-permute-start | bytes 3145736 | tf_op jit(solution)/shard_map/ppermute | solution.py:1196
  251.3 36.8 %all-to-all-start.2 = ((bf16[2,128,8,512]{3,1,0,2:T(8,128)(2,1)}), bf16[2,128,8,512]{3,1,0,2:T(8,128)(2,1)}, u32[]{:S(2)}, u32[]{:S(2)}) async-start(bf16[2,128,8,512]{3,1,0,2:T(8,128)(2,1)} %copy.156), calls=%async_computation.2 | async-start | bytes 4194304 | tf_op jit(solution)/shard_map/all_to_all | solution.py:1342
  260.9 34.3 %collective-permute-start.13 = (bf16[256,2048]{1,0:T(8,128)(2,1)}, bf16[256,2048]{1,0:T(8,128)(2,1)}, u32[]{:S(2)}, u32[]{:S(2)}) collective-permute-start(bf16[256,2048]{1,0:T(8,128)(2,1)} %flipped.2), channel_id=1, source_target_pairs={{0,3},{1,0},{2,1},{3,2},{4,7},{5,4},{6,5},{7,6},{8,11},{9,8},{10,9... | collective-permute-start | bytes 3145736 | tf_op jit(solution)/shard_map/ppermute | solution.py:1196
  265.2 49.3 %collective-permute-start.14 = (bf16[256,2048]{1,0:T(8,128)(2,1)}, bf16[256,2048]{1,0:T(8,128)(2,1)}, u32[]{:S(2)}, u32[]{:S(2)}) collective-permute-start(bf16[256,2048]{1,0:T(8,128)(2,1)} %collective-permute-done.8), channel_id=1, source_target_pairs={{0,1},{1,2},{2,3},{3,0},{4,5},{5,6},{6,7},{7,4},{8,9},{9,10},{10,1... | collective-permute-start | bytes 3145736 | tf_op jit(solution)/shard_map/ppermute | solution.py:1196
  282.9 45.7 %collective-permute-start.12 = (bf16[256,2048]{1,0:T(8,128)(2,1)}, bf16[256,2048]{1,0:T(8,128)(2,1)}, u32[]{:S(2)}, u32[]{:S(2)}) collective-permute-start(bf16[256,2048]{1,0:T(8,128)(2,1)} %slice.1257), channel_id=1, source_target_pairs={{0,8},{8,0},{1,9},{9,1},{2,10},{10,2},{3,11},{11,3},{4,12},{12,4},... | collective-permute-start | bytes 3145736 | tf_op jit(solution)/shard_map/ppermute | solution.py:1191
  291.4 65.1 %collective-permute-start.16 = (bf16[256,2048]{1,0:T(8,128)(2,1)}, bf16[256,2048]{1,0:T(8,128)(2,1)}, u32[]{:S(2)}, u32[]{:S(2)}) collective-permute-start(bf16[256,2048]{1,0:T(8,128)(2,1)} %collective-permute-done.8), channel_id=1, source_target_pairs={{0,16},{16,0},{1,17},{17,1},{2,18},{18,2},{3,19},{19,3},{4,20},{20... | collective-permute-start | bytes 3145736 | tf_op jit(solution)/shard_map/ppermute | solution.py:1191
  314.5 41.9 %collective-permute-start.17 = (bf16[256,2048]{1,0:T(8,128)(2,1)}, bf16[256,2048]{1,0:T(8,128)(2,1)}, u32[]{:S(2)}, u32[]{:S(2)}) collective-permute-start(bf16[256,2048]{1,0:T(8,128)(2,1)} %collective-permute-done.14), channel_id=1, source_target_pairs={{0,16},{16,0},{1,17},{17,1},{2,18},{18,2},{3,19},{19,3},{4,20},{20... | collective-permute-start | bytes 3145736 | tf_op jit(solution)/shard_map/ppermute | solution.py:1191
  315.1 46.6 %collective-permute-start.18 = (bf16[256,2048]{1,0:T(8,128)(2,1)}, bf16[256,2048]{1,0:T(8,128)(2,1)}, u32[]{:S(2)}, u32[]{:S(2)}) collective-permute-start(bf16[256,2048]{1,0:T(8,128)(2,1)} %collective-permute-done.13), channel_id=1, source_target_pairs={{0,16},{16,0},{1,17},{17,1},{2,18},{18,2},{3,19},{19,3},{4,20},{20... | collective-permute-start | bytes 3145736 | tf_op jit(solution)/shard_map/ppermute | solution.py:1191
  332.8 35.8 %collective-permute-start.15 = (bf16[256,2048]{1,0:T(8,128)(2,1)S(1)}, bf16[256,2048]{1,0:T(8,128)(2,1)}, u32[]{:S(2)}, u32[]{:S(2)}) collective-permute-start(bf16[256,2048]{1,0:T(8,128)(2,1)S(1)} %fusion.26), channel_id=1, source_target_pairs={{0,8},{8,0},{1,9},{9,1},{2,10},{10,2},{3,11},{11,3},{4,12},{12,4},... | collective-permute-start | bytes 3145736 | tf_op jit(solution)/shard_map/ppermute | solution.py:1191
  375.0 48.1 %collective-permute-start.24 = (bf16[256,2048]{1,0:T(8,128)(2,1)}, bf16[256,2048]{1,0:T(8,128)(2,1)}, u32[]{:S(2)}, u32[]{:S(2)}) collective-permute-start(bf16[256,2048]{1,0:T(8,128)(2,1)} %slice.1256), channel_id=1, source_target_pairs={{0,8},{8,0},{1,9},{9,1},{2,10},{10,2},{3,11},{11,3},{4,12},{12,4},... | collective-permute-start | bytes 3145736 | tf_op jit(solution)/shard_map/ppermute | solution.py:1191
  398.4 82.3 %all-to-all-start.3 = ((bf16[32,72,512]{2,1,0:T(8,128)(2,1)}), bf16[32,72,512]{2,1,0:T(8,128)(2,1)}, u32[]{:S(2)}, u32[]{:S(2)}) async-start(bf16[32,72,512]{2,1,0:T(8,128)(2,1)} %bitcast.214), calls=%async_computation.3 | async-start | bytes 4718592 | tf_op jit(solution)/shard_map/all_to_all | solution.py:1346
  403.7 65.3 %collective-permute-start.23 = (bf16[256,2048]{1,0:T(8,128)(2,1)}, bf16[256,2048]{1,0:T(8,128)(2,1)}, u32[]{:S(2)}, u32[]{:S(2)}) collective-permute-start(bf16[256,2048]{1,0:T(8,128)(2,1)} %copy-done.80), channel_id=1, source_target_pairs={{0,1},{1,2},{2,3},{3,0},{4,5},{5,6},{6,7},{7,4},{8,9},{9,10},{10,1... | collective-permute-start | bytes 3145736 | tf_op jit(solution)/shard_map/ppermute | solution.py:1196
  426.6 42.5 %collective-permute-start.28 = (bf16[256,2048]{1,0:T(8,128)(2,1)S(1)}, bf16[256,2048]{1,0:T(8,128)(2,1)S(1)}, u32[]{:S(2)}, u32[]{:S(2)}) collective-permute-start(bf16[256,2048]{1,0:T(8,128)(2,1)S(1)} %fusion.21), channel_id=1, source_target_pairs={{0,8},{8,0},{1,9},{9,1},{2,10},{10,2},{3,11},{11,3},{4,12},{12,4},... | collective-permute-start | bytes 3145736 | tf_op jit(solution)/shard_map/ppermute | solution.py:1191
  470.6 41.1 %collective-permute-start.25 = (bf16[256,2048]{1,0:T(8,128)(2,1)}, bf16[256,2048]{1,0:T(8,128)(2,1)}, u32[]{:S(2)}, u32[]{:S(2)}) collective-permute-start(bf16[256,2048]{1,0:T(8,128)(2,1)} %copy-done.80), channel_id=1, source_target_pairs={{0,16},{16,0},{1,17},{17,1},{2,18},{18,2},{3,19},{19,3},{4,20},{20... | collective-permute-start | bytes 3145736 | tf_op jit(solution)/shard_map/ppermute | solution.py:1191
  474.7 45.8 %collective-permute-start.26 = (bf16[256,2048]{1,0:T(8,128)(2,1)}, bf16[256,2048]{1,0:T(8,128)(2,1)}, u32[]{:S(2)}, u32[]{:S(2)}) collective-permute-start(bf16[256,2048]{1,0:T(8,128)(2,1)} %collective-permute-done.23), channel_id=1, source_target_pairs={{0,16},{16,0},{1,17},{17,1},{2,18},{18,2},{3,19},{19,3},{4,20},{20... | collective-permute-start | bytes 3145736 | tf_op jit(solution)/shard_map/ppermute | solution.py:1191
  475.0 67.7 %collective-permute-start.27 = (bf16[256,2048]{1,0:T(8,128)(2,1)}, bf16[256,2048]{1,0:T(8,128)(2,1)}, u32[]{:S(2)}, u32[]{:S(2)}) collective-permute-start(bf16[256,2048]{1,0:T(8,128)(2,1)} %collective-permute-done.22), channel_id=1, source_target_pairs={{0,16},{16,0},{1,17},{17,1},{2,18},{18,2},{3,19},{19,3},{4,20},{20... | collective-permute-start | bytes 3145736 | tf_op jit(solution)/shard_map/ppermute | solution.py:1191
  487.5 75.2 %collective-permute-start.31 = (bf16[256,2048]{1,0:T(8,128)(2,1)S(1)}, bf16[256,2048]{1,0:T(8,128)(2,1)S(1)}, u32[]{:S(2)}, u32[]{:S(2)}) collective-permute-start(bf16[256,2048]{1,0:T(8,128)(2,1)S(1)} %get-tuple-element.434), channel_id=1, source_target_pairs={{0,8},{8,0},{1,9},{9,1},{2,10},{10,2},{3,11},{11,3},{4,12},{12,4},... | collective-permute-start | bytes 3145736 | tf_op jit(solution)/shard_map/ppermute | solution.py:1191
  491.2 88.0 %collective-permute-start.33 = (bf16[256,2048]{1,0:T(8,128)(2,1)S(1)}, bf16[256,2048]{1,0:T(8,128)(2,1)}, u32[]{:S(2)}, u32[]{:S(2)}) collective-permute-start(bf16[256,2048]{1,0:T(8,128)(2,1)S(1)} %get-tuple-element.433), channel_id=1, source_target_pairs={{0,8},{8,0},{1,9},{9,1},{2,10},{10,2},{3,11},{11,3},{4,12},{12,4},... | collective-permute-start | bytes 3145736 | tf_op jit(solution)/shard_map/ppermute | solution.py:1191
  581.1 29.0 %collective-permute-start.30 = (bf16[512,2048]{1,0:T(8,128)(2,1)}, bf16[512,2048]{1,0:T(8,128)(2,1)}, u32[]{:S(2)}, u32[]{:S(2)}) collective-permute-start(bf16[512,2048]{1,0:T(8,128)(2,1)} %get-tuple-element.269), channel_id=1, source_target_pairs={{0,4},{4,0},{1,5},{5,1},{2,6},{6,2},{3,7},{7,3},{8,12},{12,8},{9,1... | collective-permute-start | bytes 6291464 | tf_op jit(solution)/shard_map/ppermute | solution.py:1191
  609.6 40.8 %collective-permute-start.39 = (bf16[512,2048]{1,0:T(8,128)(2,1)}, bf16[512,2048]{1,0:T(8,128)(2,1)}, u32[]{:S(2)}, u32[]{:S(2)}) collective-permute-start(bf16[512,2048]{1,0:T(8,128)(2,1)} %get-tuple-element.273), channel_id=1, source_target_pairs={{0,4},{4,0},{1,5},{5,1},{2,6},{6,2},{3,7},{7,3},{8,12},{12,8},{9,1... | collective-permute-start | bytes 6291464 | tf_op jit(solution)/shard_map/ppermute | solution.py:1191
  648.8 44.9 %collective-permute-start.37 = (bf16[256,2048]{1,0:T(8,128)(2,1)}, bf16[256,2048]{1,0:T(8,128)(2,1)}, u32[]{:S(2)}, u32[]{:S(2)}) collective-permute-start(bf16[256,2048]{1,0:T(8,128)(2,1)} %slice.1254), channel_id=1, source_target_pairs={{0,8},{8,0},{1,9},{9,1},{2,10},{10,2},{3,11},{11,3},{4,12},{12,4},... | collective-permute-start | bytes 3145736 | tf_op jit(solution)/shard_map/ppermute | solution.py:1191
  676.8 70.0 %collective-permute-start.35 = (bf16[256,2048]{1,0:T(8,128)(2,1)}, bf16[256,2048]{1,0:T(8,128)(2,1)}, u32[]{:S(2)}, u32[]{:S(2)}) collective-permute-start(bf16[256,2048]{1,0:T(8,128)(2,1)} %slice.1255), channel_id=1, source_target_pairs={{0,8},{8,0},{1,9},{9,1},{2,10},{10,2},{3,11},{11,3},{4,12},{12,4},... | collective-permute-start | bytes 3145736 | tf_op jit(solution)/shard_map/ppermute | solution.py:1191
  693.3 53.6 %collective-permute-start.40 = (bf16[256,2048]{1,0:T(8,128)(2,1)}, bf16[256,2048]{1,0:T(8,128)(2,1)}, u32[]{:S(2)}, u32[]{:S(2)}) collective-permute-start(bf16[256,2048]{1,0:T(8,128)(2,1)} %slice.1253), channel_id=1, source_target_pairs={{0,8},{8,0},{1,9},{9,1},{2,10},{10,2},{3,11},{11,3},{4,12},{12,4},... | collective-permute-start | bytes 3145736 | tf_op jit(solution)/shard_map/ppermute | solution.py:1191
  710.7 61.1 %collective-permute-start.43 = (bf16[256,2048]{1,0:T(8,128)(2,1)}, bf16[256,2048]{1,0:T(8,128)(2,1)}, u32[]{:S(2)}, u32[]{:S(2)}) collective-permute-start(bf16[256,2048]{1,0:T(8,128)(2,1)} %convert_element_type.264), channel_id=1, source_target_pairs={{0,8},{8,0},{1,9},{9,1},{2,10},{10,2},{3,11},{11,3},{4,12},{12,4},... | collective-permute-start | bytes 3145736 | tf_op jit(solution)/shard_map/ppermute | solution.py:1191
  758.9 93.8 %all-to-all-start.4 = ((bf16[32,72,512]{2,1,0:T(8,128)(2,1)}), bf16[32,72,512]{2,1,0:T(8,128)(2,1)}, u32[]{:S(2)}, u32[]{:S(2)}) async-start(bf16[32,72,512]{2,1,0:T(8,128)(2,1)} %bitcast.212), calls=%async_computation.4 | async-start | bytes 4718592 | tf_op jit(solution)/shard_map/all_to_all | solution.py:1346
  774.0 116.2 %collective-permute-start.48 = (bf16[1024,2048]{1,0:T(8,128)(2,1)}, bf16[1024,2048]{1,0:T(8,128)(2,1)}, u32[]{:S(2)}, u32[]{:S(2)}) collective-permute-start(bf16[1024,2048]{1,0:T(8,128)(2,1)} %cross_sums.12), channel_id=1, source_target_pairs={{0,16},{16,0},{1,17},{17,1},{2,18},{18,2},{3,19},{19,3},{4,20},{20... | collective-permute-start | bytes 12582920 | tf_op jit(solution)/shard_map/ppermute | solution.py:1191
  775.7 45.5 %collective-permute-start.42 = (bf16[256,2048]{1,0:T(8,128)(2,1)}, bf16[256,2048]{1,0:T(8,128)(2,1)}, u32[]{:S(2)}, u32[]{:S(2)}) collective-permute-start(bf16[256,2048]{1,0:T(8,128)(2,1)} %convert_element_type.274), channel_id=1, source_target_pairs={{0,8},{8,0},{1,9},{9,1},{2,10},{10,2},{3,11},{11,3},{4,12},{12,4},... | collective-permute-start | bytes 3145736 | tf_op jit(solution)/shard_map/ppermute | solution.py:1191
  836.2 184.6 %collective-permute-start.52 = (bf16[1024,2048]{1,0:T(8,128)(2,1)}, bf16[1024,2048]{1,0:T(8,128)(2,1)}, u32[]{:S(2)}, u32[]{:S(2)}) collective-permute-start(bf16[1024,2048]{1,0:T(8,128)(2,1)} %cross_sums.14), channel_id=1, source_target_pairs={{0,16},{16,0},{1,17},{17,1},{2,18},{18,2},{3,19},{19,3},{4,20},{20... | collective-permute-start | bytes 12582920 | tf_op jit(solution)/shard_map/ppermute | solution.py:1191
  893.0 62.9 %collective-permute-start.49 = (bf16[256,2048]{1,0:T(8,128)(2,1)}, bf16[256,2048]{1,0:T(8,128)(2,1)}, u32[]{:S(2)}, u32[]{:S(2)}) collective-permute-start(bf16[256,2048]{1,0:T(8,128)(2,1)} %add_pieces.16), channel_id=1, source_target_pairs={{0,1},{1,2},{2,3},{3,0},{4,5},{5,6},{6,7},{7,4},{8,9},{9,10},{10,1... | collective-permute-start | bytes 3145736 | tf_op jit(solution)/shard_map/ppermute | solution.py:1196
  896.3 98.2 %collective-permute-start.47 = (bf16[256,2048]{1,0:T(8,128)(2,1)}, bf16[256,2048]{1,0:T(8,128)(2,1)}, u32[]{:S(2)}, u32[]{:S(2)}) collective-permute-start(bf16[256,2048]{1,0:T(8,128)(2,1)} %slice.1251), channel_id=1, source_target_pairs={{0,8},{8,0},{1,9},{9,1},{2,10},{10,2},{3,11},{11,3},{4,12},{12,4},... | collective-permute-start | bytes 3145736 | tf_op jit(solution)/shard_map/ppermute | solution.py:1191
  899.2 117.2 %collective-permute-start.54 = (bf16[256,2048]{1,0:T(8,128)(2,1)}, bf16[256,2048]{1,0:T(8,128)(2,1)}, u32[]{:S(2)}, u32[]{:S(2)}) collective-permute-start(bf16[256,2048]{1,0:T(8,128)(2,1)} %add_pieces.17), channel_id=1, source_target_pairs={{0,3},{1,0},{2,1},{3,2},{4,7},{5,4},{6,5},{7,6},{8,11},{9,8},{10,9... | collective-permute-start | bytes 3145736 | tf_op jit(solution)/shard_map/ppermute | solution.py:1196
  978.8 37.6 %collective-permute-start.53 = (bf16[256,2048]{1,0:T(8,128)(2,1)}, bf16[256,2048]{1,0:T(8,128)(2,1)}, u32[]{:S(2)}, u32[]{:S(2)}) collective-permute-start(bf16[256,2048]{1,0:T(8,128)(2,1)} %add_pieces.18), channel_id=1, source_target_pairs={{0,1},{1,2},{2,3},{3,0},{4,5},{5,6},{6,7},{7,4},{8,9},{9,10},{10,1... | collective-permute-start | bytes 3145736 | tf_op jit(solution)/shard_map/ppermute | solution.py:1196
  990.3 77.6 %collective-permute-start.55 = (bf16[512,2048]{1,0:T(8,128)(2,1)}, bf16[512,2048]{1,0:T(8,128)(2,1)S(1)}, u32[]{:S(2)}, u32[]{:S(2)}) collective-permute-start(bf16[512,2048]{1,0:T(8,128)(2,1)} %copy-done.97), channel_id=1, source_target_pairs={{0,16},{16,0},{1,17},{17,1},{2,18},{18,2},{3,19},{19,3},{4,20},{20... | collective-permute-start | bytes 6291464 | tf_op jit(solution)/shard_map/ppermute | solution.py:1191
  1034.4 35.7 %collective-permute-start.51 = (bf16[256,2048]{1,0:T(8,128)(2,1)}, bf16[256,2048]{1,0:T(8,128)(2,1)}, u32[]{:S(2)}, u32[]{:S(2)}) collective-permute-start(bf16[256,2048]{1,0:T(8,128)(2,1)} %slice.1250), channel_id=1, source_target_pairs={{0,8},{8,0},{1,9},{9,1},{2,10},{10,2},{3,11},{11,3},{4,12},{12,4},... | collective-permute-start | bytes 3145736 | tf_op jit(solution)/shard_map/ppermute | solution.py:1191
  1038.4 48.7 %collective-permute-start.61 = (bf16[256,2048]{1,0:T(8,128)(2,1)}, bf16[256,2048]{1,0:T(8,128)(2,1)}, u32[]{:S(2)}, u32[]{:S(2)}) collective-permute-start(bf16[256,2048]{1,0:T(8,128)(2,1)} %add_pieces.21), channel_id=1, source_target_pairs={{0,3},{1,0},{2,1},{3,2},{4,7},{5,4},{6,5},{7,6},{8,11},{9,8},{10,9... | collective-permute-start | bytes 3145736 | tf_op jit(solution)/shard_map/ppermute | solution.py:1196
  1040.5 84.2 %collective-permute-start.66 = (bf16[512,2048]{1,0:T(8,128)(2,1)}, bf16[512,2048]{1,0:T(8,128)(2,1)S(1)}, u32[]{:S(2)}, u32[]{:S(2)}) collective-permute-start(bf16[512,2048]{1,0:T(8,128)(2,1)} %copy-done.98), channel_id=1, source_target_pairs={{0,16},{16,0},{1,17},{17,1},{2,18},{18,2},{3,19},{19,3},{4,20},{20... | collective-permute-start | bytes 6291464 | tf_op jit(solution)/shard_map/ppermute | solution.py:1191
  1064.7 48.6 %collective-permute-start.58 = (bf16[256,2048]{1,0:T(8,128)(2,1)}, bf16[256,2048]{1,0:T(8,128)(2,1)}, u32[]{:S(2)}, u32[]{:S(2)}) collective-permute-start(bf16[256,2048]{1,0:T(8,128)(2,1)} %add_pieces.19), channel_id=1, source_target_pairs={{0,8},{8,0},{1,9},{9,1},{2,10},{10,2},{3,11},{11,3},{4,12},{12,4},... | collective-permute-start | bytes 3145736 | tf_op jit(solution)/shard_map/ppermute | solution.py:1191
  1068.0 45.3 %collective-permute-start.59 = (bf16[256,2048]{1,0:T(8,128)(2,1)}, bf16[256,2048]{1,0:T(8,128)(2,1)}, u32[]{:S(2)}, u32[]{:S(2)}) collective-permute-start(bf16[256,2048]{1,0:T(8,128)(2,1)} %add_pieces.19), channel_id=1, source_target_pairs={{0,16},{16,0},{1,17},{17,1},{2,18},{18,2},{3,19},{19,3},{4,20},{20... | collective-permute-start | bytes 3145736 | tf_op jit(solution)/shard_map/ppermute | solution.py:1191
  1070.0 39.6 %collective-permute-start.60 = (bf16[256,2048]{1,0:T(8,128)(2,1)}, bf16[256,2048]{1,0:T(8,128)(2,1)}, u32[]{:S(2)}, u32[]{:S(2)}) collective-permute-start(bf16[256,2048]{1,0:T(8,128)(2,1)} %add_pieces.22), channel_id=1, source_target_pairs={{0,1},{1,2},{2,3},{3,0},{4,5},{5,6},{6,7},{7,4},{8,9},{9,10},{10,1... | collective-permute-start | bytes 3145736 | tf_op jit(solution)/shard_map/ppermute | solution.py:1196
  1087.1 35.3 %collective-permute-start.57 = (bf16[128,2048]{1,0:T(8,128)(2,1)S(1)}, bf16[128,2048]{1,0:T(8,128)(2,1)}, u32[]{:S(2)}, u32[]{:S(2)}) collective-permute-start(bf16[128,2048]{1,0:T(8,128)(2,1)S(1)} %copy-done.85), channel_id=1, source_target_pairs={{0,1},{1,2},{2,3},{3,0},{4,5},{5,6},{6,7},{7,4},{8,9},{9,10},{10,1... | collective-permute-start | bytes 1572872 | tf_op jit(solution)/shard_map/ppermute | solution.py:1196
  1145.1 80.6 %all-to-all-start.6 = ((bf16[32,72,512]{2,1,0:T(8,128)(2,1)}), bf16[32,72,512]{2,1,0:T(8,128)(2,1)S(1)}, u32[]{:S(2)}, u32[]{:S(2)}) async-start(bf16[32,72,512]{2,1,0:T(8,128)(2,1)} %bitcast.211), calls=%async_computation.6 | async-start | bytes 4718592 | tf_op jit(solution)/shard_map/all_to_all | solution.py:1346
  1148.0 90.1 %collective-permute-start.70 = (bf16[256,2048]{1,0:T(8,128)(2,1)S(1)}, bf16[256,2048]{1,0:T(8,128)(2,1)}, u32[]{:S(2)}, u32[]{:S(2)}) collective-permute-start(bf16[256,2048]{1,0:T(8,128)(2,1)S(1)} %copy-done.75), channel_id=1, source_target_pairs={{0,8},{8,0},{1,9},{9,1},{2,10},{10,2},{3,11},{11,3},{4,12},{12,4},... | collective-permute-start | bytes 3145736 | tf_op jit(solution)/shard_map/ppermute | solution.py:1191
  1149.8 88.3 %collective-permute-start.71 = (bf16[256,2048]{1,0:T(8,128)(2,1)S(1)}, bf16[256,2048]{1,0:T(8,128)(2,1)}, u32[]{:S(2)}, u32[]{:S(2)}) collective-permute-start(bf16[256,2048]{1,0:T(8,128)(2,1)S(1)} %copy-done.75), channel_id=1, source_target_pairs={{0,16},{16,0},{1,17},{17,1},{2,18},{18,2},{3,19},{19,3},{4,20},{20... | collective-permute-start | bytes 3145736 | tf_op jit(solution)/shard_map/ppermute | solution.py:1191
  1151.2 47.7 %collective-permute-start.63 = (bf16[128,2048]{1,0:T(8,128)(2,1)}, bf16[128,2048]{1,0:T(8,128)(2,1)}, u32[]{:S(2)}, u32[]{:S(2)}) collective-permute-start(bf16[128,2048]{1,0:T(8,128)(2,1)} %add_pieces.24), channel_id=1, source_target_pairs={{0,3},{1,0},{2,1},{3,2},{4,7},{5,4},{6,5},{7,6},{8,11},{9,8},{10,9... | collective-permute-start | bytes 1572872 | tf_op jit(solution)/shard_map/ppermute | solution.py:1196
  1154.7 59.4 %collective-permute-start.62 = (bf16[128,2048]{1,0:T(8,128)(2,1)}, bf16[128,2048]{1,0:T(8,128)(2,1)}, u32[]{:S(2)}, u32[]{:S(2)}) collective-permute-start(bf16[128,2048]{1,0:T(8,128)(2,1)} %add_pieces.26), channel_id=1, source_target_pairs={{0,1},{1,2},{2,3},{3,0},{4,5},{5,6},{6,7},{7,4},{8,9},{9,10},{10,1... | collective-permute-start | bytes 1572872 | tf_op jit(solution)/shard_map/ppermute | solution.py:1196
  1154.7 81.1 %collective-permute-start.72 = (bf16[128,2048]{1,0:T(8,128)(2,1)}, bf16[128,2048]{1,0:T(8,128)(2,1)}, u32[]{:S(2)}, u32[]{:S(2)}) collective-permute-start(bf16[128,2048]{1,0:T(8,128)(2,1)} %add_pieces.27), channel_id=1, source_target_pairs={{0,1},{1,2},{2,3},{3,0},{4,5},{5,6},{6,7},{7,4},{8,9},{9,10},{10,1... | collective-permute-start | bytes 1572872 | tf_op jit(solution)/shard_map/ppermute | solution.py:1196
  1259.3 34.9 %collective-permute-start.78 = (bf16[128,2048]{1,0:T(8,128)(2,1)S(1)}, bf16[128,2048]{1,0:T(8,128)(2,1)S(1)}, u32[]{:S(2)}, u32[]{:S(2)}) collective-permute-start(bf16[128,2048]{1,0:T(8,128)(2,1)S(1)} %copy-done.84), channel_id=1, source_target_pairs={{0,3},{1,0},{2,1},{3,2},{4,7},{5,4},{6,5},{7,6},{8,11},{9,8},{10,9... | collective-permute-start | bytes 1572872 | tf_op jit(solution)/shard_map/ppermute | solution.py:1196
  1259.3 41.6 %collective-permute-start.77 = (bf16[128,2048]{1,0:T(8,128)(2,1)}, bf16[128,2048]{1,0:T(8,128)(2,1)S(1)}, u32[]{:S(2)}, u32[]{:S(2)}) collective-permute-start(bf16[128,2048]{1,0:T(8,128)(2,1)} %add_pieces.30), channel_id=1, source_target_pairs={{0,1},{1,2},{2,3},{3,0},{4,5},{5,6},{6,7},{7,4},{8,9},{9,10},{10,1... | collective-permute-start | bytes 1572872 | tf_op jit(solution)/shard_map/ppermute | solution.py:1196
  1304.3 48.9 %collective-permute-start.80 = (bf16[512,2048]{1,0:T(8,128)(2,1)S(1)}, bf16[512,2048]{1,0:T(8,128)(2,1)}, u32[]{:S(2)}, u32[]{:S(2)}) collective-permute-start(bf16[512,2048]{1,0:T(8,128)(2,1)S(1)} %constant_dynamic-update-slice_fusion.26.near_low.near_high), channel_id=1, source_target_pairs={{0,4},{4,0},{1,5},{5,1},{2,6},{6,2},{3,7},{7,3},{8,12},{12,8},{9,1... | collective-permute-start | bytes 6291464 | tf_op jit(solution)/shard_map/ppermute | solution.py:1191
  1307.9 57.4 %all-to-all-start.5 = ((bf16[2,1024,1,512]{3,0,2,1:T(2,128)(2,1)}), bf16[2,1024,1,512]{3,0,2,1:T(2,128)(2,1)}, u32[]{:S(2)}, u32[]{:S(2)}) async-start(bf16[2,1024,1,512]{3,0,2,1:T(2,128)(2,1)} %copy.161), calls=%async_computation.5 | async-start | bytes 4194304 | tf_op jit(solution)/shard_map/all_to_all | solution.py:1414
  1312.8 36.5 %collective-permute-start.81 = (bf16[128,2048]{1,0:T(8,128)(2,1)S(1)}, bf16[128,2048]{1,0:T(8,128)(2,1)S(1)}, u32[]{:S(2)}, u32[]{:S(2)}) collective-permute-start(bf16[128,2048]{1,0:T(8,128)(2,1)S(1)} %copy-done.79), channel_id=1, source_target_pairs={{0,8},{8,0},{1,9},{9,1},{2,10},{10,2},{3,11},{11,3},{4,12},{12,4},... | collective-permute-start | bytes 1572872 | tf_op jit(solution)/shard_map/ppermute | solution.py:1191
  1314.8 34.5 %collective-permute-start.82 = (bf16[128,2048]{1,0:T(8,128)(2,1)S(1)}, bf16[128,2048]{1,0:T(8,128)(2,1)S(1)}, u32[]{:S(2)}, u32[]{:S(2)}) collective-permute-start(bf16[128,2048]{1,0:T(8,128)(2,1)S(1)} %copy-done.79), channel_id=1, source_target_pairs={{0,16},{16,0},{1,17},{17,1},{2,18},{18,2},{3,19},{19,3},{4,20},{20... | collective-permute-start | bytes 1572872 | tf_op jit(solution)/shard_map/ppermute | solution.py:1191
  1361.8 61.0 %collective-permute-start.85 = (bf16[512,2048]{1,0:T(8,128)(2,1)}, bf16[512,2048]{1,0:T(8,128)(2,1)}, u32[]{:S(2)}, u32[]{:S(2)}) collective-permute-start(bf16[512,2048]{1,0:T(8,128)(2,1)} %constant_dynamic-update-slice_fusion.31.near_low.near_high), channel_id=1, source_target_pairs={{0,4},{4,0},{1,5},{5,1},{2,6},{6,2},{3,7},{7,3},{8,12},{12,8},{9,1... | collective-permute-start | bytes 6291464 | tf_op jit(solution)/shard_map/ppermute | solution.py:1191
  1365.3 55.0 %all-to-all-start.7 = ((bf16[2,1024,1,512]{3,0,2,1:T(2,128)(2,1)}), bf16[2,1024,1,512]{3,0,2,1:T(2,128)(2,1)S(1)}, u32[]{:S(2)}, u32[]{:S(2)}) async-start(bf16[2,1024,1,512]{3,0,2,1:T(2,128)(2,1)} %copy.165), calls=%async_computation.7 | async-start | bytes 4194304 | tf_op jit(solution)/shard_map/all_to_all | solution.py:1414
  (152 other events, 1965.0 us)

commit v3 on v2

--- a/solution.py
+++ b/solution.py
@@ -1160,6 +1160,214 @@
     )(query, key, value, weight)
 
 
+def rows_call(kernel, name, grid_rows, ins, outs, sums=0):
+    tall = 128
+    cols = 2048
+    steps = grid_rows // tall
+
+    def spec(array, first):
+        if first is None:
+            return pl.BlockSpec(array.shape, lambda i: (0, 0))
+        return pl.BlockSpec((tall, cols), lambda i: (first * steps + i, 0))
+
+    out_specs = [pl.BlockSpec((tall, cols), lambda i: (i, 0)) for _ in outs]
+    out_shape = [jax.ShapeDtypeStruct((grid_rows, cols), kind) for kind in outs]
+    if sums:
+        out_specs.append(pl.BlockSpec((8, cols), lambda i: (0, 0)))
+        out_shape.append(jax.ShapeDtypeStruct((8, cols), jnp.float32))
+    return pl.pallas_call(
+        kernel,
+        grid=(steps,),
+        in_specs=[spec(array, first) for array, first in ins],
+        out_specs=out_specs,
+        out_shape=out_shape,
+        compiler_params=settings(),
+        cost_estimate=light(),
+        name=name,
+    )(*[array for array, _ in ins])
+
+
+def wide(ref):
+    return ref[...].astype(jnp.float32)
+
+
+def norm_in_kernel(rows_ref, gain_ref, shift_ref, out_ref):
+    normed, _ = normalize(wide(rows_ref))
+    out_ref[...] = (normed * gain_ref[...] + shift_ref[...]).astype(out_ref.dtype)
+
+
+def norm_in(tok, m, gain, shift_by):
+    return rows_call(
+        norm_in_kernel, "norm_in", tok.shape[0] // 2, [(tok, m), (gain, None), (shift_by, None)], [jnp.bfloat16]
+    )[0]
+
+
+def resid_kernel(rows_ref, kept_ref, got_ref, bias_ref, gain_ref, shift_ref, resid_ref, out_ref):
+    resid = wide(rows_ref) + kept_ref[...] + wide(got_ref) + bias_ref[...]
+    resid_ref[...] = resid
+    normed, _ = normalize(resid.astype(jnp.bfloat16).astype(jnp.float32))
+    out_ref[...] = (normed * gain_ref[...] + shift_ref[...]).astype(out_ref.dtype)
+
+
+def resid_norm(tok, m, kept, got, bias, gain, shift_by):
+    ins = [(tok, m), (kept, 0), (got, 0), (bias, None), (gain, None), (shift_by, None)]
+    return rows_call(resid_kernel, "resid_norm", kept.shape[0], ins, [jnp.float32, jnp.bfloat16])
+
+
+def layer_kernel(resid_ref, kept_ref, got_ref, bias_ref, out_ref):
+    out_ref[...] = (resid_ref[...] + kept_ref[...] + wide(got_ref) + bias_ref[...]).astype(out_ref.dtype)
+
+
+def layer_rows_of(resid, kept, got, bias):
+    ins = [(resid, 0), (kept, 0), (got, 0), (bias, None)]
+    return rows_call(layer_kernel, "layer_rows", kept.shape[0], ins, [jnp.bfloat16])[0]
+
+
+def add_sums(sums_ref, parts):
+    @pl.when(pl.program_id(0) == 0)
+    def _():
+        sums_ref[...] = jnp.zeros_like(sums_ref)
+
+    for index, part in enumerate(parts):
+        sums_ref[index : index + 1, :] += jnp.sum(part, axis=0, keepdims=True)
+
+
+def norm_back_rows(grad, normed, inverse, gain):
+    scaled = grad * gain
+    first_mean = jnp.mean(scaled, axis=1, keepdims=True)
+    second_mean = jnp.mean(scaled * normed, axis=1, keepdims=True)
+    return inverse * (scaled - first_mean - normed * second_mean)
+
+
+def second_back_kernel(kept_ref, got_ref, resid_ref, cot_ref, gain_ref, grad_ref, low_ref, sums_ref):
+    grad = (kept_ref[...] + wide(got_ref)).astype(jnp.bfloat16).astype(jnp.float32)
+    normed, inverse = normalize(resid_ref[...].astype(jnp.bfloat16).astype(jnp.float32))
+    cot = wide(cot_ref)
+    total = cot + norm_back_rows(grad, normed, inverse, gain_ref[...])
+    grad_ref[...] = total
+    low_ref[...] = total.astype(low_ref.dtype)
+    add_sums(sums_ref, (total, cot, grad * normed, grad))
+
+
+def second_back_rows(kept, got, resid, cot, m, gain):
+    ins = [(kept, 0), (got, 0), (resid, 0), (cot, m), (gain, None)]
+    return rows_call(second_back_kernel, "second_back", kept.shape[0], ins, [jnp.float32, jnp.bfloat16], sums=4)
+
+
+def first_back_kernel(kept_ref, got_ref, rows_ref, resid_grad_ref, gain_ref, out_ref, sums_ref):
+    grad = (kept_ref[...] + wide(got_ref)).astype(jnp.bfloat16).astype(jnp.float32)
+    normed, inverse = normalize(wide(rows_ref))
+    back = norm_back_rows(grad, normed, inverse, gain_ref[...])
+    out_ref[...] = (resid_grad_ref[...] + back).astype(out_ref.dtype)
+    add_sums(sums_ref, (grad * normed, grad))
+
+
+def first_back_rows(kept, got, tok, m, resid_grad, gain):
+    ins = [(kept, 0), (got, 0), (tok, m), (resid_grad, 0), (gain, None)]
+    return rows_call(first_back_kernel, "first_back", kept.shape[0], ins, [jnp.bfloat16], sums=2)
+
+
+def middle_kernel(near_top, near_low, got_top, got_low, kept_ref, moving_ref):
+    kept_ref[...] = near_top[...] + wide(got_top)
+    moving_ref[...] = (near_low[...] + wide(got_low)).astype(moving_ref.dtype)
+
+
+def middle_rows(near, got):
+    ins = [(near, 0), (near, 1), (got, 0), (got, 1)]
+    return rows_call(middle_kernel, "middle_rows", near.shape[0] // 2, ins, [jnp.float32, jnp.bfloat16])
+
+
+def join_kernel(count, *refs):
+    sources, out_ref = refs[:count], refs[count]
+    offset = 0
+    for source in sources:
+        rows = source.shape[0]
+        out_ref[pl.ds(offset, rows), :] = source[...]
+        offset += rows
+
+
+def join_rows(arrays):
+    count = len(arrays)
+    rows = sum(array.shape[0] for array in arrays)
+    cols = arrays[0].shape[1]
+    chunk = cols // 4
+    return pl.pallas_call(
+        functools.partial(join_kernel, count),
+        grid=(4,),
+        in_specs=[pl.BlockSpec((array.shape[0], chunk), lambda i: (0, i)) for array in arrays],
+        out_specs=pl.BlockSpec((rows, chunk), lambda i: (0, i)),
+        out_shape=jax.ShapeDtypeStruct((rows, cols), arrays[0].dtype),
+        compiler_params=settings(),
+        cost_estimate=light(),
+        name="join_rows",
+    )(*arrays)
+
+
+def attn_join_kernel(count, *refs):
+    sources, qkv_ref, out_w_ref, bias_ref = refs[:count], *refs[count:]
+    rows = HEAD_DIM
+    for index, source in enumerate(sources):
+        for k in range(3):
+            qkv_ref[pl.ds((k * count + index) * rows, rows), :] = source[pl.ds(k * rows, rows), :]
+        out_w_ref[pl.ds(index * rows, rows), :] = source[pl.ds(3 * rows, rows), :]
+        bias_ref[pl.ds(index * 8, 8), :] = source[pl.ds(4 * rows, 8), :]
+
+
+def attn_join(arrays):
+    count = len(arrays)
+    cols = arrays[0].shape[1]
+    kind = arrays[0].dtype
+    chunk = cols // 4
+    sizes = (3 * count * HEAD_DIM, count * HEAD_DIM, count * 8)
+    return pl.pallas_call(
+        functools.partial(attn_join_kernel, count),
+        grid=(4,),
+        in_specs=[pl.BlockSpec((array.shape[0], chunk), lambda i: (0, i)) for array in arrays],
+        out_specs=[pl.BlockSpec((size, chunk), lambda i: (0, i)) for size in sizes],
+        out_shape=[jax.ShapeDtypeStruct((size, cols), kind) for size in sizes],
+        compiler_params=settings(),
+        cost_estimate=light(),
+        name="attn_join",
+    )(*arrays)
+
+
+def cross_pair_kernel(rights, *refs):
+    out_ref = refs[-1]
+    lefts, right_refs = refs[:4], refs[4:-1]
+    for which in range(2):
+        right = right_refs[:4] if rights == 1 or which == 0 else right_refs[4:]
+        near_a, far_a, near_b, far_b = right
+        left_a, left_b = lefts[2 * which], lefts[2 * which + 1]
+        rows = near_a.shape[0]
+        top, low = pl.ds(0, rows), pl.ds(rows, rows)
+        total = tn_dot(left_a[top, :], near_a[...]) + tn_dot(left_a[low, :], far_a[...])
+        total = total + tn_dot(left_b[top, :], near_b[...]) + tn_dot(left_b[low, :], far_b[...])
+        total = total.astype(out_ref.dtype)
+        for piece in range(total.shape[0] // HEAD_DIM):
+            at = pl.ds((2 * piece + which) * HEAD_DIM, HEAD_DIM)
+            out_ref[at, :] = total[piece * HEAD_DIM : (piece + 1) * HEAD_DIM, :]
+
+
+def cross_pair(first, second, rights, half):
+    rows = first[0].shape[0]
+    cols = rights[0][0].shape[1]
+    tall = first[0].shape[1] // 2
+    wide_cols = 1024
+    left_spec = pl.BlockSpec((rows, tall), lambda i: (0, half))
+    right_spec = pl.BlockSpec((rows // 2, wide_cols), lambda i: (0, i))
+    flat = [array for right in rights for array in right]
+    return pl.pallas_call(
+        functools.partial(cross_pair_kernel, len(rights)),
+        grid=(cols // wide_cols,),
+        in_specs=[left_spec] * 4 + [right_spec] * len(flat),
+        out_specs=pl.BlockSpec((2 * tall, wide_cols), lambda i: (0, i)),
+        out_shape=jax.ShapeDtypeStruct((2 * tall, cols), jnp.bfloat16),
+        compiler_params=settings(),
+        cost_estimate=light(),
+        name="cross_pair",
+    )(*first, *second, *flat)
+
+
 SWAP = [(0, 1), (1, 0)]
 PLANE = ("y", "x", "core")
 EVERY = ("z", "y", "x", "core")
@@ -1213,17 +1421,8 @@
 
 def plane_end(started, order):
     piece, by_x, by_y, corner_top, corner_low = started
-    near = order.mark(joined([piece, by_x, by_y, *order.take((corner_top, corner_low))]))
+    near = order.mark(join_rows([piece, by_x, by_y, *order.take((corner_top, corner_low))]))
     return (near, swap_along(near, "core"))
-
-
-def total_all(vector):
-    for axis in ("core", "x", "y"):
-        vector = vector + swap_along(vector, axis)
-    size = lax.axis_size("z")
-    for step in (1, 2):
-        vector = vector + lax.ppermute(vector, "z", [(i, i ^ step) for i in range(size)])
-    return vector
 
 
 def held_before(bound, residue, parts):
@@ -1352,7 +1551,7 @@
         return settle_rows(own_row, got.reshape(depth, parts * SLOTS, col_width), MICRO * own_rows)
 
     gain_one, shift_one, gain_two, shift_two, out_b, down_b = (
-        array.astype(jnp.float32)
+        array.astype(jnp.float32)[None, :]
         for array in (attn_gain, attn_shift, mlp_gain, mlp_shift, out_bias, down_bias)
     )
 
@@ -1381,7 +1580,7 @@
 
     def team_middle(started):
         own, by_x = started
-        near = order.mark(joined([own, order.take(by_x)]))
+        near = order.mark(join_rows([own, order.take(by_x)]))
         return (near, swap_along(near, "core"))
 
     def team_end(started):
@@ -1393,15 +1592,13 @@
         return (near, swap_along(far, "core"))
 
     def sum_middle(started):
-        kept, got = started
-        quarter = kept.shape[0] // 2
-        kept = kept + order.take(got).astype(jnp.float32)
-        moving = order.mark(kept[quarter:].astype(jnp.bfloat16))
-        return (kept[:quarter], swap_along(moving, "x"))
+        near, got = started
+        kept, moving = order.mark(middle_rows(near, order.take(got)))
+        return (kept, swap_along(moving, "x"))
 
     def sum_end(started):
         kept, got = started
-        return kept + order.take(got).astype(jnp.float32)
+        return (kept, order.take(got))
 
     def unsettle(array):
         return unsettle_rows(own_row, array, depth).reshape(-1, col_width)
@@ -1415,97 +1612,89 @@
         return back.reshape(MICRO, tok_rows, col_width)
 
     order.mark(attn_mine)
-    attn_1, attn_3 = up_down(attn_mine)
+    attn_1 = shift(attn_mine, 1)
     tok_spread = spread_out(tokens)
+    attn_1 = order.step(attn_1)
+    attn_2 = shift(attn_1, 1)
+    attn_y1 = swap_along(attn_1, "y")
+    tok_spread = order.step(tok_spread)
+    attn_2 = order.step(attn_2)
+    attn_3 = shift(order.take(attn_mine), -1)
+    attn_y2 = swap_along(attn_2, "y")
     tok_sent = order.mark(boxes(order.take(tok_spread)))
     tok_got = box_exchange(tok_sent)
-    attn_1, attn_2, attn_y1 = onward(attn_1)
     attn_3, attn_y3 = swapped(attn_3)
-    attn_2, attn_y2 = swapped(attn_2)
     tok = order.mark(settle(order.take(tok_got)))
     up_1, up_3 = up_down(up_mine)
     cot_spread = spread_out(after(cotangent, tok))
 
-    def normed_rows(rows, gain, shift_by):
-        normed, inverse = normalize(rows)
-        return (normed, inverse, order.mark((normed * gain + shift_by).astype(jnp.bfloat16)))
-
-    rows_a = tok[:own_rows].astype(jnp.float32)
-    rows_b = tok[own_rows:].astype(jnp.float32)
-    normed_one_a, inverse_one_a, first_a = normed_rows(order.take(rows_a), gain_one, shift_one)
-    first_a = team_start(first_a)
-    normed_one_b, inverse_one_b, first_b = normed_rows(order.take(rows_b), gain_one, shift_one)
-    first_b = team_start(first_b)
+    first_a = team_start(order.mark(norm_in(tok, 0, gain_one, shift_one)))
+    first_b = team_start(order.mark(norm_in(order.take(tok), 1, gain_one, shift_one)))
     attn_all = [attn_mine, attn_1, attn_2, attn_3, attn_other, *order.take((attn_y1, attn_y2, attn_y3))]
-    qkv_w = joined([piece[k * head_rows : (k + 1) * head_rows] for k in range(3) for piece in attn_all])
-    out_w = joined([piece[3 * head_rows : 4 * head_rows] for piece in attn_all])
-    order.mark((qkv_w, out_w))
-    bias_all = [piece[4 * head_rows].astype(jnp.float32) for piece in attn_all]
-    query_b = joined([bias[:head_rows] for bias in bias_all])
-    value_b = joined([bias[head_rows : 2 * head_rows] for bias in bias_all])
-    up_b = joined([bias[2 * head_rows : 2 * head_rows + half_units] for bias in bias_all])[None, :]
-    qkv_b = joined([query_b, jnp.zeros_like(query_b), value_b])[None, :]
+    qkv_w, out_w, bias_w = order.mark(attn_join(attn_all))
+    bias_w = bias_w.reshape(2 * depth, 8, width)[:, 0, :].astype(jnp.float32)
+    query_b = bias_w[:, :head_rows].reshape(1, -1)
+    value_b = bias_w[:, head_rows : 2 * head_rows].reshape(1, -1)
+    up_b = bias_w[:, 2 * head_rows : 2 * head_rows + half_units].reshape(1, -1)
+    qkv_b = jnp.concatenate([query_b, jnp.zeros_like(query_b), value_b], axis=1)
     no_b = jnp.zeros((1, out_w.shape[0]), jnp.float32)
 
-    first_a = team_end(team_middle(first_a))
+    first_a = team_middle(first_a)
+    cot_sent = order.mark(boxes(order.take(cot_spread)))
+    first_a = team_end(first_a)
+    up_1, up_2, up_y1 = onward(up_1)
+    up_3, up_y3 = swapped(up_3)
     qkv_a = order.mark(project(*order.take(first_a), qkv_w, qkv_b))
-    up_1, up_2, up_y1 = onward(up_1)
     mixed_a = order.mark(attend(order.take(qkv_a), rank, *infos[0]))
+    up_y1 = order.step(up_y1)
+    up_2, up_y2 = swapped(up_2)
+    down_1, down_3 = up_down(down_mine)
     first_b = team_middle(first_b)
     sum_a1 = sum_start(mixed_a, out_w)
     first_b = team_end(first_b)
     qkv_b_ = order.mark(project(*order.take(first_b), qkv_w, qkv_b))
+    up_y3 = order.step(up_y3)
     sum_a1 = sum_middle(sum_a1)
-    up_3, up_y3 = swapped(up_3)
-    down_1, down_3 = up_down(down_mine)
     mixed_b = order.mark(attend(order.take(qkv_b_), rank, *infos[1]))
-    up_2, up_y2 = swapped(up_2)
-    sum_b1 = sum_start(mixed_b, out_w)
-    resid_a = rows_a + sum_end(sum_a1) + out_b
-    normed_two_a, inverse_two_a, second_a = normed_rows(
-        resid_a.astype(jnp.bfloat16).astype(jnp.float32), gain_two, shift_two
-    )
+    up_y2 = order.step(up_y2)
+    down_1, down_2, down_y1 = onward(down_1)
+    resid_a, second_a = order.mark(resid_norm(tok, 0, *sum_end(sum_a1), out_b, gain_two, shift_two))
     second_a = team_start(second_a)
-    sum_b1 = sum_middle(sum_b1)
-    cot_sent = order.mark(boxes(order.take(cot_spread)))
-    down_1, down_2, down_y1 = onward(down_1)
-    up_w = order.mark(joined([up_mine, up_1, up_2, up_3, up_other, *order.take((up_y1, up_y2, up_y3))]))
-    second_a = team_end(team_middle(second_a))
     down_3, down_y3 = swapped(down_3)
     cot_got = box_exchange(order.take(cot_sent))
+    sum_b1 = sum_start(mixed_b, out_w)
+    up_w = order.mark(join_rows([up_mine, up_1, up_2, up_3, up_other, *order.take((up_y1, up_y2, up_y3))]))
+    sum_b1 = sum_middle(sum_b1)
+    down_y1 = order.step(down_y1)
+    second_a = team_end(team_middle(second_a))
 
     hidden_a, slope_a = order.mark(expand(*order.take(second_a), up_w, up_b))
-    resid_b = rows_b + sum_end(sum_b1) + out_b
-    normed_two_b, inverse_two_b, second_b = normed_rows(
-        resid_b.astype(jnp.bfloat16).astype(jnp.float32), gain_two, shift_two
-    )
+    down_2, down_y2 = swapped(down_2)
+    down_y3 = order.step(down_y3)
+    resid_b, second_b = order.mark(resid_norm(tok, 1, *sum_end(sum_b1), out_b, gain_two, shift_two))
     second_b = team_start(second_b)
-    down_2, down_y2 = swapped(down_2)
-    second_b = team_middle(second_b)
     cot = order.mark(settle(order.take(cot_got)))
     cot_own = cot.reshape(MICRO, own_rows, width)
+    second_b = team_middle(second_b)
+    cot_parts = [team_start(cot_own[m]) for m in range(MICRO)]
     second_b = team_end(second_b)
-    cot_parts = [team_start(cot_own[m]) for m in range(MICRO)]
     hidden_b, slope_b = order.mark(expand(*order.take(second_b), up_w, up_b))
     down_w = order.mark(
-        joined([down_mine, down_1, down_2, down_3, down_other, *order.take((down_y1, down_y2, down_y3))])
+        join_rows([down_mine, down_1, down_2, down_3, down_other, *order.take((down_y1, down_y2, down_y3))])
     )
     sum_a4 = sum_start(hidden_a, down_w)
     cot_parts[0] = team_middle(cot_parts[0])
     sum_b4 = sum_start(hidden_b, down_w)
+    cot_a = team_end(cot_parts[0])
+
+    low_a, up_sum_a = order.mark(expand_back(*order.take(cot_a), down_w, slope_a))
     cot_parts[1] = team_middle(cot_parts[1])
-    cot_a = team_end(cot_parts[0])
-    cot_own_a, cot_own_b = cot_own[0].astype(jnp.float32), cot_own[1].astype(jnp.float32)
-
-    low_a, up_sum_a = order.mark(expand_back(*order.take(cot_a), down_w, slope_a))
+    sum_a2 = sum_start(low_a, up_w)
     cot_b = team_end(cot_parts[1])
-    sum_a2 = sum_start(low_a, up_w)
-    sum_a4 = sum_middle(sum_a4)
     low_b, up_sum_b = order.mark(expand_back(*order.take(cot_b), down_w, slope_b))
     up_sum_a, up_sum_b = up_sum_a[0], up_sum_b[0]
     sum_a2 = sum_middle(sum_a2)
     sum_b2 = sum_start(low_b, up_w)
-    sum_b4 = sum_middle(sum_b4)
 
     def cross_half(left_a, right_a, left_b, right_b, half):
         size = left_a.shape[1] // 2
@@ -1515,29 +1704,37 @@
     down_swap = swap_along(down_far, "y")
     sum_b2 = sum_middle(sum_b2)
 
-    def second_back(started, normed_two, inverse_two, cot_rows):
-        grad = sum_end(started).astype(jnp.bfloat16).astype(jnp.float32)
-        back, gain_part, shift_part = norm_backward(grad, normed_two, inverse_two, gain_two)
-        resid_grad = cot_rows + back
-        low = order.mark(resid_grad.astype(jnp.bfloat16))
-        return (resid_grad, low, gain_part, shift_part)
-
-    resid_grad_a, attn_low_a, gain_two_a, shift_two_a = second_back(
-        sum_a2, normed_two_a, inverse_two_a, cot_own_a
-    )
+    def second_back(started, resid, m):
+        return order.mark(second_back_rows(*sum_end(started), resid, cot, m, gain_two))
+
+    resid_grad_a, attn_low_a, norm_sums_a = second_back(sum_a2, resid_a, 0)
     attn_low_a = team_start(attn_low_a)
     down_near = cross_half(hidden_a, cot_a, hidden_b, cot_b, 0)
-    layer_a = (resid_a + sum_end(sum_a4) + down_b).astype(jnp.bfloat16)
-    layer_b = (resid_b + sum_end(sum_b4) + down_b).astype(jnp.bfloat16)
-    layer_sent = order.mark(unsettle(order.take(joined([layer_a, layer_b]))))
-    layer_got = box_exchange(layer_sent)
+    resid_grad_b, attn_low_b, norm_sums_b = second_back(sum_b2, resid_b, 1)
+    attn_low_b = team_start(attn_low_b)
+    sum_a4 = sum_middle(sum_a4)
     up_far = cross_half(low_a, second_a, low_b, second_b, 1)
-    up_swap = swap_along(up_far, "y")
-    resid_grad_b, attn_low_b, gain_two_b, shift_two_b = second_back(
-        sum_b2, normed_two_b, inverse_two_b, cot_own_b
-    )
-    attn_low_b = team_start(attn_low_b)
-    attn_low_a = team_end(team_middle(attn_low_a))
+    attn_low_a = team_middle(attn_low_a)
+    sum_b4 = sum_middle(sum_b4)
+    attn_low_a = team_end(attn_low_a)
+
+    def ring_start(near, got):
+        got = order.take(got)
+        far_2 = order.mark(add_rows(near, got, 2))
+        move = shift(far_2, 1)
+        far_1 = order.mark(add_rows(near, order.take(got), 1))
+        back = shift(far_1, -1)
+        return (near, got, move, back)
+
+    def ring_middle(started):
+        near, got, move, back = started
+        far_3 = order.mark(add_three(near, got, order.take(move), 3))
+        return (near, got, shift(far_3, 1), back)
+
+    def ring_end(started):
+        near, got, move, back = started
+        move, back = order.take((move, back))
+        return order.mark(add_four(near, got, move, back, 0))
 
     def attn_back(attn_low, qkv, m):
         mixed_grad = order.mark(project(*order.take(attn_low), out_w, no_b))
@@ -1549,11 +1746,41 @@
 
     *lows_a, sums_a = attn_back(attn_low_a, qkv_a, 0)
     attn_low_b = team_middle(attn_low_b)
+    down_ring = ring_start(down_near, down_swap)
+    up_swap = swap_along(order.take(up_far), "y")
     sum_a3 = sum_start_three(lows_a, qkv_w)
     attn_low_b = team_end(attn_low_b)
     up_near = cross_half(low_a, second_a, low_b, second_b, 0)
-    layer_held = order.mark(unbox(order.take(layer_got)))
-    layer_out = spread_back(layer_held)
+    sum_a3 = sum_middle(sum_a3)
+    layer_a = order.mark(layer_rows_of(resid_a, *sum_end(sum_a4), down_b))
+    layer_b = order.mark(layer_rows_of(resid_b, *sum_end(sum_b4), down_b))
+    layer_sent = order.mark(unsettle(join_rows([layer_a, layer_b])))
+    down_ring = ring_middle(down_ring)
+    layer_got = box_exchange(order.take(layer_sent))
+
+    def pack_small():
+        slots = jnp.arange(8 * depth, dtype=jnp.int32)
+        index = jnp.arange(2 * depth, dtype=jnp.int32)
+        owner = lax.rem(z - index % depth + depth, depth)
+        flip = jnp.where(index < depth, y, 1 - y)
+        hot = (slots[:, None] == (owner * 8 + 2 * team + flip)[None, :]).astype(jnp.float32)
+
+        def place(vector):
+            local = vector.reshape(2 * depth, -1)
+            return jnp.dot(hot, local, precision=lax.Precision.HIGHEST).reshape(-1)
+
+        head_sums = sums_a + sums_b
+        norm_sums = norm_sums_a + norm_sums_b
+        back_sums = back_sums_a + back_sums_b
+        return jnp.concatenate(
+            [
+                place(head_sums[0]),
+                place(head_sums[1]),
+                place(up_sum_a + up_sum_b),
+                norm_sums[:4].reshape(-1),
+                back_sums[:2].reshape(-1),
+            ]
+        ).reshape(-1, 128)
 
     def ring_start(near, got):
         piece = near.shape[0] // depth
@@ -1574,109 +1801,86 @@
         move, back = order.take((move, back))
         return order.mark(add_four(near, got, move, back, 0))
 
-    sum_a3 = sum_middle(sum_a3)
-    down_ring = ring_start(down_near, down_swap)
     *lows_b, sums_b = attn_back(attn_low_b, qkv_b_, 1)
-    down_ring = ring_middle(down_ring)
+    def first_back(started, resid_grad, m):
+        return order.mark(first_back_rows(*sum_end(started), tok, m, resid_grad, gain_one))
+
+    firsts = (*first_a, *first_b)
+
+    def one_half(half):
+        lefts = order.take((lows_a[0], lows_b[0]))
+        return order.mark(cross_pair(lefts, (lows_a[1], lows_b[1]), (firsts,), half))
+
+    def two_half(half):
+        lefts = order.take((lows_a[2], lows_b[2]))
+        rights = (firsts, (*attn_low_a, *attn_low_b))
+        return order.mark(cross_pair(lefts, (mixed_a, mixed_b), rights, half))
+
+    input_a, back_sums_a = first_back(sum_a3, resid_grad_a, 0)
+    up_ring = ring_start(up_near, up_swap)
     sum_b3 = sum_start_three(lows_b, qkv_w)
-
-    def first_back(started, normed_one, inverse_one, resid_grad):
-        grad = sum_end(started).astype(jnp.bfloat16).astype(jnp.float32)
-        back, gain_part, shift_part = norm_backward(grad, normed_one, inverse_one, gain_one)
-        return (order.mark((resid_grad + back).astype(jnp.bfloat16)), gain_part, shift_part)
-
-    def by_piece(arrays):
-        rows = head_rows
-        return order.mark(joined([a[k * rows : (k + 1) * rows] for k in range(depth) for a in arrays]))
-
-    def cross_heads(index, half):
-        left_a, right_a, left_b, right_b = (
-            (lows_a[index], first_a, lows_b[index], first_b)
-            if index < 3
-            else (mixed_a, attn_low_a, mixed_b, attn_low_b)
-        )
-        return cross_half(left_a, right_a, left_b, right_b, half)
-
-    one_far = by_piece([cross_heads(0, 1), cross_heads(1, 1)])
+    one_far = one_half(1)
     one_swap = swap_along(one_far, "y")
     sum_b3 = sum_middle(sum_b3)
-    input_a, gain_one_a, shift_one_a = first_back(sum_a3, normed_one_a, inverse_one_a, resid_grad_a)
-    two_far = by_piece([cross_heads(2, 1), cross_heads(3, 1)])
+    two_far = two_half(1)
     two_swap = swap_along(two_far, "y")
     down_total = ring_end(down_ring)
-    up_ring = ring_start(up_near, up_swap)
-    one_near = by_piece([cross_heads(0, 0), cross_heads(1, 0)])
-    input_b, gain_one_b, shift_one_b = first_back(sum_b3, normed_one_b, inverse_one_b, resid_grad_b)
-    input_sent = order.mark(unsettle(order.take(joined([input_a, input_b]))))
-    input_got = box_exchange(input_sent)
-    two_near = by_piece([cross_heads(2, 0), cross_heads(3, 0)])
+    down_plane = plane_start(down_total)
+    layer_held = order.mark(unbox(order.take(layer_got)))
+    layer_out = spread_back(layer_held)
+    one_near = one_half(0)
     up_ring = ring_middle(up_ring)
+    input_b, back_sums_b = first_back(sum_b3, resid_grad_b, 1)
+    input_sent = order.mark(unsettle(join_rows([input_a, input_b])))
     one_ring = ring_start(one_near, one_swap)
-    down_plane = plane_start(down_total)
+    layer_out = order.step(layer_out)
+    input_got = box_exchange(order.take(input_sent))
+    two_near = two_half(0)
     up_total = ring_end(up_ring)
+    up_plane = plane_start(up_total)
+    one_ring = ring_middle(one_ring)
+    two_ring = ring_start(two_near, two_swap)
     down_plane = plane_middle(down_plane, order)
-    one_ring = ring_middle(one_ring)
-    up_plane = plane_start(up_total)
-    own = jnp.full((1,), eighth, jnp.int32)
-    two_ring = ring_start(two_near, two_swap)
-    down_plane = plane_end(down_plane, order)
-    down_grad = order.mark(stack_pieces(*order.take(down_plane), own, False))
+    small = order.mark(order.take(pack_small()))
+    small_got = swap_along(small, "core")
     one_total = ring_end(one_ring)
     one_plane = plane_start(one_total)
+    two_ring = ring_middle(two_ring)
+    small = order.mark(small + order.take(small_got))
+    small_got = swap_along(small, "x")
+    down_plane = plane_end(down_plane, order)
+    own = jnp.full((1,), eighth, jnp.int32)
+    up_plane = plane_middle(up_plane, order)
     input_held = order.mark(unbox(order.take(input_got)))
     input_grad = spread_back(input_held)
-    two_ring = ring_middle(two_ring)
-    up_plane = plane_middle(up_plane, order)
+    down_grad = order.mark(stack_pieces(*order.take(down_plane), own, False))
+    two_total = ring_end(two_ring)
+    two_plane = plane_start(two_total)
+    small = order.mark(small + order.take(small_got))
+    small_got = swap_along(small, "y")
     up_plane = plane_end(up_plane, order)
     one_plane = plane_middle(one_plane, order)
     up_grad = order.mark(stack_pieces(*order.take(up_plane), own, True))
-    two_total = ring_end(two_ring)
-    two_plane = plane_start(two_total)
     one_plane = plane_end(one_plane, order)
+    small = order.mark(small + order.take(small_got))
+    small_got = lax.ppermute(small, "z", [(i, i ^ 1) for i in range(depth)])
     two_plane = plane_middle(two_plane, order)
+    input_grad = order.step(input_grad)
     query_grad, key_grad = order.mark(stack_heads(*order.take(one_plane), own, (True, True)))
     two_plane = plane_end(two_plane, order)
+    small = order.mark(small + order.take(small_got))
+    small_got = lax.ppermute(small, "z", [(i, i ^ 2) for i in range(depth)])
     value_grad, out_w_grad = order.mark(stack_heads(*order.take(two_plane), own, (True, False)))
-    kept = []
-    for sums, up_sum, resid_grad, cot_rows, norms in (
-        (sums_a, up_sum_a, resid_grad_a, cot_own_a, (gain_one_a, shift_one_a, gain_two_a, shift_two_a)),
-        (sums_b, up_sum_b, resid_grad_b, cot_own_b, (gain_one_b, shift_one_b, gain_two_b, shift_two_b)),
-    ):
-        kept.append(
-            dict(
-                query_b=sums[0],
-                value_b=sums[1],
-                up_b=up_sum,
-                vectors=(jnp.sum(resid_grad, axis=0), jnp.sum(cot_rows, axis=0)) + norms,
-            )
-        )
-
-    def place(vector, shard_size, size):
-        whole = jnp.zeros((depth * shard_size,), jnp.float32)
-        for index in range(2 * depth):
-            half = y if index < depth else 1 - y
-            owner = lax.rem(z - index % depth + depth, depth)
-            whole = lax.dynamic_update_slice(
-                whole,
-                vector[index * size : (index + 1) * size],
-                (owner * shard_size + (2 * team + half) * size,),
-            )
-        return whole
-
-    small = [kept[0][name] + kept[1][name] for name in ("query_b", "value_b", "up_b")]
-    vectors = [
-        place(small[0], shard_heads, HEAD_DIM),
-        place(small[1], shard_heads, HEAD_DIM),
-        place(small[2], up_weight.shape[1], half_units),
-    ] + [kept[0]["vectors"][k] + kept[1]["vectors"][k] for k in range(6)]
-    sizes = [vector.shape[0] for vector in vectors]
-    packed = total_all(jnp.concatenate(vectors).reshape(-1, 128)).reshape(-1)
+    packed = small + order.take(small_got)
+    packed = packed.reshape(-1)
     pieces = []
     offset = 0
-    for size in sizes:
+    heads_all = depth * shard_heads
+    for size in (heads_all, heads_all, depth * up_weight.shape[1]) + (width,) * 6:
         pieces.append(packed[offset : offset + size])
         offset += size
-    query_b_grad, value_b_grad, up_b_grad, out_b_grad, down_b_grad, *norm_grads = pieces
+    query_b_grad, value_b_grad, up_b_grad, out_b_grad, down_b_grad, gain_two_g, shift_two_g, *norm_grads = pieces
+    norm_grads = norm_grads + [gain_two_g, shift_two_g]
 
     def own_shard(vector):
         size = vector.shape[0] // depth

time: 1440 us -> 1330 us (0.924)
  Pallas kernels: 545 us -> 674 us
  local copies, waits for them, and re-layouts: 204 us -> 98.1 us
  other arithmetic: 89.6 us -> 9.74 us
  waiting for transfers between devices: 425 us -> 364 us
    pallas_call x0 -> x39, Pallas kernels: none -> 191 us  [the longest x18 74.7 us: rows_call(): pl.pallas_call(kernel, grid=(steps,), in_specs=[spec(array, first) for ar...]
    ppermute x21, waiting for transfers between devices: 227 us -> 138 us  [shift(): lax.ppermute(array, 'z', [(i, (i + step) % size) for i in range(size)])]
    unnamed x323 -> x175, local copies, waits for them, and re-layouts: 134 us -> 47.7 us
    pallas_call x12 -> x4, Pallas kernels: 115 us -> 57.6 us  [cross_sums(): pl.pallas_call(cross_kernel, grid=(size // tall,), in_specs=[left_spec, r...]
    ppermute x68, waiting for transfers between devices: 161 us -> 197 us  [swap_along(): return lax.ppermute(array, axis, SWAP)]
    convert_element_type x24 -> x1, other arithmetic: 25.1 us -> 0.03 us  [layer(): bias_w = bias_w.reshape(2 * depth, 8, width)[:, 0, :].astype(jnp.float32)]
    reduce_sum x12 -> x0, other arithmetic: 24.3 us -> none  [the longest x3 11.1 us: norm_backward(): gain_grad = jnp.sum(grad_in * normed, axis=0)]
    concatenate x11 -> x1, other arithmetic: 19.4 us -> 0.6 us  [layer(): qkv_b = jnp.concatenate([query_b, jnp.zeros_like(query_b), value_b], axis=1)]
  transfers between devices with their start and end apart: 99 -> 99, of which waited for: 32 -> 29; matrix products, arithmetic and copies ran while one was open for 17% -> 4% of each run, Pallas kernels for 37% -> 46%
where the time goes in v3:
time: 1330 us; the launch traced here: 1310 us
  Pallas kernels  674 us (51%)
  waiting for transfers between devices  364 us (27%)
  starting transfers between devices  167 us (13%)
  local copies, waits for them, and re-layouts  98.1 us (7%)
    ppermute x68, waiting for transfers between devices, swap_along(): return lax.ppermute(array, axis, SWAP)  197 us
    ppermute x21, waiting for transfers between devices, shift(): lax.ppermute(array, 'z', [(i, (i + step) % size) for i in range(size)])  138 us
    pallas_call x18, Pallas kernels, rows_call(): pl.pallas_call(kernel, grid=(steps,), in_specs=[spec(array, first) for ar...  74.7 us
    ppermute x21, starting transfers between devices, shift(): lax.ppermute(array, 'z', [(i, (i + step) % size) for i in range(size)])  72.2 us
    pallas_call x16, Pallas kernels, join_rows(): pl.pallas_call(functools.partial(join_kernel, count), grid=(4,), in_specs...  69.5 us
    pallas_call x6, Pallas kernels, partial_sums(): pl.pallas_call(partial_kernel, grid=(cols // WIDE,), in_specs=[whole((row...  65 us
    ppermute x68, starting transfers between devices, swap_along(): return lax.ppermute(array, axis, SWAP)  62.7 us
    pallas_call x4, Pallas kernels, cross_sums(): pl.pallas_call(cross_kernel, grid=(size // tall,), in_specs=[left_spec, r...  57.6 us
  transfers between devices with their start and end apart: 99, of which 29 were waited for; matrix products, arithmetic and copies ran while one was open for 4% of the time, Pallas kernels for 46%

profile of v3, /device:TPU:0, one launch (start us, length us, event | category | flops | bytes accessed | tf_op | source)
XLA Modules:
  0.0 1314.6 jit_solution(11410850434358751241)
XLA Ops:
  20.1 18.3 %collective-permute-done.refs_1_ = bf16[264,2048]{1,0:T(8,128)(2,1)S(1)} collective-permute-done((bf16[264,2048]{1,0:T(8,128)(2,1)}, bf16[264,2048]{1,0:T(8,128)(2,1)S(1)}, u32[]{:S(2)}, u32[]{:S(2)}) %collective-permute-start) | collective-permute-done | bytes 1081376 | tf_op jit(solution)/shard_map/ppermute | solution.py:1404
  46.3 19.0 %collective-permute-done.1.refs_2_ = bf16[264,2048]{1,0:T(8,128)(2,1)} collective-permute-done((bf16[264,2048]{1,0:T(8,128)(2,1)S(1)}, bf16[264,2048]{1,0:T(8,128)(2,1)}, u32[]{:S(2)}, u32[]{:S(2)}) %collective-permute-start.1) | collective-permute-done | bytes 1081376 | tf_op jit(solution)/shard_map/ppermute | solution.py:1404
  65.3 8.7 pick_rows.2
  84.2 56.7 %collective-permute-done.2.refs_3_ = bf16[264,2048]{1,0:T(8,128)(2,1)} collective-permute-done((bf16[264,2048]{1,0:T(8,128)(2,1)S(1)}, bf16[264,2048]{1,0:T(8,128)(2,1)}, u32[]{:S(2)}, u32[]{:S(2)}) %collective-permute-start.2) | collective-permute-done | bytes 1081376 | tf_op jit(solution)/shard_map/ppermute | solution.py:1404
  157.5 17.0 %collective-permute-done.6.refs_7_ = bf16[264,2048]{1,0:T(8,128)(2,1)S(1)} collective-permute-done((bf16[264,2048]{1,0:T(8,128)(2,1)}, bf16[264,2048]{1,0:T(8,128)(2,1)S(1)}, u32[]{:S(2)}, u32[]{:S(2)}) %collective-permute-start.6) | collective-permute-done | bytes 1081376 | tf_op jit(solution)/shard_map/ppermute | solution.py:1399
  175.5 7.1 attn_join.1
  196.3 9.5 collective-permute-start.9
  208.4 12.7 all-to-all-done.2
  224.2 8.7 pick_rows.3
  233.5 9.8 collective-permute-start.11
  245.6 6.5 collective-permute-done.8.refs_3_
  252.1 11.7 project.4.query_ref.key_ref.value_ref
  265.7 18.3 %attend.2.left_ref.refs_2_ = bf16[1024,512]{1,0:T(8,128)(2,1)S(1)} custom-call(s32[1]{0:T(128)} %bitcast.10.rank_ref, bf16[1024,1536]{1,0:T(8,128)(2,1)S(1)} %copy-done.1, bf16[1024,1536]{1,0:T(8,128)(2,1)S(1)} %copy-done.1, bf16[1024,1536]{1,0:T(8,128)(2,1)S(1)} %copy-done.1, s32[1024,2]{1,0:T(8,128)S(1)} %copy.162.key_info_ref, ...), custom_call_target="tpu_custom_call" | custom-call | flops 1048576 | bytes 4096 | tf_op jit(solution)/shard_map/attend/pallas_call | solution.py:565
  289.0 6.0 partial_sums.6
  301.9 11.6 project.5.query_ref.key_ref.value_ref
  313.5 8.1 collective-permute-done.14.refs_7_
  337.8 18.3 %attend.3.left_ref.refs_3_ = bf16[1024,512]{1,0:T(8,128)(2,1)S(1)} custom-call(s32[1]{0:T(128)} %bitcast.10.rank_ref, bf16[1024,1536]{1,0:T(8,128)(2,1)S(1)} %copy-done, bf16[1024,1536]{1,0:T(8,128)(2,1)S(1)} %copy-done, bf16[1024,1536]{1,0:T(8,128)(2,1)S(1)} %copy-done, s32[1024,2]{1,0:T(8,128)S(1)} %copy-done.13, s32[2,1024]{1,0:T(2,128)S(1)} %pad_add_fusion.3.query_info_ref), custom_call_target="tpu_custom_call" | custom-call | flops 1048576 | bytes 4096 | tf_op jit(solution)/shard_map/attend/pallas_call | solution.py:565
  361.3 6.0 partial_sums.7
  376.2 7.0 join_rows.18.weight_ref
  387.3 33.5 %collective-permute-done.20.refs_5_ = bf16[256,2048]{1,0:T(8,128)(2,1)} collective-permute-done((bf16[256,2048]{1,0:T(8,128)(2,1)}, bf16[256,2048]{1,0:T(8,128)(2,1)}, u32[]{:S(2)}, u32[]{:S(2)}) %collective-permute-start.20) | collective-permute-done | bytes 1048608 | tf_op jit(solution)/shard_map/ppermute | solution.py:1399
  430.7 17.4 %expand.2 = (bf16[1024,2048]{1,0:T(8,128)(2,1)}, bf16[1024,2048]{1,0:T(8,128)(2,1)}) custom-call(bf16[512,2048]{1,0:T(8,128)(2,1)} %join_rows.19.near_ref.near_a, bf16[512,2048]{1,0:T(8,128)(2,1)} %copy-done.21, bf16[2048,2048]{1,0:T(8,128)(2,1)} %join_rows.18.weight_ref, f32[1,2048]{1,0:T(1,128)} %bitcast.166), custom_call_target="tpu_custom_call" | custom-call | flops 1048576 | bytes 4096 | tf_op jit(solution)/shard_map/expand/pallas_call | solution.py:769
  464.2 18.9 %collective-permute-done.28.refs_1_ = bf16[256,2048]{1,0:T(8,128)(2,1)} collective-permute-done((bf16[256,2048]{1,0:T(8,128)(2,1)}, bf16[256,2048]{1,0:T(8,128)(2,1)}, u32[]{:S(2)}, u32[]{:S(2)}) %collective-permute-start.28) | collective-permute-done | bytes 1048608 | tf_op jit(solution)/shard_map/ppermute | solution.py:1399
  492.6 17.5 %expand.3 = (bf16[1024,2048]{1,0:T(8,128)(2,1)}, bf16[1024,2048]{1,0:T(8,128)(2,1)}) custom-call(bf16[512,2048]{1,0:T(8,128)(2,1)} %join_rows.20.near_ref.near_b, bf16[512,2048]{1,0:T(8,128)(2,1)} %copy-done.22, bf16[2048,2048]{1,0:T(8,128)(2,1)} %join_rows.18.weight_ref, f32[1,2048]{1,0:T(1,128)} %bitcast.167), custom_call_target="tpu_custom_call" | custom-call | flops 1048576 | bytes 4096 | tf_op jit(solution)/shard_map/expand/pallas_call | solution.py:769
  512.9 7.0 join_rows.21.weight_ref
  519.8 13.2 %partial_sums.8 = (f32[512,2048]{1,0:T(8,128)}, bf16[512,2048]{1,0:T(8,128)(2,1)}) custom-call(bf16[1024,2048]{1,0:T(8,128)(2,1)} %get-tuple-element.367.left_ref.left_a, bf16[2048,2048]{1,0:T(8,128)(2,1)} %join_rows.21.weight_ref), custom_call_target="tpu_custom_call" | custom-call | flops 1048576 | bytes 4096 | tf_op jit(solution)/shard_map/partial_sums/pallas_call | solution.py:830
  539.4 13.3 %partial_sums.9 = (f32[512,2048]{1,0:T(8,128)}, bf16[512,2048]{1,0:T(8,128)(2,1)}) custom-call(bf16[1024,2048]{1,0:T(8,128)(2,1)} %get-tuple-element.336.left_ref.left_b, bf16[2048,2048]{1,0:T(8,128)(2,1)} %join_rows.21.weight_ref), custom_call_target="tpu_custom_call" | custom-call | flops 1048576 | bytes 4096 | tf_op jit(solution)/shard_map/partial_sums/pallas_call | solution.py:830
  554.1 14.4 %expand_back.2 = (bf16[1024,2048]{1,0:T(8,128)(2,1)}, f32[8,2048]{1,0:T(8,128)}) custom-call(bf16[512,2048]{1,0:T(8,128)(2,1)} %join_rows.22.near_ref.near_a, bf16[512,2048]{1,0:T(8,128)(2,1)} %copy-done.23, bf16[2048,2048]{1,0:T(8,128)(2,1)} %join_rows.21.weight_ref, bf16[1024,2048]{1,0:T(8,128)(2,1)} %get-tuple-element.315.slope_ref), custom_call_target="tpu_custom_call" | custom-call | flops 1048576 | bytes 4096 | tf_op jit(solution)/shard_map/expand_back/pallas_call | solution.py:800
  573.4 13.4 %partial_sums.10 = (f32[512,2048]{1,0:T(8,128)}, bf16[512,2048]{1,0:T(8,128)(2,1)}) custom-call(bf16[1024,2048]{1,0:T(8,128)(2,1)} %get-tuple-element.396.left_ref.left_a, bf16[2048,2048]{1,0:T(8,128)(2,1)} %join_rows.18.weight_ref), custom_call_target="tpu_custom_call" | custom-call | flops 1048576 | bytes 4096 | tf_op jit(solution)/shard_map/partial_sums/pallas_call | solution.py:830
  588.5 14.5 %expand_back.3 = (bf16[1024,2048]{1,0:T(8,128)(2,1)}, f32[8,2048]{1,0:T(8,128)}) custom-call(bf16[512,2048]{1,0:T(8,128)(2,1)} %join_rows.23.near_ref.near_b, bf16[512,2048]{1,0:T(8,128)(2,1)} %copy-done.24, bf16[2048,2048]{1,0:T(8,128)(2,1)} %join_rows.21.weight_ref, bf16[1024,2048]{1,0:T(8,128)(2,1)} %get-tuple-element.328.slope_ref), custom_call_target="tpu_custom_call" | custom-call | flops 1048576 | bytes 4096 | tf_op jit(solution)/shard_map/expand_back/pallas_call | solution.py:800
  608.4 13.2 %partial_sums.11 = (f32[512,2048]{1,0:T(8,128)}, bf16[512,2048]{1,0:T(8,128)(2,1)}) custom-call(bf16[1024,2048]{1,0:T(8,128)(2,1)} %get-tuple-element.356.left_ref.left_b, bf16[2048,2048]{1,0:T(8,128)(2,1)} %join_rows.18.weight_ref), custom_call_target="tpu_custom_call" | custom-call | flops 1048576 | bytes 4096 | tf_op jit(solution)/shard_map/partial_sums/pallas_call | solution.py:830
  622.8 14.3 %cross_sums.4 = bf16[1024,2048]{1,0:T(8,128)(2,1)} custom-call(bf16[1024,2048]{1,0:T(8,128)(2,1)} %get-tuple-element.367.left_ref.left_a, bf16[512,2048]{1,0:T(8,128)(2,1)} %join_rows.22.near_ref.near_a, bf16[512,2048]{1,0:T(8,128)(2,1)} %copy-done.23, bf16[1024,2048]{1,0:T(8,128)(2,1)} %get-tuple-element.336.left_ref.left_b, ...), custom_call_target="tpu_custom_call" | custom-call | flops 1048576 | bytes 4096 | tf_op jit(solution)/shard_map/cross_sums/pallas_call | solution.py:864
  648.4 5.4 second_back.2
  654.5 14.3 %cross_sums.5.refs_0_ = bf16[1024,2048]{1,0:T(8,128)(2,1)} custom-call(bf16[1024,2048]{1,0:T(8,128)(2,1)} %get-tuple-element.367.left_ref.left_a, bf16[512,2048]{1,0:T(8,128)(2,1)} %join_rows.22.near_ref.near_a, bf16[512,2048]{1,0:T(8,128)(2,1)} %copy-done.23, bf16[1024,2048]{1,0:T(8,128)(2,1)} %get-tuple-element.336.left_ref.left_b, ...), custom_call_target="tpu_custom_call" | custom-call | flops 1048576 | bytes 4096 | tf_op jit(solution)/shard_map/cross_sums/pallas_call | solution.py:864
  670.9 5.4 second_back.3
  681.7 14.8 %cross_sums.6 = bf16[1024,2048]{1,0:T(8,128)(2,1)} custom-call(bf16[1024,2048]{1,0:T(8,128)(2,1)} %get-tuple-element.396.left_ref.left_a, bf16[512,2048]{1,0:T(8,128)(2,1)} %join_rows.19.near_ref.near_a, bf16[512,2048]{1,0:T(8,128)(2,1)} %copy-done.21, bf16[1024,2048]{1,0:T(8,128)(2,1)} %get-tuple-element.356.left_ref.left_b, ...), custom_call_target="tpu_custom_call" | custom-call | flops 1048576 | bytes 4096 | tf_op jit(solution)/shard_map/cross_sums/pallas_call | solution.py:864
  707.7 6.3 project.6.grad_ref
  715.3 27.3 %attend_back.2 = (bf16[1024,512]{1,0:T(8,128)(2,1)S(1)}, bf16[1024,512]{1,0:T(8,128)(2,1)S(1)}, bf16[1024,512]{1,0:T(8,128)(2,1)S(1)}, f32[8,512]{1,0:T(8,128)S(1)}) custom-call(s32[1]{0:T(128)} %bitcast.10.rank_ref, bf16[1024,1536]{1,0:T(8,128)(2,1)S(1)} %copy-done.2, bf16[1024,1536]{1,0:T(8,128)(2,1)S(1)} %copy-done.2, bf16[1024,1536]{1,0:T(8,128)(2,1)S(1)} %copy-done.2, ...), custom_call_target="tpu_custom_call" | custom-call | flops 1048576 | bytes 4096 | tf_op jit(solution)/shard_map/attend_back/pallas_call | solution.py:673
  755.3 10.7 partial_three.2
  771.1 14.3 %cross_sums.7.refs_0_ = bf16[1024,2048]{1,0:T(8,128)(2,1)} custom-call(bf16[1024,2048]{1,0:T(8,128)(2,1)} %get-tuple-element.396.left_ref.left_a, bf16[512,2048]{1,0:T(8,128)(2,1)} %join_rows.19.near_ref.near_a, bf16[512,2048]{1,0:T(8,128)(2,1)} %copy-done.21, bf16[1024,2048]{1,0:T(8,128)(2,1)} %get-tuple-element.356.left_ref.left_b, ...), custom_call_target="tpu_custom_call" | custom-call | flops 1048576 | bytes 4096 | tf_op jit(solution)/shard_map/cross_sums/pallas_call | solution.py:864
  797.4 18.0 %collective-permute-done.47.got_ref = bf16[256,2048]{1,0:T(8,128)(2,1)} collective-permute-done((bf16[256,2048]{1,0:T(8,128)(2,1)}, bf16[256,2048]{1,0:T(8,128)(2,1)}, u32[]{:S(2)}, u32[]{:S(2)}) %collective-permute-start.47) | collective-permute-done | bytes 1048608 | tf_op jit(solution)/shard_map/ppermute | solution.py:1399
  835.9 6.2 project.7.grad_ref
  843.3 27.3 %attend_back.3 = (bf16[1024,512]{1,0:T(8,128)(2,1)S(1)}, bf16[1024,512]{1,0:T(8,128)(2,1)S(1)}, bf16[1024,512]{1,0:T(8,128)(2,1)S(1)}, f32[8,512]{1,0:T(8,128)S(1)}) custom-call(s32[1]{0:T(128)} %bitcast.10.rank_ref, bf16[1024,1536]{1,0:T(8,128)(2,1)S(1)} %copy-done, bf16[1024,1536]{1,0:T(8,128)(2,1)S(1)} %copy-done, bf16[1024,1536]{1,0:T(8,128)(2,1)S(1)} %copy-done, ...), custom_call_target="tpu_custom_call" | custom-call | flops 1048576 | bytes 4096 | tf_op jit(solution)/shard_map/attend_back/pallas_call | solution.py:673
  873.6 10.0 collective-permute-done.52.got_ref
  893.8 10.5 partial_three.3
  904.3 9.1 cross_pair.4
  925.5 10.8 cross_pair.5
  936.3 6.9 collective-permute-done.50.refs_3_
  945.3 20.7 %collective-permute-done.49.refs_2_ = bf16[256,2048]{1,0:T(8,128)(2,1)} collective-permute-done((bf16[256,2048]{1,0:T(8,128)(2,1)S(1)}, bf16[256,2048]{1,0:T(8,128)(2,1)}, u32[]{:S(2)}, u32[]{:S(2)}) %collective-permute-start.49) | collective-permute-done | bytes 1048608 | tf_op jit(solution)/shard_map/ppermute | solution.py:1404
  969.8 8.7 drop_rows.2
  990.9 8.8 cross_pair.6.refs_0_
  1022.9 26.5 %collective-permute-start.64 = (bf16[128,2048]{1,0:T(8,128)(2,1)}, bf16[128,2048]{1,0:T(8,128)(2,1)}, u32[]{:S(2)}, u32[]{:S(2)}) collective-permute-start(bf16[128,2048]{1,0:T(8,128)(2,1)} %add_pieces.23), channel_id=1, source_target_pairs={{0,1},{1,2},{2,3},{3,0},{4,5},{5,6},{6,7},{7,4},{8,9},{9,10},{10,1... | collective-permute-start | bytes 1572872 | tf_op jit(solution)/shard_map/ppermute | solution.py:1404
  1055.9 10.6 cross_pair.7.refs_0_
  1095.0 5.7 collective-permute-done.68.refs_2_
  1114.0 6.3 collective-permute-start.72
  1120.3 26.1 %collective-permute-done.59.refs_1_ = bf16[256,2048]{1,0:T(8,128)(2,1)S(1)} collective-permute-done((bf16[256,2048]{1,0:T(8,128)(2,1)S(1)}, bf16[256,2048]{1,0:T(8,128)(2,1)S(1)}, u32[]{:S(2)}, u32[]{:S(2)}) %collective-permute-start.59) | collective-permute-done | bytes 1048608 | tf_op jit(solution)/shard_map/ppermute | solution.py:1399
  1155.3 5.6 all-to-all-done.6
  1162.2 8.8 drop_rows.3
  1171.0 13.7 %stack_pieces.2 = f32[2048,2048]{1,0:T(8,128)} custom-call(s32[1]{0:T(128)} %bitcast.56.own_ref, bf16[1024,2048]{1,0:T(8,128)(2,1)} %join_rows.28.near_ref, bf16[1024,2048]{1,0:T(8,128)(2,1)} %copy-done.35), custom_call_target="tpu_custom_call" | custom-call | flops 1048576 | bytes 4096 | tf_op jit(solution)/shard_map/stack_pieces/pallas_call | solution.py:1047
  1197.4 11.5 collective-permute-done.78.refs_1_
  1214.3 14.3 %stack_pieces.3 = f32[2048,2048]{1,0:T(8,128)} custom-call(s32[1]{0:T(128)} %bitcast.56.own_ref, bf16[1024,2048]{1,0:T(8,128)(2,1)} %join_rows.29.near_ref, bf16[1024,2048]{1,0:T(8,128)(2,1)} %copy-done.36), custom_call_target="tpu_custom_call" | custom-call | flops 1048576 | bytes 4096 | tf_op jit(solution)/shard_map/stack_pieces/pallas_call | solution.py:1047
  1245.0 35.0 %collective-permute-done.77 = f32[192,128]{1,0:T(8,128)S(1)} collective-permute-done((f32[192,128]{1,0:T(8,128)S(1)}, f32[192,128]{1,0:T(8,128)S(1)}, u32[]{:S(2)}, u32[]{:S(2)}) %collective-permute-start.77) | collective-permute-done | bytes 98336 | tf_op jit(solution)/shard_map/ppermute | solution.py:1399
  1285.2 7.0 stack_heads.2
  1296.9 5.2 collective-permute-done.89
  1304.9 7.0 stack_heads.3
  (557 shorter events, 442.4 us)
Async XLA Ops:
  9.3 29.1 %collective-permute-start = (bf16[264,2048]{1,0:T(8,128)(2,1)}, bf16[264,2048]{1,0:T(8,128)(2,1)S(1)}, u32[]{:S(2)}, u32[]{:S(2)}) collective-permute-start(bf16[264,2048]{1,0:T(8,128)(2,1)} %get-tuple-element.258.refs_0_), channel_id=1, source_target_pairs={{0,1},{1,2},{2,3},{3,0},{4,5},{5,6},{6,7},{7,4},{8,9},{9,10},{10,1... | collective-permute-start | bytes 3244040 | tf_op jit(solution)/shard_map/ppermute | solution.py:1404
  14.3 30.5 %all-to-all-start = ((bf16[2,128,8,512]{3,1,0,2:T(8,128)(2,1)}), bf16[2,128,8,512]{3,1,0,2:T(8,128)(2,1)S(1)}, u32[]{:S(2)}, u32[]{:S(2)}) async-start(bf16[2,128,8,512]{3,1,0,2:T(8,128)(2,1)} %copy.155), calls=%async_computation | async-start | bytes 4194304 | tf_op jit(solution)/shard_map/all_to_all | solution.py:1541
  74.0 70.3 %all-to-all-start.1 = ((bf16[32,72,512]{2,1,0:T(8,128)(2,1)}), bf16[32,72,512]{2,1,0:T(8,128)(2,1)S(1)}, u32[]{:S(2)}, u32[]{:S(2)}) async-start(bf16[32,72,512]{2,1,0:T(8,128)(2,1)} %bitcast.129), calls=%async_computation.1 | async-start | bytes 4718592 | tf_op jit(solution)/shard_map/all_to_all | solution.py:1545
  77.9 63.0 %collective-permute-start.2 = (bf16[264,2048]{1,0:T(8,128)(2,1)S(1)}, bf16[264,2048]{1,0:T(8,128)(2,1)}, u32[]{:S(2)}, u32[]{:S(2)}) collective-permute-start(bf16[264,2048]{1,0:T(8,128)(2,1)S(1)} %copy-done.50), channel_id=1, source_target_pairs={{0,3},{1,0},{2,1},{3,2},{4,7},{5,4},{6,5},{7,6},{8,11},{9,8},{10,9... | collective-permute-start | bytes 3244040 | tf_op jit(solution)/shard_map/ppermute | solution.py:1404
  82.1 75.4 %collective-permute-start.4 = (bf16[264,2048]{1,0:T(8,128)(2,1)}, bf16[264,2048]{1,0:T(8,128)(2,1)}, u32[]{:S(2)}, u32[]{:S(2)}) collective-permute-start(bf16[264,2048]{1,0:T(8,128)(2,1)} %copy-done.51), channel_id=1, source_target_pairs={{0,16},{16,0},{1,17},{17,1},{2,18},{18,2},{3,19},{19,3},{4,20},{20... | collective-permute-start | bytes 3244040 | tf_op jit(solution)/shard_map/ppermute | solution.py:1399
  83.7 73.8 %collective-permute-start.5 = (bf16[264,2048]{1,0:T(8,128)(2,1)}, bf16[264,2048]{1,0:T(8,128)(2,1)}, u32[]{:S(2)}, u32[]{:S(2)}) collective-permute-start(bf16[264,2048]{1,0:T(8,128)(2,1)} %collective-permute-done.1.refs_2_), channel_id=1, source_target_pairs={{0,16},{16,0},{1,17},{17,1},{2,18},{18,2},{3,19},{19,3},{4,20},{20... | collective-permute-start | bytes 3244040 | tf_op jit(solution)/shard_map/ppermute | solution.py:1399
  141.0 33.6 %collective-permute-start.6 = (bf16[264,2048]{1,0:T(8,128)(2,1)}, bf16[264,2048]{1,0:T(8,128)(2,1)S(1)}, u32[]{:S(2)}, u32[]{:S(2)}) collective-permute-start(bf16[264,2048]{1,0:T(8,128)(2,1)} %collective-permute-done.2.refs_3_), channel_id=1, source_target_pairs={{0,16},{16,0},{1,17},{17,1},{2,18},{18,2},{3,19},{19,3},{4,20},{20... | collective-permute-start | bytes 3244040 | tf_op jit(solution)/shard_map/ppermute | solution.py:1399
  153.3 29.3 %collective-permute-start.3 = (bf16[256,2048]{1,0:T(8,128)(2,1)}, bf16[256,2048]{1,0:T(8,128)(2,1)S(1)}, u32[]{:S(2)}, u32[]{:S(2)}) collective-permute-start(bf16[256,2048]{1,0:T(8,128)(2,1)} %norm_in.2.refs_0_), channel_id=1, source_target_pairs={{0,8},{8,0},{1,9},{9,1},{2,10},{10,2},{3,11},{11,3},{4,12},{12,4},... | collective-permute-start | bytes 3145736 | tf_op jit(solution)/shard_map/ppermute | solution.py:1399
  187.6 45.3 %collective-permute-start.7 = (bf16[512,2048]{1,0:T(8,128)(2,1)}, bf16[512,2048]{1,0:T(8,128)(2,1)S(1)}, u32[]{:S(2)}, u32[]{:S(2)}) collective-permute-start(bf16[512,2048]{1,0:T(8,128)(2,1)} %join_rows.16.near_ref.refs_4_), channel_id=1, source_target_pairs={{0,4},{4,0},{1,5},{5,1},{2,6},{6,2},{3,7},{7,3},{8,12},{12,8},{9,1... | collective-permute-start | bytes 6291464 | tf_op jit(solution)/shard_map/ppermute | solution.py:1399
  189.6 31.5 %all-to-all-start.2 = ((bf16[2,128,8,512]{3,1,0,2:T(8,128)(2,1)}), bf16[2,128,8,512]{3,1,0,2:T(8,128)(2,1)}, u32[]{:S(2)}, u32[]{:S(2)}) async-start(bf16[2,128,8,512]{3,1,0,2:T(8,128)(2,1)} %copy.158), calls=%async_computation.2 | async-start | bytes 4194304 | tf_op jit(solution)/shard_map/all_to_all | solution.py:1541
  196.3 36.7 %collective-permute-start.9 = (bf16[256,2048]{1,0:T(8,128)(2,1)}, bf16[256,2048]{1,0:T(8,128)(2,1)}, u32[]{:S(2)}, u32[]{:S(2)}) collective-permute-start(bf16[256,2048]{1,0:T(8,128)(2,1)} %flipped.2.refs_0_), channel_id=1, source_target_pairs={{0,1},{1,2},{2,3},{3,0},{4,5},{5,6},{6,7},{7,4},{8,9},{9,10},{10,1... | collective-permute-start | bytes 3145736 | tf_op jit(solution)/shard_map/ppermute | solution.py:1404
  206.4 45.7 %collective-permute-start.8 = (bf16[256,2048]{1,0:T(8,128)(2,1)}, bf16[256,2048]{1,0:T(8,128)(2,1)}, u32[]{:S(2)}, u32[]{:S(2)}) collective-permute-start(bf16[256,2048]{1,0:T(8,128)(2,1)} %flipped.2.refs_0_), channel_id=1, source_target_pairs={{0,3},{1,0},{2,1},{3,2},{4,7},{5,4},{6,5},{7,6},{8,11},{9,8},{10,9... | collective-permute-start | bytes 3145736 | tf_op jit(solution)/shard_map/ppermute | solution.py:1404
  206.5 78.5 %collective-permute-start.10 = (bf16[256,2048]{1,0:T(8,128)(2,1)}, bf16[256,2048]{1,0:T(8,128)(2,1)}, u32[]{:S(2)}, u32[]{:S(2)}) collective-permute-start(bf16[256,2048]{1,0:T(8,128)(2,1)} %norm_in.3.refs_0_), channel_id=1, source_target_pairs={{0,8},{8,0},{1,9},{9,1},{2,10},{10,2},{3,11},{11,3},{4,12},{12,4},... | collective-permute-start | bytes 3145736 | tf_op jit(solution)/shard_map/ppermute | solution.py:1399
  232.9 52.1 %collective-permute-start.12 = (bf16[256,2048]{1,0:T(8,128)(2,1)}, bf16[256,2048]{1,0:T(8,128)(2,1)}, u32[]{:S(2)}, u32[]{:S(2)}) collective-permute-start(bf16[256,2048]{1,0:T(8,128)(2,1)} %collective-permute-done.9.refs_1_), channel_id=1, source_target_pairs={{0,16},{16,0},{1,17},{17,1},{2,18},{18,2},{3,19},{19,3},{4,20},{20... | collective-permute-start | bytes 3145736 | tf_op jit(solution)/shard_map/ppermute | solution.py:1399
  233.5 51.5 %collective-permute-start.11 = (bf16[256,2048]{1,0:T(8,128)(2,1)}, bf16[256,2048]{1,0:T(8,128)(2,1)}, u32[]{:S(2)}, u32[]{:S(2)}) collective-permute-start(bf16[256,2048]{1,0:T(8,128)(2,1)} %collective-permute-done.9.refs_1_), channel_id=1, source_target_pairs={{0,1},{1,2},{2,3},{3,0},{4,5},{5,6},{6,7},{7,4},{8,9},{9,10},{10,1... | collective-permute-start | bytes 3145736 | tf_op jit(solution)/shard_map/ppermute | solution.py:1404
  300.5 56.7 %collective-permute-start.18 = (bf16[256,2048]{1,0:T(8,128)(2,1)}, bf16[256,2048]{1,0:T(8,128)(2,1)}, u32[]{:S(2)}, u32[]{:S(2)}) collective-permute-start(bf16[256,2048]{1,0:T(8,128)(2,1)} %collective-permute-done.11.refs_2_), channel_id=1, source_target_pairs={{0,16},{16,0},{1,17},{17,1},{2,18},{18,2},{3,19},{19,3},{4,20},{20... | collective-permute-start | bytes 3145736 | tf_op jit(solution)/shard_map/ppermute | solution.py:1399
  300.5 56.6 %collective-permute-start.17 = (bf16[256,2048]{1,0:T(8,128)(2,1)}, bf16[256,2048]{1,0:T(8,128)(2,1)}, u32[]{:S(2)}, u32[]{:S(2)}) collective-permute-start(bf16[256,2048]{1,0:T(8,128)(2,1)} %get-tuple-element.292.refs_0_), channel_id=1, source_target_pairs={{0,1},{1,2},{2,3},{3,0},{4,5},{5,6},{6,7},{7,4},{8,9},{9,10},{10,1... | collective-permute-start | bytes 3145736 | tf_op jit(solution)/shard_map/ppermute | solution.py:1404
  326.8 30.3 %collective-permute-start.16 = (bf16[256,2048]{1,0:T(8,128)(2,1)}, bf16[256,2048]{1,0:T(8,128)(2,1)}, u32[]{:S(2)}, u32[]{:S(2)}) collective-permute-start(bf16[256,2048]{1,0:T(8,128)(2,1)} %get-tuple-element.291), channel_id=1, source_target_pairs={{0,8},{8,0},{1,9},{9,1},{2,10},{10,2},{3,11},{11,3},{4,12},{12,4},... | collective-permute-start | bytes 3145736 | tf_op jit(solution)/shard_map/ppermute | solution.py:1399
  328.8 32.5 %collective-permute-start.21 = (bf16[256,2048]{1,0:T(8,128)(2,1)}, bf16[256,2048]{1,0:T(8,128)(2,1)}, u32[]{:S(2)}, u32[]{:S(2)}) collective-permute-start(bf16[256,2048]{1,0:T(8,128)(2,1)} %get-tuple-element.292.refs_0_), channel_id=1, source_target_pairs={{0,3},{1,0},{2,1},{3,2},{4,7},{5,4},{6,5},{7,6},{8,11},{9,8},{10,9... | collective-permute-start | bytes 3145736 | tf_op jit(solution)/shard_map/ppermute | solution.py:1404
  367.3 91.9 %all-to-all-start.3 = ((bf16[32,72,512]{2,1,0:T(8,128)(2,1)}), bf16[32,72,512]{2,1,0:T(8,128)(2,1)}, u32[]{:S(2)}, u32[]{:S(2)}) async-start(bf16[32,72,512]{2,1,0:T(8,128)(2,1)} %bitcast.128), calls=%async_computation.3 | async-start | bytes 4718592 | tf_op jit(solution)/shard_map/all_to_all | solution.py:1545
  370.8 50.0 %collective-permute-start.20 = (bf16[256,2048]{1,0:T(8,128)(2,1)}, bf16[256,2048]{1,0:T(8,128)(2,1)}, u32[]{:S(2)}, u32[]{:S(2)}) collective-permute-start(bf16[256,2048]{1,0:T(8,128)(2,1)} %collective-permute-done.17.refs_1_), channel_id=1, source_target_pairs={{0,16},{16,0},{1,17},{17,1},{2,18},{18,2},{3,19},{19,3},{4,20},{20... | collective-permute-start | bytes 3145736 | tf_op jit(solution)/shard_map/ppermute | solution.py:1399
  372.5 48.3 %collective-permute-start.19 = (bf16[256,2048]{1,0:T(8,128)(2,1)}, bf16[256,2048]{1,0:T(8,128)(2,1)}, u32[]{:S(2)}, u32[]{:S(2)}) collective-permute-start(bf16[256,2048]{1,0:T(8,128)(2,1)} %get-tuple-element.298.refs_0_), channel_id=1, source_target_pairs={{0,8},{8,0},{1,9},{9,1},{2,10},{10,2},{3,11},{11,3},{4,12},{12,4},... | collective-permute-start | bytes 3145736 | tf_op jit(solution)/shard_map/ppermute | solution.py:1399
  424.7 28.2 %collective-permute-start.24 = (bf16[256,2048]{1,0:T(8,128)(2,1)}, bf16[256,2048]{1,0:T(8,128)(2,1)S(1)}, u32[]{:S(2)}, u32[]{:S(2)}) collective-permute-start(bf16[256,2048]{1,0:T(8,128)(2,1)} %collective-permute-done.17.refs_1_), channel_id=1, source_target_pairs={{0,1},{1,2},{2,3},{3,0},{4,5},{5,6},{6,7},{7,4},{8,9},{9,10},{10,1... | collective-permute-start | bytes 3145736 | tf_op jit(solution)/shard_map/ppermute | solution.py:1404
  424.8 28.0 %collective-permute-start.26 = (bf16[256,2048]{1,0:T(8,128)(2,1)}, bf16[256,2048]{1,0:T(8,128)(2,1)S(1)}, u32[]{:S(2)}, u32[]{:S(2)}) collective-permute-start(bf16[256,2048]{1,0:T(8,128)(2,1)} %collective-permute-done.21.refs_3_), channel_id=1, source_target_pairs={{0,16},{16,0},{1,17},{17,1},{2,18},{18,2},{3,19},{19,3},{4,20},{20... | collective-permute-start | bytes 3145736 | tf_op jit(solution)/shard_map/ppermute | solution.py:1399
  489.9 43.1 %collective-permute-start.32 = (bf16[256,2048]{1,0:T(8,128)(2,1)}, bf16[256,2048]{1,0:T(8,128)(2,1)S(1)}, u32[]{:S(2)}, u32[]{:S(2)}) collective-permute-start(bf16[256,2048]{1,0:T(8,128)(2,1)} %get-tuple-element.495.refs_0_), channel_id=1, source_target_pairs={{0,8},{8,0},{1,9},{9,1},{2,10},{10,2},{3,11},{11,3},{4,12},{12,4},... | collective-permute-start | bytes 3145736 | tf_op jit(solution)/shard_map/ppermute | solution.py:1399
  538.0 30.5 %collective-permute-start.31 = (bf16[256,2048]{1,0:T(8,128)(2,1)S(1)}, bf16[256,2048]{1,0:T(8,128)(2,1)S(1)}, u32[]{:S(2)}, u32[]{:S(2)}) collective-permute-start(bf16[256,2048]{1,0:T(8,128)(2,1)S(1)} %copy-done.37), channel_id=1, source_target_pairs={{0,8},{8,0},{1,9},{9,1},{2,10},{10,2},{3,11},{11,3},{4,12},{12,4},... | collective-permute-start | bytes 3145736 | tf_op jit(solution)/shard_map/ppermute | solution.py:1399
  621.7 54.5 %collective-permute-start.30 = (bf16[512,2048]{1,0:T(8,128)(2,1)}, bf16[512,2048]{1,0:T(8,128)(2,1)S(1)}, u32[]{:S(2)}, u32[]{:S(2)}) collective-permute-start(bf16[512,2048]{1,0:T(8,128)(2,1)} %get-tuple-element.334), channel_id=1, source_target_pairs={{0,4},{4,0},{1,5},{5,1},{2,6},{6,2},{3,7},{7,3},{8,12},{12,8},{9,1... | collective-permute-start | bytes 6291464 | tf_op jit(solution)/shard_map/ppermute | solution.py:1399
  642.4 28.4 %collective-permute-start.37 = (bf16[256,2048]{1,0:T(8,128)(2,1)}, bf16[256,2048]{1,0:T(8,128)(2,1)}, u32[]{:S(2)}, u32[]{:S(2)}) collective-permute-start(bf16[256,2048]{1,0:T(8,128)(2,1)} %get-tuple-element.362), channel_id=1, source_target_pairs={{0,8},{8,0},{1,9},{9,1},{2,10},{10,2},{3,11},{11,3},{4,12},{12,4},... | collective-permute-start | bytes 3145736 | tf_op jit(solution)/shard_map/ppermute | solution.py:1399
  643.8 106.0 %collective-permute-start.43 = (bf16[1024,2048]{1,0:T(8,128)(2,1)}, bf16[1024,2048]{1,0:T(8,128)(2,1)}, u32[]{:S(2)}, u32[]{:S(2)}) collective-permute-start(bf16[1024,2048]{1,0:T(8,128)(2,1)} %cross_sums.4), channel_id=1, source_target_pairs={{0,16},{16,0},{1,17},{17,1},{2,18},{18,2},{3,19},{19,3},{4,20},{20... | collective-permute-start | bytes 12582920 | tf_op jit(solution)/shard_map/ppermute | solution.py:1399
  653.8 42.7 %collective-permute-start.40 = (bf16[256,2048]{1,0:T(8,128)(2,1)}, bf16[256,2048]{1,0:T(8,128)(2,1)}, u32[]{:S(2)}, u32[]{:S(2)}) collective-permute-start(bf16[256,2048]{1,0:T(8,128)(2,1)} %get-tuple-element.365.refs_0_), channel_id=1, source_target_pairs={{0,8},{8,0},{1,9},{9,1},{2,10},{10,2},{3,11},{11,3},{4,12},{12,4},... | collective-permute-start | bytes 3145736 | tf_op jit(solution)/shard_map/ppermute | solution.py:1399
  654.5 46.5 %collective-permute-start.42 = (bf16[512,2048]{1,0:T(8,128)(2,1)}, bf16[512,2048]{1,0:T(8,128)(2,1)S(1)}, u32[]{:S(2)}, u32[]{:S(2)}) collective-permute-start(bf16[512,2048]{1,0:T(8,128)(2,1)} %get-tuple-element.338), channel_id=1, source_target_pairs={{0,4},{4,0},{1,5},{5,1},{2,6},{6,2},{3,7},{7,3},{8,12},{12,8},{9,1... | collective-permute-start | bytes 6291464 | tf_op jit(solution)/shard_map/ppermute | solution.py:1399
  700.3 45.4 %collective-permute-start.44 = (bf16[256,2048]{1,0:T(8,128)(2,1)}, bf16[256,2048]{1,0:T(8,128)(2,1)}, u32[]{:S(2)}, u32[]{:S(2)}) collective-permute-start(bf16[256,2048]{1,0:T(8,128)(2,1)} %get-tuple-element.370.refs_0_), channel_id=1, source_target_pairs={{0,8},{8,0},{1,9},{9,1},{2,10},{10,2},{3,11},{11,3},{4,12},{12,4},... | collective-permute-start | bytes 3145736 | tf_op jit(solution)/shard_map/ppermute | solution.py:1399
  766.2 122.0 %collective-permute-start.51 = (bf16[1024,2048]{1,0:T(8,128)(2,1)}, bf16[1024,2048]{1,0:T(8,128)(2,1)}, u32[]{:S(2)}, u32[]{:S(2)}) collective-permute-start(bf16[1024,2048]{1,0:T(8,128)(2,1)} %cross_sums.6), channel_id=1, source_target_pairs={{0,16},{16,0},{1,17},{17,1},{2,18},{18,2},{3,19},{19,3},{4,20},{20... | collective-permute-start | bytes 12582920 | tf_op jit(solution)/shard_map/ppermute | solution.py:1399
  768.2 47.3 %collective-permute-start.47 = (bf16[256,2048]{1,0:T(8,128)(2,1)}, bf16[256,2048]{1,0:T(8,128)(2,1)}, u32[]{:S(2)}, u32[]{:S(2)}) collective-permute-start(bf16[256,2048]{1,0:T(8,128)(2,1)} %get-tuple-element.379), channel_id=1, source_target_pairs={{0,8},{8,0},{1,9},{9,1},{2,10},{10,2},{3,11},{11,3},{4,12},{12,4},... | collective-permute-start | bytes 3145736 | tf_op jit(solution)/shard_map/ppermute | solution.py:1399
  769.6 57.8 %collective-permute-start.48 = (bf16[256,2048]{1,0:T(8,128)(2,1)}, bf16[256,2048]{1,0:T(8,128)(2,1)}, u32[]{:S(2)}, u32[]{:S(2)}) collective-permute-start(bf16[256,2048]{1,0:T(8,128)(2,1)} %add_pieces.16), channel_id=1, source_target_pairs={{0,1},{1,2},{2,3},{3,0},{4,5},{5,6},{6,7},{7,4},{8,9},{9,10},{10,1... | collective-permute-start | bytes 3145736 | tf_op jit(solution)/shard_map/ppermute | solution.py:1404
  830.7 139.0 %all-to-all-start.4 = ((bf16[32,72,512]{2,1,0:T(8,128)(2,1)}), bf16[32,72,512]{2,1,0:T(8,128)(2,1)}, u32[]{:S(2)}, u32[]{:S(2)}) async-start(bf16[32,72,512]{2,1,0:T(8,128)(2,1)} %bitcast.127), calls=%async_computation.4 | async-start | bytes 4718592 | tf_op jit(solution)/shard_map/all_to_all | solution.py:1545
  834.3 49.3 %collective-permute-start.52 = (bf16[256,2048]{1,0:T(8,128)(2,1)}, bf16[256,2048]{1,0:T(8,128)(2,1)}, u32[]{:S(2)}, u32[]{:S(2)}) collective-permute-start(bf16[256,2048]{1,0:T(8,128)(2,1)} %get-tuple-element.399), channel_id=1, source_target_pairs={{0,8},{8,0},{1,9},{9,1},{2,10},{10,2},{3,11},{11,3},{4,12},{12,4},... | collective-permute-start | bytes 3145736 | tf_op jit(solution)/shard_map/ppermute | solution.py:1399
  913.5 89.8 %collective-permute-start.54 = (bf16[512,2048]{1,0:T(8,128)(2,1)}, bf16[512,2048]{1,0:T(8,128)(2,1)}, u32[]{:S(2)}, u32[]{:S(2)}) collective-permute-start(bf16[512,2048]{1,0:T(8,128)(2,1)} %cross_pair.4), channel_id=1, source_target_pairs={{0,16},{16,0},{1,17},{17,1},{2,18},{18,2},{3,19},{19,3},{4,20},{20... | collective-permute-start | bytes 6291464 | tf_op jit(solution)/shard_map/ppermute | solution.py:1399
  915.3 27.8 %collective-permute-start.50 = (bf16[256,2048]{1,0:T(8,128)(2,1)S(1)}, bf16[256,2048]{1,0:T(8,128)(2,1)S(1)}, u32[]{:S(2)}, u32[]{:S(2)}) collective-permute-start(bf16[256,2048]{1,0:T(8,128)(2,1)S(1)} %copy-done.53), channel_id=1, source_target_pairs={{0,3},{1,0},{2,1},{3,2},{4,7},{5,4},{6,5},{7,6},{8,11},{9,8},{10,9... | collective-permute-start | bytes 3145736 | tf_op jit(solution)/shard_map/ppermute | solution.py:1404
  919.6 46.5 %collective-permute-start.49 = (bf16[256,2048]{1,0:T(8,128)(2,1)S(1)}, bf16[256,2048]{1,0:T(8,128)(2,1)}, u32[]{:S(2)}, u32[]{:S(2)}) collective-permute-start(bf16[256,2048]{1,0:T(8,128)(2,1)S(1)} %copy-done.55), channel_id=1, source_target_pairs={{0,1},{1,2},{2,3},{3,0},{4,5},{5,6},{6,7},{7,4},{8,9},{9,10},{10,1... | collective-permute-start | bytes 3145736 | tf_op jit(solution)/shard_map/ppermute | solution.py:1404
  919.6 80.2 %collective-permute-start.56 = (bf16[256,2048]{1,0:T(8,128)(2,1)}, bf16[256,2048]{1,0:T(8,128)(2,1)}, u32[]{:S(2)}, u32[]{:S(2)}) collective-permute-start(bf16[256,2048]{1,0:T(8,128)(2,1)} %add_pieces.19), channel_id=1, source_target_pairs={{0,1},{1,2},{2,3},{3,0},{4,5},{5,6},{6,7},{7,4},{8,9},{9,10},{10,1... | collective-permute-start | bytes 3145736 | tf_op jit(solution)/shard_map/ppermute | solution.py:1404
  925.0 80.2 %collective-permute-start.55 = (bf16[256,2048]{1,0:T(8,128)(2,1)}, bf16[256,2048]{1,0:T(8,128)(2,1)}, u32[]{:S(2)}, u32[]{:S(2)}) collective-permute-start(bf16[256,2048]{1,0:T(8,128)(2,1)} %get-tuple-element.425), channel_id=1, source_target_pairs={{0,8},{8,0},{1,9},{9,1},{2,10},{10,2},{3,11},{11,3},{4,12},{12,4},... | collective-permute-start | bytes 3145736 | tf_op jit(solution)/shard_map/ppermute | solution.py:1399
  944.1 130.4 %collective-permute-start.63 = (bf16[512,2048]{1,0:T(8,128)(2,1)}, bf16[512,2048]{1,0:T(8,128)(2,1)S(1)}, u32[]{:S(2)}, u32[]{:S(2)}) collective-permute-start(bf16[512,2048]{1,0:T(8,128)(2,1)} %cross_pair.5), channel_id=1, source_target_pairs={{0,16},{16,0},{1,17},{17,1},{2,18},{18,2},{3,19},{19,3},{4,20},{20... | collective-permute-start | bytes 6291464 | tf_op jit(solution)/shard_map/ppermute | solution.py:1399
  983.5 68.3 %all-to-all-start.5 = ((bf16[2,1024,1,512]{3,0,2,1:T(2,128)(2,1)}), bf16[2,1024,1,512]{3,0,2,1:T(2,128)(2,1)}, u32[]{:S(2)}, u32[]{:S(2)}) async-start(bf16[2,1024,1,512]{3,0,2,1:T(2,128)(2,1)} %copy.167), calls=%async_computation.5 | async-start | bytes 4194304 | tf_op jit(solution)/shard_map/all_to_all | solution.py:1611
  987.8 35.1 %collective-permute-start.58 = (bf16[256,2048]{1,0:T(8,128)(2,1)}, bf16[256,2048]{1,0:T(8,128)(2,1)}, u32[]{:S(2)}, u32[]{:S(2)}) collective-permute-start(bf16[256,2048]{1,0:T(8,128)(2,1)} %add_pieces.20), channel_id=1, source_target_pairs={{0,3},{1,0},{2,1},{3,2},{4,7},{5,4},{6,5},{7,6},{8,11},{9,8},{10,9... | collective-permute-start | bytes 3145736 | tf_op jit(solution)/shard_map/ppermute | solution.py:1404
  1003.1 48.7 %collective-permute-start.57 = (bf16[256,2048]{1,0:T(8,128)(2,1)}, bf16[256,2048]{1,0:T(8,128)(2,1)}, u32[]{:S(2)}, u32[]{:S(2)}) collective-permute-start(bf16[256,2048]{1,0:T(8,128)(2,1)} %add_pieces.22), channel_id=1, source_target_pairs={{0,1},{1,2},{2,3},{3,0},{4,5},{5,6},{6,7},{7,4},{8,9},{9,10},{10,1... | collective-permute-start | bytes 3145736 | tf_op jit(solution)/shard_map/ppermute | solution.py:1404
  1003.3 76.8 %collective-permute-start.61 = (bf16[256,2048]{1,0:T(8,128)(2,1)S(1)}, bf16[256,2048]{1,0:T(8,128)(2,1)}, u32[]{:S(2)}, u32[]{:S(2)}) collective-permute-start(bf16[256,2048]{1,0:T(8,128)(2,1)S(1)} %copy-done.38), channel_id=1, source_target_pairs={{0,8},{8,0},{1,9},{9,1},{2,10},{10,2},{3,11},{11,3},{4,12},{12,4},... | collective-permute-start | bytes 3145736 | tf_op jit(solution)/shard_map/ppermute | solution.py:1399
  1005.2 74.9 %collective-permute-start.62 = (bf16[256,2048]{1,0:T(8,128)(2,1)S(1)}, bf16[256,2048]{1,0:T(8,128)(2,1)}, u32[]{:S(2)}, u32[]{:S(2)}) collective-permute-start(bf16[256,2048]{1,0:T(8,128)(2,1)S(1)} %copy-done.38), channel_id=1, source_target_pairs={{0,16},{16,0},{1,17},{17,1},{2,18},{18,2},{3,19},{19,3},{4,20},{20... | collective-permute-start | bytes 3145736 | tf_op jit(solution)/shard_map/ppermute | solution.py:1399
  1022.9 47.3 %collective-permute-start.64 = (bf16[128,2048]{1,0:T(8,128)(2,1)}, bf16[128,2048]{1,0:T(8,128)(2,1)}, u32[]{:S(2)}, u32[]{:S(2)}) collective-permute-start(bf16[128,2048]{1,0:T(8,128)(2,1)} %add_pieces.23), channel_id=1, source_target_pairs={{0,1},{1,2},{2,3},{3,0},{4,5},{5,6},{6,7},{7,4},{8,9},{9,10},{10,1... | collective-permute-start | bytes 1572872 | tf_op jit(solution)/shard_map/ppermute | solution.py:1404
  1051.8 40.3 %collective-permute-start.70 = (bf16[128,2048]{1,0:T(8,128)(2,1)}, bf16[128,2048]{1,0:T(8,128)(2,1)}, u32[]{:S(2)}, u32[]{:S(2)}) collective-permute-start(bf16[128,2048]{1,0:T(8,128)(2,1)} %add_pieces.24), channel_id=1, source_target_pairs={{0,3},{1,0},{2,1},{3,2},{4,7},{5,4},{6,5},{7,6},{8,11},{9,8},{10,9... | collective-permute-start | bytes 1572872 | tf_op jit(solution)/shard_map/ppermute | solution.py:1404
  1087.0 73.8 %all-to-all-start.6 = ((bf16[32,72,512]{2,1,0:T(8,128)(2,1)}), bf16[32,72,512]{2,1,0:T(8,128)(2,1)S(1)}, u32[]{:S(2)}, u32[]{:S(2)}) async-start(bf16[32,72,512]{2,1,0:T(8,128)(2,1)} %bitcast.125), calls=%async_computation.6 | async-start | bytes 4718592 | tf_op jit(solution)/shard_map/all_to_all | solution.py:1545
  1108.8 43.1 %collective-permute-start.73 = (bf16[1024,2048]{1,0:T(8,128)(2,1)}, bf16[1024,2048]{1,0:T(8,128)(2,1)S(1)}, u32[]{:S(2)}, u32[]{:S(2)}) collective-permute-start(bf16[1024,2048]{1,0:T(8,128)(2,1)} %join_rows.28.near_ref), channel_id=1, source_target_pairs={{0,4},{4,0},{1,5},{5,1},{2,6},{6,2},{3,7},{7,3},{8,12},{12,8},{9,1... | collective-permute-start | bytes 12582920 | tf_op jit(solution)/shard_map/ppermute | solution.py:1399
  1108.8 37.6 %collective-permute-start.59 = (bf16[256,2048]{1,0:T(8,128)(2,1)S(1)}, bf16[256,2048]{1,0:T(8,128)(2,1)S(1)}, u32[]{:S(2)}, u32[]{:S(2)}) collective-permute-start(bf16[256,2048]{1,0:T(8,128)(2,1)S(1)} %copy-done.39), channel_id=1, source_target_pairs={{0,8},{8,0},{1,9},{9,1},{2,10},{10,2},{3,11},{11,3},{4,12},{12,4},... | collective-permute-start | bytes 3145736 | tf_op jit(solution)/shard_map/ppermute | solution.py:1399
  1111.5 37.9 %collective-permute-start.60 = (bf16[256,2048]{1,0:T(8,128)(2,1)S(1)}, bf16[256,2048]{1,0:T(8,128)(2,1)S(1)}, u32[]{:S(2)}, u32[]{:S(2)}) collective-permute-start(bf16[256,2048]{1,0:T(8,128)(2,1)S(1)} %copy-done.39), channel_id=1, source_target_pairs={{0,16},{16,0},{1,17},{17,1},{2,18},{18,2},{3,19},{19,3},{4,20},{20... | collective-permute-start | bytes 3145736 | tf_op jit(solution)/shard_map/ppermute | solution.py:1399
  1114.0 70.7 %collective-permute-start.72 = (bf16[128,2048]{1,0:T(8,128)(2,1)}, bf16[128,2048]{1,0:T(8,128)(2,1)}, u32[]{:S(2)}, u32[]{:S(2)}) collective-permute-start(bf16[128,2048]{1,0:T(8,128)(2,1)} %add_pieces.28), channel_id=1, source_target_pairs={{0,3},{1,0},{2,1},{3,2},{4,7},{5,4},{6,5},{7,6},{8,11},{9,8},{10,9... | collective-permute-start | bytes 1572872 | tf_op jit(solution)/shard_map/ppermute | solution.py:1404
  1120.3 64.4 %collective-permute-start.71 = (bf16[128,2048]{1,0:T(8,128)(2,1)}, bf16[128,2048]{1,0:T(8,128)(2,1)}, u32[]{:S(2)}, u32[]{:S(2)}) collective-permute-start(bf16[128,2048]{1,0:T(8,128)(2,1)} %add_pieces.30), channel_id=1, source_target_pairs={{0,1},{1,2},{2,3},{3,0},{4,5},{5,6},{6,7},{7,4},{8,9},{9,10},{10,1... | collective-permute-start | bytes 1572872 | tf_op jit(solution)/shard_map/ppermute | solution.py:1404
  1150.3 37.9 %collective-permute-start.80 = (bf16[128,2048]{1,0:T(8,128)(2,1)}, bf16[128,2048]{1,0:T(8,128)(2,1)S(1)}, u32[]{:S(2)}, u32[]{:S(2)}) collective-permute-start(bf16[128,2048]{1,0:T(8,128)(2,1)} %slice.156), channel_id=1, source_target_pairs={{0,8},{8,0},{1,9},{9,1},{2,10},{10,2},{3,11},{11,3},{4,12},{12,4},... | collective-permute-start | bytes 1572872 | tf_op jit(solution)/shard_map/ppermute | solution.py:1399
  1151.2 37.1 %collective-permute-start.81 = (bf16[128,2048]{1,0:T(8,128)(2,1)}, bf16[128,2048]{1,0:T(8,128)(2,1)S(1)}, u32[]{:S(2)}, u32[]{:S(2)}) collective-permute-start(bf16[128,2048]{1,0:T(8,128)(2,1)} %slice.157), channel_id=1, source_target_pairs={{0,16},{16,0},{1,17},{17,1},{2,18},{18,2},{3,19},{19,3},{4,20},{20... | collective-permute-start | bytes 1572872 | tf_op jit(solution)/shard_map/ppermute | solution.py:1399
  1153.9 33.5 %collective-permute-start.76 = (f32[192,128]{1,0:T(8,128)S(1)}, f32[192,128]{1,0:T(8,128)}, u32[]{:S(2)}, u32[]{:S(2)}) collective-permute-start(f32[192,128]{1,0:T(8,128)S(1)} %add.533), channel_id=1, source_target_pairs={{0,8},{8,0},{1,9},{9,1},{2,10},{10,2},{3,11},{11,3},{4,12},{12,4},... | collective-permute-start | bytes 294920 | tf_op jit(solution)/shard_map/ppermute | solution.py:1399
  1233.8 51.4 %collective-permute-start.85 = (bf16[512,2048]{1,0:T(8,128)(2,1)}, bf16[512,2048]{1,0:T(8,128)(2,1)}, u32[]{:S(2)}, u32[]{:S(2)}) collective-permute-start(bf16[512,2048]{1,0:T(8,128)(2,1)} %join_rows.30.near_low.near_high), channel_id=1, source_target_pairs={{0,4},{4,0},{1,5},{5,1},{2,6},{6,2},{3,7},{7,3},{8,12},{12,8},{9,1... | collective-permute-start | bytes 6291464 | tf_op jit(solution)/shard_map/ppermute | solution.py:1399
  1237.3 45.4 %all-to-all-start.7 = ((bf16[2,1024,1,512]{3,0,2,1:T(2,128)(2,1)}), bf16[2,1024,1,512]{3,0,2,1:T(2,128)(2,1)S(1)}, u32[]{:S(2)}, u32[]{:S(2)}) async-start(bf16[2,1024,1,512]{3,0,2,1:T(2,128)(2,1)} %copy.170), calls=%async_computation.7 | async-start | bytes 4194304 | tf_op jit(solution)/shard_map/all_to_all | solution.py:1611
  1241.1 39.0 %collective-permute-start.74 = (bf16[128,2048]{1,0:T(8,128)(2,1)S(1)}, bf16[128,2048]{1,0:T(8,128)(2,1)S(1)}, u32[]{:S(2)}, u32[]{:S(2)}) collective-permute-start(bf16[128,2048]{1,0:T(8,128)(2,1)S(1)} %copy-done.45), channel_id=1, source_target_pairs={{0,8},{8,0},{1,9},{9,1},{2,10},{10,2},{3,11},{11,3},{4,12},{12,4},... | collective-permute-start | bytes 1572872 | tf_op jit(solution)/shard_map/ppermute | solution.py:1399
  1243.0 37.1 %collective-permute-start.75 = (bf16[128,2048]{1,0:T(8,128)(2,1)S(1)}, bf16[128,2048]{1,0:T(8,128)(2,1)S(1)}, u32[]{:S(2)}, u32[]{:S(2)}) collective-permute-start(bf16[128,2048]{1,0:T(8,128)(2,1)S(1)} %copy-done.45), channel_id=1, source_target_pairs={{0,16},{16,0},{1,17},{17,1},{2,18},{18,2},{3,19},{19,3},{4,20},{20... | collective-permute-start | bytes 1572872 | tf_op jit(solution)/shard_map/ppermute | solution.py:1399
  1244.5 35.5 %collective-permute-start.77 = (f32[192,128]{1,0:T(8,128)S(1)}, f32[192,128]{1,0:T(8,128)S(1)}, u32[]{:S(2)}, u32[]{:S(2)}) collective-permute-start(f32[192,128]{1,0:T(8,128)S(1)} %add.534), channel_id=1, source_target_pairs={{0,16},{16,0},{1,17},{17,1},{2,18},{18,2},{3,19},{19,3},{4,20},{20... | collective-permute-start | bytes 294920 | tf_op jit(solution)/shard_map/ppermute | solution.py:1399
  (118 other events, 1213.7 us)

commit v4 on v3

--- a/solution.py
+++ b/solution.py
@@ -1661,12 +1661,13 @@
     resid_a, second_a = order.mark(resid_norm(tok, 0, *sum_end(sum_a1), out_b, gain_two, shift_two))
     second_a = team_start(second_a)
     down_3, down_y3 = swapped(down_3)
-    cot_got = box_exchange(order.take(cot_sent))
     sum_b1 = sum_start(mixed_b, out_w)
     up_w = order.mark(join_rows([up_mine, up_1, up_2, up_3, up_other, *order.take((up_y1, up_y2, up_y3))]))
     sum_b1 = sum_middle(sum_b1)
     down_y1 = order.step(down_y1)
-    second_a = team_end(team_middle(second_a))
+    second_a = team_middle(second_a)
+    cot_got = box_exchange(order.take(cot_sent))
+    second_a = team_end(second_a)
 
     hidden_a, slope_a = order.mark(expand(*order.take(second_a), up_w, up_b))
     down_2, down_y2 = swapped(down_2)
@@ -1824,11 +1825,11 @@
     sum_b3 = sum_middle(sum_b3)
     two_far = two_half(1)
     two_swap = swap_along(two_far, "y")
-    down_total = ring_end(down_ring)
-    down_plane = plane_start(down_total)
     layer_held = order.mark(unbox(order.take(layer_got)))
     layer_out = spread_back(layer_held)
     one_near = one_half(0)
+    down_total = ring_end(down_ring)
+    down_plane = plane_start(down_total)
     up_ring = ring_middle(up_ring)
     input_b, back_sums_b = first_back(sum_b3, resid_grad_b, 1)
     input_sent = order.mark(unsettle(join_rows([input_a, input_b])))
@@ -1850,10 +1851,10 @@
     small_got = swap_along(small, "x")
     down_plane = plane_end(down_plane, order)
     own = jnp.full((1,), eighth, jnp.int32)
-    up_plane = plane_middle(up_plane, order)
+    down_grad = order.mark(stack_pieces(*order.take(down_plane), own, False))
     input_held = order.mark(unbox(order.take(input_got)))
     input_grad = spread_back(input_held)
-    down_grad = order.mark(stack_pieces(*order.take(down_plane), own, False))
+    up_plane = plane_middle(up_plane, order)
     two_total = ring_end(two_ring)
     two_plane = plane_start(two_total)
     small = order.mark(small + order.take(small_got))
@@ -1861,15 +1862,15 @@
     up_plane = plane_end(up_plane, order)
     one_plane = plane_middle(one_plane, order)
     up_grad = order.mark(stack_pieces(*order.take(up_plane), own, True))
-    one_plane = plane_end(one_plane, order)
+    two_plane = plane_middle(two_plane, order)
     small = order.mark(small + order.take(small_got))
     small_got = lax.ppermute(small, "z", [(i, i ^ 1) for i in range(depth)])
-    two_plane = plane_middle(two_plane, order)
+    one_plane = plane_end(one_plane, order)
     input_grad = order.step(input_grad)
     query_grad, key_grad = order.mark(stack_heads(*order.take(one_plane), own, (True, True)))
-    two_plane = plane_end(two_plane, order)
     small = order.mark(small + order.take(small_got))
     small_got = lax.ppermute(small, "z", [(i, i ^ 2) for i in range(depth)])
+    two_plane = plane_end(two_plane, order)
     value_grad, out_w_grad = order.mark(stack_heads(*order.take(two_plane), own, (True, False)))
     packed = small + order.take(small_got)
     packed = packed.reshape(-1)

time: 1330 us -> 1320 us (level)
    ppermute x68, waiting for transfers between devices: 197 us -> 107 us  [swap_along(): return lax.ppermute(array, axis, SWAP)]
    ppermute x21, waiting for transfers between devices: 138 us -> 185 us  [shift(): lax.ppermute(array, 'z', [(i, (i + step) % size) for i in range(size)])]
    all_to_all x4, waiting for transfers between devices: 5.56 us -> 32.7 us  [box_exchange(): return lax.all_to_all(sent, EVERY, split_axis=0, concat_axis=0, tiled=True)]
    all_to_all x2, waiting for transfers between devices: 0.01 us -> 22.2 us  [spread_back(): back = lax.all_to_all(held, PLANE, split_axis=1, concat_axis=2, tiled=True)]
    unnamed x175 -> x169, local copies, waits for them, and re-layouts: 47.7 us -> 46.6 us
where the time goes in v4:
time: 1320 us; the launch traced here: 1310 us
  Pallas kernels  674 us (51%)
  waiting for transfers between devices  364 us (28%)
  starting transfers between devices  161 us (12%)
  local copies, waits for them, and re-layouts  98.2 us (7%)
    ppermute x21, waiting for transfers between devices, shift(): lax.ppermute(array, 'z', [(i, (i + step) % size) for i in range(size)])  185 us
    ppermute x68, waiting for transfers between devices, swap_along(): return lax.ppermute(array, axis, SWAP)  107 us
    pallas_call x18, Pallas kernels, rows_call(): pl.pallas_call(kernel, grid=(steps,), in_specs=[spec(array, first) for ar...  74.7 us
    pallas_call x16, Pallas kernels, join_rows(): pl.pallas_call(functools.partial(join_kernel, count), grid=(4,), in_specs...  69.8 us
    pallas_call x6, Pallas kernels, partial_sums(): pl.pallas_call(partial_kernel, grid=(cols // WIDE,), in_specs=[whole((row...  64.9 us
    ppermute x21, starting transfers between devices, shift(): lax.ppermute(array, 'z', [(i, (i + step) % size) for i in range(size)])  64.3 us
    pallas_call x4, Pallas kernels, cross_sums(): pl.pallas_call(cross_kernel, grid=(size // tall,), in_specs=[left_spec, r...  57.6 us
    pallas_call x2, Pallas kernels, attend_back(): pl.pallas_call(attend_back_kernel, grid_spec=pltpu.PrefetchScalarGridSpec...  54.6 us
  transfers between devices with their start and end apart: 99, of which 29 were waited for; matrix products, arithmetic and copies ran while one was open for 4% of the time, Pallas kernels for 46%

profile of v4, /device:TPU:0, one launch (start us, length us, event | category | flops | bytes accessed | tf_op | source)
XLA Modules:
  0.0 1308.4 jit_solution(15304368331339024206)
XLA Ops:
  20.1 18.3 %collective-permute-done.refs_1_ = bf16[264,2048]{1,0:T(8,128)(2,1)S(1)} collective-permute-done((bf16[264,2048]{1,0:T(8,128)(2,1)}, bf16[264,2048]{1,0:T(8,128)(2,1)S(1)}, u32[]{:S(2)}, u32[]{:S(2)}) %collective-permute-start) | collective-permute-done | bytes 1081376 | tf_op jit(solution)/shard_map/ppermute | solution.py:1404
  46.3 19.0 %collective-permute-done.1.refs_2_ = bf16[264,2048]{1,0:T(8,128)(2,1)} collective-permute-done((bf16[264,2048]{1,0:T(8,128)(2,1)S(1)}, bf16[264,2048]{1,0:T(8,128)(2,1)}, u32[]{:S(2)}, u32[]{:S(2)}) %collective-permute-start.1) | collective-permute-done | bytes 1081376 | tf_op jit(solution)/shard_map/ppermute | solution.py:1404
  65.3 8.7 pick_rows.2
  84.2 56.7 %collective-permute-done.2.refs_3_ = bf16[264,2048]{1,0:T(8,128)(2,1)} collective-permute-done((bf16[264,2048]{1,0:T(8,128)(2,1)S(1)}, bf16[264,2048]{1,0:T(8,128)(2,1)}, u32[]{:S(2)}, u32[]{:S(2)}) %collective-permute-start.2) | collective-permute-done | bytes 1081376 | tf_op jit(solution)/shard_map/ppermute | solution.py:1404
  157.5 17.0 %collective-permute-done.6.refs_7_ = bf16[264,2048]{1,0:T(8,128)(2,1)S(1)} collective-permute-done((bf16[264,2048]{1,0:T(8,128)(2,1)}, bf16[264,2048]{1,0:T(8,128)(2,1)S(1)}, u32[]{:S(2)}, u32[]{:S(2)}) %collective-permute-start.6) | collective-permute-done | bytes 1081376 | tf_op jit(solution)/shard_map/ppermute | solution.py:1399
  175.5 7.2 attn_join.1
  196.3 9.5 collective-permute-start.9
  208.4 12.7 all-to-all-done.2
  224.2 8.7 pick_rows.3
  233.6 9.7 collective-permute-start.11
  245.6 6.5 collective-permute-done.8.refs_3_
  252.1 11.7 project.4.query_ref.key_ref.value_ref
  265.7 18.3 %attend.2.left_ref.refs_2_ = bf16[1024,512]{1,0:T(8,128)(2,1)S(1)} custom-call(s32[1]{0:T(128)} %bitcast.10.rank_ref, bf16[1024,1536]{1,0:T(8,128)(2,1)S(1)} %copy-done.1, bf16[1024,1536]{1,0:T(8,128)(2,1)S(1)} %copy-done.1, bf16[1024,1536]{1,0:T(8,128)(2,1)S(1)} %copy-done.1, s32[1024,2]{1,0:T(8,128)S(1)} %copy.162.key_info_ref, ...), custom_call_target="tpu_custom_call" | custom-call | flops 1048576 | bytes 4096 | tf_op jit(solution)/shard_map/attend/pallas_call | solution.py:565
  288.9 6.0 partial_sums.6
  301.9 11.6 project.5.query_ref.key_ref.value_ref
  313.5 8.1 collective-permute-done.14.refs_7_
  337.7 18.3 %attend.3.left_ref.refs_3_ = bf16[1024,512]{1,0:T(8,128)(2,1)S(1)} custom-call(s32[1]{0:T(128)} %bitcast.10.rank_ref, bf16[1024,1536]{1,0:T(8,128)(2,1)S(1)} %copy-done, bf16[1024,1536]{1,0:T(8,128)(2,1)S(1)} %copy-done, bf16[1024,1536]{1,0:T(8,128)(2,1)S(1)} %copy-done, s32[1024,2]{1,0:T(8,128)S(1)} %copy-done.13, s32[2,1024]{1,0:T(2,128)S(1)} %pad_add_fusion.3.query_info_ref), custom_call_target="tpu_custom_call" | custom-call | flops 1048576 | bytes 4096 | tf_op jit(solution)/shard_map/attend/pallas_call | solution.py:565
  371.6 7.0 join_rows.18.weight_ref
  382.7 10.5 collective-permute-done.20.refs_5_
  408.8 17.4 %expand.2 = (bf16[1024,2048]{1,0:T(8,128)(2,1)}, bf16[1024,2048]{1,0:T(8,128)(2,1)}) custom-call(bf16[512,2048]{1,0:T(8,128)(2,1)} %join_rows.19.near_ref.near_a, bf16[512,2048]{1,0:T(8,128)(2,1)} %copy-done.21, bf16[2048,2048]{1,0:T(8,128)(2,1)} %join_rows.18.weight_ref, f32[1,2048]{1,0:T(1,128)} %bitcast.166), custom_call_target="tpu_custom_call" | custom-call | flops 1048576 | bytes 4096 | tf_op jit(solution)/shard_map/expand/pallas_call | solution.py:769
  426.2 41.0 %collective-permute-done.24.refs_2_ = bf16[256,2048]{1,0:T(8,128)(2,1)S(1)} collective-permute-done((bf16[256,2048]{1,0:T(8,128)(2,1)}, bf16[256,2048]{1,0:T(8,128)(2,1)S(1)}, u32[]{:S(2)}, u32[]{:S(2)}) %collective-permute-start.24) | collective-permute-done | bytes 1048608 | tf_op jit(solution)/shard_map/ppermute | solution.py:1404
  484.0 13.4 %collective-permute-done.28.refs_1_ = bf16[256,2048]{1,0:T(8,128)(2,1)} collective-permute-done((bf16[256,2048]{1,0:T(8,128)(2,1)}, bf16[256,2048]{1,0:T(8,128)(2,1)}, u32[]{:S(2)}, u32[]{:S(2)}) %collective-permute-start.28) | collective-permute-done | bytes 1048608 | tf_op jit(solution)/shard_map/ppermute | solution.py:1399
  507.0 17.5 %expand.3 = (bf16[1024,2048]{1,0:T(8,128)(2,1)}, bf16[1024,2048]{1,0:T(8,128)(2,1)}) custom-call(bf16[512,2048]{1,0:T(8,128)(2,1)} %join_rows.20.near_ref.near_b, bf16[512,2048]{1,0:T(8,128)(2,1)} %copy-done.22, bf16[2048,2048]{1,0:T(8,128)(2,1)} %join_rows.18.weight_ref, f32[1,2048]{1,0:T(1,128)} %bitcast.167), custom_call_target="tpu_custom_call" | custom-call | flops 1048576 | bytes 4096 | tf_op jit(solution)/shard_map/expand/pallas_call | solution.py:769
  527.4 7.0 join_rows.21.weight_ref
  534.4 13.2 %partial_sums.8 = (f32[512,2048]{1,0:T(8,128)}, bf16[512,2048]{1,0:T(8,128)(2,1)}) custom-call(bf16[1024,2048]{1,0:T(8,128)(2,1)} %get-tuple-element.367.left_ref.left_a, bf16[2048,2048]{1,0:T(8,128)(2,1)} %join_rows.21.weight_ref), custom_call_target="tpu_custom_call" | custom-call | flops 1048576 | bytes 4096 | tf_op jit(solution)/shard_map/partial_sums/pallas_call | solution.py:830
  554.1 13.2 %partial_sums.9 = (f32[512,2048]{1,0:T(8,128)}, bf16[512,2048]{1,0:T(8,128)(2,1)}) custom-call(bf16[1024,2048]{1,0:T(8,128)(2,1)} %get-tuple-element.336.left_ref.left_b, bf16[2048,2048]{1,0:T(8,128)(2,1)} %join_rows.21.weight_ref), custom_call_target="tpu_custom_call" | custom-call | flops 1048576 | bytes 4096 | tf_op jit(solution)/shard_map/partial_sums/pallas_call | solution.py:830
  568.6 14.4 %expand_back.2 = (bf16[1024,2048]{1,0:T(8,128)(2,1)}, f32[8,2048]{1,0:T(8,128)}) custom-call(bf16[512,2048]{1,0:T(8,128)(2,1)} %join_rows.22.near_ref.near_a, bf16[512,2048]{1,0:T(8,128)(2,1)} %copy-done.23, bf16[2048,2048]{1,0:T(8,128)(2,1)} %join_rows.21.weight_ref, bf16[1024,2048]{1,0:T(8,128)(2,1)} %get-tuple-element.315.slope_ref), custom_call_target="tpu_custom_call" | custom-call | flops 1048576 | bytes 4096 | tf_op jit(solution)/shard_map/expand_back/pallas_call | solution.py:800
  588.0 13.4 %partial_sums.10 = (f32[512,2048]{1,0:T(8,128)}, bf16[512,2048]{1,0:T(8,128)(2,1)}) custom-call(bf16[1024,2048]{1,0:T(8,128)(2,1)} %get-tuple-element.396.left_ref.left_a, bf16[2048,2048]{1,0:T(8,128)(2,1)} %join_rows.18.weight_ref), custom_call_target="tpu_custom_call" | custom-call | flops 1048576 | bytes 4096 | tf_op jit(solution)/shard_map/partial_sums/pallas_call | solution.py:830
  603.1 14.4 %expand_back.3 = (bf16[1024,2048]{1,0:T(8,128)(2,1)}, f32[8,2048]{1,0:T(8,128)}) custom-call(bf16[512,2048]{1,0:T(8,128)(2,1)} %join_rows.23.near_ref.near_b, bf16[512,2048]{1,0:T(8,128)(2,1)} %copy-done.24, bf16[2048,2048]{1,0:T(8,128)(2,1)} %join_rows.21.weight_ref, bf16[1024,2048]{1,0:T(8,128)(2,1)} %get-tuple-element.328.slope_ref), custom_call_target="tpu_custom_call" | custom-call | flops 1048576 | bytes 4096 | tf_op jit(solution)/shard_map/expand_back/pallas_call | solution.py:800
  622.9 13.2 %partial_sums.11 = (f32[512,2048]{1,0:T(8,128)}, bf16[512,2048]{1,0:T(8,128)(2,1)}) custom-call(bf16[1024,2048]{1,0:T(8,128)(2,1)} %get-tuple-element.356.left_ref.left_b, bf16[2048,2048]{1,0:T(8,128)(2,1)} %join_rows.18.weight_ref), custom_call_target="tpu_custom_call" | custom-call | flops 1048576 | bytes 4096 | tf_op jit(solution)/shard_map/partial_sums/pallas_call | solution.py:830
  637.1 14.3 %cross_sums.4 = bf16[1024,2048]{1,0:T(8,128)(2,1)} custom-call(bf16[1024,2048]{1,0:T(8,128)(2,1)} %get-tuple-element.367.left_ref.left_a, bf16[512,2048]{1,0:T(8,128)(2,1)} %join_rows.22.near_ref.near_a, bf16[512,2048]{1,0:T(8,128)(2,1)} %copy-done.23, bf16[1024,2048]{1,0:T(8,128)(2,1)} %get-tuple-element.336.left_ref.left_b, ...), custom_call_target="tpu_custom_call" | custom-call | flops 1048576 | bytes 4096 | tf_op jit(solution)/shard_map/cross_sums/pallas_call | solution.py:864
  668.9 14.3 %cross_sums.5.refs_0_ = bf16[1024,2048]{1,0:T(8,128)(2,1)} custom-call(bf16[1024,2048]{1,0:T(8,128)(2,1)} %get-tuple-element.367.left_ref.left_a, bf16[512,2048]{1,0:T(8,128)(2,1)} %join_rows.22.near_ref.near_a, bf16[512,2048]{1,0:T(8,128)(2,1)} %copy-done.23, bf16[1024,2048]{1,0:T(8,128)(2,1)} %get-tuple-element.336.left_ref.left_b, ...), custom_call_target="tpu_custom_call" | custom-call | flops 1048576 | bytes 4096 | tf_op jit(solution)/shard_map/cross_sums/pallas_call | solution.py:864
  696.2 14.8 %cross_sums.6 = bf16[1024,2048]{1,0:T(8,128)(2,1)} custom-call(bf16[1024,2048]{1,0:T(8,128)(2,1)} %get-tuple-element.396.left_ref.left_a, bf16[512,2048]{1,0:T(8,128)(2,1)} %join_rows.19.near_ref.near_a, bf16[512,2048]{1,0:T(8,128)(2,1)} %copy-done.21, bf16[1024,2048]{1,0:T(8,128)(2,1)} %get-tuple-element.356.left_ref.left_b, ...), custom_call_target="tpu_custom_call" | custom-call | flops 1048576 | bytes 4096 | tf_op jit(solution)/shard_map/cross_sums/pallas_call | solution.py:864
  722.0 6.3 project.6.grad_ref
  729.6 27.3 %attend_back.2 = (bf16[1024,512]{1,0:T(8,128)(2,1)S(1)}, bf16[1024,512]{1,0:T(8,128)(2,1)S(1)}, bf16[1024,512]{1,0:T(8,128)(2,1)S(1)}, f32[8,512]{1,0:T(8,128)S(1)}) custom-call(s32[1]{0:T(128)} %bitcast.10.rank_ref, bf16[1024,1536]{1,0:T(8,128)(2,1)S(1)} %copy-done.2, bf16[1024,1536]{1,0:T(8,128)(2,1)S(1)} %copy-done.2, bf16[1024,1536]{1,0:T(8,128)(2,1)S(1)} %copy-done.2, ...), custom_call_target="tpu_custom_call" | custom-call | flops 1048576 | bytes 4096 | tf_op jit(solution)/shard_map/attend_back/pallas_call | solution.py:673
  769.6 10.7 partial_three.2
  784.3 10.2 collective-permute-start.48
  796.0 14.3 %cross_sums.7.refs_0_ = bf16[1024,2048]{1,0:T(8,128)(2,1)} custom-call(bf16[1024,2048]{1,0:T(8,128)(2,1)} %get-tuple-element.396.left_ref.left_a, bf16[512,2048]{1,0:T(8,128)(2,1)} %join_rows.19.near_ref.near_a, bf16[512,2048]{1,0:T(8,128)(2,1)} %copy-done.21, bf16[1024,2048]{1,0:T(8,128)(2,1)} %get-tuple-element.356.left_ref.left_b, ...), custom_call_target="tpu_custom_call" | custom-call | flops 1048576 | bytes 4096 | tf_op jit(solution)/shard_map/cross_sums/pallas_call | solution.py:864
  817.8 12.3 collective-permute-done.47.got_ref
  845.4 13.7 %all-to-all-start.4 = ((bf16[32,72,512]{2,1,0:T(8,128)(2,1)}), bf16[32,72,512]{2,1,0:T(8,128)(2,1)}, u32[]{:S(2)}, u32[]{:S(2)}) async-start(bf16[32,72,512]{2,1,0:T(8,128)(2,1)} %bitcast.127), calls=%async_computation.4 | async-start | bytes 4718592 | tf_op jit(solution)/shard_map/all_to_all | solution.py:1545
  860.9 6.2 project.7.grad_ref
  868.3 27.3 %attend_back.3 = (bf16[1024,512]{1,0:T(8,128)(2,1)S(1)}, bf16[1024,512]{1,0:T(8,128)(2,1)S(1)}, bf16[1024,512]{1,0:T(8,128)(2,1)S(1)}, f32[8,512]{1,0:T(8,128)S(1)}) custom-call(s32[1]{0:T(128)} %bitcast.10.rank_ref, bf16[1024,1536]{1,0:T(8,128)(2,1)S(1)} %copy-done, bf16[1024,1536]{1,0:T(8,128)(2,1)S(1)} %copy-done, bf16[1024,1536]{1,0:T(8,128)(2,1)S(1)} %copy-done, ...), custom_call_target="tpu_custom_call" | custom-call | flops 1048576 | bytes 4096 | tf_op jit(solution)/shard_map/attend_back/pallas_call | solution.py:673
  898.6 10.0 collective-permute-done.50.got_ref
  918.8 10.5 partial_three.3
  929.4 9.1 cross_pair.4
  950.4 10.7 cross_pair.5
  961.1 6.9 collective-permute-done.56.refs_3_
  970.3 8.7 drop_rows.2
  994.0 8.8 cross_pair.6.refs_0_
  1006.4 7.0 collective-permute-done.54.refs_2_
  1038.7 19.6 %collective-permute-done.61.refs_2_ = bf16[256,2048]{1,0:T(8,128)(2,1)} collective-permute-done((bf16[256,2048]{1,0:T(8,128)(2,1)}, bf16[256,2048]{1,0:T(8,128)(2,1)}, u32[]{:S(2)}, u32[]{:S(2)}) %collective-permute-start.61) | collective-permute-done | bytes 1048608 | tf_op jit(solution)/shard_map/ppermute | solution.py:1404
  1065.7 10.6 cross_pair.7.refs_0_
  1093.2 6.2 all-to-all-start.6
  1103.2 7.4 collective-permute-done.66.refs_2_
  1119.8 8.5 collective-permute-start.78
  1130.3 13.8 %stack_pieces.2 = f32[2048,2048]{1,0:T(8,128)} custom-call(s32[1]{0:T(128)} %bitcast.51.own_ref, bf16[1024,2048]{1,0:T(8,128)(2,1)} %join_rows.28.near_ref, bf16[1024,2048]{1,0:T(8,128)(2,1)} %copy-done.36), custom_call_target="tpu_custom_call" | custom-call | flops 1048576 | bytes 4096 | tf_op jit(solution)/shard_map/stack_pieces/pallas_call | solution.py:1047
  1144.2 27.1 %all-to-all-done.6 = bf16[32,72,512]{2,1,0:T(8,128)(2,1)S(1)} async-done(((bf16[32,72,512]{2,1,0:T(8,128)(2,1)}), bf16[32,72,512]{2,1,0:T(8,128)(2,1)S(1)}, u32[]{:S(2)}, u32[]{:S(2)}) %all-to-all-start.6) | async-done | bytes 2359328 | tf_op jit(solution)/shard_map/all_to_all | solution.py:1545
  1172.7 8.7 drop_rows.3
  1188.5 9.9 collective-permute-done.76
  1208.9 10.7 collective-permute-done.70.refs_1_
  1224.1 14.3 %stack_pieces.3 = f32[2048,2048]{1,0:T(8,128)} custom-call(s32[1]{0:T(128)} %bitcast.51.own_ref, bf16[1024,2048]{1,0:T(8,128)(2,1)} %join_rows.29.near_ref, bf16[1024,2048]{1,0:T(8,128)(2,1)} %copy-done.35), custom_call_target="tpu_custom_call" | custom-call | flops 1048576 | bytes 4096 | tf_op jit(solution)/shard_map/stack_pieces/pallas_call | solution.py:1047
  1255.8 22.2 %all-to-all-done.7 = bf16[2,1024,1,512]{3,0,2,1:T(2,128)(2,1)S(1)} async-done(((bf16[2,1024,1,512]{3,0,2,1:T(2,128)(2,1)}), bf16[2,1024,1,512]{3,0,2,1:T(2,128)(2,1)S(1)}, u32[]{:S(2)}, u32[]{:S(2)}) %all-to-all-start.7) | async-done | bytes 2097184 | tf_op jit(solution)/shard_map/all_to_all | solution.py:1611
  1280.5 7.0 stack_heads.2
  1298.6 7.0 stack_heads.3
  (551 shorter events, 446.3 us)
Async XLA Ops:
  9.3 29.1 %collective-permute-start = (bf16[264,2048]{1,0:T(8,128)(2,1)}, bf16[264,2048]{1,0:T(8,128)(2,1)S(1)}, u32[]{:S(2)}, u32[]{:S(2)}) collective-permute-start(bf16[264,2048]{1,0:T(8,128)(2,1)} %get-tuple-element.258.refs_0_), channel_id=1, source_target_pairs={{0,1},{1,2},{2,3},{3,0},{4,5},{5,6},{6,7},{7,4},{8,9},{9,10},{10,1... | collective-permute-start | bytes 3244040 | tf_op jit(solution)/shard_map/ppermute | solution.py:1404
  14.3 30.5 %all-to-all-start = ((bf16[2,128,8,512]{3,1,0,2:T(8,128)(2,1)}), bf16[2,128,8,512]{3,1,0,2:T(8,128)(2,1)S(1)}, u32[]{:S(2)}, u32[]{:S(2)}) async-start(bf16[2,128,8,512]{3,1,0,2:T(8,128)(2,1)} %copy.155), calls=%async_computation | async-start | bytes 4194304 | tf_op jit(solution)/shard_map/all_to_all | solution.py:1541
  74.0 70.3 %all-to-all-start.1 = ((bf16[32,72,512]{2,1,0:T(8,128)(2,1)}), bf16[32,72,512]{2,1,0:T(8,128)(2,1)S(1)}, u32[]{:S(2)}, u32[]{:S(2)}) async-start(bf16[32,72,512]{2,1,0:T(8,128)(2,1)} %bitcast.129), calls=%async_computation.1 | async-start | bytes 4718592 | tf_op jit(solution)/shard_map/all_to_all | solution.py:1545
  77.9 63.0 %collective-permute-start.2 = (bf16[264,2048]{1,0:T(8,128)(2,1)S(1)}, bf16[264,2048]{1,0:T(8,128)(2,1)}, u32[]{:S(2)}, u32[]{:S(2)}) collective-permute-start(bf16[264,2048]{1,0:T(8,128)(2,1)S(1)} %copy-done.49), channel_id=1, source_target_pairs={{0,3},{1,0},{2,1},{3,2},{4,7},{5,4},{6,5},{7,6},{8,11},{9,8},{10,9... | collective-permute-start | bytes 3244040 | tf_op jit(solution)/shard_map/ppermute | solution.py:1404
  82.1 75.4 %collective-permute-start.4 = (bf16[264,2048]{1,0:T(8,128)(2,1)}, bf16[264,2048]{1,0:T(8,128)(2,1)}, u32[]{:S(2)}, u32[]{:S(2)}) collective-permute-start(bf16[264,2048]{1,0:T(8,128)(2,1)} %copy-done.50), channel_id=1, source_target_pairs={{0,16},{16,0},{1,17},{17,1},{2,18},{18,2},{3,19},{19,3},{4,20},{20... | collective-permute-start | bytes 3244040 | tf_op jit(solution)/shard_map/ppermute | solution.py:1399
  83.7 73.8 %collective-permute-start.5 = (bf16[264,2048]{1,0:T(8,128)(2,1)}, bf16[264,2048]{1,0:T(8,128)(2,1)}, u32[]{:S(2)}, u32[]{:S(2)}) collective-permute-start(bf16[264,2048]{1,0:T(8,128)(2,1)} %collective-permute-done.1.refs_2_), channel_id=1, source_target_pairs={{0,16},{16,0},{1,17},{17,1},{2,18},{18,2},{3,19},{19,3},{4,20},{20... | collective-permute-start | bytes 3244040 | tf_op jit(solution)/shard_map/ppermute | solution.py:1399
  141.0 33.6 %collective-permute-start.6 = (bf16[264,2048]{1,0:T(8,128)(2,1)}, bf16[264,2048]{1,0:T(8,128)(2,1)S(1)}, u32[]{:S(2)}, u32[]{:S(2)}) collective-permute-start(bf16[264,2048]{1,0:T(8,128)(2,1)} %collective-permute-done.2.refs_3_), channel_id=1, source_target_pairs={{0,16},{16,0},{1,17},{17,1},{2,18},{18,2},{3,19},{19,3},{4,20},{20... | collective-permute-start | bytes 3244040 | tf_op jit(solution)/shard_map/ppermute | solution.py:1399
  153.3 29.4 %collective-permute-start.3 = (bf16[256,2048]{1,0:T(8,128)(2,1)}, bf16[256,2048]{1,0:T(8,128)(2,1)S(1)}, u32[]{:S(2)}, u32[]{:S(2)}) collective-permute-start(bf16[256,2048]{1,0:T(8,128)(2,1)} %norm_in.2.refs_0_), channel_id=1, source_target_pairs={{0,8},{8,0},{1,9},{9,1},{2,10},{10,2},{3,11},{11,3},{4,12},{12,4},... | collective-permute-start | bytes 3145736 | tf_op jit(solution)/shard_map/ppermute | solution.py:1399
  187.6 45.3 %collective-permute-start.7 = (bf16[512,2048]{1,0:T(8,128)(2,1)}, bf16[512,2048]{1,0:T(8,128)(2,1)S(1)}, u32[]{:S(2)}, u32[]{:S(2)}) collective-permute-start(bf16[512,2048]{1,0:T(8,128)(2,1)} %join_rows.16.near_ref.refs_4_), channel_id=1, source_target_pairs={{0,4},{4,0},{1,5},{5,1},{2,6},{6,2},{3,7},{7,3},{8,12},{12,8},{9,1... | collective-permute-start | bytes 6291464 | tf_op jit(solution)/shard_map/ppermute | solution.py:1399
  189.7 31.5 %all-to-all-start.2 = ((bf16[2,128,8,512]{3,1,0,2:T(8,128)(2,1)}), bf16[2,128,8,512]{3,1,0,2:T(8,128)(2,1)}, u32[]{:S(2)}, u32[]{:S(2)}) async-start(bf16[2,128,8,512]{3,1,0,2:T(8,128)(2,1)} %copy.158), calls=%async_computation.2 | async-start | bytes 4194304 | tf_op jit(solution)/shard_map/all_to_all | solution.py:1541
  196.3 36.7 %collective-permute-start.9 = (bf16[256,2048]{1,0:T(8,128)(2,1)}, bf16[256,2048]{1,0:T(8,128)(2,1)}, u32[]{:S(2)}, u32[]{:S(2)}) collective-permute-start(bf16[256,2048]{1,0:T(8,128)(2,1)} %flipped.2.refs_0_), channel_id=1, source_target_pairs={{0,1},{1,2},{2,3},{3,0},{4,5},{5,6},{6,7},{7,4},{8,9},{9,10},{10,1... | collective-permute-start | bytes 3145736 | tf_op jit(solution)/shard_map/ppermute | solution.py:1404
  206.4 45.7 %collective-permute-start.8 = (bf16[256,2048]{1,0:T(8,128)(2,1)}, bf16[256,2048]{1,0:T(8,128)(2,1)}, u32[]{:S(2)}, u32[]{:S(2)}) collective-permute-start(bf16[256,2048]{1,0:T(8,128)(2,1)} %flipped.2.refs_0_), channel_id=1, source_target_pairs={{0,3},{1,0},{2,1},{3,2},{4,7},{5,4},{6,5},{7,6},{8,11},{9,8},{10,9... | collective-permute-start | bytes 3145736 | tf_op jit(solution)/shard_map/ppermute | solution.py:1404
  206.5 78.5 %collective-permute-start.10 = (bf16[256,2048]{1,0:T(8,128)(2,1)}, bf16[256,2048]{1,0:T(8,128)(2,1)}, u32[]{:S(2)}, u32[]{:S(2)}) collective-permute-start(bf16[256,2048]{1,0:T(8,128)(2,1)} %norm_in.3.refs_0_), channel_id=1, source_target_pairs={{0,8},{8,0},{1,9},{9,1},{2,10},{10,2},{3,11},{11,3},{4,12},{12,4},... | collective-permute-start | bytes 3145736 | tf_op jit(solution)/shard_map/ppermute | solution.py:1399
  233.0 52.0 %collective-permute-start.12 = (bf16[256,2048]{1,0:T(8,128)(2,1)}, bf16[256,2048]{1,0:T(8,128)(2,1)}, u32[]{:S(2)}, u32[]{:S(2)}) collective-permute-start(bf16[256,2048]{1,0:T(8,128)(2,1)} %collective-permute-done.9.refs_1_), channel_id=1, source_target_pairs={{0,16},{16,0},{1,17},{17,1},{2,18},{18,2},{3,19},{19,3},{4,20},{20... | collective-permute-start | bytes 3145736 | tf_op jit(solution)/shard_map/ppermute | solution.py:1399
  233.6 51.4 %collective-permute-start.11 = (bf16[256,2048]{1,0:T(8,128)(2,1)}, bf16[256,2048]{1,0:T(8,128)(2,1)}, u32[]{:S(2)}, u32[]{:S(2)}) collective-permute-start(bf16[256,2048]{1,0:T(8,128)(2,1)} %collective-permute-done.9.refs_1_), channel_id=1, source_target_pairs={{0,1},{1,2},{2,3},{3,0},{4,5},{5,6},{6,7},{7,4},{8,9},{9,10},{10,1... | collective-permute-start | bytes 3145736 | tf_op jit(solution)/shard_map/ppermute | solution.py:1404
  294.9 27.7 %collective-permute-start.13 = (bf16[512,2048]{1,0:T(8,128)(2,1)}, bf16[512,2048]{1,0:T(8,128)(2,1)}, u32[]{:S(2)}, u32[]{:S(2)}) collective-permute-start(bf16[512,2048]{1,0:T(8,128)(2,1)} %get-tuple-element.284), channel_id=1, source_target_pairs={{0,4},{4,0},{1,5},{5,1},{2,6},{6,2},{3,7},{7,3},{8,12},{12,8},{9,1... | collective-permute-start | bytes 6291464 | tf_op jit(solution)/shard_map/ppermute | solution.py:1399
  300.4 56.6 %collective-permute-start.18 = (bf16[256,2048]{1,0:T(8,128)(2,1)}, bf16[256,2048]{1,0:T(8,128)(2,1)}, u32[]{:S(2)}, u32[]{:S(2)}) collective-permute-start(bf16[256,2048]{1,0:T(8,128)(2,1)} %collective-permute-done.11.refs_2_), channel_id=1, source_target_pairs={{0,16},{16,0},{1,17},{17,1},{2,18},{18,2},{3,19},{19,3},{4,20},{20... | collective-permute-start | bytes 3145736 | tf_op jit(solution)/shard_map/ppermute | solution.py:1399
  300.5 56.6 %collective-permute-start.17 = (bf16[256,2048]{1,0:T(8,128)(2,1)}, bf16[256,2048]{1,0:T(8,128)(2,1)}, u32[]{:S(2)}, u32[]{:S(2)}) collective-permute-start(bf16[256,2048]{1,0:T(8,128)(2,1)} %get-tuple-element.292.refs_0_), channel_id=1, source_target_pairs={{0,1},{1,2},{2,3},{3,0},{4,5},{5,6},{6,7},{7,4},{8,9},{9,10},{10,1... | collective-permute-start | bytes 3145736 | tf_op jit(solution)/shard_map/ppermute | solution.py:1404
  326.8 30.3 %collective-permute-start.16 = (bf16[256,2048]{1,0:T(8,128)(2,1)}, bf16[256,2048]{1,0:T(8,128)(2,1)}, u32[]{:S(2)}, u32[]{:S(2)}) collective-permute-start(bf16[256,2048]{1,0:T(8,128)(2,1)} %get-tuple-element.291), channel_id=1, source_target_pairs={{0,8},{8,0},{1,9},{9,1},{2,10},{10,2},{3,11},{11,3},{4,12},{12,4},... | collective-permute-start | bytes 3145736 | tf_op jit(solution)/shard_map/ppermute | solution.py:1399
  328.7 32.6 %collective-permute-start.21 = (bf16[256,2048]{1,0:T(8,128)(2,1)}, bf16[256,2048]{1,0:T(8,128)(2,1)}, u32[]{:S(2)}, u32[]{:S(2)}) collective-permute-start(bf16[256,2048]{1,0:T(8,128)(2,1)} %get-tuple-element.292.refs_0_), channel_id=1, source_target_pairs={{0,3},{1,0},{2,1},{3,2},{4,7},{5,4},{6,5},{7,6},{8,11},{9,8},{10,9... | collective-permute-start | bytes 3145736 | tf_op jit(solution)/shard_map/ppermute | solution.py:1404
  398.3 80.7 %all-to-all-start.3 = ((bf16[32,72,512]{2,1,0:T(8,128)(2,1)}), bf16[32,72,512]{2,1,0:T(8,128)(2,1)}, u32[]{:S(2)}, u32[]{:S(2)}) async-start(bf16[32,72,512]{2,1,0:T(8,128)(2,1)} %bitcast.128), calls=%async_computation.3 | async-start | bytes 4718592 | tf_op jit(solution)/shard_map/all_to_all | solution.py:1545
  401.9 65.2 %collective-permute-start.24 = (bf16[256,2048]{1,0:T(8,128)(2,1)}, bf16[256,2048]{1,0:T(8,128)(2,1)S(1)}, u32[]{:S(2)}, u32[]{:S(2)}) collective-permute-start(bf16[256,2048]{1,0:T(8,128)(2,1)} %collective-permute-done.17.refs_1_), channel_id=1, source_target_pairs={{0,1},{1,2},{2,3},{3,0},{4,5},{5,6},{6,7},{7,4},{8,9},{9,10},{10,1... | collective-permute-start | bytes 3145736 | tf_op jit(solution)/shard_map/ppermute | solution.py:1404
  403.8 63.4 %collective-permute-start.26 = (bf16[256,2048]{1,0:T(8,128)(2,1)}, bf16[256,2048]{1,0:T(8,128)(2,1)S(1)}, u32[]{:S(2)}, u32[]{:S(2)}) collective-permute-start(bf16[256,2048]{1,0:T(8,128)(2,1)} %collective-permute-done.21.refs_3_), channel_id=1, source_target_pairs={{0,16},{16,0},{1,17},{17,1},{2,18},{18,2},{3,19},{19,3},{4,20},{20... | collective-permute-start | bytes 3145736 | tf_op jit(solution)/shard_map/ppermute | solution.py:1399
  405.3 61.9 %collective-permute-start.27 = (bf16[256,2048]{1,0:T(8,128)(2,1)}, bf16[256,2048]{1,0:T(8,128)(2,1)}, u32[]{:S(2)}, u32[]{:S(2)}) collective-permute-start(bf16[256,2048]{1,0:T(8,128)(2,1)} %get-tuple-element.308), channel_id=1, source_target_pairs={{0,8},{8,0},{1,9},{9,1},{2,10},{10,2},{3,11},{11,3},{4,12},{12,4},... | collective-permute-start | bytes 3145736 | tf_op jit(solution)/shard_map/ppermute | solution.py:1399
  504.9 42.7 %collective-permute-start.32 = (bf16[256,2048]{1,0:T(8,128)(2,1)}, bf16[256,2048]{1,0:T(8,128)(2,1)S(1)}, u32[]{:S(2)}, u32[]{:S(2)}) collective-permute-start(bf16[256,2048]{1,0:T(8,128)(2,1)} %get-tuple-element.495.refs_0_), channel_id=1, source_target_pairs={{0,8},{8,0},{1,9},{9,1},{2,10},{10,2},{3,11},{11,3},{4,12},{12,4},... | collective-permute-start | bytes 3145736 | tf_op jit(solution)/shard_map/ppermute | solution.py:1399
  552.5 30.6 %collective-permute-start.31 = (bf16[256,2048]{1,0:T(8,128)(2,1)S(1)}, bf16[256,2048]{1,0:T(8,128)(2,1)S(1)}, u32[]{:S(2)}, u32[]{:S(2)}) collective-permute-start(bf16[256,2048]{1,0:T(8,128)(2,1)S(1)} %copy-done.37), channel_id=1, source_target_pairs={{0,8},{8,0},{1,9},{9,1},{2,10},{10,2},{3,11},{11,3},{4,12},{12,4},... | collective-permute-start | bytes 3145736 | tf_op jit(solution)/shard_map/ppermute | solution.py:1399
  636.3 54.5 %collective-permute-start.30 = (bf16[512,2048]{1,0:T(8,128)(2,1)}, bf16[512,2048]{1,0:T(8,128)(2,1)S(1)}, u32[]{:S(2)}, u32[]{:S(2)}) collective-permute-start(bf16[512,2048]{1,0:T(8,128)(2,1)} %get-tuple-element.334), channel_id=1, source_target_pairs={{0,4},{4,0},{1,5},{5,1},{2,6},{6,2},{3,7},{7,3},{8,12},{12,8},{9,1... | collective-permute-start | bytes 6291464 | tf_op jit(solution)/shard_map/ppermute | solution.py:1399
  656.8 28.6 %collective-permute-start.37 = (bf16[256,2048]{1,0:T(8,128)(2,1)}, bf16[256,2048]{1,0:T(8,128)(2,1)}, u32[]{:S(2)}, u32[]{:S(2)}) collective-permute-start(bf16[256,2048]{1,0:T(8,128)(2,1)} %get-tuple-element.362), channel_id=1, source_target_pairs={{0,8},{8,0},{1,9},{9,1},{2,10},{10,2},{3,11},{11,3},{4,12},{12,4},... | collective-permute-start | bytes 3145736 | tf_op jit(solution)/shard_map/ppermute | solution.py:1399
  658.3 105.7 %collective-permute-start.43 = (bf16[1024,2048]{1,0:T(8,128)(2,1)}, bf16[1024,2048]{1,0:T(8,128)(2,1)}, u32[]{:S(2)}, u32[]{:S(2)}) collective-permute-start(bf16[1024,2048]{1,0:T(8,128)(2,1)} %cross_sums.4), channel_id=1, source_target_pairs={{0,16},{16,0},{1,17},{17,1},{2,18},{18,2},{3,19},{19,3},{4,20},{20... | collective-permute-start | bytes 12582920 | tf_op jit(solution)/shard_map/ppermute | solution.py:1399
  668.3 42.7 %collective-permute-start.40 = (bf16[256,2048]{1,0:T(8,128)(2,1)}, bf16[256,2048]{1,0:T(8,128)(2,1)}, u32[]{:S(2)}, u32[]{:S(2)}) collective-permute-start(bf16[256,2048]{1,0:T(8,128)(2,1)} %get-tuple-element.365.refs_0_), channel_id=1, source_target_pairs={{0,8},{8,0},{1,9},{9,1},{2,10},{10,2},{3,11},{11,3},{4,12},{12,4},... | collective-permute-start | bytes 3145736 | tf_op jit(solution)/shard_map/ppermute | solution.py:1399
  668.9 46.4 %collective-permute-start.42 = (bf16[512,2048]{1,0:T(8,128)(2,1)}, bf16[512,2048]{1,0:T(8,128)(2,1)S(1)}, u32[]{:S(2)}, u32[]{:S(2)}) collective-permute-start(bf16[512,2048]{1,0:T(8,128)(2,1)} %get-tuple-element.338), channel_id=1, source_target_pairs={{0,4},{4,0},{1,5},{5,1},{2,6},{6,2},{3,7},{7,3},{8,12},{12,8},{9,1... | collective-permute-start | bytes 6291464 | tf_op jit(solution)/shard_map/ppermute | solution.py:1399
  714.8 45.1 %collective-permute-start.44 = (bf16[256,2048]{1,0:T(8,128)(2,1)}, bf16[256,2048]{1,0:T(8,128)(2,1)}, u32[]{:S(2)}, u32[]{:S(2)}) collective-permute-start(bf16[256,2048]{1,0:T(8,128)(2,1)} %get-tuple-element.370.refs_0_), channel_id=1, source_target_pairs={{0,8},{8,0},{1,9},{9,1},{2,10},{10,2},{3,11},{11,3},{4,12},{12,4},... | collective-permute-start | bytes 3145736 | tf_op jit(solution)/shard_map/ppermute | solution.py:1399
  780.3 30.0 %collective-permute-start.45 = (bf16[512,2048]{1,0:T(8,128)(2,1)}, bf16[512,2048]{1,0:T(8,128)(2,1)}, u32[]{:S(2)}, u32[]{:S(2)}) collective-permute-start(bf16[512,2048]{1,0:T(8,128)(2,1)} %get-tuple-element.394), channel_id=1, source_target_pairs={{0,4},{4,0},{1,5},{5,1},{2,6},{6,2},{3,7},{7,3},{8,12},{12,8},{9,1... | collective-permute-start | bytes 6291464 | tf_op jit(solution)/shard_map/ppermute | solution.py:1399
  780.5 132.7 %collective-permute-start.49 = (bf16[1024,2048]{1,0:T(8,128)(2,1)}, bf16[1024,2048]{1,0:T(8,128)(2,1)}, u32[]{:S(2)}, u32[]{:S(2)}) collective-permute-start(bf16[1024,2048]{1,0:T(8,128)(2,1)} %cross_sums.6), channel_id=1, source_target_pairs={{0,16},{16,0},{1,17},{17,1},{2,18},{18,2},{3,19},{19,3},{4,20},{20... | collective-permute-start | bytes 12582920 | tf_op jit(solution)/shard_map/ppermute | solution.py:1399
  782.3 32.1 %collective-permute-start.39 = (bf16[256,2048]{1,0:T(8,128)(2,1)}, bf16[256,2048]{1,0:T(8,128)(2,1)}, u32[]{:S(2)}, u32[]{:S(2)}) collective-permute-start(bf16[256,2048]{1,0:T(8,128)(2,1)} %get-tuple-element.374), channel_id=1, source_target_pairs={{0,8},{8,0},{1,9},{9,1},{2,10},{10,2},{3,11},{11,3},{4,12},{12,4},... | collective-permute-start | bytes 3145736 | tf_op jit(solution)/shard_map/ppermute | solution.py:1399
  783.1 47.0 %collective-permute-start.47 = (bf16[256,2048]{1,0:T(8,128)(2,1)}, bf16[256,2048]{1,0:T(8,128)(2,1)}, u32[]{:S(2)}, u32[]{:S(2)}) collective-permute-start(bf16[256,2048]{1,0:T(8,128)(2,1)} %get-tuple-element.379), channel_id=1, source_target_pairs={{0,8},{8,0},{1,9},{9,1},{2,10},{10,2},{3,11},{11,3},{4,12},{12,4},... | collective-permute-start | bytes 3145736 | tf_op jit(solution)/shard_map/ppermute | solution.py:1399
  784.3 57.9 %collective-permute-start.48 = (bf16[256,2048]{1,0:T(8,128)(2,1)}, bf16[256,2048]{1,0:T(8,128)(2,1)}, u32[]{:S(2)}, u32[]{:S(2)}) collective-permute-start(bf16[256,2048]{1,0:T(8,128)(2,1)} %add_pieces.16), channel_id=1, source_target_pairs={{0,1},{1,2},{2,3},{3,0},{4,5},{5,6},{6,7},{7,4},{8,9},{9,10},{10,1... | collective-permute-start | bytes 3145736 | tf_op jit(solution)/shard_map/ppermute | solution.py:1404
  845.4 124.9 %all-to-all-start.4 = ((bf16[32,72,512]{2,1,0:T(8,128)(2,1)}), bf16[32,72,512]{2,1,0:T(8,128)(2,1)}, u32[]{:S(2)}, u32[]{:S(2)}) async-start(bf16[32,72,512]{2,1,0:T(8,128)(2,1)} %bitcast.127), calls=%async_computation.4 | async-start | bytes 4718592 | tf_op jit(solution)/shard_map/all_to_all | solution.py:1545
  859.1 49.5 %collective-permute-start.50 = (bf16[256,2048]{1,0:T(8,128)(2,1)}, bf16[256,2048]{1,0:T(8,128)(2,1)}, u32[]{:S(2)}, u32[]{:S(2)}) collective-permute-start(bf16[256,2048]{1,0:T(8,128)(2,1)} %get-tuple-element.399), channel_id=1, source_target_pairs={{0,8},{8,0},{1,9},{9,1},{2,10},{10,2},{3,11},{11,3},{4,12},{12,4},... | collective-permute-start | bytes 3145736 | tf_op jit(solution)/shard_map/ppermute | solution.py:1399
  938.5 80.3 %collective-permute-start.52 = (bf16[512,2048]{1,0:T(8,128)(2,1)}, bf16[512,2048]{1,0:T(8,128)(2,1)}, u32[]{:S(2)}, u32[]{:S(2)}) collective-permute-start(bf16[512,2048]{1,0:T(8,128)(2,1)} %cross_pair.4), channel_id=1, source_target_pairs={{0,16},{16,0},{1,17},{17,1},{2,18},{18,2},{3,19},{19,3},{4,20},{20... | collective-permute-start | bytes 6291464 | tf_op jit(solution)/shard_map/ppermute | solution.py:1399
  940.3 27.7 %collective-permute-start.56 = (bf16[256,2048]{1,0:T(8,128)(2,1)S(1)}, bf16[256,2048]{1,0:T(8,128)(2,1)S(1)}, u32[]{:S(2)}, u32[]{:S(2)}) collective-permute-start(bf16[256,2048]{1,0:T(8,128)(2,1)S(1)} %copy-done.52), channel_id=1, source_target_pairs={{0,3},{1,0},{2,1},{3,2},{4,7},{5,4},{6,5},{7,6},{8,11},{9,8},{10,9... | collective-permute-start | bytes 3145736 | tf_op jit(solution)/shard_map/ppermute | solution.py:1404
  944.4 46.5 %collective-permute-start.55 = (bf16[256,2048]{1,0:T(8,128)(2,1)S(1)}, bf16[256,2048]{1,0:T(8,128)(2,1)}, u32[]{:S(2)}, u32[]{:S(2)}) collective-permute-start(bf16[256,2048]{1,0:T(8,128)(2,1)S(1)} %copy-done.54), channel_id=1, source_target_pairs={{0,1},{1,2},{2,3},{3,0},{4,5},{5,6},{6,7},{7,4},{8,9},{9,10},{10,1... | collective-permute-start | bytes 3145736 | tf_op jit(solution)/shard_map/ppermute | solution.py:1404
  944.4 69.0 %collective-permute-start.54 = (bf16[256,2048]{1,0:T(8,128)(2,1)}, bf16[256,2048]{1,0:T(8,128)(2,1)}, u32[]{:S(2)}, u32[]{:S(2)}) collective-permute-start(bf16[256,2048]{1,0:T(8,128)(2,1)} %add_pieces.19), channel_id=1, source_target_pairs={{0,1},{1,2},{2,3},{3,0},{4,5},{5,6},{6,7},{7,4},{8,9},{9,10},{10,1... | collective-permute-start | bytes 3145736 | tf_op jit(solution)/shard_map/ppermute | solution.py:1404
  949.8 69.7 %collective-permute-start.53 = (bf16[256,2048]{1,0:T(8,128)(2,1)}, bf16[256,2048]{1,0:T(8,128)(2,1)}, u32[]{:S(2)}, u32[]{:S(2)}) collective-permute-start(bf16[256,2048]{1,0:T(8,128)(2,1)} %get-tuple-element.425), channel_id=1, source_target_pairs={{0,8},{8,0},{1,9},{9,1},{2,10},{10,2},{3,11},{11,3},{4,12},{12,4},... | collective-permute-start | bytes 3145736 | tf_op jit(solution)/shard_map/ppermute | solution.py:1399
  969.0 113.3 %collective-permute-start.59 = (bf16[512,2048]{1,0:T(8,128)(2,1)}, bf16[512,2048]{1,0:T(8,128)(2,1)S(1)}, u32[]{:S(2)}, u32[]{:S(2)}) collective-permute-start(bf16[512,2048]{1,0:T(8,128)(2,1)} %cross_pair.5), channel_id=1, source_target_pairs={{0,16},{16,0},{1,17},{17,1},{2,18},{18,2},{3,19},{19,3},{4,20},{20... | collective-permute-start | bytes 6291464 | tf_op jit(solution)/shard_map/ppermute | solution.py:1399
  984.0 77.6 %all-to-all-start.5 = ((bf16[2,1024,1,512]{3,0,2,1:T(2,128)(2,1)}), bf16[2,1024,1,512]{3,0,2,1:T(2,128)(2,1)}, u32[]{:S(2)}, u32[]{:S(2)}) async-start(bf16[2,1024,1,512]{3,0,2,1:T(2,128)(2,1)} %copy.167), calls=%async_computation.5 | async-start | bytes 4194304 | tf_op jit(solution)/shard_map/all_to_all | solution.py:1611
  990.9 45.0 %collective-permute-start.62 = (bf16[256,2048]{1,0:T(8,128)(2,1)}, bf16[256,2048]{1,0:T(8,128)(2,1)}, u32[]{:S(2)}, u32[]{:S(2)}) collective-permute-start(bf16[256,2048]{1,0:T(8,128)(2,1)} %add_pieces.20), channel_id=1, source_target_pairs={{0,3},{1,0},{2,1},{3,2},{4,7},{5,4},{6,5},{7,6},{8,11},{9,8},{10,9... | collective-permute-start | bytes 3145736 | tf_op jit(solution)/shard_map/ppermute | solution.py:1404
  1016.6 41.7 %collective-permute-start.61 = (bf16[256,2048]{1,0:T(8,128)(2,1)}, bf16[256,2048]{1,0:T(8,128)(2,1)}, u32[]{:S(2)}, u32[]{:S(2)}) collective-permute-start(bf16[256,2048]{1,0:T(8,128)(2,1)} %add_pieces.22), channel_id=1, source_target_pairs={{0,1},{1,2},{2,3},{3,0},{4,5},{5,6},{6,7},{7,4},{8,9},{9,10},{10,1... | collective-permute-start | bytes 3145736 | tf_op jit(solution)/shard_map/ppermute | solution.py:1404
  1018.9 69.9 %collective-permute-start.57 = (bf16[256,2048]{1,0:T(8,128)(2,1)S(1)}, bf16[256,2048]{1,0:T(8,128)(2,1)}, u32[]{:S(2)}, u32[]{:S(2)}) collective-permute-start(bf16[256,2048]{1,0:T(8,128)(2,1)S(1)} %copy-done.38), channel_id=1, source_target_pairs={{0,8},{8,0},{1,9},{9,1},{2,10},{10,2},{3,11},{11,3},{4,12},{12,4},... | collective-permute-start | bytes 3145736 | tf_op jit(solution)/shard_map/ppermute | solution.py:1399
  1019.5 69.3 %collective-permute-start.58 = (bf16[256,2048]{1,0:T(8,128)(2,1)S(1)}, bf16[256,2048]{1,0:T(8,128)(2,1)}, u32[]{:S(2)}, u32[]{:S(2)}) collective-permute-start(bf16[256,2048]{1,0:T(8,128)(2,1)S(1)} %copy-done.38), channel_id=1, source_target_pairs={{0,16},{16,0},{1,17},{17,1},{2,18},{18,2},{3,19},{19,3},{4,20},{20... | collective-permute-start | bytes 3145736 | tf_op jit(solution)/shard_map/ppermute | solution.py:1399
  1035.9 44.1 %collective-permute-start.60 = (bf16[128,2048]{1,0:T(8,128)(2,1)}, bf16[128,2048]{1,0:T(8,128)(2,1)}, u32[]{:S(2)}, u32[]{:S(2)}) collective-permute-start(bf16[128,2048]{1,0:T(8,128)(2,1)} %add_pieces.23), channel_id=1, source_target_pairs={{0,1},{1,2},{2,3},{3,0},{4,5},{5,6},{6,7},{7,4},{8,9},{9,10},{10,1... | collective-permute-start | bytes 1572872 | tf_op jit(solution)/shard_map/ppermute | solution.py:1404
  1058.4 41.9 %collective-permute-start.68 = (bf16[128,2048]{1,0:T(8,128)(2,1)}, bf16[128,2048]{1,0:T(8,128)(2,1)}, u32[]{:S(2)}, u32[]{:S(2)}) collective-permute-start(bf16[128,2048]{1,0:T(8,128)(2,1)} %add_pieces.24), channel_id=1, source_target_pairs={{0,3},{1,0},{2,1},{3,2},{4,7},{5,4},{6,5},{7,6},{8,11},{9,8},{10,9... | collective-permute-start | bytes 1572872 | tf_op jit(solution)/shard_map/ppermute | solution.py:1404
  1093.2 78.1 %all-to-all-start.6 = ((bf16[32,72,512]{2,1,0:T(8,128)(2,1)}), bf16[32,72,512]{2,1,0:T(8,128)(2,1)S(1)}, u32[]{:S(2)}, u32[]{:S(2)}) async-start(bf16[32,72,512]{2,1,0:T(8,128)(2,1)} %bitcast.125), calls=%async_computation.6 | async-start | bytes 4718592 | tf_op jit(solution)/shard_map/all_to_all | solution.py:1545
  1117.8 63.6 %collective-permute-start.72 = (bf16[256,2048]{1,0:T(8,128)(2,1)S(1)}, bf16[256,2048]{1,0:T(8,128)(2,1)}, u32[]{:S(2)}, u32[]{:S(2)}) collective-permute-start(bf16[256,2048]{1,0:T(8,128)(2,1)S(1)} %copy-done.39), channel_id=1, source_target_pairs={{0,8},{8,0},{1,9},{9,1},{2,10},{10,2},{3,11},{11,3},{4,12},{12,4},... | collective-permute-start | bytes 3145736 | tf_op jit(solution)/shard_map/ppermute | solution.py:1399
  1118.4 63.0 %collective-permute-start.73 = (bf16[256,2048]{1,0:T(8,128)(2,1)S(1)}, bf16[256,2048]{1,0:T(8,128)(2,1)}, u32[]{:S(2)}, u32[]{:S(2)}) collective-permute-start(bf16[256,2048]{1,0:T(8,128)(2,1)S(1)} %copy-done.39), channel_id=1, source_target_pairs={{0,16},{16,0},{1,17},{17,1},{2,18},{18,2},{3,19},{19,3},{4,20},{20... | collective-permute-start | bytes 3145736 | tf_op jit(solution)/shard_map/ppermute | solution.py:1399
  1119.8 66.1 %collective-permute-start.78 = (bf16[128,2048]{1,0:T(8,128)(2,1)}, bf16[128,2048]{1,0:T(8,128)(2,1)}, u32[]{:S(2)}, u32[]{:S(2)}) collective-permute-start(bf16[128,2048]{1,0:T(8,128)(2,1)} %add_pieces.28), channel_id=1, source_target_pairs={{0,3},{1,0},{2,1},{3,2},{4,7},{5,4},{6,5},{7,6},{8,11},{9,8},{10,9... | collective-permute-start | bytes 1572872 | tf_op jit(solution)/shard_map/ppermute | solution.py:1404
  1128.3 57.6 %collective-permute-start.77 = (bf16[128,2048]{1,0:T(8,128)(2,1)}, bf16[128,2048]{1,0:T(8,128)(2,1)}, u32[]{:S(2)}, u32[]{:S(2)}) collective-permute-start(bf16[128,2048]{1,0:T(8,128)(2,1)} %add_pieces.30), channel_id=1, source_target_pairs={{0,1},{1,2},{2,3},{3,0},{4,5},{5,6},{6,7},{7,4},{8,9},{9,10},{10,1... | collective-permute-start | bytes 1572872 | tf_op jit(solution)/shard_map/ppermute | solution.py:1404
  1205.4 33.0 %collective-permute-start.82 = (bf16[128,2048]{1,0:T(8,128)(2,1)S(1)}, bf16[128,2048]{1,0:T(8,128)(2,1)S(1)}, u32[]{:S(2)}, u32[]{:S(2)}) collective-permute-start(bf16[128,2048]{1,0:T(8,128)(2,1)S(1)} %copy-done.43), channel_id=1, source_target_pairs={{0,8},{8,0},{1,9},{9,1},{2,10},{10,2},{3,11},{11,3},{4,12},{12,4},... | collective-permute-start | bytes 1572872 | tf_op jit(solution)/shard_map/ppermute | solution.py:1399
  1207.2 31.3 %collective-permute-start.83 = (bf16[128,2048]{1,0:T(8,128)(2,1)S(1)}, bf16[128,2048]{1,0:T(8,128)(2,1)S(1)}, u32[]{:S(2)}, u32[]{:S(2)}) collective-permute-start(bf16[128,2048]{1,0:T(8,128)(2,1)S(1)} %copy-done.43), channel_id=1, source_target_pairs={{0,16},{16,0},{1,17},{17,1},{2,18},{18,2},{3,19},{19,3},{4,20},{20... | collective-permute-start | bytes 1572872 | tf_op jit(solution)/shard_map/ppermute | solution.py:1399
  1243.7 36.8 %collective-permute-start.85 = (bf16[512,2048]{1,0:T(8,128)(2,1)}, bf16[512,2048]{1,0:T(8,128)(2,1)}, u32[]{:S(2)}, u32[]{:S(2)}) collective-permute-start(bf16[512,2048]{1,0:T(8,128)(2,1)} %join_rows.30.near_low.near_high), channel_id=1, source_target_pairs={{0,4},{4,0},{1,5},{5,1},{2,6},{6,2},{3,7},{7,3},{8,12},{12,8},{9,1... | collective-permute-start | bytes 6291464 | tf_op jit(solution)/shard_map/ppermute | solution.py:1399
  1247.2 30.8 %all-to-all-start.7 = ((bf16[2,1024,1,512]{3,0,2,1:T(2,128)(2,1)}), bf16[2,1024,1,512]{3,0,2,1:T(2,128)(2,1)S(1)}, u32[]{:S(2)}, u32[]{:S(2)}) async-start(bf16[2,1024,1,512]{3,0,2,1:T(2,128)(2,1)} %copy.170), calls=%async_computation.7 | async-start | bytes 4194304 | tf_op jit(solution)/shard_map/all_to_all | solution.py:1611
  1252.4 35.1 %collective-permute-start.86 = (bf16[64,2048]{1,0:T(8,128)(2,1)}, bf16[64,2048]{1,0:T(8,128)(2,1)S(1)}, u32[]{:S(2)}, u32[]{:S(2)}) collective-permute-start(bf16[64,2048]{1,0:T(8,128)(2,1)} %slice.160), channel_id=1, source_target_pairs={{0,8},{8,0},{1,9},{9,1},{2,10},{10,2},{3,11},{11,3},{4,12},{12,4},... | collective-permute-start | bytes 786440 | tf_op jit(solution)/shard_map/ppermute | solution.py:1399
  1254.4 33.2 %collective-permute-start.87 = (bf16[64,2048]{1,0:T(8,128)(2,1)}, bf16[64,2048]{1,0:T(8,128)(2,1)S(1)}, u32[]{:S(2)}, u32[]{:S(2)}) collective-permute-start(bf16[64,2048]{1,0:T(8,128)(2,1)} %slice.161), channel_id=1, source_target_pairs={{0,16},{16,0},{1,17},{17,1},{2,18},{18,2},{3,19},{19,3},{4,20},{20... | collective-permute-start | bytes 786440 | tf_op jit(solution)/shard_map/ppermute | solution.py:1399
  1255.8 31.7 %collective-permute-start.88 = (f32[192,128]{1,0:T(8,128)S(1)}, f32[192,128]{1,0:T(8,128)S(1)}, u32[]{:S(2)}, u32[]{:S(2)}) collective-permute-start(f32[192,128]{1,0:T(8,128)S(1)} %add.535), channel_id=1, source_target_pairs={{0,1},{1,0},{2,3},{3,2},{4,5},{5,4},{6,7},{7,6},{8,9},{9,8},{10,11... | collective-permute-start | bytes 294920 | tf_op jit(solution)/shard_map/ppermute | solution.py:1867
  (115 other events, 1195.3 us)

commit v5 on v4

--- a/solution.py
+++ b/solution.py
@@ -1661,13 +1661,12 @@
     resid_a, second_a = order.mark(resid_norm(tok, 0, *sum_end(sum_a1), out_b, gain_two, shift_two))
     second_a = team_start(second_a)
     down_3, down_y3 = swapped(down_3)
+    cot_got = box_exchange(order.take(cot_sent))
     sum_b1 = sum_start(mixed_b, out_w)
     up_w = order.mark(join_rows([up_mine, up_1, up_2, up_3, up_other, *order.take((up_y1, up_y2, up_y3))]))
     sum_b1 = sum_middle(sum_b1)
     down_y1 = order.step(down_y1)
-    second_a = team_middle(second_a)
-    cot_got = box_exchange(order.take(cot_sent))
-    second_a = team_end(second_a)
+    second_a = team_end(team_middle(second_a))
 
     hidden_a, slope_a = order.mark(expand(*order.take(second_a), up_w, up_b))
     down_2, down_y2 = swapped(down_2)
@@ -1866,8 +1865,8 @@
     small = order.mark(small + order.take(small_got))
     small_got = lax.ppermute(small, "z", [(i, i ^ 1) for i in range(depth)])
     one_plane = plane_end(one_plane, order)
+    query_grad, key_grad = order.mark(stack_heads(*order.take(one_plane), own, (True, True)))
     input_grad = order.step(input_grad)
-    query_grad, key_grad = order.mark(stack_heads(*order.take(one_plane), own, (True, True)))
     small = order.mark(small + order.take(small_got))
     small_got = lax.ppermute(small, "z", [(i, i ^ 2) for i in range(depth)])
     two_plane = plane_end(two_plane, order)

time: 1320 us -> 1290 us (0.977)
  starting transfers between devices: 161 us -> 140 us
    ppermute x68, waiting for transfers between devices: 107 us -> 145 us  [swap_along(): return lax.ppermute(array, axis, SWAP)]
    ppermute x21, waiting for transfers between devices: 185 us -> 149 us  [shift(): lax.ppermute(array, 'z', [(i, (i + step) % size) for i in range(size)])]
  transfers between devices with their start and end apart: 99 -> 99, of which waited for: 29 -> 29; matrix products, arithmetic and copies ran while one was open for 4% -> 4% of each run, Pallas kernels for 46% -> 47%
where the time goes in v5:
time: 1290 us; the launch traced here: 1280 us
  Pallas kernels  674 us (52%)
  waiting for transfers between devices  360 us (28%)
  starting transfers between devices  140 us (11%)
  local copies, waits for them, and re-layouts  98.2 us (8%)
    ppermute x21, waiting for transfers between devices, shift(): lax.ppermute(array, 'z', [(i, (i + step) % size) for i in range(size)])  149 us
    ppermute x68, waiting for transfers between devices, swap_along(): return lax.ppermute(array, axis, SWAP)  145 us
    pallas_call x18, Pallas kernels, rows_call(): pl.pallas_call(kernel, grid=(steps,), in_specs=[spec(array, first) for ar...  74.7 us
    pallas_call x16, Pallas kernels, join_rows(): pl.pallas_call(functools.partial(join_kernel, count), grid=(4,), in_specs...  69.8 us
    pallas_call x6, Pallas kernels, partial_sums(): pl.pallas_call(partial_kernel, grid=(cols // WIDE,), in_specs=[whole((row...  64.9 us
    pallas_call x4, Pallas kernels, cross_sums(): pl.pallas_call(cross_kernel, grid=(size // tall,), in_specs=[left_spec, r...  57.6 us
    ppermute x68, starting transfers between devices, swap_along(): return lax.ppermute(array, axis, SWAP)  55 us
    pallas_call x2, Pallas kernels, attend_back(): pl.pallas_call(attend_back_kernel, grid_spec=pltpu.PrefetchScalarGridSpec...  54.6 us
  transfers between devices with their start and end apart: 99, of which 29 were waited for; matrix products, arithmetic and copies ran while one was open for 4% of the time, Pallas kernels for 47%

profile of v5, /device:TPU:0, one launch (start us, length us, event | category | flops | bytes accessed | tf_op | source)
XLA Modules:
  0.0 1283.3 jit_solution(8013739675386942239)
XLA Ops:
  20.1 18.3 %collective-permute-done.refs_1_ = bf16[264,2048]{1,0:T(8,128)(2,1)S(1)} collective-permute-done((bf16[264,2048]{1,0:T(8,128)(2,1)}, bf16[264,2048]{1,0:T(8,128)(2,1)S(1)}, u32[]{:S(2)}, u32[]{:S(2)}) %collective-permute-start) | collective-permute-done | bytes 1081376 | tf_op jit(solution)/shard_map/ppermute | solution.py:1404
  46.3 19.0 %collective-permute-done.1.refs_2_ = bf16[264,2048]{1,0:T(8,128)(2,1)} collective-permute-done((bf16[264,2048]{1,0:T(8,128)(2,1)S(1)}, bf16[264,2048]{1,0:T(8,128)(2,1)}, u32[]{:S(2)}, u32[]{:S(2)}) %collective-permute-start.1) | collective-permute-done | bytes 1081376 | tf_op jit(solution)/shard_map/ppermute | solution.py:1404
  65.3 8.7 pick_rows.2
  84.2 56.7 %collective-permute-done.2.refs_3_ = bf16[264,2048]{1,0:T(8,128)(2,1)} collective-permute-done((bf16[264,2048]{1,0:T(8,128)(2,1)S(1)}, bf16[264,2048]{1,0:T(8,128)(2,1)}, u32[]{:S(2)}, u32[]{:S(2)}) %collective-permute-start.2) | collective-permute-done | bytes 1081376 | tf_op jit(solution)/shard_map/ppermute | solution.py:1404
  157.5 17.0 %collective-permute-done.6.refs_7_ = bf16[264,2048]{1,0:T(8,128)(2,1)S(1)} collective-permute-done((bf16[264,2048]{1,0:T(8,128)(2,1)}, bf16[264,2048]{1,0:T(8,128)(2,1)S(1)}, u32[]{:S(2)}, u32[]{:S(2)}) %collective-permute-start.6) | collective-permute-done | bytes 1081376 | tf_op jit(solution)/shard_map/ppermute | solution.py:1399
  175.5 7.2 attn_join.1
  196.3 9.5 collective-permute-start.9
  208.4 12.7 all-to-all-done.2
  224.2 8.7 pick_rows.3
  233.6 9.7 collective-permute-start.11
  245.6 6.5 collective-permute-done.8.refs_3_
  252.1 11.7 project.4.query_ref.key_ref.value_ref
  265.7 18.3 %attend.2.left_ref.refs_2_ = bf16[1024,512]{1,0:T(8,128)(2,1)S(1)} custom-call(s32[1]{0:T(128)} %bitcast.10.rank_ref, bf16[1024,1536]{1,0:T(8,128)(2,1)S(1)} %copy-done.1, bf16[1024,1536]{1,0:T(8,128)(2,1)S(1)} %copy-done.1, bf16[1024,1536]{1,0:T(8,128)(2,1)S(1)} %copy-done.1, s32[1024,2]{1,0:T(8,128)S(1)} %copy.162.key_info_ref, ...), custom_call_target="tpu_custom_call" | custom-call | flops 1048576 | bytes 4096 | tf_op jit(solution)/shard_map/attend/pallas_call | solution.py:565
  288.9 6.0 partial_sums.6
  301.9 11.6 project.5.query_ref.key_ref.value_ref
  313.5 8.1 collective-permute-done.14.refs_7_
  337.8 18.3 %attend.3.left_ref.refs_3_ = bf16[1024,512]{1,0:T(8,128)(2,1)S(1)} custom-call(s32[1]{0:T(128)} %bitcast.10.rank_ref, bf16[1024,1536]{1,0:T(8,128)(2,1)S(1)} %copy-done, bf16[1024,1536]{1,0:T(8,128)(2,1)S(1)} %copy-done, bf16[1024,1536]{1,0:T(8,128)(2,1)S(1)} %copy-done, s32[1024,2]{1,0:T(8,128)S(1)} %copy-done.13, s32[2,1024]{1,0:T(2,128)S(1)} %pad_add_fusion.3.query_info_ref), custom_call_target="tpu_custom_call" | custom-call | flops 1048576 | bytes 4096 | tf_op jit(solution)/shard_map/attend/pallas_call | solution.py:565
  361.3 6.0 partial_sums.7
  376.2 7.0 join_rows.18.weight_ref
  387.3 33.5 %collective-permute-done.20.refs_5_ = bf16[256,2048]{1,0:T(8,128)(2,1)} collective-permute-done((bf16[256,2048]{1,0:T(8,128)(2,1)}, bf16[256,2048]{1,0:T(8,128)(2,1)}, u32[]{:S(2)}, u32[]{:S(2)}) %collective-permute-start.20) | collective-permute-done | bytes 1048608 | tf_op jit(solution)/shard_map/ppermute | solution.py:1399
  430.8 17.4 %expand.2 = (bf16[1024,2048]{1,0:T(8,128)(2,1)}, bf16[1024,2048]{1,0:T(8,128)(2,1)}) custom-call(bf16[512,2048]{1,0:T(8,128)(2,1)} %join_rows.19.near_ref.near_a, bf16[512,2048]{1,0:T(8,128)(2,1)} %copy-done.21, bf16[2048,2048]{1,0:T(8,128)(2,1)} %join_rows.18.weight_ref, f32[1,2048]{1,0:T(1,128)} %bitcast.166), custom_call_target="tpu_custom_call" | custom-call | flops 1048576 | bytes 4096 | tf_op jit(solution)/shard_map/expand/pallas_call | solution.py:769
  464.2 18.9 %collective-permute-done.28.refs_1_ = bf16[256,2048]{1,0:T(8,128)(2,1)} collective-permute-done((bf16[256,2048]{1,0:T(8,128)(2,1)}, bf16[256,2048]{1,0:T(8,128)(2,1)}, u32[]{:S(2)}, u32[]{:S(2)}) %collective-permute-start.28) | collective-permute-done | bytes 1048608 | tf_op jit(solution)/shard_map/ppermute | solution.py:1399
  492.7 17.5 %expand.3 = (bf16[1024,2048]{1,0:T(8,128)(2,1)}, bf16[1024,2048]{1,0:T(8,128)(2,1)}) custom-call(bf16[512,2048]{1,0:T(8,128)(2,1)} %join_rows.20.near_ref.near_b, bf16[512,2048]{1,0:T(8,128)(2,1)} %copy-done.22, bf16[2048,2048]{1,0:T(8,128)(2,1)} %join_rows.18.weight_ref, f32[1,2048]{1,0:T(1,128)} %bitcast.167), custom_call_target="tpu_custom_call" | custom-call | flops 1048576 | bytes 4096 | tf_op jit(solution)/shard_map/expand/pallas_call | solution.py:769
  512.9 7.0 join_rows.21.weight_ref
  519.9 13.2 %partial_sums.8 = (f32[512,2048]{1,0:T(8,128)}, bf16[512,2048]{1,0:T(8,128)(2,1)}) custom-call(bf16[1024,2048]{1,0:T(8,128)(2,1)} %get-tuple-element.367.left_ref.left_a, bf16[2048,2048]{1,0:T(8,128)(2,1)} %join_rows.21.weight_ref), custom_call_target="tpu_custom_call" | custom-call | flops 1048576 | bytes 4096 | tf_op jit(solution)/shard_map/partial_sums/pallas_call | solution.py:830
  539.4 13.2 %partial_sums.9 = (f32[512,2048]{1,0:T(8,128)}, bf16[512,2048]{1,0:T(8,128)(2,1)}) custom-call(bf16[1024,2048]{1,0:T(8,128)(2,1)} %get-tuple-element.336.left_ref.left_b, bf16[2048,2048]{1,0:T(8,128)(2,1)} %join_rows.21.weight_ref), custom_call_target="tpu_custom_call" | custom-call | flops 1048576 | bytes 4096 | tf_op jit(solution)/shard_map/partial_sums/pallas_call | solution.py:830
  553.9 14.4 %expand_back.2 = (bf16[1024,2048]{1,0:T(8,128)(2,1)}, f32[8,2048]{1,0:T(8,128)}) custom-call(bf16[512,2048]{1,0:T(8,128)(2,1)} %join_rows.22.near_ref.near_a, bf16[512,2048]{1,0:T(8,128)(2,1)} %copy-done.23, bf16[2048,2048]{1,0:T(8,128)(2,1)} %join_rows.21.weight_ref, bf16[1024,2048]{1,0:T(8,128)(2,1)} %get-tuple-element.315.slope_ref), custom_call_target="tpu_custom_call" | custom-call | flops 1048576 | bytes 4096 | tf_op jit(solution)/shard_map/expand_back/pallas_call | solution.py:800
  573.3 13.4 %partial_sums.10 = (f32[512,2048]{1,0:T(8,128)}, bf16[512,2048]{1,0:T(8,128)(2,1)}) custom-call(bf16[1024,2048]{1,0:T(8,128)(2,1)} %get-tuple-element.396.left_ref.left_a, bf16[2048,2048]{1,0:T(8,128)(2,1)} %join_rows.18.weight_ref), custom_call_target="tpu_custom_call" | custom-call | flops 1048576 | bytes 4096 | tf_op jit(solution)/shard_map/partial_sums/pallas_call | solution.py:830
  588.4 14.4 %expand_back.3 = (bf16[1024,2048]{1,0:T(8,128)(2,1)}, f32[8,2048]{1,0:T(8,128)}) custom-call(bf16[512,2048]{1,0:T(8,128)(2,1)} %join_rows.23.near_ref.near_b, bf16[512,2048]{1,0:T(8,128)(2,1)} %copy-done.24, bf16[2048,2048]{1,0:T(8,128)(2,1)} %join_rows.21.weight_ref, bf16[1024,2048]{1,0:T(8,128)(2,1)} %get-tuple-element.328.slope_ref), custom_call_target="tpu_custom_call" | custom-call | flops 1048576 | bytes 4096 | tf_op jit(solution)/shard_map/expand_back/pallas_call | solution.py:800
  608.2 13.2 %partial_sums.11 = (f32[512,2048]{1,0:T(8,128)}, bf16[512,2048]{1,0:T(8,128)(2,1)}) custom-call(bf16[1024,2048]{1,0:T(8,128)(2,1)} %get-tuple-element.356.left_ref.left_b, bf16[2048,2048]{1,0:T(8,128)(2,1)} %join_rows.18.weight_ref), custom_call_target="tpu_custom_call" | custom-call | flops 1048576 | bytes 4096 | tf_op jit(solution)/shard_map/partial_sums/pallas_call | solution.py:830
  622.6 14.3 %cross_sums.4 = bf16[1024,2048]{1,0:T(8,128)(2,1)} custom-call(bf16[1024,2048]{1,0:T(8,128)(2,1)} %get-tuple-element.367.left_ref.left_a, bf16[512,2048]{1,0:T(8,128)(2,1)} %join_rows.22.near_ref.near_a, bf16[512,2048]{1,0:T(8,128)(2,1)} %copy-done.23, bf16[1024,2048]{1,0:T(8,128)(2,1)} %get-tuple-element.336.left_ref.left_b, ...), custom_call_target="tpu_custom_call" | custom-call | flops 1048576 | bytes 4096 | tf_op jit(solution)/shard_map/cross_sums/pallas_call | solution.py:864
  648.3 5.4 second_back.2
  654.4 14.3 %cross_sums.5.refs_0_ = bf16[1024,2048]{1,0:T(8,128)(2,1)} custom-call(bf16[1024,2048]{1,0:T(8,128)(2,1)} %get-tuple-element.367.left_ref.left_a, bf16[512,2048]{1,0:T(8,128)(2,1)} %join_rows.22.near_ref.near_a, bf16[512,2048]{1,0:T(8,128)(2,1)} %copy-done.23, bf16[1024,2048]{1,0:T(8,128)(2,1)} %get-tuple-element.336.left_ref.left_b, ...), custom_call_target="tpu_custom_call" | custom-call | flops 1048576 | bytes 4096 | tf_op jit(solution)/shard_map/cross_sums/pallas_call | solution.py:864
  670.7 5.4 second_back.3
  681.5 14.8 %cross_sums.6 = bf16[1024,2048]{1,0:T(8,128)(2,1)} custom-call(bf16[1024,2048]{1,0:T(8,128)(2,1)} %get-tuple-element.396.left_ref.left_a, bf16[512,2048]{1,0:T(8,128)(2,1)} %join_rows.19.near_ref.near_a, bf16[512,2048]{1,0:T(8,128)(2,1)} %copy-done.21, bf16[1024,2048]{1,0:T(8,128)(2,1)} %get-tuple-element.356.left_ref.left_b, ...), custom_call_target="tpu_custom_call" | custom-call | flops 1048576 | bytes 4096 | tf_op jit(solution)/shard_map/cross_sums/pallas_call | solution.py:864
  707.6 6.3 project.6.grad_ref
  715.1 27.3 %attend_back.2 = (bf16[1024,512]{1,0:T(8,128)(2,1)S(1)}, bf16[1024,512]{1,0:T(8,128)(2,1)S(1)}, bf16[1024,512]{1,0:T(8,128)(2,1)S(1)}, f32[8,512]{1,0:T(8,128)S(1)}) custom-call(s32[1]{0:T(128)} %bitcast.10.rank_ref, bf16[1024,1536]{1,0:T(8,128)(2,1)S(1)} %copy-done.2, bf16[1024,1536]{1,0:T(8,128)(2,1)S(1)} %copy-done.2, bf16[1024,1536]{1,0:T(8,128)(2,1)S(1)} %copy-done.2, ...), custom_call_target="tpu_custom_call" | custom-call | flops 1048576 | bytes 4096 | tf_op jit(solution)/shard_map/attend_back/pallas_call | solution.py:673
  755.1 10.7 partial_three.2
  770.9 14.3 %cross_sums.7.refs_0_ = bf16[1024,2048]{1,0:T(8,128)(2,1)} custom-call(bf16[1024,2048]{1,0:T(8,128)(2,1)} %get-tuple-element.396.left_ref.left_a, bf16[512,2048]{1,0:T(8,128)(2,1)} %join_rows.19.near_ref.near_a, bf16[512,2048]{1,0:T(8,128)(2,1)} %copy-done.21, bf16[1024,2048]{1,0:T(8,128)(2,1)} %get-tuple-element.356.left_ref.left_b, ...), custom_call_target="tpu_custom_call" | custom-call | flops 1048576 | bytes 4096 | tf_op jit(solution)/shard_map/cross_sums/pallas_call | solution.py:864
  797.2 18.0 %collective-permute-done.47.got_ref = bf16[256,2048]{1,0:T(8,128)(2,1)} collective-permute-done((bf16[256,2048]{1,0:T(8,128)(2,1)}, bf16[256,2048]{1,0:T(8,128)(2,1)}, u32[]{:S(2)}, u32[]{:S(2)}) %collective-permute-start.47) | collective-permute-done | bytes 1048608 | tf_op jit(solution)/shard_map/ppermute | solution.py:1399
  835.7 6.2 project.7.grad_ref
  843.1 27.3 %attend_back.3 = (bf16[1024,512]{1,0:T(8,128)(2,1)S(1)}, bf16[1024,512]{1,0:T(8,128)(2,1)S(1)}, bf16[1024,512]{1,0:T(8,128)(2,1)S(1)}, f32[8,512]{1,0:T(8,128)S(1)}) custom-call(s32[1]{0:T(128)} %bitcast.10.rank_ref, bf16[1024,1536]{1,0:T(8,128)(2,1)S(1)} %copy-done, bf16[1024,1536]{1,0:T(8,128)(2,1)S(1)} %copy-done, bf16[1024,1536]{1,0:T(8,128)(2,1)S(1)} %copy-done, ...), custom_call_target="tpu_custom_call" | custom-call | flops 1048576 | bytes 4096 | tf_op jit(solution)/shard_map/attend_back/pallas_call | solution.py:673
  873.4 9.9 collective-permute-done.50.got_ref
  893.6 10.5 partial_three.3
  904.1 9.1 cross_pair.4
  925.3 10.7 cross_pair.5
  936.0 6.9 collective-permute-done.56.refs_3_
  945.2 8.7 drop_rows.2
  968.9 8.8 cross_pair.6.refs_0_
  981.4 7.0 collective-permute-done.54.refs_2_
  1013.7 19.6 %collective-permute-done.61.refs_2_ = bf16[256,2048]{1,0:T(8,128)(2,1)} collective-permute-done((bf16[256,2048]{1,0:T(8,128)(2,1)}, bf16[256,2048]{1,0:T(8,128)(2,1)}, u32[]{:S(2)}, u32[]{:S(2)}) %collective-permute-start.61) | collective-permute-done | bytes 1048608 | tf_op jit(solution)/shard_map/ppermute | solution.py:1404
  1040.7 10.6 cross_pair.7.refs_0_
  1068.1 6.2 all-to-all-start.6
  1078.2 7.4 collective-permute-done.66.refs_2_
  1094.8 8.5 collective-permute-start.78
  1105.3 13.8 %stack_pieces.2 = f32[2048,2048]{1,0:T(8,128)} custom-call(s32[1]{0:T(128)} %bitcast.51.own_ref, bf16[1024,2048]{1,0:T(8,128)(2,1)} %join_rows.28.near_ref, bf16[1024,2048]{1,0:T(8,128)(2,1)} %copy-done.36), custom_call_target="tpu_custom_call" | custom-call | flops 1048576 | bytes 4096 | tf_op jit(solution)/shard_map/stack_pieces/pallas_call | solution.py:1047
  1119.2 27.1 %all-to-all-done.6 = bf16[32,72,512]{2,1,0:T(8,128)(2,1)S(1)} async-done(((bf16[32,72,512]{2,1,0:T(8,128)(2,1)}), bf16[32,72,512]{2,1,0:T(8,128)(2,1)S(1)}, u32[]{:S(2)}, u32[]{:S(2)}) %all-to-all-start.6) | async-done | bytes 2359328 | tf_op jit(solution)/shard_map/all_to_all | solution.py:1545
  1147.7 8.7 drop_rows.3
  1163.5 9.9 collective-permute-done.76
  1183.9 10.7 collective-permute-done.70.refs_1_
  1199.1 14.3 %stack_pieces.3 = f32[2048,2048]{1,0:T(8,128)} custom-call(s32[1]{0:T(128)} %bitcast.51.own_ref, bf16[1024,2048]{1,0:T(8,128)(2,1)} %join_rows.29.near_ref, bf16[1024,2048]{1,0:T(8,128)(2,1)} %copy-done.35), custom_call_target="tpu_custom_call" | custom-call | flops 1048576 | bytes 4096 | tf_op jit(solution)/shard_map/stack_pieces/pallas_call | solution.py:1047
  1230.8 22.2 %all-to-all-done.7 = bf16[2,1024,1,512]{3,0,2,1:T(2,128)(2,1)S(1)} async-done(((bf16[2,1024,1,512]{3,0,2,1:T(2,128)(2,1)}), bf16[2,1024,1,512]{3,0,2,1:T(2,128)(2,1)S(1)}, u32[]{:S(2)}, u32[]{:S(2)}) %all-to-all-start.7) | async-done | bytes 2097184 | tf_op jit(solution)/shard_map/all_to_all | solution.py:1611
  1255.5 7.0 stack_heads.2
  1273.6 7.0 stack_heads.3
  (551 shorter events, 435.2 us)
Async XLA Ops:
  9.3 29.1 %collective-permute-start = (bf16[264,2048]{1,0:T(8,128)(2,1)}, bf16[264,2048]{1,0:T(8,128)(2,1)S(1)}, u32[]{:S(2)}, u32[]{:S(2)}) collective-permute-start(bf16[264,2048]{1,0:T(8,128)(2,1)} %get-tuple-element.258.refs_0_), channel_id=1, source_target_pairs={{0,1},{1,2},{2,3},{3,0},{4,5},{5,6},{6,7},{7,4},{8,9},{9,10},{10,1... | collective-permute-start | bytes 3244040 | tf_op jit(solution)/shard_map/ppermute | solution.py:1404
  14.3 30.5 %all-to-all-start = ((bf16[2,128,8,512]{3,1,0,2:T(8,128)(2,1)}), bf16[2,128,8,512]{3,1,0,2:T(8,128)(2,1)S(1)}, u32[]{:S(2)}, u32[]{:S(2)}) async-start(bf16[2,128,8,512]{3,1,0,2:T(8,128)(2,1)} %copy.155), calls=%async_computation | async-start | bytes 4194304 | tf_op jit(solution)/shard_map/all_to_all | solution.py:1541
  38.4 27.0 %collective-permute-start.1 = (bf16[264,2048]{1,0:T(8,128)(2,1)S(1)}, bf16[264,2048]{1,0:T(8,128)(2,1)}, u32[]{:S(2)}, u32[]{:S(2)}) collective-permute-start(bf16[264,2048]{1,0:T(8,128)(2,1)S(1)} %collective-permute-done.refs_1_), channel_id=1, source_target_pairs={{0,1},{1,2},{2,3},{3,0},{4,5},{5,6},{6,7},{7,4},{8,9},{9,10},{10,1... | collective-permute-start | bytes 3244040 | tf_op jit(solution)/shard_map/ppermute | solution.py:1404
  74.0 70.3 %all-to-all-start.1 = ((bf16[32,72,512]{2,1,0:T(8,128)(2,1)}), bf16[32,72,512]{2,1,0:T(8,128)(2,1)S(1)}, u32[]{:S(2)}, u32[]{:S(2)}) async-start(bf16[32,72,512]{2,1,0:T(8,128)(2,1)} %bitcast.129), calls=%async_computation.1 | async-start | bytes 4718592 | tf_op jit(solution)/shard_map/all_to_all | solution.py:1545
  77.9 63.0 %collective-permute-start.2 = (bf16[264,2048]{1,0:T(8,128)(2,1)S(1)}, bf16[264,2048]{1,0:T(8,128)(2,1)}, u32[]{:S(2)}, u32[]{:S(2)}) collective-permute-start(bf16[264,2048]{1,0:T(8,128)(2,1)S(1)} %copy-done.49), channel_id=1, source_target_pairs={{0,3},{1,0},{2,1},{3,2},{4,7},{5,4},{6,5},{7,6},{8,11},{9,8},{10,9... | collective-permute-start | bytes 3244040 | tf_op jit(solution)/shard_map/ppermute | solution.py:1404
  82.1 75.4 %collective-permute-start.4 = (bf16[264,2048]{1,0:T(8,128)(2,1)}, bf16[264,2048]{1,0:T(8,128)(2,1)}, u32[]{:S(2)}, u32[]{:S(2)}) collective-permute-start(bf16[264,2048]{1,0:T(8,128)(2,1)} %copy-done.50), channel_id=1, source_target_pairs={{0,16},{16,0},{1,17},{17,1},{2,18},{18,2},{3,19},{19,3},{4,20},{20... | collective-permute-start | bytes 3244040 | tf_op jit(solution)/shard_map/ppermute | solution.py:1399
  83.7 73.8 %collective-permute-start.5 = (bf16[264,2048]{1,0:T(8,128)(2,1)}, bf16[264,2048]{1,0:T(8,128)(2,1)}, u32[]{:S(2)}, u32[]{:S(2)}) collective-permute-start(bf16[264,2048]{1,0:T(8,128)(2,1)} %collective-permute-done.1.refs_2_), channel_id=1, source_target_pairs={{0,16},{16,0},{1,17},{17,1},{2,18},{18,2},{3,19},{19,3},{4,20},{20... | collective-permute-start | bytes 3244040 | tf_op jit(solution)/shard_map/ppermute | solution.py:1399
  141.0 33.6 %collective-permute-start.6 = (bf16[264,2048]{1,0:T(8,128)(2,1)}, bf16[264,2048]{1,0:T(8,128)(2,1)S(1)}, u32[]{:S(2)}, u32[]{:S(2)}) collective-permute-start(bf16[264,2048]{1,0:T(8,128)(2,1)} %collective-permute-done.2.refs_3_), channel_id=1, source_target_pairs={{0,16},{16,0},{1,17},{17,1},{2,18},{18,2},{3,19},{19,3},{4,20},{20... | collective-permute-start | bytes 3244040 | tf_op jit(solution)/shard_map/ppermute | solution.py:1399
  153.3 29.4 %collective-permute-start.3 = (bf16[256,2048]{1,0:T(8,128)(2,1)}, bf16[256,2048]{1,0:T(8,128)(2,1)S(1)}, u32[]{:S(2)}, u32[]{:S(2)}) collective-permute-start(bf16[256,2048]{1,0:T(8,128)(2,1)} %norm_in.2.refs_0_), channel_id=1, source_target_pairs={{0,8},{8,0},{1,9},{9,1},{2,10},{10,2},{3,11},{11,3},{4,12},{12,4},... | collective-permute-start | bytes 3145736 | tf_op jit(solution)/shard_map/ppermute | solution.py:1399
  187.6 45.3 %collective-permute-start.7 = (bf16[512,2048]{1,0:T(8,128)(2,1)}, bf16[512,2048]{1,0:T(8,128)(2,1)S(1)}, u32[]{:S(2)}, u32[]{:S(2)}) collective-permute-start(bf16[512,2048]{1,0:T(8,128)(2,1)} %join_rows.16.near_ref.refs_4_), channel_id=1, source_target_pairs={{0,4},{4,0},{1,5},{5,1},{2,6},{6,2},{3,7},{7,3},{8,12},{12,8},{9,1... | collective-permute-start | bytes 6291464 | tf_op jit(solution)/shard_map/ppermute | solution.py:1399
  189.7 31.5 %all-to-all-start.2 = ((bf16[2,128,8,512]{3,1,0,2:T(8,128)(2,1)}), bf16[2,128,8,512]{3,1,0,2:T(8,128)(2,1)}, u32[]{:S(2)}, u32[]{:S(2)}) async-start(bf16[2,128,8,512]{3,1,0,2:T(8,128)(2,1)} %copy.158), calls=%async_computation.2 | async-start | bytes 4194304 | tf_op jit(solution)/shard_map/all_to_all | solution.py:1541
  196.3 36.7 %collective-permute-start.9 = (bf16[256,2048]{1,0:T(8,128)(2,1)}, bf16[256,2048]{1,0:T(8,128)(2,1)}, u32[]{:S(2)}, u32[]{:S(2)}) collective-permute-start(bf16[256,2048]{1,0:T(8,128)(2,1)} %flipped.2.refs_0_), channel_id=1, source_target_pairs={{0,1},{1,2},{2,3},{3,0},{4,5},{5,6},{6,7},{7,4},{8,9},{9,10},{10,1... | collective-permute-start | bytes 3145736 | tf_op jit(solution)/shard_map/ppermute | solution.py:1404
  206.4 45.7 %collective-permute-start.8 = (bf16[256,2048]{1,0:T(8,128)(2,1)}, bf16[256,2048]{1,0:T(8,128)(2,1)}, u32[]{:S(2)}, u32[]{:S(2)}) collective-permute-start(bf16[256,2048]{1,0:T(8,128)(2,1)} %flipped.2.refs_0_), channel_id=1, source_target_pairs={{0,3},{1,0},{2,1},{3,2},{4,7},{5,4},{6,5},{7,6},{8,11},{9,8},{10,9... | collective-permute-start | bytes 3145736 | tf_op jit(solution)/shard_map/ppermute | solution.py:1404
  206.5 78.5 %collective-permute-start.10 = (bf16[256,2048]{1,0:T(8,128)(2,1)}, bf16[256,2048]{1,0:T(8,128)(2,1)}, u32[]{:S(2)}, u32[]{:S(2)}) collective-permute-start(bf16[256,2048]{1,0:T(8,128)(2,1)} %norm_in.3.refs_0_), channel_id=1, source_target_pairs={{0,8},{8,0},{1,9},{9,1},{2,10},{10,2},{3,11},{11,3},{4,12},{12,4},... | collective-permute-start | bytes 3145736 | tf_op jit(solution)/shard_map/ppermute | solution.py:1399
  233.0 52.0 %collective-permute-start.12 = (bf16[256,2048]{1,0:T(8,128)(2,1)}, bf16[256,2048]{1,0:T(8,128)(2,1)}, u32[]{:S(2)}, u32[]{:S(2)}) collective-permute-start(bf16[256,2048]{1,0:T(8,128)(2,1)} %collective-permute-done.9.refs_1_), channel_id=1, source_target_pairs={{0,16},{16,0},{1,17},{17,1},{2,18},{18,2},{3,19},{19,3},{4,20},{20... | collective-permute-start | bytes 3145736 | tf_op jit(solution)/shard_map/ppermute | solution.py:1399
  233.6 51.4 %collective-permute-start.11 = (bf16[256,2048]{1,0:T(8,128)(2,1)}, bf16[256,2048]{1,0:T(8,128)(2,1)}, u32[]{:S(2)}, u32[]{:S(2)}) collective-permute-start(bf16[256,2048]{1,0:T(8,128)(2,1)} %collective-permute-done.9.refs_1_), channel_id=1, source_target_pairs={{0,1},{1,2},{2,3},{3,0},{4,5},{5,6},{6,7},{7,4},{8,9},{9,10},{10,1... | collective-permute-start | bytes 3145736 | tf_op jit(solution)/shard_map/ppermute | solution.py:1404
  294.9 27.7 %collective-permute-start.13 = (bf16[512,2048]{1,0:T(8,128)(2,1)}, bf16[512,2048]{1,0:T(8,128)(2,1)}, u32[]{:S(2)}, u32[]{:S(2)}) collective-permute-start(bf16[512,2048]{1,0:T(8,128)(2,1)} %get-tuple-element.284), channel_id=1, source_target_pairs={{0,4},{4,0},{1,5},{5,1},{2,6},{6,2},{3,7},{7,3},{8,12},{12,8},{9,1... | collective-permute-start | bytes 6291464 | tf_op jit(solution)/shard_map/ppermute | solution.py:1399
  300.4 56.7 %collective-permute-start.18 = (bf16[256,2048]{1,0:T(8,128)(2,1)}, bf16[256,2048]{1,0:T(8,128)(2,1)}, u32[]{:S(2)}, u32[]{:S(2)}) collective-permute-start(bf16[256,2048]{1,0:T(8,128)(2,1)} %collective-permute-done.11.refs_2_), channel_id=1, source_target_pairs={{0,16},{16,0},{1,17},{17,1},{2,18},{18,2},{3,19},{19,3},{4,20},{20... | collective-permute-start | bytes 3145736 | tf_op jit(solution)/shard_map/ppermute | solution.py:1399
  300.5 56.6 %collective-permute-start.17 = (bf16[256,2048]{1,0:T(8,128)(2,1)}, bf16[256,2048]{1,0:T(8,128)(2,1)}, u32[]{:S(2)}, u32[]{:S(2)}) collective-permute-start(bf16[256,2048]{1,0:T(8,128)(2,1)} %get-tuple-element.292.refs_0_), channel_id=1, source_target_pairs={{0,1},{1,2},{2,3},{3,0},{4,5},{5,6},{6,7},{7,4},{8,9},{9,10},{10,1... | collective-permute-start | bytes 3145736 | tf_op jit(solution)/shard_map/ppermute | solution.py:1404
  326.8 30.3 %collective-permute-start.16 = (bf16[256,2048]{1,0:T(8,128)(2,1)}, bf16[256,2048]{1,0:T(8,128)(2,1)}, u32[]{:S(2)}, u32[]{:S(2)}) collective-permute-start(bf16[256,2048]{1,0:T(8,128)(2,1)} %get-tuple-element.291), channel_id=1, source_target_pairs={{0,8},{8,0},{1,9},{9,1},{2,10},{10,2},{3,11},{11,3},{4,12},{12,4},... | collective-permute-start | bytes 3145736 | tf_op jit(solution)/shard_map/ppermute | solution.py:1399
  328.8 32.6 %collective-permute-start.21 = (bf16[256,2048]{1,0:T(8,128)(2,1)}, bf16[256,2048]{1,0:T(8,128)(2,1)}, u32[]{:S(2)}, u32[]{:S(2)}) collective-permute-start(bf16[256,2048]{1,0:T(8,128)(2,1)} %get-tuple-element.292.refs_0_), channel_id=1, source_target_pairs={{0,3},{1,0},{2,1},{3,2},{4,7},{5,4},{6,5},{7,6},{8,11},{9,8},{10,9... | collective-permute-start | bytes 3145736 | tf_op jit(solution)/shard_map/ppermute | solution.py:1404
  367.3 91.9 %all-to-all-start.3 = ((bf16[32,72,512]{2,1,0:T(8,128)(2,1)}), bf16[32,72,512]{2,1,0:T(8,128)(2,1)}, u32[]{:S(2)}, u32[]{:S(2)}) async-start(bf16[32,72,512]{2,1,0:T(8,128)(2,1)} %bitcast.128), calls=%async_computation.3 | async-start | bytes 4718592 | tf_op jit(solution)/shard_map/all_to_all | solution.py:1545
  370.9 50.0 %collective-permute-start.20 = (bf16[256,2048]{1,0:T(8,128)(2,1)}, bf16[256,2048]{1,0:T(8,128)(2,1)}, u32[]{:S(2)}, u32[]{:S(2)}) collective-permute-start(bf16[256,2048]{1,0:T(8,128)(2,1)} %collective-permute-done.17.refs_1_), channel_id=1, source_target_pairs={{0,16},{16,0},{1,17},{17,1},{2,18},{18,2},{3,19},{19,3},{4,20},{20... | collective-permute-start | bytes 3145736 | tf_op jit(solution)/shard_map/ppermute | solution.py:1399
  372.5 48.3 %collective-permute-start.19 = (bf16[256,2048]{1,0:T(8,128)(2,1)}, bf16[256,2048]{1,0:T(8,128)(2,1)}, u32[]{:S(2)}, u32[]{:S(2)}) collective-permute-start(bf16[256,2048]{1,0:T(8,128)(2,1)} %get-tuple-element.298.refs_0_), channel_id=1, source_target_pairs={{0,8},{8,0},{1,9},{9,1},{2,10},{10,2},{3,11},{11,3},{4,12},{12,4},... | collective-permute-start | bytes 3145736 | tf_op jit(solution)/shard_map/ppermute | solution.py:1399
  424.7 28.2 %collective-permute-start.24 = (bf16[256,2048]{1,0:T(8,128)(2,1)}, bf16[256,2048]{1,0:T(8,128)(2,1)S(1)}, u32[]{:S(2)}, u32[]{:S(2)}) collective-permute-start(bf16[256,2048]{1,0:T(8,128)(2,1)} %collective-permute-done.17.refs_1_), channel_id=1, source_target_pairs={{0,1},{1,2},{2,3},{3,0},{4,5},{5,6},{6,7},{7,4},{8,9},{9,10},{10,1... | collective-permute-start | bytes 3145736 | tf_op jit(solution)/shard_map/ppermute | solution.py:1404
  424.9 28.0 %collective-permute-start.26 = (bf16[256,2048]{1,0:T(8,128)(2,1)}, bf16[256,2048]{1,0:T(8,128)(2,1)S(1)}, u32[]{:S(2)}, u32[]{:S(2)}) collective-permute-start(bf16[256,2048]{1,0:T(8,128)(2,1)} %collective-permute-done.21.refs_3_), channel_id=1, source_target_pairs={{0,16},{16,0},{1,17},{17,1},{2,18},{18,2},{3,19},{19,3},{4,20},{20... | collective-permute-start | bytes 3145736 | tf_op jit(solution)/shard_map/ppermute | solution.py:1399
  490.0 43.1 %collective-permute-start.32 = (bf16[256,2048]{1,0:T(8,128)(2,1)}, bf16[256,2048]{1,0:T(8,128)(2,1)S(1)}, u32[]{:S(2)}, u32[]{:S(2)}) collective-permute-start(bf16[256,2048]{1,0:T(8,128)(2,1)} %get-tuple-element.495.refs_0_), channel_id=1, source_target_pairs={{0,8},{8,0},{1,9},{9,1},{2,10},{10,2},{3,11},{11,3},{4,12},{12,4},... | collective-permute-start | bytes 3145736 | tf_op jit(solution)/shard_map/ppermute | solution.py:1399
  538.0 30.4 %collective-permute-start.31 = (bf16[256,2048]{1,0:T(8,128)(2,1)S(1)}, bf16[256,2048]{1,0:T(8,128)(2,1)S(1)}, u32[]{:S(2)}, u32[]{:S(2)}) collective-permute-start(bf16[256,2048]{1,0:T(8,128)(2,1)S(1)} %copy-done.37), channel_id=1, source_target_pairs={{0,8},{8,0},{1,9},{9,1},{2,10},{10,2},{3,11},{11,3},{4,12},{12,4},... | collective-permute-start | bytes 3145736 | tf_op jit(solution)/shard_map/ppermute | solution.py:1399
  621.6 54.5 %collective-permute-start.30 = (bf16[512,2048]{1,0:T(8,128)(2,1)}, bf16[512,2048]{1,0:T(8,128)(2,1)S(1)}, u32[]{:S(2)}, u32[]{:S(2)}) collective-permute-start(bf16[512,2048]{1,0:T(8,128)(2,1)} %get-tuple-element.334), channel_id=1, source_target_pairs={{0,4},{4,0},{1,5},{5,1},{2,6},{6,2},{3,7},{7,3},{8,12},{12,8},{9,1... | collective-permute-start | bytes 6291464 | tf_op jit(solution)/shard_map/ppermute | solution.py:1399
  642.3 28.4 %collective-permute-start.37 = (bf16[256,2048]{1,0:T(8,128)(2,1)}, bf16[256,2048]{1,0:T(8,128)(2,1)}, u32[]{:S(2)}, u32[]{:S(2)}) collective-permute-start(bf16[256,2048]{1,0:T(8,128)(2,1)} %get-tuple-element.362), channel_id=1, source_target_pairs={{0,8},{8,0},{1,9},{9,1},{2,10},{10,2},{3,11},{11,3},{4,12},{12,4},... | collective-permute-start | bytes 3145736 | tf_op jit(solution)/shard_map/ppermute | solution.py:1399
  643.6 105.9 %collective-permute-start.43 = (bf16[1024,2048]{1,0:T(8,128)(2,1)}, bf16[1024,2048]{1,0:T(8,128)(2,1)}, u32[]{:S(2)}, u32[]{:S(2)}) collective-permute-start(bf16[1024,2048]{1,0:T(8,128)(2,1)} %cross_sums.4), channel_id=1, source_target_pairs={{0,16},{16,0},{1,17},{17,1},{2,18},{18,2},{3,19},{19,3},{4,20},{20... | collective-permute-start | bytes 12582920 | tf_op jit(solution)/shard_map/ppermute | solution.py:1399
  653.6 42.7 %collective-permute-start.40 = (bf16[256,2048]{1,0:T(8,128)(2,1)}, bf16[256,2048]{1,0:T(8,128)(2,1)}, u32[]{:S(2)}, u32[]{:S(2)}) collective-permute-start(bf16[256,2048]{1,0:T(8,128)(2,1)} %get-tuple-element.365.refs_0_), channel_id=1, source_target_pairs={{0,8},{8,0},{1,9},{9,1},{2,10},{10,2},{3,11},{11,3},{4,12},{12,4},... | collective-permute-start | bytes 3145736 | tf_op jit(solution)/shard_map/ppermute | solution.py:1399
  654.4 46.4 %collective-permute-start.42 = (bf16[512,2048]{1,0:T(8,128)(2,1)}, bf16[512,2048]{1,0:T(8,128)(2,1)S(1)}, u32[]{:S(2)}, u32[]{:S(2)}) collective-permute-start(bf16[512,2048]{1,0:T(8,128)(2,1)} %get-tuple-element.338), channel_id=1, source_target_pairs={{0,4},{4,0},{1,5},{5,1},{2,6},{6,2},{3,7},{7,3},{8,12},{12,8},{9,1... | collective-permute-start | bytes 6291464 | tf_op jit(solution)/shard_map/ppermute | solution.py:1399
  700.1 45.3 %collective-permute-start.44 = (bf16[256,2048]{1,0:T(8,128)(2,1)}, bf16[256,2048]{1,0:T(8,128)(2,1)}, u32[]{:S(2)}, u32[]{:S(2)}) collective-permute-start(bf16[256,2048]{1,0:T(8,128)(2,1)} %get-tuple-element.370.refs_0_), channel_id=1, source_target_pairs={{0,8},{8,0},{1,9},{9,1},{2,10},{10,2},{3,11},{11,3},{4,12},{12,4},... | collective-permute-start | bytes 3145736 | tf_op jit(solution)/shard_map/ppermute | solution.py:1399
  766.1 122.0 %collective-permute-start.49 = (bf16[1024,2048]{1,0:T(8,128)(2,1)}, bf16[1024,2048]{1,0:T(8,128)(2,1)}, u32[]{:S(2)}, u32[]{:S(2)}) collective-permute-start(bf16[1024,2048]{1,0:T(8,128)(2,1)} %cross_sums.6), channel_id=1, source_target_pairs={{0,16},{16,0},{1,17},{17,1},{2,18},{18,2},{3,19},{19,3},{4,20},{20... | collective-permute-start | bytes 12582920 | tf_op jit(solution)/shard_map/ppermute | solution.py:1399
  768.0 47.3 %collective-permute-start.47 = (bf16[256,2048]{1,0:T(8,128)(2,1)}, bf16[256,2048]{1,0:T(8,128)(2,1)}, u32[]{:S(2)}, u32[]{:S(2)}) collective-permute-start(bf16[256,2048]{1,0:T(8,128)(2,1)} %get-tuple-element.379), channel_id=1, source_target_pairs={{0,8},{8,0},{1,9},{9,1},{2,10},{10,2},{3,11},{11,3},{4,12},{12,4},... | collective-permute-start | bytes 3145736 | tf_op jit(solution)/shard_map/ppermute | solution.py:1399
  769.5 57.9 %collective-permute-start.48 = (bf16[256,2048]{1,0:T(8,128)(2,1)}, bf16[256,2048]{1,0:T(8,128)(2,1)}, u32[]{:S(2)}, u32[]{:S(2)}) collective-permute-start(bf16[256,2048]{1,0:T(8,128)(2,1)} %add_pieces.16), channel_id=1, source_target_pairs={{0,1},{1,2},{2,3},{3,0},{4,5},{5,6},{6,7},{7,4},{8,9},{9,10},{10,1... | collective-permute-start | bytes 3145736 | tf_op jit(solution)/shard_map/ppermute | solution.py:1404
  830.5 114.7 %all-to-all-start.4 = ((bf16[32,72,512]{2,1,0:T(8,128)(2,1)}), bf16[32,72,512]{2,1,0:T(8,128)(2,1)}, u32[]{:S(2)}, u32[]{:S(2)}) async-start(bf16[32,72,512]{2,1,0:T(8,128)(2,1)} %bitcast.127), calls=%async_computation.4 | async-start | bytes 4718592 | tf_op jit(solution)/shard_map/all_to_all | solution.py:1545
  834.1 49.3 %collective-permute-start.50 = (bf16[256,2048]{1,0:T(8,128)(2,1)}, bf16[256,2048]{1,0:T(8,128)(2,1)}, u32[]{:S(2)}, u32[]{:S(2)}) collective-permute-start(bf16[256,2048]{1,0:T(8,128)(2,1)} %get-tuple-element.399), channel_id=1, source_target_pairs={{0,8},{8,0},{1,9},{9,1},{2,10},{10,2},{3,11},{11,3},{4,12},{12,4},... | collective-permute-start | bytes 3145736 | tf_op jit(solution)/shard_map/ppermute | solution.py:1399
  913.3 80.5 %collective-permute-start.52 = (bf16[512,2048]{1,0:T(8,128)(2,1)}, bf16[512,2048]{1,0:T(8,128)(2,1)}, u32[]{:S(2)}, u32[]{:S(2)}) collective-permute-start(bf16[512,2048]{1,0:T(8,128)(2,1)} %cross_pair.4), channel_id=1, source_target_pairs={{0,16},{16,0},{1,17},{17,1},{2,18},{18,2},{3,19},{19,3},{4,20},{20... | collective-permute-start | bytes 6291464 | tf_op jit(solution)/shard_map/ppermute | solution.py:1399
  915.2 27.8 %collective-permute-start.56 = (bf16[256,2048]{1,0:T(8,128)(2,1)S(1)}, bf16[256,2048]{1,0:T(8,128)(2,1)S(1)}, u32[]{:S(2)}, u32[]{:S(2)}) collective-permute-start(bf16[256,2048]{1,0:T(8,128)(2,1)S(1)} %copy-done.52), channel_id=1, source_target_pairs={{0,3},{1,0},{2,1},{3,2},{4,7},{5,4},{6,5},{7,6},{8,11},{9,8},{10,9... | collective-permute-start | bytes 3145736 | tf_op jit(solution)/shard_map/ppermute | solution.py:1404
  919.4 46.5 %collective-permute-start.55 = (bf16[256,2048]{1,0:T(8,128)(2,1)S(1)}, bf16[256,2048]{1,0:T(8,128)(2,1)}, u32[]{:S(2)}, u32[]{:S(2)}) collective-permute-start(bf16[256,2048]{1,0:T(8,128)(2,1)S(1)} %copy-done.54), channel_id=1, source_target_pairs={{0,1},{1,2},{2,3},{3,0},{4,5},{5,6},{6,7},{7,4},{8,9},{9,10},{10,1... | collective-permute-start | bytes 3145736 | tf_op jit(solution)/shard_map/ppermute | solution.py:1404
  919.4 69.0 %collective-permute-start.54 = (bf16[256,2048]{1,0:T(8,128)(2,1)}, bf16[256,2048]{1,0:T(8,128)(2,1)}, u32[]{:S(2)}, u32[]{:S(2)}) collective-permute-start(bf16[256,2048]{1,0:T(8,128)(2,1)} %add_pieces.19), channel_id=1, source_target_pairs={{0,1},{1,2},{2,3},{3,0},{4,5},{5,6},{6,7},{7,4},{8,9},{9,10},{10,1... | collective-permute-start | bytes 3145736 | tf_op jit(solution)/shard_map/ppermute | solution.py:1404
  924.8 69.6 %collective-permute-start.53 = (bf16[256,2048]{1,0:T(8,128)(2,1)}, bf16[256,2048]{1,0:T(8,128)(2,1)}, u32[]{:S(2)}, u32[]{:S(2)}) collective-permute-start(bf16[256,2048]{1,0:T(8,128)(2,1)} %get-tuple-element.425), channel_id=1, source_target_pairs={{0,8},{8,0},{1,9},{9,1},{2,10},{10,2},{3,11},{11,3},{4,12},{12,4},... | collective-permute-start | bytes 3145736 | tf_op jit(solution)/shard_map/ppermute | solution.py:1399
  944.0 113.3 %collective-permute-start.59 = (bf16[512,2048]{1,0:T(8,128)(2,1)}, bf16[512,2048]{1,0:T(8,128)(2,1)S(1)}, u32[]{:S(2)}, u32[]{:S(2)}) collective-permute-start(bf16[512,2048]{1,0:T(8,128)(2,1)} %cross_pair.5), channel_id=1, source_target_pairs={{0,16},{16,0},{1,17},{17,1},{2,18},{18,2},{3,19},{19,3},{4,20},{20... | collective-permute-start | bytes 6291464 | tf_op jit(solution)/shard_map/ppermute | solution.py:1399
  959.0 77.6 %all-to-all-start.5 = ((bf16[2,1024,1,512]{3,0,2,1:T(2,128)(2,1)}), bf16[2,1024,1,512]{3,0,2,1:T(2,128)(2,1)}, u32[]{:S(2)}, u32[]{:S(2)}) async-start(bf16[2,1024,1,512]{3,0,2,1:T(2,128)(2,1)} %copy.167), calls=%async_computation.5 | async-start | bytes 4194304 | tf_op jit(solution)/shard_map/all_to_all | solution.py:1611
  965.9 45.0 %collective-permute-start.62 = (bf16[256,2048]{1,0:T(8,128)(2,1)}, bf16[256,2048]{1,0:T(8,128)(2,1)}, u32[]{:S(2)}, u32[]{:S(2)}) collective-permute-start(bf16[256,2048]{1,0:T(8,128)(2,1)} %add_pieces.20), channel_id=1, source_target_pairs={{0,3},{1,0},{2,1},{3,2},{4,7},{5,4},{6,5},{7,6},{8,11},{9,8},{10,9... | collective-permute-start | bytes 3145736 | tf_op jit(solution)/shard_map/ppermute | solution.py:1404
  991.6 41.7 %collective-permute-start.61 = (bf16[256,2048]{1,0:T(8,128)(2,1)}, bf16[256,2048]{1,0:T(8,128)(2,1)}, u32[]{:S(2)}, u32[]{:S(2)}) collective-permute-start(bf16[256,2048]{1,0:T(8,128)(2,1)} %add_pieces.22), channel_id=1, source_target_pairs={{0,1},{1,2},{2,3},{3,0},{4,5},{5,6},{6,7},{7,4},{8,9},{9,10},{10,1... | collective-permute-start | bytes 3145736 | tf_op jit(solution)/shard_map/ppermute | solution.py:1404
  993.9 69.9 %collective-permute-start.57 = (bf16[256,2048]{1,0:T(8,128)(2,1)S(1)}, bf16[256,2048]{1,0:T(8,128)(2,1)}, u32[]{:S(2)}, u32[]{:S(2)}) collective-permute-start(bf16[256,2048]{1,0:T(8,128)(2,1)S(1)} %copy-done.38), channel_id=1, source_target_pairs={{0,8},{8,0},{1,9},{9,1},{2,10},{10,2},{3,11},{11,3},{4,12},{12,4},... | collective-permute-start | bytes 3145736 | tf_op jit(solution)/shard_map/ppermute | solution.py:1399
  994.4 69.4 %collective-permute-start.58 = (bf16[256,2048]{1,0:T(8,128)(2,1)S(1)}, bf16[256,2048]{1,0:T(8,128)(2,1)}, u32[]{:S(2)}, u32[]{:S(2)}) collective-permute-start(bf16[256,2048]{1,0:T(8,128)(2,1)S(1)} %copy-done.38), channel_id=1, source_target_pairs={{0,16},{16,0},{1,17},{17,1},{2,18},{18,2},{3,19},{19,3},{4,20},{20... | collective-permute-start | bytes 3145736 | tf_op jit(solution)/shard_map/ppermute | solution.py:1399
  1010.9 44.1 %collective-permute-start.60 = (bf16[128,2048]{1,0:T(8,128)(2,1)}, bf16[128,2048]{1,0:T(8,128)(2,1)}, u32[]{:S(2)}, u32[]{:S(2)}) collective-permute-start(bf16[128,2048]{1,0:T(8,128)(2,1)} %add_pieces.23), channel_id=1, source_target_pairs={{0,1},{1,2},{2,3},{3,0},{4,5},{5,6},{6,7},{7,4},{8,9},{9,10},{10,1... | collective-permute-start | bytes 1572872 | tf_op jit(solution)/shard_map/ppermute | solution.py:1404
  1033.4 41.9 %collective-permute-start.68 = (bf16[128,2048]{1,0:T(8,128)(2,1)}, bf16[128,2048]{1,0:T(8,128)(2,1)}, u32[]{:S(2)}, u32[]{:S(2)}) collective-permute-start(bf16[128,2048]{1,0:T(8,128)(2,1)} %add_pieces.24), channel_id=1, source_target_pairs={{0,3},{1,0},{2,1},{3,2},{4,7},{5,4},{6,5},{7,6},{8,11},{9,8},{10,9... | collective-permute-start | bytes 1572872 | tf_op jit(solution)/shard_map/ppermute | solution.py:1404
  1068.1 78.1 %all-to-all-start.6 = ((bf16[32,72,512]{2,1,0:T(8,128)(2,1)}), bf16[32,72,512]{2,1,0:T(8,128)(2,1)S(1)}, u32[]{:S(2)}, u32[]{:S(2)}) async-start(bf16[32,72,512]{2,1,0:T(8,128)(2,1)} %bitcast.125), calls=%async_computation.6 | async-start | bytes 4718592 | tf_op jit(solution)/shard_map/all_to_all | solution.py:1545
  1092.7 63.6 %collective-permute-start.72 = (bf16[256,2048]{1,0:T(8,128)(2,1)S(1)}, bf16[256,2048]{1,0:T(8,128)(2,1)}, u32[]{:S(2)}, u32[]{:S(2)}) collective-permute-start(bf16[256,2048]{1,0:T(8,128)(2,1)S(1)} %copy-done.39), channel_id=1, source_target_pairs={{0,8},{8,0},{1,9},{9,1},{2,10},{10,2},{3,11},{11,3},{4,12},{12,4},... | collective-permute-start | bytes 3145736 | tf_op jit(solution)/shard_map/ppermute | solution.py:1399
  1093.4 63.0 %collective-permute-start.73 = (bf16[256,2048]{1,0:T(8,128)(2,1)S(1)}, bf16[256,2048]{1,0:T(8,128)(2,1)}, u32[]{:S(2)}, u32[]{:S(2)}) collective-permute-start(bf16[256,2048]{1,0:T(8,128)(2,1)S(1)} %copy-done.39), channel_id=1, source_target_pairs={{0,16},{16,0},{1,17},{17,1},{2,18},{18,2},{3,19},{19,3},{4,20},{20... | collective-permute-start | bytes 3145736 | tf_op jit(solution)/shard_map/ppermute | solution.py:1399
  1094.8 66.1 %collective-permute-start.78 = (bf16[128,2048]{1,0:T(8,128)(2,1)}, bf16[128,2048]{1,0:T(8,128)(2,1)}, u32[]{:S(2)}, u32[]{:S(2)}) collective-permute-start(bf16[128,2048]{1,0:T(8,128)(2,1)} %add_pieces.28), channel_id=1, source_target_pairs={{0,3},{1,0},{2,1},{3,2},{4,7},{5,4},{6,5},{7,6},{8,11},{9,8},{10,9... | collective-permute-start | bytes 1572872 | tf_op jit(solution)/shard_map/ppermute | solution.py:1404
  1103.3 57.6 %collective-permute-start.77 = (bf16[128,2048]{1,0:T(8,128)(2,1)}, bf16[128,2048]{1,0:T(8,128)(2,1)}, u32[]{:S(2)}, u32[]{:S(2)}) collective-permute-start(bf16[128,2048]{1,0:T(8,128)(2,1)} %add_pieces.30), channel_id=1, source_target_pairs={{0,1},{1,2},{2,3},{3,0},{4,5},{5,6},{6,7},{7,4},{8,9},{9,10},{10,1... | collective-permute-start | bytes 1572872 | tf_op jit(solution)/shard_map/ppermute | solution.py:1404
  1180.4 33.0 %collective-permute-start.82 = (bf16[128,2048]{1,0:T(8,128)(2,1)S(1)}, bf16[128,2048]{1,0:T(8,128)(2,1)S(1)}, u32[]{:S(2)}, u32[]{:S(2)}) collective-permute-start(bf16[128,2048]{1,0:T(8,128)(2,1)S(1)} %copy-done.43), channel_id=1, source_target_pairs={{0,8},{8,0},{1,9},{9,1},{2,10},{10,2},{3,11},{11,3},{4,12},{12,4},... | collective-permute-start | bytes 1572872 | tf_op jit(solution)/shard_map/ppermute | solution.py:1399
  1182.1 31.3 %collective-permute-start.83 = (bf16[128,2048]{1,0:T(8,128)(2,1)S(1)}, bf16[128,2048]{1,0:T(8,128)(2,1)S(1)}, u32[]{:S(2)}, u32[]{:S(2)}) collective-permute-start(bf16[128,2048]{1,0:T(8,128)(2,1)S(1)} %copy-done.43), channel_id=1, source_target_pairs={{0,16},{16,0},{1,17},{17,1},{2,18},{18,2},{3,19},{19,3},{4,20},{20... | collective-permute-start | bytes 1572872 | tf_op jit(solution)/shard_map/ppermute | solution.py:1399
  1218.7 36.8 %collective-permute-start.85 = (bf16[512,2048]{1,0:T(8,128)(2,1)}, bf16[512,2048]{1,0:T(8,128)(2,1)}, u32[]{:S(2)}, u32[]{:S(2)}) collective-permute-start(bf16[512,2048]{1,0:T(8,128)(2,1)} %join_rows.30.near_low.near_high), channel_id=1, source_target_pairs={{0,4},{4,0},{1,5},{5,1},{2,6},{6,2},{3,7},{7,3},{8,12},{12,8},{9,1... | collective-permute-start | bytes 6291464 | tf_op jit(solution)/shard_map/ppermute | solution.py:1399
  1222.2 30.8 %all-to-all-start.7 = ((bf16[2,1024,1,512]{3,0,2,1:T(2,128)(2,1)}), bf16[2,1024,1,512]{3,0,2,1:T(2,128)(2,1)S(1)}, u32[]{:S(2)}, u32[]{:S(2)}) async-start(bf16[2,1024,1,512]{3,0,2,1:T(2,128)(2,1)} %copy.170), calls=%async_computation.7 | async-start | bytes 4194304 | tf_op jit(solution)/shard_map/all_to_all | solution.py:1611
  1227.4 35.1 %collective-permute-start.86 = (bf16[64,2048]{1,0:T(8,128)(2,1)}, bf16[64,2048]{1,0:T(8,128)(2,1)S(1)}, u32[]{:S(2)}, u32[]{:S(2)}) collective-permute-start(bf16[64,2048]{1,0:T(8,128)(2,1)} %slice.160), channel_id=1, source_target_pairs={{0,8},{8,0},{1,9},{9,1},{2,10},{10,2},{3,11},{11,3},{4,12},{12,4},... | collective-permute-start | bytes 786440 | tf_op jit(solution)/shard_map/ppermute | solution.py:1399
  1229.3 33.2 %collective-permute-start.87 = (bf16[64,2048]{1,0:T(8,128)(2,1)}, bf16[64,2048]{1,0:T(8,128)(2,1)S(1)}, u32[]{:S(2)}, u32[]{:S(2)}) collective-permute-start(bf16[64,2048]{1,0:T(8,128)(2,1)} %slice.161), channel_id=1, source_target_pairs={{0,16},{16,0},{1,17},{17,1},{2,18},{18,2},{3,19},{19,3},{4,20},{20... | collective-permute-start | bytes 786440 | tf_op jit(solution)/shard_map/ppermute | solution.py:1399
  1230.8 31.7 %collective-permute-start.88 = (f32[192,128]{1,0:T(8,128)S(1)}, f32[192,128]{1,0:T(8,128)S(1)}, u32[]{:S(2)}, u32[]{:S(2)}) collective-permute-start(f32[192,128]{1,0:T(8,128)S(1)} %add.535), channel_id=1, source_target_pairs={{0,1},{1,0},{2,3},{3,2},{4,5},{5,4},{6,7},{7,6},{8,9},{9,8},{10,11... | collective-permute-start | bytes 294920 | tf_op jit(solution)/shard_map/ppermute | solution.py:1866
  (115 other events, 1186.5 us)
